TPU v7x, 32 devices: a whole 2x2x4 slice. The times are simulated.
32 devices in a mesh: groups: 2 (over x), expert: 16 (over z, y, core).
Axes of the slice: x: 2, y: 2, z: 4, core: 2. Of those that a mesh axis runs over, the one named last changes fastest.
Arguments:
- resid: bfloat16 [4096, 4096], P(('groups', 'expert')), parts along dimension 0, may hold values from -6 to 6
- queries: bfloat16 [4096, 4096], P(('groups', 'expert')), parts along dimension 0, may hold values from -8 to 8
- keys: bfloat16 [4096, 256], P(('groups', 'expert')), parts along dimension 0, may hold values from -6 to 6
- values: bfloat16 [4096, 256], P(('groups', 'expert')), parts along dimension 0, may hold values from -6 to 6
- doc_ids: int32 [4096], P(('groups', 'expert')), parts along dimension 0, may hold values from 0 to 3, never falling along the last dimension, each value on 1 to 1280 neighbouring positions
- norm_gain: float32 [4096], replicated, may hold values from 0.1 to 1.9
- routes: int32 [4096, 4], P(('groups', 'expert')), parts along dimension 0, may hold values from 0 to 127, as said below
- route_weights: float32 [4096, 4], P(('groups', 'expert')), parts along dimension 0, may hold values from 0.2 to 1
- w_gate: bfloat16 [16, 4096, 384], P('expert'), may hold values from -0.09375 to 0.09375
- w_up: bfloat16 [16, 4096, 384], P('expert'), may hold values from -0.09375 to 0.09375
- w_down: bfloat16 [16, 384, 4096], P('expert'), may hold values from -0.15625 to 0.15625
Outputs:
- layer_out: bfloat16 [4096, 4096], P(('groups', 'expert')), parts along dimension 0
There are 2 independent parts, one for each index of `groups`. A program takes and returns all parts, laid end to end along the dimension named above; an argument that names none is the same for every part. Nothing has to cross between parts.
Inputs may be any that keep to these rules, and one draw needn't show every extreme that they name: Each token names 4 different experts; in the tokens of one device no expert is named by more than 6 routes, and in every draw some expert below 4 is named by exactly 6 routes in the tokens of every device. `doc_ids`: document ids never fall along the sequence; no document is longer than 1280 tokens.
All inputs are finite; a program needn't handle non-finite values.
Results may differ from a plain program's by a relative error of at most 0.0045.
Values may be sent and summed in bfloat16 or wider, within the bound.
No kernel may reach another device: no remote copies, remote signals or barrier semaphores. Data moves between devices by JAX's collectives and lax.ppermute only.
A program may use at most 128 MiB of HBM per device.

v0:
```python
import functools
import math

import jax
import jax.numpy as jnp
from jax import lax
from jax.experimental import pallas as pl
from jax.experimental.pallas import tpu as pltpu
from jax.sharding import PartitionSpec as P

HEAD = 128
QUERY_HEADS = 32
KV_HEADS = 2
GROUP = QUERY_HEADS // KV_HEADS
SHARDS = 4
SLOTS = 8
TILE = 128
KEYS = 256
KV_ROWS = TILE + 16
SCALE = 1.0 / math.sqrt(HEAD)
LOW = -1e30
EXTRA = 16
F32 = jnp.float32
BF16 = jnp.bfloat16
VMEM = pl.BlockSpec(memory_space=pltpu.VMEM)
SMEM = pl.BlockSpec(memory_space=pltpu.SMEM)
ANY = pl.BlockSpec(memory_space=pl.ANY)
HBM = pl.BlockSpec(memory_space=pltpu.HBM)


def dot(a, b, ca=1, cb=0):
    return lax.dot_general(a, b, (((ca,), (cb,)), ((), ())), preferred_element_type=F32)


def reach(n):
    longest = n * TILE // 2 + 256
    return (longest - 1 + TILE - 1) // TILE


def slot_rows(routes, experts):
    members = jnp.concatenate(
        [jnp.max((routes == e).astype(F32), axis=0, keepdims=True) for e in experts], axis=0
    )
    count = len(experts)
    padded = -(-count // 8) * 8
    wide = members
    if padded > count:
        wide = jnp.concatenate([members, jnp.zeros((padded - count, TILE), F32)], axis=0)
    before = lax.broadcasted_iota(jnp.int32, (TILE, TILE), 0) < lax.broadcasted_iota(
        jnp.int32, (TILE, TILE), 1
    )
    ranks = dot(wide.astype(BF16), before.astype(F32).astype(BF16))
    return members, ranks


def pack_kernel(docs_ref, keys_ref, values_ref, out_ref, docs, values, sems):
    moves = [
        pltpu.make_async_copy(values_ref, values, sems.at[0]),
        pltpu.make_async_copy(docs_ref, docs, sems.at[1]),
        pltpu.make_async_copy(
            keys_ref, out_ref.at[pl.ds(0, TILE), pl.ds(0, KV_HEADS * HEAD)], sems.at[2]
        ),
    ]
    for move in moves:
        move.start()
    moves[0].wait()
    for h in range(KV_HEADS):
        out_ref[0:TILE, (KV_HEADS + h) * HEAD : (KV_HEADS + h + 1) * HEAD] = (
            values[:, h * HEAD : (h + 1) * HEAD].astype(F32).T.astype(BF16)
        )
    moves[1].wait()
    out_ref[TILE:KV_ROWS, :] = jnp.zeros((KV_ROWS - TILE, 4 * HEAD), BF16)
    out_ref[TILE:KV_ROWS, 0:HEAD] = jnp.broadcast_to(
        docs[...].astype(F32), (KV_ROWS - TILE, TILE)
    ).astype(BF16)
    moves[2].wait()


def select_kernel(planes, pos_ref, *refs):
    sources, (qs_ref, xs_ref, facts_ref) = refs[:4], refs[4:7]
    routes_ref, docs_ref, q_ref, x_ref, sems = refs[7:]
    moves = [
        pltpu.make_async_copy(source, target, sems.at[i])
        for i, (source, target) in enumerate(zip(sources, refs[7:11]))
    ]
    for move in moves:
        move.start()
    for move in moves:
        move.wait()
    z = pos_ref[0] // SHARDS
    members, ranks = slot_rows(routes_ref[...], [lax.rem(z + k, planes) for k in range(planes)])
    docs = docs_ref[...].astype(F32)
    lane_slot = (lax.broadcasted_iota(jnp.int32, (TILE, TILE), 0) % SLOTS).astype(F32)
    token = lax.broadcasted_iota(jnp.int32, (1, TILE), 1).astype(F32)
    facts = jnp.concatenate(
        [token, docs, jnp.ones((1, TILE), F32), jnp.zeros((5, TILE), F32)], axis=0
    ).astype(BF16)
    picks = [
        jnp.where(ranks[k : k + 1] == lane_slot, members[k : k + 1], 0.0) for k in range(planes)
    ]
    chooser = jnp.concatenate([p[:SLOTS] for p in picks], axis=0).astype(BF16)
    q_rows = dot(chooser, q_ref[...])
    xs_ref[...] = dot(chooser, x_ref[...])
    for k in range(planes):
        known = dot(facts, picks[k].astype(BF16), 1, 1)
        facts_ref[:, k * TILE : (k + 1) * TILE] = jnp.concatenate(
            [known[0:1], known[1:2] + (1.0 - known[2:3]) * docs[:, 0:1], known[2:]], axis=0
        )
        for h in range(KV_HEADS):
            stack = jnp.concatenate(
                [
                    q_rows[k * SLOTS : (k + 1) * SLOTS, a * HEAD : (a + 1) * HEAD]
                    for a in range(h * GROUP, (h + 1) * GROUP)
                ],
                axis=0,
            )
            qs_ref[h, :, k * TILE : (k + 1) * TILE] = stack.T.astype(BF16)


def doc_starts(n, pos, held):
    sums = [jnp.zeros((1, TILE), F32) for _ in range(3)]
    for s in range(n):
        docs = held[s, TILE:KV_ROWS, 0:HEAD].astype(F32)[0:1]
        ahead = (pos - s < 0).astype(F32)
        behind = (pos - s > reach(n)).astype(F32)
        known = 1.0 - ahead - behind
        docs = jnp.where(known > 0.5, docs, 0.0) + 9.0 * ahead
        for d in range(3):
            sums[d] = sums[d] + jnp.where(docs < d + 1.0, 1.0, 0.0)
    return [jnp.sum(s, axis=1, keepdims=True) for s in sums]


def starts_of(docs, starts):
    first = jnp.zeros_like(docs)
    for d in range(3):
        first = jnp.where(docs == d + 1.0, starts[d], first)
    return first


def flash(pos, held, queries, kv_heads, sides, acc_ref, bias_ref, places, firsts):
    lanes = places[0].shape[1]
    chains = range(len(queries))
    for i in chains:
        acc_ref[i] = jnp.zeros((HEAD + EXTRA, lanes), F32)
    lowest = functools.reduce(jnp.minimum, [jnp.min(first) for first in firsts])
    highest = functools.reduce(jnp.maximum, [jnp.max(first) for first in firsts])
    low = lowest.astype(jnp.int32) // KEYS
    last = pos // (KEYS // TILE)
    clear = jnp.minimum((highest.astype(jnp.int32) + KEYS - 1) // KEYS, last)

    def scores(kb, i, masked):
        h = kv_heads[i]
        keys = jnp.concatenate(
            [held[2 * kb + t, 0:TILE, h * HEAD : (h + 1) * HEAD] for t in range(2)], axis=0
        )
        result = dot(keys, queries[i]())
        if masked:
            result = result + bias_ref[sides[i]]
        return result

    def hide(kb):
        key_at = (kb * KEYS + lax.broadcasted_iota(jnp.int32, (KEYS, 1), 0)).astype(F32)
        for side, (place, first) in enumerate(zip(places, firsts)):
            bias_ref[side] = jnp.where((key_at >= first) & (key_at <= place), 0.0, LOW)

    def over_keys(step, state):
        def edge(j, carried):
            kb = jnp.where(j < clear - low, low + j, last)
            hide(kb)
            return step(kb, carried, True)

        state = lax.fori_loop(0, clear - low + 1, edge, state)
        return lax.fori_loop(clear, last, lambda kb, carried: step(kb, carried, False), state)

    def eights(x):
        return x.reshape(KEYS // 8, 8, lanes)

    def find(kb, carried, masked):
        return tuple(
            jnp.maximum(carried[i], jnp.max(eights(scores(kb, i, masked)), axis=0)) for i in chains
        )

    tops = over_keys(find, tuple(jnp.full((8, lanes), LOW, F32) for _ in chains))
    tops = [jnp.max(top, axis=0, keepdims=True) for top in tops]

    def add(kb, carried, masked):
        for i in chains:
            at = (KV_HEADS + kv_heads[i]) * HEAD
            values = jnp.concatenate(
                [held[2 * kb + t, 0:TILE, at : at + HEAD] for t in range(2)], axis=1
            )
            values = jnp.concatenate([values, jnp.ones((EXTRA, KEYS), BF16)], axis=0)
            weights = jnp.exp(((scores(kb, i, masked) - tops[i]) * SCALE).astype(BF16))
            acc_ref[i] += dot(values, weights)
        return carried

    over_keys(add, 0)
    return [(acc_ref[i, 0:HEAD] / acc_ref[i, HEAD : HEAD + 1]).T for i in chains]


def routed_kernel(n, senders, pos_ref, gain_ref, qs_ref, xs_ref, facts_ref, *refs):
    planes = n // SHARDS
    count = len(senders)
    pieces = refs[:count]
    outs = refs[count : count + planes]
    held = refs[count + planes]
    acc, bias, state, gain, sems = refs[count + planes + 1 :]
    pos = pos_ref[0]
    z, y, c = pos // SHARDS, (pos // 2) % 2, pos % 2
    copies = []
    for i, (flip_c, flip_y, k) in enumerate(senders):
        sender = lax.rem(z - k + planes, planes) * SHARDS + (y ^ flip_y) * 2 + (c ^ flip_c)
        copies.append(pltpu.make_async_copy(pieces[i], held.at[sender], sems.at[i]))
    copies.append(pltpu.make_async_copy(gain_ref, gain, sems.at[count]))
    for copy in copies:
        copy.start()
    for copy in copies:
        copy.wait()
    starts = doc_starts(n, pos, held)
    lanes = 2 * TILE
    base = (pos * TILE).astype(F32)
    for pair in range(0, planes // 2, 2):
        parts = range(pair, min(pair + 2, planes // 2))
        columns = [slice(part * lanes, (part + 1) * lanes) for part in parts]
        chains = [(i, h) for i in range(len(parts)) for h in range(KV_HEADS)]
        done = flash(
            pos,
            held,
            [lambda i=i, h=h: qs_ref[h, :, columns[i]] for i, h in chains],
            [h for _, h in chains],
            [i for i, _ in chains],
            acc,
            bias,
            [facts_ref[0:1, at] + base for at in columns],
            [starts_of(facts_ref[1:2, at], starts) for at in columns],
        )
        for (i, h), rows in zip(chains, done):
            for k in range(2):
                row = (parts[i] * 2 + k) * SLOTS
                for g in range(GROUP):
                    lane = (h * GROUP + g) * HEAD
                    state[row : row + SLOTS, lane : lane + HEAD] = (
                        xs_ref[row : row + SLOTS, lane : lane + HEAD]
                        + rows[k * TILE + g * SLOTS : k * TILE + (g + 1) * SLOTS]
                    )
    for k in range(planes):
        hidden = state[k * SLOTS : (k + 1) * SLOTS, :]
        mean = jnp.mean(hidden * hidden, axis=1, keepdims=True)
        outs[k][...] = (hidden * lax.rsqrt(mean + 1e-06) * gain[...]).astype(BF16)


def expert_kernel(n, count, *refs):
    pieces = refs[:count]
    wg, wu, wd = refs[count : count + 3]
    keep_ref, send_ref, rows = refs[count + 4 :]
    width = rows.shape[1]
    total = n * SLOTS
    out_rows = min(total, 16 * SLOTS)
    half = total // 2
    step = 1024
    for at in range(0, total, out_rows):
        for col in range(0, width, step):
            parts, first = [], 0
            for piece in pieces:
                size = piece.shape[0]
                low, high = max(at - first, 0), min(at + out_rows - first, size)
                if low < high:
                    parts.append(piece[low:high, col : col + step].astype(F32))
                first += size
            rows[:, col : col + step] = jnp.concatenate(parts, axis=0).astype(BF16)
        gate = dot(rows[...], wg[...])
        up = dot(rows[...], wu[...])
        act = (gate / (1.0 + jnp.exp(-gate)) * up).astype(BF16)
        for col in range(0, width, step):
            part = dot(act, wd[:, col : col + step]).astype(BF16)
            if out_rows > half:
                keep_ref[:, col : col + step] = part[:half]
                send_ref[:, col : col + step] = part[half:]
            elif at < half:
                keep_ref[at : at + out_rows, col : col + step] = part
            else:
                send_ref[at - half : at - half + out_rows, col : col + step] = part


def own_kernel(n, part, loads, pos_ref, held, q_ref, x_ref, _, *refs):
    sources, (h_ref, done_ref) = refs[:loads], refs[loads : loads + 2]
    targets = refs[loads + 2 : 2 * loads + 2]
    acc, bias, qt, sems = refs[2 * loads + 2 :]
    moves = [
        pltpu.make_async_copy(source.at[0], target, sems.at[i])
        for i, (source, target) in enumerate(zip(sources, targets))
    ]
    for move in moves:
        move.start()
    done_ref[...] = jnp.zeros((8, TILE), F32)
    pos = pos_ref[0]
    starts = doc_starts(n, pos, held)
    first = starts_of(held[pos, TILE:KV_ROWS, 0:HEAD].astype(F32)[0:1], starts)
    place = (pos * TILE + lax.broadcasted_iota(jnp.int32, (1, TILE), 1)).astype(F32)
    place = jnp.concatenate([place] * 2, axis=1)
    first = jnp.concatenate([first] * 2, axis=1)

    for a in range(8):
        qt[a // 2, :, (a % 2) * TILE : (a % 2 + 1) * TILE] = (
            q_ref[:, a * HEAD : (a + 1) * HEAD].astype(F32).T.astype(BF16)
        )
    done = flash(
        pos,
        held,
        [lambda i=i: qt[i] for i in range(4)],
        [part // 2] * 4,
        [0] * 4,
        acc,
        bias,
        [place],
        [first],
    )
    for i in range(4):
        for g in range(2):
            lane = (2 * i + g) * HEAD
            h_ref[:, lane : lane + HEAD] = (
                x_ref[:, lane : lane + HEAD].astype(F32) + done[i][g * TILE : (g + 1) * TILE]
            )
    for move in moves:
        move.wait()


def combine_kernel(planes, pos_ref, routes_ref, gates_ref, *refs):
    halves, parts, out_ref = refs[:4], refs[4 : 4 + planes], refs[4 + planes]
    z = pos_ref[0] // SHARDS
    routes = routes_ref[...]
    gates = gates_ref[...]
    experts = [lax.rem(z + k, planes) for k in range(planes)]
    members, ranks = slot_rows(routes, experts)
    slot = lax.broadcasted_iota(jnp.int32, (SLOTS, TILE), 0).astype(F32)
    mix = []
    for k, e in enumerate(experts):
        gate = jnp.sum(jnp.where(routes == e, gates, 0.0), axis=0, keepdims=True)
        mix.append(jnp.where(ranks[k : k + 1] == slot, gate, 0.0))
    mix = jnp.concatenate(mix, axis=0).T
    mix_high = mix.astype(BF16)
    mix_low = (mix - mix_high.astype(F32)).astype(BF16)
    size = halves[0].shape[1]
    for i, h in enumerate(halves):
        columns = slice(i * size, (i + 1) * size)
        rows = jnp.concatenate([p[:, columns].astype(F32) for p in parts], axis=0).astype(BF16)
        out_ref[:, columns] = (h[...] + dot(mix_high, rows) + dot(mix_low, rows)).astype(BF16)


def pin(x):
    return pltpu.with_memory_space_constraint(x, pltpu.HBM)


def params(mib):
    return pltpu.CompilerParams(vmem_limit_bytes=mib * 1024 * 1024)


def local(
    resid, queries, keys, values, doc_ids, norm_gain, routes, route_weights, w_gate, w_up, w_down
):
    n = lax.axis_size("expert")
    planes = n // SHARDS
    pos = lax.axis_index("expert").astype(jnp.int32).reshape(1)
    tokens, width = queries.shape
    hidden = w_gate.shape[2]
    routes_t = routes.T
    gates_t = route_weights.T
    docs = doc_ids.reshape(1, tokens)
    small = 24 if n <= 16 else 60
    back = reach(n)

    packed = pl.pallas_call(
        pack_kernel,
        out_shape=jax.ShapeDtypeStruct((KV_ROWS, 4 * HEAD), BF16),
        in_specs=[HBM] * 3,
        out_specs=VMEM,
        scratch_shapes=[
            pltpu.VMEM((1, tokens), jnp.int32),
            pltpu.VMEM((tokens, KV_HEADS * HEAD), BF16),
            pltpu.SemaphoreType.DMA((3,)),
        ],
        compiler_params=params(8),
        name="pack",
    )(pin(docs), pin(keys), pin(values))

    def move(value, pairs):
        return lax.ppermute(value, "expert", pairs)

    def needed(k, y_from, y_to):
        gaps = [
            k * SHARDS + 2 * (y_to - y_from) + (to - of) for to in range(2) for of in range(2)
        ]
        return any(0 <= gap <= back for gap in gaps)

    far = max(k for k in range(planes) if any(needed(k, a, b) for a in (0, 1) for b in (0, 1)))
    q_rows, x_rows, facts = pl.pallas_call(
        functools.partial(select_kernel, planes),
        out_shape=[
            jax.ShapeDtypeStruct((KV_HEADS, HEAD, planes * TILE), BF16),
            jax.ShapeDtypeStruct((planes * SLOTS, width), F32),
            jax.ShapeDtypeStruct((8, planes * TILE), F32),
        ],
        in_specs=[SMEM] + [HBM] * 4,
        out_specs=[VMEM] * 3,
        scratch_shapes=[
            pltpu.VMEM(routes_t.shape, jnp.int32),
            pltpu.VMEM(docs.shape, jnp.int32),
            pltpu.VMEM(queries.shape, BF16),
            pltpu.VMEM(resid.shape, BF16),
            pltpu.SemaphoreType.DMA((4,)),
        ],
        compiler_params=params(small),
        name="select",
    )(pos, pin(routes_t), pin(docs), pin(queries), pin(resid))

    flip_y = [(s, s ^ 2) for s in range(n)]
    flip_c = [(s, s ^ 1) for s in range(n)]
    kv = {(0, 0, 0): packed}
    for k in range(far + 1):
        pairs = [(s, s ^ 2 if s >= k * SHARDS else s) for s in range(n)]
        across, onward = move(kv[0, 0, k], pairs), None
        if k < far:
            used = [
                any(needed(j, y, to) for to in (0, 1) for j in range(k + 1, far + 1))
                for y in (0, 1)
            ]
            pairs = [(s, (s + SHARDS) % n if used[s // 2 % 2] else s) for s in range(n)]
            onward = move(kv[0, 0, k], pairs)
            across, onward, q_rows = lax.optimization_barrier((across, onward, q_rows))
            kv[0, 0, k + 1] = onward
        kv[0, 1, k] = across
    for (_, side, k), piece in list(kv.items()):
        kv[1, side, k] = move(piece, flip_c)

    *sent, held = pl.pallas_call(
        functools.partial(routed_kernel, n, list(kv)),
        out_shape=[jax.ShapeDtypeStruct((SLOTS, width), BF16)] * planes
        + [jax.ShapeDtypeStruct((n, KV_ROWS, 4 * HEAD), BF16)],
        in_specs=[SMEM, HBM] + [VMEM] * 3 + [ANY] * len(kv),
        out_specs=[VMEM] * (planes + 1),
        scratch_shapes=[
            pltpu.VMEM((4, HEAD + EXTRA, 2 * TILE), F32),
            pltpu.VMEM((2, KEYS, 2 * TILE), F32),
            pltpu.VMEM((planes * SLOTS, width), F32),
            pltpu.VMEM((1, width), F32),
            pltpu.SemaphoreType.DMA((len(kv) + 1,)),
        ],
        compiler_params=params(small),
        name="routed",
    )(pos, pin(norm_gain.reshape(1, width)), q_rows, x_rows, facts, *kv.values())

    def own(part, after, *sources):
        columns = pl.BlockSpec((tokens, 8 * HEAD), lambda i: (0, part))
        return pl.pallas_call(
            functools.partial(own_kernel, n, part, len(sources)),
            out_shape=[
                jax.ShapeDtypeStruct((tokens, 8 * HEAD), F32),
                jax.ShapeDtypeStruct((8, TILE), F32),
            ]
            + [jax.ShapeDtypeStruct(w.shape[1:], BF16) for w in sources],
            grid=(1,),
            in_specs=[SMEM, VMEM, columns, columns, ANY] + [HBM] * len(sources),
            out_specs=[
                pl.BlockSpec((tokens, 8 * HEAD), lambda i: (0, 0)),
                pl.BlockSpec((8, TILE), lambda i: (0, 0)),
            ]
            + [VMEM] * len(sources),
            scratch_shapes=[
                pltpu.VMEM((4, HEAD + EXTRA, 2 * TILE), F32),
                pltpu.VMEM((1, KEYS, 2 * TILE), F32),
                pltpu.VMEM((4, HEAD, 2 * TILE), BF16),
                pltpu.SemaphoreType.DMA((3,)),
            ],
            compiler_params=params(small),
            cost_estimate=pl.CostEstimate(
                flops=2_000_000_000, bytes_accessed=8_000_000, transcendentals=2_000_000
            ),
            name="own",
        )(pos, held, queries, resid, after, *map(pin, sources))

    half0, done, *weights = own(0, sent[0], w_gate, w_up, w_down)
    half1, late = own(1, done)
    halves = [half0, half1]

    come = [
        move(sent[k], [(s, (s + k * SHARDS) % n) for s in range(n)]) for k in range(1, planes)
    ]
    next_door = move(sent[0], flip_y)
    come, next_door, done = lax.optimization_barrier((come, next_door, done))
    here = [sent[0], jnp.concatenate(come, axis=0)]
    there = [next_door, move(here[1], flip_y)]
    mate = move(jnp.concatenate(here, axis=0), flip_c)
    there, mate, late = lax.optimization_barrier((there, mate, late))
    pieces = here + there + [mate, move(jnp.concatenate(there, axis=0), flip_c)]

    half = jax.ShapeDtypeStruct((n * SLOTS // 2, width), BF16)
    keep, send = pl.pallas_call(
        functools.partial(expert_kernel, n, len(pieces)),
        out_shape=[half, half],
        in_specs=[VMEM] * (len(pieces) + 3) + [ANY],
        out_specs=[VMEM, VMEM],
        scratch_shapes=[pltpu.VMEM((16 * SLOTS, width), BF16)],
        compiler_params=params(16),
        cost_estimate=pl.CostEstimate(
            flops=1_200_000_000, bytes_accessed=12_000_000, transcendentals=50_000
        ),
        name="expert",
    )(*pieces, *weights, late)

    halves += [own(part, keep)[0] for part in range(2, 4)]

    total = keep.astype(F32) + move(send, [(s, s ^ 1) for s in range(n)]).astype(F32)
    quarter = n * SLOTS // 4
    other = move(total[quarter:].astype(BF16), [(s, s ^ 2) for s in range(n)])
    total = (total[:quarter] + other.astype(F32)).astype(BF16)
    parts = [total[:SLOTS]]
    for k in range(1, planes):
        parts.append(
            move(
                total[k * SLOTS : (k + 1) * SLOTS], [(s, (s - k * SHARDS) % n) for s in range(n)]
            )
        )

    return pl.pallas_call(
        functools.partial(combine_kernel, planes),
        out_shape=jax.ShapeDtypeStruct((tokens, width), BF16),
        in_specs=[SMEM] + [VMEM] * (6 + planes),
        out_specs=VMEM,
        compiler_params=params(small),
        name="combine",
    )(pos, routes_t, gates_t, *halves, *parts)


def solution(mesh):
    rows = P(("groups", "expert"), None)
    in_specs = (rows,) * 4 + (P(("groups", "expert")), P(), rows, rows) + (
        P("expert", None, None),
    ) * 3
    return jax.shard_map(local, mesh=mesh, in_specs=in_specs, out_specs=rows, check_vma=False)
```

profile of v0, /device:TPU:22, one launch (start us, length us, event | category | flops | bytes accessed | tf_op | source)
XLA Modules:
  0.0 91.9 jit_solution(12221389289182146233)
XLA Ops:
  0.0 1.1 %pack.1.refs_0_ = bf16[144,512]{1,0:T(8,128)(2,1)S(1)} custom-call(s32[1,128]{1,0:T(1,128)} %bitcast.9, bf16[128,256]{1,0:T(8,128)(2,1)} %keys_ref.1, bf16[128,256]{1,0:T(8,128)(2,1)} %values_ref.1), custom_call_target="tpu_custom_call" | custom-call | tf_op jit(solution)/shard_map/pack/pallas_call | solution.py:372
  1.1 1.6 %collective-permute-start.1 = (bf16[144,512]{1,0:T(8,128)(2,1)S(1)}, bf16[144,512]{1,0:T(8,128)(2,1)S(1)}, u32[]{:S(2)}, u32[]{:S(2)}) collective-permute-start(bf16[144,512]{1,0:T(8,128)(2,1)S(1)} %pack.1.refs_0_), channel_id=1, source_target_pairs={{0,4},{1,5},{2,6},{3,7},{4,8},{5,9},{6,10},{7,11},{8,12},{9,13},{1... | collective-permute-start | bytes 442376 | tf_op jit(solution)/shard_map/ppermute | solution.py:387
  2.8 0.5 collective-permute-start
  3.3 2.2 %select.1 = (bf16[2,128,512]{2,1,0:T(8,128)(2,1)S(1)}, f32[32,4096]{1,0:T(8,128)S(1)}, f32[8,512]{1,0:T(8,128)S(1)}) custom-call(s32[1]{0:T(128)} %bitcast.pos_ref, s32[4,128]{1,0:T(4,128)} %bitcast.5, s32[1,128]{1,0:T(1,128)} %bitcast.10, bf16[128,4096]{1,0:T(8,128)(2,1)} %q_ref.7, bf16[128,4096]{1,0:T(8,128)(2,1)} %x_ref.7), custom_call_target="tpu_custom_call" | custom-call | tf_op jit(solution)/shard_map/select/pallas_call | solution.py:396
  5.5 1.3 %collective-permute-done.1.refs_1_ = bf16[144,512]{1,0:T(8,128)(2,1)S(1)} collective-permute-done((bf16[144,512]{1,0:T(8,128)(2,1)S(1)}, bf16[144,512]{1,0:T(8,128)(2,1)S(1)}, u32[]{:S(2)}, u32[]{:S(2)}) %collective-permute-start.1) | collective-permute-done | bytes 147488 | tf_op jit(solution)/shard_map/ppermute | solution.py:387
  6.8 1.3 %collective-permute-done.refs_2_ = bf16[144,512]{1,0:T(8,128)(2,1)S(1)} collective-permute-done((bf16[144,512]{1,0:T(8,128)(2,1)S(1)}, bf16[144,512]{1,0:T(8,128)(2,1)S(1)}, u32[]{:S(2)}, u32[]{:S(2)}) %collective-permute-start) | collective-permute-done | bytes 147488 | tf_op jit(solution)/shard_map/ppermute | solution.py:387
  8.1 0.4 collective-permute-start.3
  8.4 2.4 %collective-permute-start.2 = (bf16[144,512]{1,0:T(8,128)(2,1)S(1)}, bf16[144,512]{1,0:T(8,128)(2,1)S(1)}, u32[]{:S(2)}, u32[]{:S(2)}) collective-permute-start(bf16[144,512]{1,0:T(8,128)(2,1)S(1)} %collective-permute-done.1.refs_1_), channel_id=1, source_target_pairs={{0,0},{1,1},{2,2},{3,3},{4,6},{5,7},{6,4},{7,5},{8,10},{9,11},{10,... | collective-permute-start | bytes 442376 | tf_op jit(solution)/shard_map/ppermute | solution.py:387
  10.8 2.4 %collective-permute-done.3.refs_3_ = bf16[144,512]{1,0:T(8,128)(2,1)S(1)} collective-permute-done((bf16[144,512]{1,0:T(8,128)(2,1)S(1)}, bf16[144,512]{1,0:T(8,128)(2,1)S(1)}, u32[]{:S(2)}, u32[]{:S(2)}) %collective-permute-start.3) | collective-permute-done | bytes 147488 | tf_op jit(solution)/shard_map/ppermute | solution.py:387
  13.2 2.2 %collective-permute-done.2.refs_4_ = bf16[144,512]{1,0:T(8,128)(2,1)S(1)} collective-permute-done((bf16[144,512]{1,0:T(8,128)(2,1)S(1)}, bf16[144,512]{1,0:T(8,128)(2,1)S(1)}, u32[]{:S(2)}, u32[]{:S(2)}) %collective-permute-start.2) | collective-permute-done | bytes 147488 | tf_op jit(solution)/shard_map/ppermute | solution.py:387
  15.5 3.9 %collective-permute-start.5 = (bf16[144,512]{1,0:T(8,128)(2,1)S(1)}, bf16[144,512]{1,0:T(8,128)(2,1)S(1)}, u32[]{:S(2)}, u32[]{:S(2)}) collective-permute-start(bf16[144,512]{1,0:T(8,128)(2,1)S(1)} %collective-permute-done.3.refs_3_), channel_id=1, source_target_pairs={{0,0},{1,1},{2,6},{3,7},{4,4},{5,5},{6,10},{7,11},{8,8},{9,9},{10,... | collective-permute-start | bytes 442376 | tf_op jit(solution)/shard_map/ppermute | solution.py:387
  19.4 1.9 %collective-permute-start.4 = (bf16[144,512]{1,0:T(8,128)(2,1)S(1)}, bf16[144,512]{1,0:T(8,128)(2,1)S(1)}, u32[]{:S(2)}, u32[]{:S(2)}) collective-permute-start(bf16[144,512]{1,0:T(8,128)(2,1)S(1)} %collective-permute-done.3.refs_3_), channel_id=1, source_target_pairs={{0,0},{1,1},{2,2},{3,3},{4,4},{5,5},{6,6},{7,7},{8,10},{9,11},{10,... | collective-permute-start | bytes 442376 | tf_op jit(solution)/shard_map/ppermute | solution.py:387
  21.3 0.1 collective-permute-start.7
  21.4 0.5 collective-permute-start.8
  21.9 0.1 collective-permute-start.9
  22.0 0.5 collective-permute-done.5.refs_5_
  22.5 3.9 %collective-permute-done.4.refs_6_ = bf16[144,512]{1,0:T(8,128)(2,1)S(1)} collective-permute-done((bf16[144,512]{1,0:T(8,128)(2,1)S(1)}, bf16[144,512]{1,0:T(8,128)(2,1)S(1)}, u32[]{:S(2)}, u32[]{:S(2)}) %collective-permute-start.4) | collective-permute-done | bytes 147488 | tf_op jit(solution)/shard_map/ppermute | solution.py:387
  26.4 0.7 collective-permute-start.6
  27.1 0.1 collective-permute-start.10
  27.2 0.5 collective-permute-start.11
  27.7 0.1 collective-permute-start.12
  27.7 0.4 collective-permute-start.13
  28.2 0.1 collective-permute-start.14
  28.3 0.5 collective-permute-done.11.refs_12_
  28.7 0.5 collective-permute-done.13.refs_14_
  29.2 0.3 collective-permute-done.14.refs_15_
  29.6 13.2 %routed.1 = (bf16[8,4096]{1,0:T(8,128)(2,1)S(1)}, bf16[8,4096]{1,0:T(8,128)(2,1)S(1)}, bf16[8,4096]{1,0:T(8,128)(2,1)S(1)}, bf16[8,4096]{1,0:T(8,128)(2,1)S(1)}, bf16[16,144,512]{2,1,0:T(8,128)(2,1)S(1)}) custom-call(s32[1]{0:T(128)} %bitcast.pos_ref, f32[1,4096]{1,0:T(1,128)} %bitcast.8, bf16[2,128,512]{2,1,0:T(8,128)(2,1)S(1)} %get-tuple-element.46.qs_ref, ...), custom_call_target="tpu_custom_call" | custom-call | tf_op jit(solution)/shard_map/routed/pallas_call | solution.py:435
  42.8 1.3 %collective-permute-start.15 = (bf16[8,4096]{1,0:T(8,128)(2,1)S(1)}, bf16[8,4096]{1,0:T(8,128)(2,1)S(1)}, u32[]{:S(2)}, u32[]{:S(2)}) collective-permute-start(bf16[8,4096]{1,0:T(8,128)(2,1)S(1)} %get-tuple-element.58), channel_id=1, source_target_pairs={{0,4},{1,5},{2,6},{3,7},{4,8},{5,9},{6,10},{7,11},{8,12},{9,13},{1... | collective-permute-start | bytes 196616 | tf_op jit(solution)/shard_map/ppermute | solution.py:387
  44.0 1.5 %collective-permute-start.17 = (bf16[8,4096]{1,0:T(8,128)(2,1)S(1)}, bf16[8,4096]{1,0:T(8,128)(2,1)S(1)}, u32[]{:S(2)}, u32[]{:S(2)}) collective-permute-start(bf16[8,4096]{1,0:T(8,128)(2,1)S(1)} %get-tuple-element.60), channel_id=1, source_target_pairs={{0,12},{1,13},{2,14},{3,15},{4,0},{5,1},{6,2},{7,3},{8,4},{9,5},{1... | collective-permute-start | bytes 196616 | tf_op jit(solution)/shard_map/ppermute | solution.py:387
  45.6 8.6 %own.4 = (f32[128,1024]{1,0:T(8,128)S(1)}, f32[8,128]{1,0:T(8,128)S(1)}, bf16[4096,384]{1,0:T(8,128)(2,1)S(1)}, bf16[4096,384]{1,0:T(8,128)(2,1)S(1)}, bf16[384,4096]{1,0:T(8,128)(2,1)S(1)}) custom-call(s32[1]{0:T(128)} %bitcast.pos_ref, bf16[16,144,512]{2,1,0:T(8,128)(2,1)S(1)} %get-tuple-element.53.held, bf16[128,4096]{1,0:T(8,128)(2,1)S(1)} %copy-done, ...), custom_call_target="tpu_custom_call" | custom-call | flops 2000000000 | bytes 8000000 | tf_op jit(solution)/shard_map/own/pallas_call | solution.py:454
  54.3 0.1 collective-permute-start.20
  54.4 0.7 collective-permute-start.19
  55.1 8.6 %own.5 = (f32[128,1024]{1,0:T(8,128)S(1)}, f32[8,128]{1,0:T(8,128)S(1)}) custom-call(s32[1]{0:T(128)} %bitcast.pos_ref, bf16[16,144,512]{2,1,0:T(8,128)(2,1)S(1)} %get-tuple-element.53.held, bf16[128,4096]{1,0:T(8,128)(2,1)S(1)} %copy-done, bf16[128,4096]{1,0:T(8,128)(2,1)S(1)} %copy-done.1, f32[8,128]{1,0:T(8,128)S(1)} %get-tuple-element.56._), custom_call_target="tpu_custom_call" | custom-call | flops 2000000000 | bytes 8000000 | tf_op jit(solution)/shard_map/own/pallas_call | solution.py:454
  63.8 0.2 collective-permute-start.21
  64.0 1.4 %collective-permute-done.21.refs_5_ = bf16[32,4096]{1,0:T(8,128)(2,1)S(1)} collective-permute-done((bf16[32,4096]{1,0:T(8,128)(2,1)S(1)}, bf16[32,4096]{1,0:T(8,128)(2,1)S(1)}, u32[]{:S(2)}, u32[]{:S(2)}) %collective-permute-start.21) | collective-permute-done | bytes 262176 | tf_op jit(solution)/shard_map/ppermute | solution.py:387
  65.4 2.0 %expert.1 = (bf16[64,4096]{1,0:T(8,128)(2,1)S(1)}, bf16[64,4096]{1,0:T(8,128)(2,1)S(1)}) custom-call(bf16[8,4096]{1,0:T(8,128)(2,1)S(1)} %get-tuple-element.54._.refs_0_, bf16[24,4096]{1,0:T(8,128)(2,1)S(1)} %constant_dynamic-update-slice_fusion.refs_1_, bf16[8,4096]{1,0:T(8,128)(2,1)S(1)} %collective-permute-done.18.refs_2_, ...), custom_call_target="tpu_custom_call" | custom-call | flops 1200000000 | bytes 12000000 | tf_op jit(solution)/shard_map/expert/pallas_call | solution.py:497
  67.4 0.2 collective-permute-start.22
  67.6 1.7 %collective-permute-done.22 = bf16[64,4096]{1,0:T(8,128)(2,1)S(1)} collective-permute-done((bf16[64,4096]{1,0:T(8,128)(2,1)S(1)}, bf16[64,4096]{1,0:T(8,128)(2,1)S(1)}, u32[]{:S(2)}, u32[]{:S(2)}) %collective-permute-start.22) | collective-permute-done | bytes 524320 | tf_op jit(solution)/shard_map/ppermute | solution.py:387
  69.3 0.1 convert_add_fusion
  69.5 0.1 collective-permute-start.23
  69.6 9.2 %own.7 = (f32[128,1024]{1,0:T(8,128)S(1)}, f32[8,128]{1,0:T(8,128)}) custom-call(s32[1]{0:T(128)} %bitcast.pos_ref, bf16[16,144,512]{2,1,0:T(8,128)(2,1)S(1)} %get-tuple-element.53.held, bf16[128,4096]{1,0:T(8,128)(2,1)S(1)} %copy-done, bf16[128,4096]{1,0:T(8,128)(2,1)S(1)} %copy-done.1, bf16[64,4096]{1,0:T(8,128)(2,1)S(1)} %get-tuple-element.73._), custom_call_target="tpu_custom_call" | custom-call | flops 2000000000 | bytes 8000000 | tf_op jit(solution)/shard_map/own/pallas_call | solution.py:454
  78.8 0.1 collective-permute-start.26
  78.9 0.1 collective-permute-start.25
  79.0 0.0 copy-start.2
  79.0 0.0 copy-start.3
  79.0 1.9 %collective-permute-start.24 = (bf16[8,4096]{1,0:T(8,128)(2,1)S(1)}, bf16[8,4096]{1,0:T(8,128)(2,1)S(1)}, u32[]{:S(2)}, u32[]{:S(2)}) collective-permute-start(bf16[8,4096]{1,0:T(8,128)(2,1)S(1)} %get-tuple-element.79), channel_id=1, source_target_pairs={{0,12},{1,13},{2,14},{3,15},{4,0},{5,1},{6,2},{7,3},{8,4},{9,5},{1... | collective-permute-start | bytes 196616 | tf_op jit(solution)/shard_map/ppermute | solution.py:387
  80.9 9.0 %own.6 = (f32[128,1024]{1,0:T(8,128)S(1)}, f32[8,128]{1,0:T(8,128)}) custom-call(s32[1]{0:T(128)} %bitcast.pos_ref, bf16[16,144,512]{2,1,0:T(8,128)(2,1)S(1)} %get-tuple-element.53.held, bf16[128,4096]{1,0:T(8,128)(2,1)S(1)} %copy-done, bf16[128,4096]{1,0:T(8,128)(2,1)S(1)} %copy-done.1, bf16[64,4096]{1,0:T(8,128)(2,1)S(1)} %get-tuple-element.73._), custom_call_target="tpu_custom_call" | custom-call | flops 2000000000 | bytes 8000000 | tf_op jit(solution)/shard_map/own/pallas_call | solution.py:454
  90.0 1.9 %combine.1 = bf16[128,4096]{1,0:T(8,128)(2,1)} custom-call(s32[1]{0:T(128)} %bitcast.pos_ref, s32[4,128]{1,0:T(4,128)S(1)} %bitcast.6, f32[4,128]{1,0:T(4,128)S(1)} %bitcast.7, f32[128,1024]{1,0:T(8,128)S(1)} %get-tuple-element.55.refs_0_, f32[128,1024]{1,0:T(8,128)S(1)} %get-tuple-element.57.refs_1_, f32[128,1024]{1,0:T(8,128)S(1)} %get-tuple-element.74.refs_2_, ...), custom_call_target="tpu_custom_call" | custom-call | tf_op jit(solution)/shard_map/combine/pallas_call | solution.py:524
  (32 shorter events, 0.2 us)
Async XLA Ops:
  0.0 45.6 %copy-start = (bf16[128,4096]{1,0:T(8,128)(2,1)S(1)}, bf16[128,4096]{1,0:T(8,128)(2,1)}, u32[]{:S(2)}) copy-start(bf16[128,4096]{1,0:T(8,128)(2,1)} %q_ref.7) | copy-start | bytes 3145732
  0.0 45.6 %copy-start.1 = (bf16[128,4096]{1,0:T(8,128)(2,1)S(1)}, bf16[128,4096]{1,0:T(8,128)(2,1)}, u32[]{:S(2)}) copy-start(bf16[128,4096]{1,0:T(8,128)(2,1)} %x_ref.7) | copy-start | bytes 3145732
  1.1 5.6 %collective-permute-start.1 = (bf16[144,512]{1,0:T(8,128)(2,1)S(1)}, bf16[144,512]{1,0:T(8,128)(2,1)S(1)}, u32[]{:S(2)}, u32[]{:S(2)}) collective-permute-start(bf16[144,512]{1,0:T(8,128)(2,1)S(1)} %pack.1.refs_0_), channel_id=1, source_target_pairs={{0,4},{1,5},{2,6},{3,7},{4,8},{5,9},{6,10},{7,11},{8,12},{9,13},{1... | collective-permute-start | bytes 442376 | tf_op jit(solution)/shard_map/ppermute | solution.py:387
  2.8 5.3 %collective-permute-start = (bf16[144,512]{1,0:T(8,128)(2,1)S(1)}, bf16[144,512]{1,0:T(8,128)(2,1)S(1)}, u32[]{:S(2)}, u32[]{:S(2)}) collective-permute-start(bf16[144,512]{1,0:T(8,128)(2,1)S(1)} %pack.1.refs_0_), channel_id=1, source_target_pairs={{0,2},{1,3},{2,0},{3,1},{4,6},{5,7},{6,4},{7,5},{8,10},{9,11},{10,... | collective-permute-start | bytes 442376 | tf_op jit(solution)/shard_map/ppermute | solution.py:387
  8.1 5.1 %collective-permute-start.3 = (bf16[144,512]{1,0:T(8,128)(2,1)S(1)}, bf16[144,512]{1,0:T(8,128)(2,1)S(1)}, u32[]{:S(2)}, u32[]{:S(2)}) collective-permute-start(bf16[144,512]{1,0:T(8,128)(2,1)S(1)} %collective-permute-done.1.refs_1_), channel_id=1, source_target_pairs={{0,4},{1,5},{2,6},{3,7},{4,8},{5,9},{6,10},{7,11},{8,12},{9,13},{1... | collective-permute-start | bytes 442376 | tf_op jit(solution)/shard_map/ppermute | solution.py:387
  8.4 7.0 %collective-permute-start.2 = (bf16[144,512]{1,0:T(8,128)(2,1)S(1)}, bf16[144,512]{1,0:T(8,128)(2,1)S(1)}, u32[]{:S(2)}, u32[]{:S(2)}) collective-permute-start(bf16[144,512]{1,0:T(8,128)(2,1)S(1)} %collective-permute-done.1.refs_1_), channel_id=1, source_target_pairs={{0,0},{1,1},{2,2},{3,3},{4,6},{5,7},{6,4},{7,5},{8,10},{9,11},{10,... | collective-permute-start | bytes 442376 | tf_op jit(solution)/shard_map/ppermute | solution.py:387
  15.5 7.0 %collective-permute-start.5 = (bf16[144,512]{1,0:T(8,128)(2,1)S(1)}, bf16[144,512]{1,0:T(8,128)(2,1)S(1)}, u32[]{:S(2)}, u32[]{:S(2)}) collective-permute-start(bf16[144,512]{1,0:T(8,128)(2,1)S(1)} %collective-permute-done.3.refs_3_), channel_id=1, source_target_pairs={{0,0},{1,1},{2,6},{3,7},{4,4},{5,5},{6,10},{7,11},{8,8},{9,9},{10,... | collective-permute-start | bytes 442376 | tf_op jit(solution)/shard_map/ppermute | solution.py:387
  19.4 7.0 %collective-permute-start.4 = (bf16[144,512]{1,0:T(8,128)(2,1)S(1)}, bf16[144,512]{1,0:T(8,128)(2,1)S(1)}, u32[]{:S(2)}, u32[]{:S(2)}) collective-permute-start(bf16[144,512]{1,0:T(8,128)(2,1)S(1)} %collective-permute-done.3.refs_3_), channel_id=1, source_target_pairs={{0,0},{1,1},{2,2},{3,3},{4,4},{5,5},{6,6},{7,7},{8,10},{9,11},{10,... | collective-permute-start | bytes 442376 | tf_op jit(solution)/shard_map/ppermute | solution.py:387
  21.3 5.9 %collective-permute-start.7 = (bf16[144,512]{1,0:T(8,128)(2,1)S(1)}, bf16[144,512]{1,0:T(8,128)(2,1)S(1)}, u32[]{:S(2)}, u32[]{:S(2)}) collective-permute-start(bf16[144,512]{1,0:T(8,128)(2,1)S(1)} %pack.1.refs_0_), channel_id=1, source_target_pairs={{0,1},{1,0},{2,3},{3,2},{4,5},{5,4},{6,7},{7,6},{8,9},{9,8},{10,11... | collective-permute-start | bytes 442376 | tf_op jit(solution)/shard_map/ppermute | solution.py:387
  21.4 6.4 %collective-permute-start.8 = (bf16[144,512]{1,0:T(8,128)(2,1)S(1)}, bf16[144,512]{1,0:T(8,128)(2,1)S(1)}, u32[]{:S(2)}, u32[]{:S(2)}) collective-permute-start(bf16[144,512]{1,0:T(8,128)(2,1)S(1)} %collective-permute-done.1.refs_1_), channel_id=1, source_target_pairs={{0,1},{1,0},{2,3},{3,2},{4,5},{5,4},{6,7},{7,6},{8,9},{9,8},{10,11... | collective-permute-start | bytes 442376 | tf_op jit(solution)/shard_map/ppermute | solution.py:387
  21.9 5.8 %collective-permute-start.9 = (bf16[144,512]{1,0:T(8,128)(2,1)S(1)}, bf16[144,512]{1,0:T(8,128)(2,1)S(1)}, u32[]{:S(2)}, u32[]{:S(2)}) collective-permute-start(bf16[144,512]{1,0:T(8,128)(2,1)S(1)} %collective-permute-done.refs_2_), channel_id=1, source_target_pairs={{0,1},{1,0},{2,3},{3,2},{4,5},{5,4},{6,7},{7,6},{8,9},{9,8},{10,11... | collective-permute-start | bytes 442376 | tf_op jit(solution)/shard_map/ppermute | solution.py:387
  26.4 1.8 %collective-permute-start.6 = (bf16[144,512]{1,0:T(8,128)(2,1)S(1)}, bf16[144,512]{1,0:T(8,128)(2,1)S(1)}, u32[]{:S(2)}, u32[]{:S(2)}) collective-permute-start(bf16[144,512]{1,0:T(8,128)(2,1)S(1)} %collective-permute-done.5.refs_5_), channel_id=1, source_target_pairs={{0,0},{1,1},{2,2},{3,3},{4,4},{5,5},{6,6},{7,7},{8,8},{9,9},{10,10... | collective-permute-start | bytes 442376 | tf_op jit(solution)/shard_map/ppermute | solution.py:387
  27.1 1.7 %collective-permute-start.10 = (bf16[144,512]{1,0:T(8,128)(2,1)S(1)}, bf16[144,512]{1,0:T(8,128)(2,1)S(1)}, u32[]{:S(2)}, u32[]{:S(2)}) collective-permute-start(bf16[144,512]{1,0:T(8,128)(2,1)S(1)} %collective-permute-done.3.refs_3_), channel_id=1, source_target_pairs={{0,1},{1,0},{2,3},{3,2},{4,5},{5,4},{6,7},{7,6},{8,9},{9,8},{10,11... | collective-permute-start | bytes 442376 | tf_op jit(solution)/shard_map/ppermute | solution.py:387
  27.2 1.6 %collective-permute-start.11 = (bf16[144,512]{1,0:T(8,128)(2,1)S(1)}, bf16[144,512]{1,0:T(8,128)(2,1)S(1)}, u32[]{:S(2)}, u32[]{:S(2)}) collective-permute-start(bf16[144,512]{1,0:T(8,128)(2,1)S(1)} %collective-permute-done.2.refs_4_), channel_id=1, source_target_pairs={{0,1},{1,0},{2,3},{3,2},{4,5},{5,4},{6,7},{7,6},{8,9},{9,8},{10,11... | collective-permute-start | bytes 442376 | tf_op jit(solution)/shard_map/ppermute | solution.py:387
  27.7 1.6 %collective-permute-start.12 = (bf16[144,512]{1,0:T(8,128)(2,1)S(1)}, bf16[144,512]{1,0:T(8,128)(2,1)S(1)}, u32[]{:S(2)}, u32[]{:S(2)}) collective-permute-start(bf16[144,512]{1,0:T(8,128)(2,1)S(1)} %collective-permute-done.5.refs_5_), channel_id=1, source_target_pairs={{0,1},{1,0},{2,3},{3,2},{4,5},{5,4},{6,7},{7,6},{8,9},{9,8},{10,11... | collective-permute-start | bytes 442376 | tf_op jit(solution)/shard_map/ppermute | solution.py:387
  27.7 1.5 %collective-permute-start.13 = (bf16[144,512]{1,0:T(8,128)(2,1)S(1)}, bf16[144,512]{1,0:T(8,128)(2,1)S(1)}, u32[]{:S(2)}, u32[]{:S(2)}) collective-permute-start(bf16[144,512]{1,0:T(8,128)(2,1)S(1)} %collective-permute-done.4.refs_6_), channel_id=1, source_target_pairs={{0,1},{1,0},{2,3},{3,2},{4,5},{5,4},{6,7},{7,6},{8,9},{9,8},{10,11... | collective-permute-start | bytes 442376 | tf_op jit(solution)/shard_map/ppermute | solution.py:387
  28.2 1.4 %collective-permute-start.14 = (bf16[144,512]{1,0:T(8,128)(2,1)S(1)}, bf16[144,512]{1,0:T(8,128)(2,1)S(1)}, u32[]{:S(2)}, u32[]{:S(2)}) collective-permute-start(bf16[144,512]{1,0:T(8,128)(2,1)S(1)} %collective-permute-done.6.refs_7_), channel_id=1, source_target_pairs={{0,1},{1,0},{2,3},{3,2},{4,5},{5,4},{6,7},{7,6},{8,9},{9,8},{10,11... | collective-permute-start | bytes 442376 | tf_op jit(solution)/shard_map/ppermute | solution.py:387
  42.8 11.4 %collective-permute-start.15 = (bf16[8,4096]{1,0:T(8,128)(2,1)S(1)}, bf16[8,4096]{1,0:T(8,128)(2,1)S(1)}, u32[]{:S(2)}, u32[]{:S(2)}) collective-permute-start(bf16[8,4096]{1,0:T(8,128)(2,1)S(1)} %get-tuple-element.58), channel_id=1, source_target_pairs={{0,4},{1,5},{2,6},{3,7},{4,8},{5,9},{6,10},{7,11},{8,12},{9,13},{1... | collective-permute-start | bytes 196616 | tf_op jit(solution)/shard_map/ppermute | solution.py:387
  44.0 10.2 %collective-permute-start.16 = (bf16[8,4096]{1,0:T(8,128)(2,1)S(1)}, bf16[8,4096]{1,0:T(8,128)(2,1)S(1)}, u32[]{:S(2)}, u32[]{:S(2)}) collective-permute-start(bf16[8,4096]{1,0:T(8,128)(2,1)S(1)} %get-tuple-element.59), channel_id=1, source_target_pairs={{0,8},{1,9},{2,10},{3,11},{4,12},{5,13},{6,14},{7,15},{8,0},{9,1},... | collective-permute-start | bytes 196616 | tf_op jit(solution)/shard_map/ppermute | solution.py:387
  44.0 10.2 %collective-permute-start.17 = (bf16[8,4096]{1,0:T(8,128)(2,1)S(1)}, bf16[8,4096]{1,0:T(8,128)(2,1)S(1)}, u32[]{:S(2)}, u32[]{:S(2)}) collective-permute-start(bf16[8,4096]{1,0:T(8,128)(2,1)S(1)} %get-tuple-element.60), channel_id=1, source_target_pairs={{0,12},{1,13},{2,14},{3,15},{4,0},{5,1},{6,2},{7,3},{8,4},{9,5},{1... | collective-permute-start | bytes 196616 | tf_op jit(solution)/shard_map/ppermute | solution.py:387
  45.6 8.7 %collective-permute-start.18 = (bf16[8,4096]{1,0:T(8,128)(2,1)S(1)}, bf16[8,4096]{1,0:T(8,128)(2,1)S(1)}, u32[]{:S(2)}, u32[]{:S(2)}) collective-permute-start(bf16[8,4096]{1,0:T(8,128)(2,1)S(1)} %get-tuple-element.54._.refs_0_), channel_id=1, source_target_pairs={{0,2},{1,3},{2,0},{3,1},{4,6},{5,7},{6,4},{7,5},{8,10},{9,11},{10,... | collective-permute-start | bytes 196616 | tf_op jit(solution)/shard_map/ppermute | solution.py:387
  54.3 9.4 %collective-permute-start.20 = (bf16[32,4096]{1,0:T(8,128)(2,1)S(1)}, bf16[32,4096]{1,0:T(8,128)(2,1)S(1)}, u32[]{:S(2)}, u32[]{:S(2)}) collective-permute-start(bf16[32,4096]{1,0:T(8,128)(2,1)S(1)} %pad_maximum_fusion), channel_id=1, source_target_pairs={{0,1},{1,0},{2,3},{3,2},{4,5},{5,4},{6,7},{7,6},{8,9},{9,8},{10,11... | collective-permute-start | bytes 786440 | tf_op jit(solution)/shard_map/ppermute | solution.py:387
  54.4 9.3 %collective-permute-start.19 = (bf16[24,4096]{1,0:T(8,128)(2,1)S(1)}, bf16[24,4096]{1,0:T(8,128)(2,1)S(1)}, u32[]{:S(2)}, u32[]{:S(2)}) collective-permute-start(bf16[24,4096]{1,0:T(8,128)(2,1)S(1)} %constant_dynamic-update-slice_fusion.refs_1_), channel_id=1, source_target_pairs={{0,2},{1,3},{2,0},{3,1},{4,6},{5,7},{6,4},{7,5},{8,10},{9,11},{10,... | collective-permute-start | bytes 589832 | tf_op jit(solution)/shard_map/ppermute | solution.py:387
  63.8 1.6 %collective-permute-start.21 = (bf16[32,4096]{1,0:T(8,128)(2,1)S(1)}, bf16[32,4096]{1,0:T(8,128)(2,1)S(1)}, u32[]{:S(2)}, u32[]{:S(2)}) collective-permute-start(bf16[32,4096]{1,0:T(8,128)(2,1)S(1)} %pad_maximum_fusion.1), channel_id=1, source_target_pairs={{0,1},{1,0},{2,3},{3,2},{4,5},{5,4},{6,7},{7,6},{8,9},{9,8},{10,11... | collective-permute-start | bytes 786440 | tf_op jit(solution)/shard_map/ppermute | solution.py:387
  67.4 2.0 %collective-permute-start.22 = (bf16[64,4096]{1,0:T(8,128)(2,1)S(1)}, bf16[64,4096]{1,0:T(8,128)(2,1)S(1)}, u32[]{:S(2)}, u32[]{:S(2)}) collective-permute-start(bf16[64,4096]{1,0:T(8,128)(2,1)S(1)} %get-tuple-element.76), channel_id=1, source_target_pairs={{0,1},{1,0},{2,3},{3,2},{4,5},{5,4},{6,7},{7,6},{8,9},{9,8},{10,11... | collective-permute-start | bytes 1572872 | tf_op jit(solution)/shard_map/ppermute | solution.py:387
  69.5 9.3 %collective-permute-start.23 = (bf16[32,4096]{1,0:T(8,128)(2,1)S(1)}, bf16[32,4096]{1,0:T(8,128)(2,1)S(1)}, u32[]{:S(2)}, u32[]{:S(2)}) collective-permute-start(bf16[32,4096]{1,0:T(8,128)(2,1)S(1)} %slice.35), channel_id=1, source_target_pairs={{0,2},{1,3},{2,0},{3,1},{4,6},{5,7},{6,4},{7,5},{8,10},{9,11},{10,... | collective-permute-start | bytes 786440 | tf_op jit(solution)/shard_map/ppermute | solution.py:387
  78.8 11.1 %collective-permute-start.26 = (bf16[8,4096]{1,0:T(8,128)(2,1)S(1)}, bf16[8,4096]{1,0:T(8,128)(2,1)S(1)}, u32[]{:S(2)}, u32[]{:S(2)}) collective-permute-start(bf16[8,4096]{1,0:T(8,128)(2,1)S(1)} %get-tuple-element.77), channel_id=1, source_target_pairs={{0,4},{1,5},{2,6},{3,7},{4,8},{5,9},{6,10},{7,11},{8,12},{9,13},{1... | collective-permute-start | bytes 196616 | tf_op jit(solution)/shard_map/ppermute | solution.py:387
  78.9 11.1 %collective-permute-start.25 = (bf16[8,4096]{1,0:T(8,128)(2,1)S(1)}, bf16[8,4096]{1,0:T(8,128)(2,1)S(1)}, u32[]{:S(2)}, u32[]{:S(2)}) collective-permute-start(bf16[8,4096]{1,0:T(8,128)(2,1)S(1)} %get-tuple-element.78), channel_id=1, source_target_pairs={{0,8},{1,9},{2,10},{3,11},{4,12},{5,13},{6,14},{7,15},{8,0},{9,1},... | collective-permute-start | bytes 196616 | tf_op jit(solution)/shard_map/ppermute | solution.py:387
  79.0 11.0 %copy-start.2 = (s32[128,4]{0,1:T(4,128)S(1)}, s32[128,4]{0,1:T(4,128)}, u32[]{:S(2)}) copy-start(s32[128,4]{0,1:T(4,128)} %param.17) | copy-start | bytes 6148
  79.0 11.0 %copy-start.3 = (f32[128,4]{0,1:T(4,128)S(1)}, f32[128,4]{0,1:T(4,128)}, u32[]{:S(2)}) copy-start(f32[128,4]{0,1:T(4,128)} %param.18) | copy-start | bytes 6148
  79.0 11.0 %collective-permute-start.24 = (bf16[8,4096]{1,0:T(8,128)(2,1)S(1)}, bf16[8,4096]{1,0:T(8,128)(2,1)S(1)}, u32[]{:S(2)}, u32[]{:S(2)}) collective-permute-start(bf16[8,4096]{1,0:T(8,128)(2,1)S(1)} %get-tuple-element.79), channel_id=1, source_target_pairs={{0,12},{1,13},{2,14},{3,15},{4,0},{5,1},{6,2},{7,3},{8,4},{9,5},{1... | collective-permute-start | bytes 196616 | tf_op jit(solution)/shard_map/ppermute | solution.py:387
where the time goes:
time: 92.2 us; the launch traced here: 91.9 us
  Pallas kernels  55.8 us (61%)
  starting transfers between devices  19.4 us (21%)
  waiting for transfers between devices  16.1 us (17%)
    pallas_call x4, Pallas kernels, own(): pl.pallas_call(functools.partial(own_kernel, n, part, len(sources)), out_...  35.4 us
    ppermute x27, starting transfers between devices, move(): return lax.ppermute(value, 'expert', pairs)  19.4 us
    ppermute x27, waiting for transfers between devices, move(): return lax.ppermute(value, 'expert', pairs)  16.1 us
    pallas_call x1, Pallas kernels, local(): pl.pallas_call(functools.partial(routed_kernel, n, list(kv)), out_shape=[...  13.2 us
    pallas_call x1, Pallas kernels, local(): pl.pallas_call(functools.partial(select_kernel, planes), out_shape=[jax.S...  2.21 us
    pallas_call x1, Pallas kernels, local(): pl.pallas_call(functools.partial(expert_kernel, n, len(pieces)), out_shap...  1.97 us
    pallas_call x1, Pallas kernels, local(): pl.pallas_call(functools.partial(combine_kernel, planes), out_shape=jax.S...  1.87 us
  transfers between devices with their start and end apart: 27, of which 11 were waited for; matrix products, arithmetic and copies ran while one was open for 0% of the time, Pallas kernels for 41%

commit v1 on v0

--- a/solution.py
+++ b/solution.py
@@ -17,7 +17,7 @@
 TILE = 128
 KEYS = 256
 KV_ROWS = TILE + 16
-SCALE = 1.0 / math.sqrt(HEAD)
+SCALE = math.log2(math.e) / math.sqrt(HEAD)
 LOW = -1e30
 EXTRA = 16
 F32 = jnp.float32
@@ -114,7 +114,8 @@
                 ],
                 axis=0,
             )
-            qs_ref[h, :, k * TILE : (k + 1) * TILE] = stack.T.astype(BF16)
+            for i, term in enumerate(two_terms(stack.T)):
+                qs_ref[h, i * HEAD : (i + 1) * HEAD, k * TILE : (k + 1) * TILE] = term
 
 
 def doc_starts(n, pos, held):
@@ -137,65 +138,89 @@
     return first
 
 
-def flash(pos, held, queries, kv_heads, sides, acc_ref, bias_ref, places, firsts):
-    lanes = places[0].shape[1]
-    chains = range(len(queries))
+def two_terms(x):
+    scaled = x.astype(F32) * SCALE
+    high = scaled.astype(BF16)
+    return high, (scaled - high.astype(F32)).astype(BF16)
+
+
+def key_steps(pos, place, first, axis, bias_ref, step, state):
+    low = jnp.min(first).astype(jnp.int32) // KEYS
+    last = pos // (KEYS // TILE)
+    clear = jnp.minimum((jnp.max(first).astype(jnp.int32) + KEYS - 1) // KEYS, last)
+    shape = (KEYS, 1) if axis == 0 else (1, KEYS)
+
+    def edge(j, carried):
+        kb = jnp.where(j < clear - low, low + j, last)
+        key_at = (kb * KEYS + lax.broadcasted_iota(jnp.int32, shape, axis)).astype(F32)
+        bias_ref[...] = jnp.where((key_at >= first) & (key_at <= place), 0.0, LOW)
+        return step(kb, carried, True)
+
+    state = lax.fori_loop(0, clear - low + 1, edge, state)
+    return lax.fori_loop(clear, last, lambda kb, carried: step(kb, carried, False), state)
+
+
+def keys_of(held, kb, h):
+    keys = jnp.concatenate(
+        [held[2 * kb + t, 0:TILE, h * HEAD : (h + 1) * HEAD] for t in range(2)], axis=0
+    )
+    return jnp.concatenate([keys, keys], axis=1)
+
+
+def values_of(held, kb, h, extra):
+    at = (KV_HEADS + h) * HEAD
+    values = jnp.concatenate(
+        [held[2 * kb + t, 0:TILE, at : at + HEAD] for t in range(2)], axis=1
+    )
+    return jnp.concatenate([values, jnp.ones((extra, KEYS), BF16)], axis=0)
+
+
+def flash(pos, held, q_ref, kv_heads, acc_ref, bias_ref, place, first):
+    lanes = place.shape[1]
+    chains = range(len(kv_heads))
     for i in chains:
         acc_ref[i] = jnp.zeros((HEAD + EXTRA, lanes), F32)
-    lowest = functools.reduce(jnp.minimum, [jnp.min(first) for first in firsts])
-    highest = functools.reduce(jnp.maximum, [jnp.max(first) for first in firsts])
-    low = lowest.astype(jnp.int32) // KEYS
-    last = pos // (KEYS // TILE)
-    clear = jnp.minimum((highest.astype(jnp.int32) + KEYS - 1) // KEYS, last)
-
-    def scores(kb, i, masked):
-        h = kv_heads[i]
-        keys = jnp.concatenate(
-            [held[2 * kb + t, 0:TILE, h * HEAD : (h + 1) * HEAD] for t in range(2)], axis=0
+
+    def step(kb, tops, masked):
+        out = []
+        for i in chains:
+            scores = dot(keys_of(held, kb, kv_heads[i]), q_ref[i])
+            if masked:
+                scores = scores + bias_ref[...]
+            top = jnp.maximum(tops[i], jnp.max(scores, axis=0, keepdims=True))
+            weights = jnp.exp2(scores - top).astype(BF16)
+            acc_ref[i] = acc_ref[i] * jnp.exp2(tops[i] - top) + dot(
+                values_of(held, kb, kv_heads[i], EXTRA), weights
+            )
+            out.append(top)
+        return tuple(out)
+
+    tops = tuple(jnp.full((1, lanes), LOW, F32) for _ in chains)
+    key_steps(pos, place, first, 0, bias_ref, step, tops)
+    return [(acc_ref[i, 0:HEAD] / acc_ref[i, HEAD : HEAD + 1]).T for i in chains]
+
+
+def flash_rows(pos, held, q_ref, h, acc_ref, top_ref, bias_ref, place, first):
+    rows = q_ref.shape[0]
+    acc_ref[...] = jnp.zeros((rows, 2 * HEAD), F32)
+    top_ref[...] = jnp.full((rows, HEAD), LOW, F32)
+
+    def step(kb, carried, masked):
+        scores = dot(q_ref[...], keys_of(held, kb, h), 1, 1)
+        if masked:
+            scores = scores + jnp.concatenate([bias_ref[...]] * (rows // TILE), axis=0)
+        old = top_ref[...]
+        top = jnp.maximum(old, jnp.max(scores, axis=1, keepdims=True))
+        top_ref[...] = top
+        weights = jnp.exp2(scores - jnp.concatenate([top, top], axis=1)).astype(BF16)
+        factor = jnp.exp2(old - top)
+        acc_ref[...] = acc_ref[...] * jnp.concatenate([factor, factor], axis=1) + dot(
+            weights, values_of(held, kb, h, HEAD), 1, 1
         )
-        result = dot(keys, queries[i]())
-        if masked:
-            result = result + bias_ref[sides[i]]
-        return result
-
-    def hide(kb):
-        key_at = (kb * KEYS + lax.broadcasted_iota(jnp.int32, (KEYS, 1), 0)).astype(F32)
-        for side, (place, first) in enumerate(zip(places, firsts)):
-            bias_ref[side] = jnp.where((key_at >= first) & (key_at <= place), 0.0, LOW)
-
-    def over_keys(step, state):
-        def edge(j, carried):
-            kb = jnp.where(j < clear - low, low + j, last)
-            hide(kb)
-            return step(kb, carried, True)
-
-        state = lax.fori_loop(0, clear - low + 1, edge, state)
-        return lax.fori_loop(clear, last, lambda kb, carried: step(kb, carried, False), state)
-
-    def eights(x):
-        return x.reshape(KEYS // 8, 8, lanes)
-
-    def find(kb, carried, masked):
-        return tuple(
-            jnp.maximum(carried[i], jnp.max(eights(scores(kb, i, masked)), axis=0)) for i in chains
-        )
-
-    tops = over_keys(find, tuple(jnp.full((8, lanes), LOW, F32) for _ in chains))
-    tops = [jnp.max(top, axis=0, keepdims=True) for top in tops]
-
-    def add(kb, carried, masked):
-        for i in chains:
-            at = (KV_HEADS + kv_heads[i]) * HEAD
-            values = jnp.concatenate(
-                [held[2 * kb + t, 0:TILE, at : at + HEAD] for t in range(2)], axis=1
-            )
-            values = jnp.concatenate([values, jnp.ones((EXTRA, KEYS), BF16)], axis=0)
-            weights = jnp.exp(((scores(kb, i, masked) - tops[i]) * SCALE).astype(BF16))
-            acc_ref[i] += dot(values, weights)
         return carried
 
-    over_keys(add, 0)
-    return [(acc_ref[i, 0:HEAD] / acc_ref[i, HEAD : HEAD + 1]).T for i in chains]
+    key_steps(pos, place, first, 1, bias_ref, step, 0)
+    return acc_ref[:, 0:HEAD] / acc_ref[:, HEAD:]
 
 
 def routed_kernel(n, senders, pos_ref, gain_ref, qs_ref, xs_ref, facts_ref, *refs):
@@ -204,7 +229,7 @@
     pieces = refs[:count]
     outs = refs[count : count + planes]
     held = refs[count + planes]
-    acc, bias, state, gain, sems = refs[count + planes + 1 :]
+    acc, bias, q_scr, state, gain, sems = refs[count + planes + 1 :]
     pos = pos_ref[0]
     z, y, c = pos // SHARDS, (pos // 2) % 2, pos % 2
     copies = []
@@ -217,31 +242,29 @@
     for copy in copies:
         copy.wait()
     starts = doc_starts(n, pos, held)
-    lanes = 2 * TILE
+    lanes = q_scr.shape[2]
     base = (pos * TILE).astype(F32)
-    for pair in range(0, planes // 2, 2):
-        parts = range(pair, min(pair + 2, planes // 2))
-        columns = [slice(part * lanes, (part + 1) * lanes) for part in parts]
-        chains = [(i, h) for i in range(len(parts)) for h in range(KV_HEADS)]
+    for part in range(planes * TILE // lanes):
+        at = slice(part * lanes, (part + 1) * lanes)
+        q_scr[...] = qs_ref[:, :, at]
         done = flash(
             pos,
             held,
-            [lambda i=i, h=h: qs_ref[h, :, columns[i]] for i, h in chains],
-            [h for _, h in chains],
-            [i for i, _ in chains],
+            q_scr,
+            range(KV_HEADS),
             acc,
             bias,
-            [facts_ref[0:1, at] + base for at in columns],
-            [starts_of(facts_ref[1:2, at], starts) for at in columns],
+            facts_ref[0:1, at] + base,
+            starts_of(facts_ref[1:2, at], starts),
         )
-        for (i, h), rows in zip(chains, done):
-            for k in range(2):
-                row = (parts[i] * 2 + k) * SLOTS
+        for h in range(KV_HEADS):
+            for k in range(lanes // TILE):
+                row = (part * (lanes // TILE) + k) * SLOTS
                 for g in range(GROUP):
                     lane = (h * GROUP + g) * HEAD
                     state[row : row + SLOTS, lane : lane + HEAD] = (
                         xs_ref[row : row + SLOTS, lane : lane + HEAD]
-                        + rows[k * TILE + g * SLOTS : k * TILE + (g + 1) * SLOTS]
+                        + done[h][k * TILE + g * SLOTS : k * TILE + (g + 1) * SLOTS]
                     )
     for k in range(planes):
         hidden = state[k * SLOTS : (k + 1) * SLOTS, :]
@@ -285,7 +308,7 @@
 def own_kernel(n, part, loads, pos_ref, held, q_ref, x_ref, _, *refs):
     sources, (h_ref, done_ref) = refs[:loads], refs[loads : loads + 2]
     targets = refs[loads + 2 : 2 * loads + 2]
-    acc, bias, qt, sems = refs[2 * loads + 2 :]
+    acc, bias, top, qt, sems = refs[2 * loads + 2 :]
     moves = [
         pltpu.make_async_copy(source.at[0], target, sems.at[i])
         for i, (source, target) in enumerate(zip(sources, targets))
@@ -297,30 +320,26 @@
     starts = doc_starts(n, pos, held)
     first = starts_of(held[pos, TILE:KV_ROWS, 0:HEAD].astype(F32)[0:1], starts)
     place = (pos * TILE + lax.broadcasted_iota(jnp.int32, (1, TILE), 1)).astype(F32)
-    place = jnp.concatenate([place] * 2, axis=1)
-    first = jnp.concatenate([first] * 2, axis=1)
-
+    if part < 2:
+        for a in range(8):
+            terms = two_terms(q_ref[:, a * HEAD : (a + 1) * HEAD].astype(F32).T)
+            for i, term in enumerate(terms):
+                qt[0, i * HEAD : (i + 1) * HEAD, a * TILE : (a + 1) * TILE] = term
+        place = jnp.concatenate([place] * 8, axis=1)
+        first = jnp.concatenate([first] * 8, axis=1)
+        (done,) = flash(pos, held, qt, [part // 2], acc, bias, place, first)
+    else:
+        for a in range(8):
+            for i, term in enumerate(two_terms(q_ref[:, a * HEAD : (a + 1) * HEAD])):
+                qt[a * TILE : (a + 1) * TILE, i * HEAD : (i + 1) * HEAD] = term
+        place = jnp.broadcast_to(place, (TILE, TILE)).T[:, 0:1]
+        first = jnp.broadcast_to(first, (TILE, TILE)).T[:, 0:1]
+        done = flash_rows(pos, held, qt, part // 2, acc, top, bias, place, first)
     for a in range(8):
-        qt[a // 2, :, (a % 2) * TILE : (a % 2 + 1) * TILE] = (
-            q_ref[:, a * HEAD : (a + 1) * HEAD].astype(F32).T.astype(BF16)
+        lane = a * HEAD
+        h_ref[:, lane : lane + HEAD] = (
+            x_ref[:, lane : lane + HEAD].astype(F32) + done[a * TILE : (a + 1) * TILE]
         )
-    done = flash(
-        pos,
-        held,
-        [lambda i=i: qt[i] for i in range(4)],
-        [part // 2] * 4,
-        [0] * 4,
-        acc,
-        bias,
-        [place],
-        [first],
-    )
-    for i in range(4):
-        for g in range(2):
-            lane = (2 * i + g) * HEAD
-            h_ref[:, lane : lane + HEAD] = (
-                x_ref[:, lane : lane + HEAD].astype(F32) + done[i][g * TILE : (g + 1) * TILE]
-            )
     for move in moves:
         move.wait()
 
@@ -396,7 +415,7 @@
     q_rows, x_rows, facts = pl.pallas_call(
         functools.partial(select_kernel, planes),
         out_shape=[
-            jax.ShapeDtypeStruct((KV_HEADS, HEAD, planes * TILE), BF16),
+            jax.ShapeDtypeStruct((KV_HEADS, 2 * HEAD, planes * TILE), BF16),
             jax.ShapeDtypeStruct((planes * SLOTS, width), F32),
             jax.ShapeDtypeStruct((8, planes * TILE), F32),
         ],
@@ -439,8 +458,9 @@
         in_specs=[SMEM, HBM] + [VMEM] * 3 + [ANY] * len(kv),
         out_specs=[VMEM] * (planes + 1),
         scratch_shapes=[
-            pltpu.VMEM((4, HEAD + EXTRA, 2 * TILE), F32),
-            pltpu.VMEM((2, KEYS, 2 * TILE), F32),
+            pltpu.VMEM((KV_HEADS, HEAD + EXTRA, 4 * TILE), F32),
+            pltpu.VMEM((KEYS, 4 * TILE), F32),
+            pltpu.VMEM((KV_HEADS, 2 * HEAD, 4 * TILE), BF16),
             pltpu.VMEM((planes * SLOTS, width), F32),
             pltpu.VMEM((1, width), F32),
             pltpu.SemaphoreType.DMA((len(kv) + 1,)),
@@ -466,9 +486,10 @@
             ]
             + [VMEM] * len(sources),
             scratch_shapes=[
-                pltpu.VMEM((4, HEAD + EXTRA, 2 * TILE), F32),
-                pltpu.VMEM((1, KEYS, 2 * TILE), F32),
-                pltpu.VMEM((4, HEAD, 2 * TILE), BF16),
+                pltpu.VMEM((1, HEAD + EXTRA, 8 * TILE) if part < 2 else (8 * TILE, 2 * HEAD), F32),
+                pltpu.VMEM((KEYS, 8 * TILE) if part < 2 else (TILE, KEYS), F32),
+                pltpu.VMEM((8 * TILE, HEAD), F32),
+                pltpu.VMEM((1, 2 * HEAD, 8 * TILE) if part < 2 else (8 * TILE, 2 * HEAD), BF16),
                 pltpu.SemaphoreType.DMA((3,)),
             ],
             compiler_params=params(small),

time: 92.2 us -> 84.5 us (0.916)
  the two profiles are of different devices: /device:TPU:22 before, /device:TPU:0 now
where the time goes in v1:
time: 84.5 us; the launch traced here: 84.2 us
  starting transfers between devices  36 us (43%)
  waiting for transfers between devices  25.9 us (31%)
  Pallas kernels  21.8 us (26%)
    ppermute x27, starting transfers between devices, move(): return lax.ppermute(value, 'expert', pairs)  36 us
    ppermute x27, waiting for transfers between devices, move(): return lax.ppermute(value, 'expert', pairs)  25.9 us
    pallas_call x4, Pallas kernels, own(): pl.pallas_call(functools.partial(own_kernel, n, part, len(sources)), out_...  8.7 us
    pallas_call x1, Pallas kernels, local(): pl.pallas_call(functools.partial(routed_kernel, n, list(kv)), out_shape=[...  5.9 us
    pallas_call x1, Pallas kernels, local(): pl.pallas_call(functools.partial(select_kernel, planes), out_shape=[jax.S...  2.21 us
    pallas_call x1, Pallas kernels, local(): pl.pallas_call(functools.partial(expert_kernel, n, len(pieces)), out_shap...  1.96 us
    pallas_call x1, Pallas kernels, local(): pl.pallas_call(functools.partial(combine_kernel, planes), out_shape=jax.S...  1.88 us
  transfers between devices with their start and end apart: 27, of which 11 were waited for; matrix products, arithmetic and copies ran while one was open for 0% of the time, Pallas kernels for 13%

profile of v1, /device:TPU:0, one launch (start us, length us, event | category | flops | bytes accessed | tf_op | source)
XLA Modules:
  0.0 84.2 jit_solution(12836580373056520376)
XLA Ops:
  0.0 1.1 %pack.1.refs_0_ = bf16[144,512]{1,0:T(8,128)(2,1)S(1)} custom-call(s32[1,128]{1,0:T(1,128)} %bitcast.9, bf16[128,256]{1,0:T(8,128)(2,1)} %keys_ref.1, bf16[128,256]{1,0:T(8,128)(2,1)} %values_ref.1), custom_call_target="tpu_custom_call" | custom-call | tf_op jit(solution)/shard_map/pack/pallas_call | solution.py:391
  1.1 3.1 %collective-permute-start.1 = (bf16[144,512]{1,0:T(8,128)(2,1)S(1)}, bf16[144,512]{1,0:T(8,128)(2,1)S(1)}, u32[]{:S(2)}, u32[]{:S(2)}) collective-permute-start(bf16[144,512]{1,0:T(8,128)(2,1)S(1)} %pack.1.refs_0_), channel_id=1, source_target_pairs={{0,4},{1,5},{2,6},{3,7},{4,8},{5,9},{6,10},{7,11},{8,12},{9,13},{1... | collective-permute-start | bytes 442376 | tf_op jit(solution)/shard_map/ppermute | solution.py:406
  4.2 1.5 %collective-permute-start = (bf16[144,512]{1,0:T(8,128)(2,1)S(1)}, bf16[144,512]{1,0:T(8,128)(2,1)S(1)}, u32[]{:S(2)}, u32[]{:S(2)}) collective-permute-start(bf16[144,512]{1,0:T(8,128)(2,1)S(1)} %pack.1.refs_0_), channel_id=1, source_target_pairs={{0,2},{1,3},{2,0},{3,1},{4,6},{5,7},{6,4},{7,5},{8,10},{9,11},{10,... | collective-permute-start | bytes 442376 | tf_op jit(solution)/shard_map/ppermute | solution.py:406
  5.7 2.2 %select.1 = (bf16[2,256,512]{2,1,0:T(8,128)(2,1)S(1)}, f32[32,4096]{1,0:T(8,128)S(1)}, f32[8,512]{1,0:T(8,128)S(1)}) custom-call(s32[1]{0:T(128)} %bitcast.pos_ref, s32[4,128]{1,0:T(4,128)} %bitcast.5, s32[1,128]{1,0:T(1,128)} %bitcast.10, bf16[128,4096]{1,0:T(8,128)(2,1)} %q_ref.7, bf16[128,4096]{1,0:T(8,128)(2,1)} %x_ref.7), custom_call_target="tpu_custom_call" | custom-call | tf_op jit(solution)/shard_map/select/pallas_call | solution.py:415
  8.0 2.1 %collective-permute-done.1.refs_1_ = bf16[144,512]{1,0:T(8,128)(2,1)S(1)} collective-permute-done((bf16[144,512]{1,0:T(8,128)(2,1)S(1)}, bf16[144,512]{1,0:T(8,128)(2,1)S(1)}, u32[]{:S(2)}, u32[]{:S(2)}) %collective-permute-start.1) | collective-permute-done | bytes 147488 | tf_op jit(solution)/shard_map/ppermute | solution.py:406
  10.1 1.0 %collective-permute-start.3 = (bf16[144,512]{1,0:T(8,128)(2,1)S(1)}, bf16[144,512]{1,0:T(8,128)(2,1)S(1)}, u32[]{:S(2)}, u32[]{:S(2)}) collective-permute-start(bf16[144,512]{1,0:T(8,128)(2,1)S(1)} %collective-permute-done.1.refs_1_), channel_id=1, source_target_pairs={{0,4},{1,5},{2,6},{3,7},{4,8},{5,9},{6,10},{7,11},{8,12},{9,13},{1... | collective-permute-start | bytes 442376 | tf_op jit(solution)/shard_map/ppermute | solution.py:406
  11.1 0.7 collective-permute-start.2
  11.8 5.3 %collective-permute-done.3.refs_3_ = bf16[144,512]{1,0:T(8,128)(2,1)S(1)} collective-permute-done((bf16[144,512]{1,0:T(8,128)(2,1)S(1)}, bf16[144,512]{1,0:T(8,128)(2,1)S(1)}, u32[]{:S(2)}, u32[]{:S(2)}) %collective-permute-start.3) | collective-permute-done | bytes 147488 | tf_op jit(solution)/shard_map/ppermute | solution.py:406
  17.0 0.7 collective-permute-start.5
  17.7 0.7 collective-permute-start.4
  18.4 0.1 collective-permute-start.7
  18.5 0.5 collective-permute-start.8
  19.0 0.1 collective-permute-start.9
  19.0 0.7 collective-permute-start.6
  19.7 0.5 collective-permute-start.10
  20.2 0.1 collective-permute-start.11
  20.3 0.0 collective-permute-done.9.refs_10_
  20.3 0.4 collective-permute-start.12
  20.7 0.1 collective-permute-start.13
  20.8 0.4 collective-permute-start.14
  21.2 0.3 collective-permute-done.11.refs_12_
  21.6 0.5 collective-permute-done.13.refs_14_
  22.1 0.2 collective-permute-done.14.refs_15_
  22.3 5.9 %routed.1 = (bf16[8,4096]{1,0:T(8,128)(2,1)S(1)}, bf16[8,4096]{1,0:T(8,128)(2,1)S(1)}, bf16[8,4096]{1,0:T(8,128)(2,1)S(1)}, bf16[8,4096]{1,0:T(8,128)(2,1)S(1)}, bf16[16,144,512]{2,1,0:T(8,128)(2,1)S(1)}) custom-call(s32[1]{0:T(128)} %bitcast.pos_ref, f32[1,4096]{1,0:T(1,128)} %bitcast.8, bf16[2,256,512]{2,1,0:T(8,128)(2,1)S(1)} %get-tuple-element.46.qs_ref, ...), custom_call_target="tpu_custom_call" | custom-call | tf_op jit(solution)/shard_map/routed/pallas_call | solution.py:454
  28.2 4.3 %collective-permute-start.15 = (bf16[8,4096]{1,0:T(8,128)(2,1)S(1)}, bf16[8,4096]{1,0:T(8,128)(2,1)S(1)}, u32[]{:S(2)}, u32[]{:S(2)}) collective-permute-start(bf16[8,4096]{1,0:T(8,128)(2,1)S(1)} %get-tuple-element.58), channel_id=1, source_target_pairs={{0,4},{1,5},{2,6},{3,7},{4,8},{5,9},{6,10},{7,11},{8,12},{9,13},{1... | collective-permute-start | bytes 196616 | tf_op jit(solution)/shard_map/ppermute | solution.py:406
  32.6 12.6 %collective-permute-start.16 = (bf16[8,4096]{1,0:T(8,128)(2,1)S(1)}, bf16[8,4096]{1,0:T(8,128)(2,1)S(1)}, u32[]{:S(2)}, u32[]{:S(2)}) collective-permute-start(bf16[8,4096]{1,0:T(8,128)(2,1)S(1)} %get-tuple-element.59), channel_id=1, source_target_pairs={{0,8},{1,9},{2,10},{3,11},{4,12},{5,13},{6,14},{7,15},{8,0},{9,1},... | collective-permute-start | bytes 196616 | tf_op jit(solution)/shard_map/ppermute | solution.py:406
  45.1 0.1 collective-permute-start.17
  45.2 2.8 %collective-permute-start.18 = (bf16[8,4096]{1,0:T(8,128)(2,1)S(1)}, bf16[8,4096]{1,0:T(8,128)(2,1)S(1)}, u32[]{:S(2)}, u32[]{:S(2)}) collective-permute-start(bf16[8,4096]{1,0:T(8,128)(2,1)S(1)} %get-tuple-element.54._.refs_0_), channel_id=1, source_target_pairs={{0,2},{1,3},{2,0},{3,1},{4,6},{5,7},{6,4},{7,5},{8,10},{9,11},{10,... | collective-permute-start | bytes 196616 | tf_op jit(solution)/shard_map/ppermute | solution.py:406
  48.1 3.8 %own.4 = (f32[128,1024]{1,0:T(8,128)S(1)}, f32[8,128]{1,0:T(8,128)S(1)}, bf16[4096,384]{1,0:T(8,128)(2,1)S(1)}, bf16[4096,384]{1,0:T(8,128)(2,1)S(1)}, bf16[384,4096]{1,0:T(8,128)(2,1)S(1)}) custom-call(s32[1]{0:T(128)} %bitcast.pos_ref, bf16[16,144,512]{2,1,0:T(8,128)(2,1)S(1)} %get-tuple-element.53.held, bf16[128,4096]{1,0:T(8,128)(2,1)S(1)} %copy-done, ...), custom_call_target="tpu_custom_call" | custom-call | flops 2000000000 | bytes 8000000 | tf_op jit(solution)/shard_map/own/pallas_call | solution.py:474
  52.0 0.1 collective-permute-start.20
  52.1 0.5 collective-permute-start.19
  52.6 1.2 %own.5 = (f32[128,1024]{1,0:T(8,128)S(1)}, f32[8,128]{1,0:T(8,128)S(1)}) custom-call(s32[1]{0:T(128)} %bitcast.pos_ref, bf16[16,144,512]{2,1,0:T(8,128)(2,1)S(1)} %get-tuple-element.53.held, bf16[128,4096]{1,0:T(8,128)(2,1)S(1)} %copy-done, bf16[128,4096]{1,0:T(8,128)(2,1)S(1)} %copy-done.1, f32[8,128]{1,0:T(8,128)S(1)} %get-tuple-element.56._), custom_call_target="tpu_custom_call" | custom-call | flops 2000000000 | bytes 8000000 | tf_op jit(solution)/shard_map/own/pallas_call | solution.py:474
  53.8 5.6 %collective-permute-done.19.refs_3_ = bf16[24,4096]{1,0:T(8,128)(2,1)S(1)} collective-permute-done((bf16[24,4096]{1,0:T(8,128)(2,1)S(1)}, bf16[24,4096]{1,0:T(8,128)(2,1)S(1)}, u32[]{:S(2)}, u32[]{:S(2)}) %collective-permute-start.19) | collective-permute-done | bytes 196640 | tf_op jit(solution)/shard_map/ppermute | solution.py:406
  59.4 0.1 collective-permute-start.21
  59.5 1.5 %collective-permute-done.21.refs_5_ = bf16[32,4096]{1,0:T(8,128)(2,1)S(1)} collective-permute-done((bf16[32,4096]{1,0:T(8,128)(2,1)S(1)}, bf16[32,4096]{1,0:T(8,128)(2,1)S(1)}, u32[]{:S(2)}, u32[]{:S(2)}) %collective-permute-start.21) | collective-permute-done | bytes 262176 | tf_op jit(solution)/shard_map/ppermute | solution.py:406
  61.0 2.0 %expert.1 = (bf16[64,4096]{1,0:T(8,128)(2,1)S(1)}, bf16[64,4096]{1,0:T(8,128)(2,1)S(1)}) custom-call(bf16[8,4096]{1,0:T(8,128)(2,1)S(1)} %get-tuple-element.54._.refs_0_, bf16[24,4096]{1,0:T(8,128)(2,1)S(1)} %constant_dynamic-update-slice_fusion.refs_1_, bf16[8,4096]{1,0:T(8,128)(2,1)S(1)} %collective-permute-done.18.refs_2_, ...), custom_call_target="tpu_custom_call" | custom-call | flops 1200000000 | bytes 12000000 | tf_op jit(solution)/shard_map/expert/pallas_call | solution.py:518
  63.0 0.2 collective-permute-start.22
  63.2 1.8 %collective-permute-done.22 = bf16[64,4096]{1,0:T(8,128)(2,1)S(1)} collective-permute-done((bf16[64,4096]{1,0:T(8,128)(2,1)S(1)}, bf16[64,4096]{1,0:T(8,128)(2,1)S(1)}, u32[]{:S(2)}, u32[]{:S(2)}) %collective-permute-start.22) | collective-permute-done | bytes 524320 | tf_op jit(solution)/shard_map/ppermute | solution.py:406
  65.0 0.1 convert_add_fusion
  65.1 0.5 collective-permute-start.23
  65.6 1.8 %own.7 = (f32[128,1024]{1,0:T(8,128)S(1)}, f32[8,128]{1,0:T(8,128)}) custom-call(s32[1]{0:T(128)} %bitcast.pos_ref, bf16[16,144,512]{2,1,0:T(8,128)(2,1)S(1)} %get-tuple-element.53.held, bf16[128,4096]{1,0:T(8,128)(2,1)S(1)} %copy-done, bf16[128,4096]{1,0:T(8,128)(2,1)S(1)} %copy-done.1, bf16[64,4096]{1,0:T(8,128)(2,1)S(1)} %get-tuple-element.73._), custom_call_target="tpu_custom_call" | custom-call | flops 2000000000 | bytes 8000000 | tf_op jit(solution)/shard_map/own/pallas_call | solution.py:474
  67.5 6.1 %collective-permute-done.23 = bf16[32,4096]{1,0:T(8,128)(2,1)S(1)} collective-permute-done((bf16[32,4096]{1,0:T(8,128)(2,1)S(1)}, bf16[32,4096]{1,0:T(8,128)(2,1)S(1)}, u32[]{:S(2)}, u32[]{:S(2)}) %collective-permute-start.23) | collective-permute-done | bytes 262176 | tf_op jit(solution)/shard_map/ppermute | solution.py:406
  73.6 2.0 %collective-permute-start.26 = (bf16[8,4096]{1,0:T(8,128)(2,1)S(1)}, bf16[8,4096]{1,0:T(8,128)(2,1)S(1)}, u32[]{:S(2)}, u32[]{:S(2)}) collective-permute-start(bf16[8,4096]{1,0:T(8,128)(2,1)S(1)} %get-tuple-element.77), channel_id=1, source_target_pairs={{0,4},{1,5},{2,6},{3,7},{4,8},{5,9},{6,10},{7,11},{8,12},{9,13},{1... | collective-permute-start | bytes 196616 | tf_op jit(solution)/shard_map/ppermute | solution.py:406
  75.6 2.4 %collective-permute-start.24 = (bf16[8,4096]{1,0:T(8,128)(2,1)S(1)}, bf16[8,4096]{1,0:T(8,128)(2,1)S(1)}, u32[]{:S(2)}, u32[]{:S(2)}) collective-permute-start(bf16[8,4096]{1,0:T(8,128)(2,1)S(1)} %get-tuple-element.79), channel_id=1, source_target_pairs={{0,12},{1,13},{2,14},{3,15},{4,0},{5,1},{6,2},{7,3},{8,4},{9,5},{1... | collective-permute-start | bytes 196616 | tf_op jit(solution)/shard_map/ppermute | solution.py:406
  78.1 1.8 %own.6 = (f32[128,1024]{1,0:T(8,128)S(1)}, f32[8,128]{1,0:T(8,128)}) custom-call(s32[1]{0:T(128)} %bitcast.pos_ref, bf16[16,144,512]{2,1,0:T(8,128)(2,1)S(1)} %get-tuple-element.53.held, bf16[128,4096]{1,0:T(8,128)(2,1)S(1)} %copy-done, bf16[128,4096]{1,0:T(8,128)(2,1)S(1)} %copy-done.1, bf16[64,4096]{1,0:T(8,128)(2,1)S(1)} %get-tuple-element.73._), custom_call_target="tpu_custom_call" | custom-call | flops 2000000000 | bytes 8000000 | tf_op jit(solution)/shard_map/own/pallas_call | solution.py:474
  79.9 0.3 collective-permute-done.26.refs_7_
  80.2 2.1 %collective-permute-done.25.refs_6_ = bf16[8,4096]{1,0:T(8,128)(2,1)S(1)} collective-permute-done((bf16[8,4096]{1,0:T(8,128)(2,1)S(1)}, bf16[8,4096]{1,0:T(8,128)(2,1)S(1)}, u32[]{:S(2)}, u32[]{:S(2)}) %collective-permute-start.25) | collective-permute-done | bytes 65568 | tf_op jit(solution)/shard_map/ppermute | solution.py:406
  82.3 1.9 %combine.1 = bf16[128,4096]{1,0:T(8,128)(2,1)} custom-call(s32[1]{0:T(128)} %bitcast.pos_ref, s32[4,128]{1,0:T(4,128)S(1)} %bitcast.6, f32[4,128]{1,0:T(4,128)S(1)} %bitcast.7, f32[128,1024]{1,0:T(8,128)S(1)} %get-tuple-element.55.refs_0_, f32[128,1024]{1,0:T(8,128)S(1)} %get-tuple-element.57.refs_1_, f32[128,1024]{1,0:T(8,128)S(1)} %get-tuple-element.74.refs_2_, ...), custom_call_target="tpu_custom_call" | custom-call | tf_op jit(solution)/shard_map/combine/pallas_call | solution.py:545
  (32 shorter events, 0.2 us)
Async XLA Ops:
  0.0 48.1 %copy-start = (bf16[128,4096]{1,0:T(8,128)(2,1)S(1)}, bf16[128,4096]{1,0:T(8,128)(2,1)}, u32[]{:S(2)}) copy-start(bf16[128,4096]{1,0:T(8,128)(2,1)} %q_ref.7) | copy-start | bytes 3145732
  0.0 48.1 %copy-start.1 = (bf16[128,4096]{1,0:T(8,128)(2,1)S(1)}, bf16[128,4096]{1,0:T(8,128)(2,1)}, u32[]{:S(2)}) copy-start(bf16[128,4096]{1,0:T(8,128)(2,1)} %x_ref.7) | copy-start | bytes 3145732
  1.1 8.9 %collective-permute-start.1 = (bf16[144,512]{1,0:T(8,128)(2,1)S(1)}, bf16[144,512]{1,0:T(8,128)(2,1)S(1)}, u32[]{:S(2)}, u32[]{:S(2)}) collective-permute-start(bf16[144,512]{1,0:T(8,128)(2,1)S(1)} %pack.1.refs_0_), channel_id=1, source_target_pairs={{0,4},{1,5},{2,6},{3,7},{4,8},{5,9},{6,10},{7,11},{8,12},{9,13},{1... | collective-permute-start | bytes 442376 | tf_op jit(solution)/shard_map/ppermute | solution.py:406
  4.2 5.9 %collective-permute-start = (bf16[144,512]{1,0:T(8,128)(2,1)S(1)}, bf16[144,512]{1,0:T(8,128)(2,1)S(1)}, u32[]{:S(2)}, u32[]{:S(2)}) collective-permute-start(bf16[144,512]{1,0:T(8,128)(2,1)S(1)} %pack.1.refs_0_), channel_id=1, source_target_pairs={{0,2},{1,3},{2,0},{3,1},{4,6},{5,7},{6,4},{7,5},{8,10},{9,11},{10,... | collective-permute-start | bytes 442376 | tf_op jit(solution)/shard_map/ppermute | solution.py:406
  10.1 6.9 %collective-permute-start.3 = (bf16[144,512]{1,0:T(8,128)(2,1)S(1)}, bf16[144,512]{1,0:T(8,128)(2,1)S(1)}, u32[]{:S(2)}, u32[]{:S(2)}) collective-permute-start(bf16[144,512]{1,0:T(8,128)(2,1)S(1)} %collective-permute-done.1.refs_1_), channel_id=1, source_target_pairs={{0,4},{1,5},{2,6},{3,7},{4,8},{5,9},{6,10},{7,11},{8,12},{9,13},{1... | collective-permute-start | bytes 442376 | tf_op jit(solution)/shard_map/ppermute | solution.py:406
  11.1 5.9 %collective-permute-start.2 = (bf16[144,512]{1,0:T(8,128)(2,1)S(1)}, bf16[144,512]{1,0:T(8,128)(2,1)S(1)}, u32[]{:S(2)}, u32[]{:S(2)}) collective-permute-start(bf16[144,512]{1,0:T(8,128)(2,1)S(1)} %collective-permute-done.1.refs_1_), channel_id=1, source_target_pairs={{0,0},{1,1},{2,2},{3,3},{4,6},{5,7},{6,4},{7,5},{8,10},{9,11},{10,... | collective-permute-start | bytes 442376 | tf_op jit(solution)/shard_map/ppermute | solution.py:406
  17.0 2.0 %collective-permute-start.5 = (bf16[144,512]{1,0:T(8,128)(2,1)S(1)}, bf16[144,512]{1,0:T(8,128)(2,1)S(1)}, u32[]{:S(2)}, u32[]{:S(2)}) collective-permute-start(bf16[144,512]{1,0:T(8,128)(2,1)S(1)} %collective-permute-done.3.refs_3_), channel_id=1, source_target_pairs={{0,0},{1,1},{2,6},{3,7},{4,4},{5,5},{6,10},{7,11},{8,8},{9,9},{10,... | collective-permute-start | bytes 442376 | tf_op jit(solution)/shard_map/ppermute | solution.py:406
  17.7 1.3 %collective-permute-start.4 = (bf16[144,512]{1,0:T(8,128)(2,1)S(1)}, bf16[144,512]{1,0:T(8,128)(2,1)S(1)}, u32[]{:S(2)}, u32[]{:S(2)}) collective-permute-start(bf16[144,512]{1,0:T(8,128)(2,1)S(1)} %collective-permute-done.3.refs_3_), channel_id=1, source_target_pairs={{0,0},{1,1},{2,2},{3,3},{4,4},{5,5},{6,6},{7,7},{8,10},{9,11},{10,... | collective-permute-start | bytes 442376 | tf_op jit(solution)/shard_map/ppermute | solution.py:406
  18.4 1.8 %collective-permute-start.7 = (bf16[144,512]{1,0:T(8,128)(2,1)S(1)}, bf16[144,512]{1,0:T(8,128)(2,1)S(1)}, u32[]{:S(2)}, u32[]{:S(2)}) collective-permute-start(bf16[144,512]{1,0:T(8,128)(2,1)S(1)} %pack.1.refs_0_), channel_id=1, source_target_pairs={{0,1},{1,0},{2,3},{3,2},{4,5},{5,4},{6,7},{7,6},{8,9},{9,8},{10,11... | collective-permute-start | bytes 442376 | tf_op jit(solution)/shard_map/ppermute | solution.py:406
  18.5 2.3 %collective-permute-start.8 = (bf16[144,512]{1,0:T(8,128)(2,1)S(1)}, bf16[144,512]{1,0:T(8,128)(2,1)S(1)}, u32[]{:S(2)}, u32[]{:S(2)}) collective-permute-start(bf16[144,512]{1,0:T(8,128)(2,1)S(1)} %collective-permute-done.1.refs_1_), channel_id=1, source_target_pairs={{0,1},{1,0},{2,3},{3,2},{4,5},{5,4},{6,7},{7,6},{8,9},{9,8},{10,11... | collective-permute-start | bytes 442376 | tf_op jit(solution)/shard_map/ppermute | solution.py:406
  19.0 1.4 %collective-permute-start.9 = (bf16[144,512]{1,0:T(8,128)(2,1)S(1)}, bf16[144,512]{1,0:T(8,128)(2,1)S(1)}, u32[]{:S(2)}, u32[]{:S(2)}) collective-permute-start(bf16[144,512]{1,0:T(8,128)(2,1)S(1)} %collective-permute-done.refs_2_), channel_id=1, source_target_pairs={{0,1},{1,0},{2,3},{3,2},{4,5},{5,4},{6,7},{7,6},{8,9},{9,8},{10,11... | collective-permute-start | bytes 442376 | tf_op jit(solution)/shard_map/ppermute | solution.py:406
  19.0 1.8 %collective-permute-start.6 = (bf16[144,512]{1,0:T(8,128)(2,1)S(1)}, bf16[144,512]{1,0:T(8,128)(2,1)S(1)}, u32[]{:S(2)}, u32[]{:S(2)}) collective-permute-start(bf16[144,512]{1,0:T(8,128)(2,1)S(1)} %collective-permute-done.5.refs_5_), channel_id=1, source_target_pairs={{0,0},{1,1},{2,2},{3,3},{4,4},{5,5},{6,6},{7,7},{8,8},{9,9},{10,10... | collective-permute-start | bytes 442376 | tf_op jit(solution)/shard_map/ppermute | solution.py:406
  19.7 1.9 %collective-permute-start.10 = (bf16[144,512]{1,0:T(8,128)(2,1)S(1)}, bf16[144,512]{1,0:T(8,128)(2,1)S(1)}, u32[]{:S(2)}, u32[]{:S(2)}) collective-permute-start(bf16[144,512]{1,0:T(8,128)(2,1)S(1)} %collective-permute-done.3.refs_3_), channel_id=1, source_target_pairs={{0,1},{1,0},{2,3},{3,2},{4,5},{5,4},{6,7},{7,6},{8,9},{9,8},{10,11... | collective-permute-start | bytes 442376 | tf_op jit(solution)/shard_map/ppermute | solution.py:406
  20.2 1.4 %collective-permute-start.11 = (bf16[144,512]{1,0:T(8,128)(2,1)S(1)}, bf16[144,512]{1,0:T(8,128)(2,1)S(1)}, u32[]{:S(2)}, u32[]{:S(2)}) collective-permute-start(bf16[144,512]{1,0:T(8,128)(2,1)S(1)} %collective-permute-done.2.refs_4_), channel_id=1, source_target_pairs={{0,1},{1,0},{2,3},{3,2},{4,5},{5,4},{6,7},{7,6},{8,9},{9,8},{10,11... | collective-permute-start | bytes 442376 | tf_op jit(solution)/shard_map/ppermute | solution.py:406
  20.3 1.8 %collective-permute-start.12 = (bf16[144,512]{1,0:T(8,128)(2,1)S(1)}, bf16[144,512]{1,0:T(8,128)(2,1)S(1)}, u32[]{:S(2)}, u32[]{:S(2)}) collective-permute-start(bf16[144,512]{1,0:T(8,128)(2,1)S(1)} %collective-permute-done.5.refs_5_), channel_id=1, source_target_pairs={{0,1},{1,0},{2,3},{3,2},{4,5},{5,4},{6,7},{7,6},{8,9},{9,8},{10,11... | collective-permute-start | bytes 442376 | tf_op jit(solution)/shard_map/ppermute | solution.py:406
  20.7 1.4 %collective-permute-start.13 = (bf16[144,512]{1,0:T(8,128)(2,1)S(1)}, bf16[144,512]{1,0:T(8,128)(2,1)S(1)}, u32[]{:S(2)}, u32[]{:S(2)}) collective-permute-start(bf16[144,512]{1,0:T(8,128)(2,1)S(1)} %collective-permute-done.4.refs_6_), channel_id=1, source_target_pairs={{0,1},{1,0},{2,3},{3,2},{4,5},{5,4},{6,7},{7,6},{8,9},{9,8},{10,11... | collective-permute-start | bytes 442376 | tf_op jit(solution)/shard_map/ppermute | solution.py:406
  20.8 1.5 %collective-permute-start.14 = (bf16[144,512]{1,0:T(8,128)(2,1)S(1)}, bf16[144,512]{1,0:T(8,128)(2,1)S(1)}, u32[]{:S(2)}, u32[]{:S(2)}) collective-permute-start(bf16[144,512]{1,0:T(8,128)(2,1)S(1)} %collective-permute-done.6.refs_7_), channel_id=1, source_target_pairs={{0,1},{1,0},{2,3},{3,2},{4,5},{5,4},{6,7},{7,6},{8,9},{9,8},{10,11... | collective-permute-start | bytes 442376 | tf_op jit(solution)/shard_map/ppermute | solution.py:406
  28.2 23.7 %collective-permute-start.15 = (bf16[8,4096]{1,0:T(8,128)(2,1)S(1)}, bf16[8,4096]{1,0:T(8,128)(2,1)S(1)}, u32[]{:S(2)}, u32[]{:S(2)}) collective-permute-start(bf16[8,4096]{1,0:T(8,128)(2,1)S(1)} %get-tuple-element.58), channel_id=1, source_target_pairs={{0,4},{1,5},{2,6},{3,7},{4,8},{5,9},{6,10},{7,11},{8,12},{9,13},{1... | collective-permute-start | bytes 196616 | tf_op jit(solution)/shard_map/ppermute | solution.py:406
  32.6 19.4 %collective-permute-start.16 = (bf16[8,4096]{1,0:T(8,128)(2,1)S(1)}, bf16[8,4096]{1,0:T(8,128)(2,1)S(1)}, u32[]{:S(2)}, u32[]{:S(2)}) collective-permute-start(bf16[8,4096]{1,0:T(8,128)(2,1)S(1)} %get-tuple-element.59), channel_id=1, source_target_pairs={{0,8},{1,9},{2,10},{3,11},{4,12},{5,13},{6,14},{7,15},{8,0},{9,1},... | collective-permute-start | bytes 196616 | tf_op jit(solution)/shard_map/ppermute | solution.py:406
  45.1 6.8 %collective-permute-start.17 = (bf16[8,4096]{1,0:T(8,128)(2,1)S(1)}, bf16[8,4096]{1,0:T(8,128)(2,1)S(1)}, u32[]{:S(2)}, u32[]{:S(2)}) collective-permute-start(bf16[8,4096]{1,0:T(8,128)(2,1)S(1)} %get-tuple-element.60), channel_id=1, source_target_pairs={{0,12},{1,13},{2,14},{3,15},{4,0},{5,1},{6,2},{7,3},{8,4},{9,5},{1... | collective-permute-start | bytes 196616 | tf_op jit(solution)/shard_map/ppermute | solution.py:406
  45.2 6.7 %collective-permute-start.18 = (bf16[8,4096]{1,0:T(8,128)(2,1)S(1)}, bf16[8,4096]{1,0:T(8,128)(2,1)S(1)}, u32[]{:S(2)}, u32[]{:S(2)}) collective-permute-start(bf16[8,4096]{1,0:T(8,128)(2,1)S(1)} %get-tuple-element.54._.refs_0_), channel_id=1, source_target_pairs={{0,2},{1,3},{2,0},{3,1},{4,6},{5,7},{6,4},{7,5},{8,10},{9,11},{10,... | collective-permute-start | bytes 196616 | tf_op jit(solution)/shard_map/ppermute | solution.py:406
  52.0 7.4 %collective-permute-start.20 = (bf16[32,4096]{1,0:T(8,128)(2,1)S(1)}, bf16[32,4096]{1,0:T(8,128)(2,1)S(1)}, u32[]{:S(2)}, u32[]{:S(2)}) collective-permute-start(bf16[32,4096]{1,0:T(8,128)(2,1)S(1)} %pad_maximum_fusion), channel_id=1, source_target_pairs={{0,1},{1,0},{2,3},{3,2},{4,5},{5,4},{6,7},{7,6},{8,9},{9,8},{10,11... | collective-permute-start | bytes 786440 | tf_op jit(solution)/shard_map/ppermute | solution.py:406
  52.1 7.3 %collective-permute-start.19 = (bf16[24,4096]{1,0:T(8,128)(2,1)S(1)}, bf16[24,4096]{1,0:T(8,128)(2,1)S(1)}, u32[]{:S(2)}, u32[]{:S(2)}) collective-permute-start(bf16[24,4096]{1,0:T(8,128)(2,1)S(1)} %constant_dynamic-update-slice_fusion.refs_1_), channel_id=1, source_target_pairs={{0,2},{1,3},{2,0},{3,1},{4,6},{5,7},{6,4},{7,5},{8,10},{9,11},{10,... | collective-permute-start | bytes 589832 | tf_op jit(solution)/shard_map/ppermute | solution.py:406
  59.4 1.6 %collective-permute-start.21 = (bf16[32,4096]{1,0:T(8,128)(2,1)S(1)}, bf16[32,4096]{1,0:T(8,128)(2,1)S(1)}, u32[]{:S(2)}, u32[]{:S(2)}) collective-permute-start(bf16[32,4096]{1,0:T(8,128)(2,1)S(1)} %pad_maximum_fusion.1), channel_id=1, source_target_pairs={{0,1},{1,0},{2,3},{3,2},{4,5},{5,4},{6,7},{7,6},{8,9},{9,8},{10,11... | collective-permute-start | bytes 786440 | tf_op jit(solution)/shard_map/ppermute | solution.py:406
  63.0 2.0 %collective-permute-start.22 = (bf16[64,4096]{1,0:T(8,128)(2,1)S(1)}, bf16[64,4096]{1,0:T(8,128)(2,1)S(1)}, u32[]{:S(2)}, u32[]{:S(2)}) collective-permute-start(bf16[64,4096]{1,0:T(8,128)(2,1)S(1)} %get-tuple-element.76), channel_id=1, source_target_pairs={{0,1},{1,0},{2,3},{3,2},{4,5},{5,4},{6,7},{7,6},{8,9},{9,8},{10,11... | collective-permute-start | bytes 1572872 | tf_op jit(solution)/shard_map/ppermute | solution.py:406
  65.1 8.4 %collective-permute-start.23 = (bf16[32,4096]{1,0:T(8,128)(2,1)S(1)}, bf16[32,4096]{1,0:T(8,128)(2,1)S(1)}, u32[]{:S(2)}, u32[]{:S(2)}) collective-permute-start(bf16[32,4096]{1,0:T(8,128)(2,1)S(1)} %slice.35), channel_id=1, source_target_pairs={{0,2},{1,3},{2,0},{3,1},{4,6},{5,7},{6,4},{7,5},{8,10},{9,11},{10,... | collective-permute-start | bytes 786440 | tf_op jit(solution)/shard_map/ppermute | solution.py:406
  73.6 6.6 %collective-permute-start.26 = (bf16[8,4096]{1,0:T(8,128)(2,1)S(1)}, bf16[8,4096]{1,0:T(8,128)(2,1)S(1)}, u32[]{:S(2)}, u32[]{:S(2)}) collective-permute-start(bf16[8,4096]{1,0:T(8,128)(2,1)S(1)} %get-tuple-element.77), channel_id=1, source_target_pairs={{0,4},{1,5},{2,6},{3,7},{4,8},{5,9},{6,10},{7,11},{8,12},{9,13},{1... | collective-permute-start | bytes 196616 | tf_op jit(solution)/shard_map/ppermute | solution.py:406
  75.6 6.7 %collective-permute-start.25 = (bf16[8,4096]{1,0:T(8,128)(2,1)S(1)}, bf16[8,4096]{1,0:T(8,128)(2,1)S(1)}, u32[]{:S(2)}, u32[]{:S(2)}) collective-permute-start(bf16[8,4096]{1,0:T(8,128)(2,1)S(1)} %get-tuple-element.78), channel_id=1, source_target_pairs={{0,8},{1,9},{2,10},{3,11},{4,12},{5,13},{6,14},{7,15},{8,0},{9,1},... | collective-permute-start | bytes 196616 | tf_op jit(solution)/shard_map/ppermute | solution.py:406
  75.6 6.7 %copy-start.2 = (s32[128,4]{0,1:T(4,128)S(1)}, s32[128,4]{0,1:T(4,128)}, u32[]{:S(2)}) copy-start(s32[128,4]{0,1:T(4,128)} %param.17) | copy-start | bytes 6148
  75.6 6.7 %copy-start.3 = (f32[128,4]{0,1:T(4,128)S(1)}, f32[128,4]{0,1:T(4,128)}, u32[]{:S(2)}) copy-start(f32[128,4]{0,1:T(4,128)} %param.18) | copy-start | bytes 6148
  75.6 6.7 %collective-permute-start.24 = (bf16[8,4096]{1,0:T(8,128)(2,1)S(1)}, bf16[8,4096]{1,0:T(8,128)(2,1)S(1)}, u32[]{:S(2)}, u32[]{:S(2)}) collective-permute-start(bf16[8,4096]{1,0:T(8,128)(2,1)S(1)} %get-tuple-element.79), channel_id=1, source_target_pairs={{0,12},{1,13},{2,14},{3,15},{4,0},{5,1},{6,2},{7,3},{8,4},{9,5},{1... | collective-permute-start | bytes 196616 | tf_op jit(solution)/shard_map/ppermute | solution.py:406

commit v2 on v1

--- a/solution.py
+++ b/solution.py
@@ -144,15 +144,14 @@
     return high, (scaled - high.astype(F32)).astype(BF16)
 
 
-def key_steps(pos, place, first, axis, bias_ref, step, state):
+def key_steps(pos, place, first, bias_ref, step, state):
     low = jnp.min(first).astype(jnp.int32) // KEYS
     last = pos // (KEYS // TILE)
     clear = jnp.minimum((jnp.max(first).astype(jnp.int32) + KEYS - 1) // KEYS, last)
-    shape = (KEYS, 1) if axis == 0 else (1, KEYS)
 
     def edge(j, carried):
         kb = jnp.where(j < clear - low, low + j, last)
-        key_at = (kb * KEYS + lax.broadcasted_iota(jnp.int32, shape, axis)).astype(F32)
+        key_at = (kb * KEYS + lax.broadcasted_iota(jnp.int32, (KEYS, 1), 0)).astype(F32)
         bias_ref[...] = jnp.where((key_at >= first) & (key_at <= place), 0.0, LOW)
         return step(kb, carried, True)
 
@@ -167,12 +166,12 @@
     return jnp.concatenate([keys, keys], axis=1)
 
 
-def values_of(held, kb, h, extra):
+def values_of(held, kb, h):
     at = (KV_HEADS + h) * HEAD
     values = jnp.concatenate(
         [held[2 * kb + t, 0:TILE, at : at + HEAD] for t in range(2)], axis=1
     )
-    return jnp.concatenate([values, jnp.ones((extra, KEYS), BF16)], axis=0)
+    return jnp.concatenate([values, jnp.ones((EXTRA, KEYS), BF16)], axis=0)
 
 
 def flash(pos, held, q_ref, kv_heads, acc_ref, bias_ref, place, first):
@@ -190,55 +189,45 @@
             top = jnp.maximum(tops[i], jnp.max(scores, axis=0, keepdims=True))
             weights = jnp.exp2(scores - top).astype(BF16)
             acc_ref[i] = acc_ref[i] * jnp.exp2(tops[i] - top) + dot(
-                values_of(held, kb, kv_heads[i], EXTRA), weights
+                values_of(held, kb, kv_heads[i]), weights
             )
             out.append(top)
         return tuple(out)
 
     tops = tuple(jnp.full((1, lanes), LOW, F32) for _ in chains)
-    key_steps(pos, place, first, 0, bias_ref, step, tops)
+    key_steps(pos, place, first, bias_ref, step, tops)
     return [(acc_ref[i, 0:HEAD] / acc_ref[i, HEAD : HEAD + 1]).T for i in chains]
 
 
-def flash_rows(pos, held, q_ref, h, acc_ref, top_ref, bias_ref, place, first):
-    rows = q_ref.shape[0]
-    acc_ref[...] = jnp.zeros((rows, 2 * HEAD), F32)
-    top_ref[...] = jnp.full((rows, HEAD), LOW, F32)
-
-    def step(kb, carried, masked):
-        scores = dot(q_ref[...], keys_of(held, kb, h), 1, 1)
-        if masked:
-            scores = scores + jnp.concatenate([bias_ref[...]] * (rows // TILE), axis=0)
-        old = top_ref[...]
-        top = jnp.maximum(old, jnp.max(scores, axis=1, keepdims=True))
-        top_ref[...] = top
-        weights = jnp.exp2(scores - jnp.concatenate([top, top], axis=1)).astype(BF16)
-        factor = jnp.exp2(old - top)
-        acc_ref[...] = acc_ref[...] * jnp.concatenate([factor, factor], axis=1) + dot(
-            weights, values_of(held, kb, h, HEAD), 1, 1
+def place_pieces(n, senders, pos, pieces, held, sems):
+    planes = n // SHARDS
+    z, y, c = pos // SHARDS, (pos // 2) % 2, pos % 2
+    copies = []
+    for i, (piece, row, flip_c, flip_y, k) in enumerate(senders):
+        sender = lax.rem(z - k + planes, planes) * SHARDS + (y ^ flip_y) * 2 + (c ^ flip_c)
+        copy = pltpu.make_async_copy(
+            pieces[piece].at[pl.ds(row, KV_ROWS)], held.at[sender], sems.at[i]
         )
-        return carried
-
-    key_steps(pos, place, first, 1, bias_ref, step, 0)
-    return acc_ref[:, 0:HEAD] / acc_ref[:, HEAD:]
-
-
-def routed_kernel(n, senders, pos_ref, gain_ref, qs_ref, xs_ref, facts_ref, *refs):
+        copy.start()
+        copies.append(copy)
+    return copies
+
+
+def collect_kernel(n, senders, pos_ref, *refs):
+    *pieces, held, sems = refs
+    for copy in place_pieces(n, senders, pos_ref[0], pieces, held, sems):
+        copy.wait()
+
+
+def routed_kernel(n, senders, pos_ref, gain_ref, qs_ref, xs_ref, facts_ref, _, *refs):
     planes = n // SHARDS
     count = len(senders)
-    pieces = refs[:count]
-    outs = refs[count : count + planes]
-    held = refs[count + planes]
-    acc, bias, q_scr, state, gain, sems = refs[count + planes + 1 :]
+    pieces, outs, held = refs[:2], refs[2 : 2 + planes], refs[2 + planes]
+    acc, bias, q_scr, state, gain, sems = refs[3 + planes :]
     pos = pos_ref[0]
-    z, y, c = pos // SHARDS, (pos // 2) % 2, pos % 2
-    copies = []
-    for i, (flip_c, flip_y, k) in enumerate(senders):
-        sender = lax.rem(z - k + planes, planes) * SHARDS + (y ^ flip_y) * 2 + (c ^ flip_c)
-        copies.append(pltpu.make_async_copy(pieces[i], held.at[sender], sems.at[i]))
+    copies = place_pieces(n, senders, pos, pieces, held, sems)
     copies.append(pltpu.make_async_copy(gain_ref, gain, sems.at[count]))
-    for copy in copies:
-        copy.start()
+    copies[-1].start()
     for copy in copies:
         copy.wait()
     starts = doc_starts(n, pos, held)
@@ -308,7 +297,7 @@
 def own_kernel(n, part, loads, pos_ref, held, q_ref, x_ref, _, *refs):
     sources, (h_ref, done_ref) = refs[:loads], refs[loads : loads + 2]
     targets = refs[loads + 2 : 2 * loads + 2]
-    acc, bias, top, qt, sems = refs[2 * loads + 2 :]
+    acc, bias, qt, sems = refs[2 * loads + 2 :]
     moves = [
         pltpu.make_async_copy(source.at[0], target, sems.at[i])
         for i, (source, target) in enumerate(zip(sources, targets))
@@ -320,21 +309,13 @@
     starts = doc_starts(n, pos, held)
     first = starts_of(held[pos, TILE:KV_ROWS, 0:HEAD].astype(F32)[0:1], starts)
     place = (pos * TILE + lax.broadcasted_iota(jnp.int32, (1, TILE), 1)).astype(F32)
-    if part < 2:
-        for a in range(8):
-            terms = two_terms(q_ref[:, a * HEAD : (a + 1) * HEAD].astype(F32).T)
-            for i, term in enumerate(terms):
-                qt[0, i * HEAD : (i + 1) * HEAD, a * TILE : (a + 1) * TILE] = term
-        place = jnp.concatenate([place] * 8, axis=1)
-        first = jnp.concatenate([first] * 8, axis=1)
-        (done,) = flash(pos, held, qt, [part // 2], acc, bias, place, first)
-    else:
-        for a in range(8):
-            for i, term in enumerate(two_terms(q_ref[:, a * HEAD : (a + 1) * HEAD])):
-                qt[a * TILE : (a + 1) * TILE, i * HEAD : (i + 1) * HEAD] = term
-        place = jnp.broadcast_to(place, (TILE, TILE)).T[:, 0:1]
-        first = jnp.broadcast_to(first, (TILE, TILE)).T[:, 0:1]
-        done = flash_rows(pos, held, qt, part // 2, acc, top, bias, place, first)
+    for a in range(8):
+        terms = two_terms(q_ref[:, a * HEAD : (a + 1) * HEAD].astype(F32).T)
+        for i, term in enumerate(terms):
+            qt[0, i * HEAD : (i + 1) * HEAD, a * TILE : (a + 1) * TILE] = term
+    place = jnp.concatenate([place] * 8, axis=1)
+    first = jnp.concatenate([first] * 8, axis=1)
+    (done,) = flash(pos, held, qt, [part // 2], acc, bias, place, first)
     for a in range(8):
         lane = a * HEAD
         h_ref[:, lane : lane + HEAD] = (
@@ -434,28 +415,44 @@
 
     flip_y = [(s, s ^ 2) for s in range(n)]
     flip_c = [(s, s ^ 1) for s in range(n)]
-    kv = {(0, 0, 0): packed}
+    along, across = [packed], []
     for k in range(far + 1):
-        pairs = [(s, s ^ 2 if s >= k * SHARDS else s) for s in range(n)]
-        across, onward = move(kv[0, 0, k], pairs), None
+        if k == 1:
+            along[1], q_rows = lax.optimization_barrier((along[1], q_rows))
+        if k > 1:
+            along[k], across[k - 2] = lax.optimization_barrier((along[k], across[k - 2]))
         if k < far:
             used = [
                 any(needed(j, y, to) for to in (0, 1) for j in range(k + 1, far + 1))
                 for y in (0, 1)
             ]
             pairs = [(s, (s + SHARDS) % n if used[s // 2 % 2] else s) for s in range(n)]
-            onward = move(kv[0, 0, k], pairs)
-            across, onward, q_rows = lax.optimization_barrier((across, onward, q_rows))
-            kv[0, 0, k + 1] = onward
-        kv[0, 1, k] = across
-    for (_, side, k), piece in list(kv.items()):
-        kv[1, side, k] = move(piece, flip_c)
+            along.append(move(along[k], pairs))
+        pairs = [(s, s ^ 2 if s >= k * SHARDS else s) for s in range(n)]
+        across.append(move(along[k], pairs))
+    early = along + across[:-1] + [move(jnp.concatenate(along, axis=0), flip_c)]
+    late = [across[-1], move(jnp.concatenate(across, axis=0), flip_c)]
+    steps = range(far + 1)
+    early_senders = [(k, 0, 0, 0, k) for k in steps]
+    early_senders += [(far + 1 + k, 0, 0, 1, k) for k in steps[:-1]]
+    early_senders += [(2 * far + 1, k * KV_ROWS, 1, 0, k) for k in steps]
+    late_senders = [(0, 0, 0, 1, far)] + [(1, k * KV_ROWS, 1, 1, k) for k in steps]
+    held_shape = jax.ShapeDtypeStruct((n, KV_ROWS, 4 * HEAD), BF16)
+    held = pl.pallas_call(
+        functools.partial(collect_kernel, n, early_senders),
+        out_shape=held_shape,
+        in_specs=[SMEM] + [ANY] * len(early),
+        out_specs=VMEM,
+        scratch_shapes=[pltpu.SemaphoreType.DMA((len(early_senders),))],
+        compiler_params=params(small),
+        name="collect",
+    )(pos, *early)
 
     *sent, held = pl.pallas_call(
-        functools.partial(routed_kernel, n, list(kv)),
+        functools.partial(routed_kernel, n, late_senders),
         out_shape=[jax.ShapeDtypeStruct((SLOTS, width), BF16)] * planes
-        + [jax.ShapeDtypeStruct((n, KV_ROWS, 4 * HEAD), BF16)],
-        in_specs=[SMEM, HBM] + [VMEM] * 3 + [ANY] * len(kv),
+        + [held_shape],
+        in_specs=[SMEM, HBM] + [VMEM] * 4 + [ANY] * len(late),
         out_specs=[VMEM] * (planes + 1),
         scratch_shapes=[
             pltpu.VMEM((KV_HEADS, HEAD + EXTRA, 4 * TILE), F32),
@@ -463,11 +460,12 @@
             pltpu.VMEM((KV_HEADS, 2 * HEAD, 4 * TILE), BF16),
             pltpu.VMEM((planes * SLOTS, width), F32),
             pltpu.VMEM((1, width), F32),
-            pltpu.SemaphoreType.DMA((len(kv) + 1,)),
+            pltpu.SemaphoreType.DMA((len(late_senders) + 1,)),
         ],
+        input_output_aliases={5: planes},
         compiler_params=params(small),
         name="routed",
-    )(pos, pin(norm_gain.reshape(1, width)), q_rows, x_rows, facts, *kv.values())
+    )(pos, pin(norm_gain.reshape(1, width)), q_rows, x_rows, facts, held, *late)
 
     def own(part, after, *sources):
         columns = pl.BlockSpec((tokens, 8 * HEAD), lambda i: (0, part))
@@ -486,10 +484,9 @@
             ]
             + [VMEM] * len(sources),
             scratch_shapes=[
-                pltpu.VMEM((1, HEAD + EXTRA, 8 * TILE) if part < 2 else (8 * TILE, 2 * HEAD), F32),
-                pltpu.VMEM((KEYS, 8 * TILE) if part < 2 else (TILE, KEYS), F32),
-                pltpu.VMEM((8 * TILE, HEAD), F32),
-                pltpu.VMEM((1, 2 * HEAD, 8 * TILE) if part < 2 else (8 * TILE, 2 * HEAD), BF16),
+                pltpu.VMEM((1, HEAD + EXTRA, 8 * TILE), F32),
+                pltpu.VMEM((KEYS, 8 * TILE), F32),
+                pltpu.VMEM((1, 2 * HEAD, 8 * TILE), BF16),
                 pltpu.SemaphoreType.DMA((3,)),
             ],
             compiler_params=params(small),

time: 84.5 us -> 78.8 us (0.933)
  starting transfers between devices: 36 us -> 27.5 us
  waiting for transfers between devices: 25.9 us -> 29 us
  Pallas kernels: 21.8 us -> 20.6 us
    ppermute x27 -> x21, starting transfers between devices: 36 us -> 27.5 us  [move(): return lax.ppermute(value, 'expert', pairs)]
    ppermute x27 -> x21, waiting for transfers between devices: 25.9 us -> 29 us  [move(): return lax.ppermute(value, 'expert', pairs)]
    pallas_call x1 -> x2, Pallas kernels: 5.9 us -> 5.4 us  [the longest x1 3.2 us: local(): pl.pallas_call(functools.partial(routed_kernel, n, late_senders), out_sha...]
  transfers between devices with their start and end apart: 27 -> 21, of which waited for: 11 -> 11; matrix products, arithmetic and copies ran while one was open for 0% -> 0% of each run, Pallas kernels for 13% -> 16%
where the time goes in v2:
time: 78.8 us; the launch traced here: 77.8 us
  waiting for transfers between devices  29 us (37%)
  starting transfers between devices  27.5 us (35%)
  Pallas kernels  20.6 us (26%)
    ppermute x21, waiting for transfers between devices, move(): return lax.ppermute(value, 'expert', pairs)  29 us
    ppermute x21, starting transfers between devices, move(): return lax.ppermute(value, 'expert', pairs)  27.5 us
    pallas_call x4, Pallas kernels, own(): pl.pallas_call(functools.partial(own_kernel, n, part, len(sources)), out_...  8.22 us
    pallas_call x1, Pallas kernels, local(): pl.pallas_call(functools.partial(routed_kernel, n, late_senders), out_sha...  3.2 us
    pallas_call x1, Pallas kernels, local(): pl.pallas_call(functools.partial(select_kernel, planes), out_shape=[jax.S...  2.21 us
    pallas_call x1, Pallas kernels, local(): pl.pallas_call(functools.partial(collect_kernel, n, early_senders), out_s...  2.2 us
    pallas_call x1, Pallas kernels, local(): pl.pallas_call(functools.partial(expert_kernel, n, len(pieces)), out_shap...  1.97 us
    pallas_call x1, Pallas kernels, local(): pl.pallas_call(functools.partial(combine_kernel, planes), out_shape=jax.S...  1.87 us
  transfers between devices with their start and end apart: 21, of which 11 were waited for; matrix products, arithmetic and copies ran while one was open for 0% of the time, Pallas kernels for 16%

profile of v2, /device:TPU:0, one launch (start us, length us, event | category | flops | bytes accessed | tf_op | source)
XLA Modules:
  0.0 77.8 jit_solution(6016511006119016844)
XLA Ops:
  0.0 1.0 %pack.1.refs_0_ = bf16[144,512]{1,0:T(8,128)(2,1)S(1)} custom-call(s32[1,128]{1,0:T(1,128)} %bitcast.9, bf16[128,256]{1,0:T(8,128)(2,1)} %keys_ref.1, bf16[128,256]{1,0:T(8,128)(2,1)} %values_ref.1), custom_call_target="tpu_custom_call" | custom-call | tf_op jit(solution)/shard_map/pack/pallas_call | solution.py:372
  1.0 3.1 %collective-permute-start = (bf16[144,512]{1,0:T(8,128)(2,1)S(1)}, bf16[144,512]{1,0:T(8,128)(2,1)S(1)}, u32[]{:S(2)}, u32[]{:S(2)}) collective-permute-start(bf16[144,512]{1,0:T(8,128)(2,1)S(1)} %pack.1.refs_0_), channel_id=1, source_target_pairs={{0,4},{1,5},{2,6},{3,7},{4,8},{5,9},{6,10},{7,11},{8,12},{9,13},{1... | collective-permute-start | bytes 442376 | tf_op jit(solution)/shard_map/ppermute | solution.py:387
  4.1 1.5 %collective-permute-start.2 = (bf16[144,512]{1,0:T(8,128)(2,1)S(1)}, bf16[144,512]{1,0:T(8,128)(2,1)S(1)}, u32[]{:S(2)}, u32[]{:S(2)}) collective-permute-start(bf16[144,512]{1,0:T(8,128)(2,1)S(1)} %pack.1.refs_0_), channel_id=1, source_target_pairs={{0,2},{1,3},{2,0},{3,1},{4,6},{5,7},{6,4},{7,5},{8,10},{9,11},{10,... | collective-permute-start | bytes 442376 | tf_op jit(solution)/shard_map/ppermute | solution.py:387
  5.6 2.2 %select.1 = (bf16[2,256,512]{2,1,0:T(8,128)(2,1)S(1)}, f32[32,4096]{1,0:T(8,128)S(1)}, f32[8,512]{1,0:T(8,128)S(1)}) custom-call(s32[1]{0:T(128)} %bitcast.pos_ref, s32[4,128]{1,0:T(4,128)} %bitcast.5, s32[1,128]{1,0:T(1,128)} %bitcast.10, bf16[128,4096]{1,0:T(8,128)(2,1)} %q_ref.7, bf16[128,4096]{1,0:T(8,128)(2,1)} %x_ref.7), custom_call_target="tpu_custom_call" | custom-call | tf_op jit(solution)/shard_map/select/pallas_call | solution.py:396
  7.8 2.1 %collective-permute-done.refs_1_ = bf16[144,512]{1,0:T(8,128)(2,1)S(1)} collective-permute-done((bf16[144,512]{1,0:T(8,128)(2,1)S(1)}, bf16[144,512]{1,0:T(8,128)(2,1)S(1)}, u32[]{:S(2)}, u32[]{:S(2)}) %collective-permute-start) | collective-permute-done | bytes 147488 | tf_op jit(solution)/shard_map/ppermute | solution.py:387
  9.9 0.0 collective-permute-start.1
  9.9 0.7 collective-permute-start.4
  10.6 0.0 collective-permute-done.2.refs_4_
  10.6 6.3 %collective-permute-done.1.refs_2_ = bf16[144,512]{1,0:T(8,128)(2,1)S(1)} collective-permute-done((bf16[144,512]{1,0:T(8,128)(2,1)S(1)}, bf16[144,512]{1,0:T(8,128)(2,1)S(1)}, u32[]{:S(2)}, u32[]{:S(2)}) %collective-permute-start.1) | collective-permute-done | bytes 147488 | tf_op jit(solution)/shard_map/ppermute | solution.py:387
  16.9 0.7 collective-permute-start.3
  17.5 0.7 collective-permute-start.5
  18.2 0.0 collective-permute-done.3.refs_3_
  18.2 0.7 collective-permute-start.7
  19.0 0.1 collective-permute-start.6
  19.1 0.0 collective-permute-done.7.refs_0_
  19.1 0.5 collective-permute-start.8
  19.7 1.4 %collective-permute-done.6.refs_7_ = bf16[576,512]{1,0:T(8,128)(2,1)S(1)} collective-permute-done((bf16[576,512]{1,0:T(8,128)(2,1)S(1)}, bf16[576,512]{1,0:T(8,128)(2,1)S(1)}, u32[]{:S(2)}, u32[]{:S(2)}) %collective-permute-start.6) | collective-permute-done | bytes 589856 | tf_op jit(solution)/shard_map/ppermute | solution.py:387
  21.0 2.2 %collect.1._ = bf16[16,144,512]{2,1,0:T(8,128)(2,1)S(1)} custom-call(s32[1]{0:T(128)} %bitcast.pos_ref, bf16[144,512]{1,0:T(8,128)(2,1)S(1)} %pack.1.refs_0_, bf16[144,512]{1,0:T(8,128)(2,1)S(1)} %collective-permute-done.refs_1_, bf16[144,512]{1,0:T(8,128)(2,1)S(1)} %collective-permute-done.1.refs_2_, bf16[144,512]{1,0:T(8,128)(2,1)S(1)} %collective-permute-done.3.refs_3_, ...), custom_call_target="tpu_custom_call" | custom-call | tf_op jit(solution)/shard_map/collect/pallas_call | solution.py:441
  23.2 0.0 collective-permute-done.8.refs_1_
  23.3 0.0 copy-start
  23.3 0.0 copy-start.1
  23.3 3.2 %routed.1 = (bf16[8,4096]{1,0:T(8,128)(2,1)S(1)}, bf16[8,4096]{1,0:T(8,128)(2,1)S(1)}, bf16[8,4096]{1,0:T(8,128)(2,1)S(1)}, bf16[8,4096]{1,0:T(8,128)(2,1)S(1)}, bf16[16,144,512]{2,1,0:T(8,128)(2,1)S(1)}) custom-call(s32[1]{0:T(128)} %bitcast.pos_ref, f32[1,4096]{1,0:T(1,128)} %bitcast.8, ...), custom_call_target="tpu_custom_call", output_to_operand_aliasing={{4}: (5, {})} | custom-call | tf_op jit(solution)/shard_map/routed/pallas_call | solution.py:451
  26.5 1.7 %collective-permute-start.9 = (bf16[8,4096]{1,0:T(8,128)(2,1)S(1)}, bf16[8,4096]{1,0:T(8,128)(2,1)S(1)}, u32[]{:S(2)}, u32[]{:S(2)}) collective-permute-start(bf16[8,4096]{1,0:T(8,128)(2,1)S(1)} %get-tuple-element.52), channel_id=1, source_target_pairs={{0,4},{1,5},{2,6},{3,7},{4,8},{5,9},{6,10},{7,11},{8,12},{9,13},{1... | collective-permute-start | bytes 196616 | tf_op jit(solution)/shard_map/ppermute | solution.py:387
  28.2 12.0 %collective-permute-start.10 = (bf16[8,4096]{1,0:T(8,128)(2,1)S(1)}, bf16[8,4096]{1,0:T(8,128)(2,1)S(1)}, u32[]{:S(2)}, u32[]{:S(2)}) collective-permute-start(bf16[8,4096]{1,0:T(8,128)(2,1)S(1)} %get-tuple-element.53), channel_id=1, source_target_pairs={{0,8},{1,9},{2,10},{3,11},{4,12},{5,13},{6,14},{7,15},{8,0},{9,1},... | collective-permute-start | bytes 196616 | tf_op jit(solution)/shard_map/ppermute | solution.py:387
  40.2 0.7 collective-permute-start.12
  40.9 3.9 %own.4 = (f32[128,1024]{1,0:T(8,128)S(1)}, f32[8,128]{1,0:T(8,128)S(1)}, bf16[4096,384]{1,0:T(8,128)(2,1)S(1)}, bf16[4096,384]{1,0:T(8,128)(2,1)S(1)}, bf16[384,4096]{1,0:T(8,128)(2,1)S(1)}) custom-call(s32[1]{0:T(128)} %bitcast.pos_ref, bf16[16,144,512]{2,1,0:T(8,128)(2,1)S(1)} %get-tuple-element.47.held, bf16[128,4096]{1,0:T(8,128)(2,1)S(1)} %copy-done, ...), custom_call_target="tpu_custom_call" | custom-call | flops 2000000000 | bytes 8000000 | tf_op jit(solution)/shard_map/own/pallas_call | solution.py:472
  44.8 0.5 collective-permute-done.10
  45.2 0.5 collective-permute-done.11
  45.7 0.1 collective-permute-start.14
  45.8 0.5 collective-permute-start.13
  46.3 1.2 %own.5 = (f32[128,1024]{1,0:T(8,128)S(1)}, f32[8,128]{1,0:T(8,128)S(1)}) custom-call(s32[1]{0:T(128)} %bitcast.pos_ref, bf16[16,144,512]{2,1,0:T(8,128)(2,1)S(1)} %get-tuple-element.47.held, bf16[128,4096]{1,0:T(8,128)(2,1)S(1)} %copy-done, bf16[128,4096]{1,0:T(8,128)(2,1)S(1)} %copy-done.1, f32[8,128]{1,0:T(8,128)S(1)} %get-tuple-element.50._), custom_call_target="tpu_custom_call" | custom-call | flops 2000000000 | bytes 8000000 | tf_op jit(solution)/shard_map/own/pallas_call | solution.py:472
  47.5 5.6 %collective-permute-done.13.refs_3_ = bf16[24,4096]{1,0:T(8,128)(2,1)S(1)} collective-permute-done((bf16[24,4096]{1,0:T(8,128)(2,1)S(1)}, bf16[24,4096]{1,0:T(8,128)(2,1)S(1)}, u32[]{:S(2)}, u32[]{:S(2)}) %collective-permute-start.13) | collective-permute-done | bytes 196640 | tf_op jit(solution)/shard_map/ppermute | solution.py:387
  53.2 0.1 collective-permute-start.15
  53.3 1.5 %collective-permute-done.15.refs_5_ = bf16[32,4096]{1,0:T(8,128)(2,1)S(1)} collective-permute-done((bf16[32,4096]{1,0:T(8,128)(2,1)S(1)}, bf16[32,4096]{1,0:T(8,128)(2,1)S(1)}, u32[]{:S(2)}, u32[]{:S(2)}) %collective-permute-start.15) | collective-permute-done | bytes 262176 | tf_op jit(solution)/shard_map/ppermute | solution.py:387
  54.8 2.0 %expert.1 = (bf16[64,4096]{1,0:T(8,128)(2,1)S(1)}, bf16[64,4096]{1,0:T(8,128)(2,1)S(1)}) custom-call(bf16[8,4096]{1,0:T(8,128)(2,1)S(1)} %get-tuple-element.48._.refs_0_, bf16[24,4096]{1,0:T(8,128)(2,1)S(1)} %constant_dynamic-update-slice_fusion.refs_1_, bf16[8,4096]{1,0:T(8,128)(2,1)S(1)} %collective-permute-done.12.refs_2_, ...), custom_call_target="tpu_custom_call" | custom-call | flops 1200000000 | bytes 12000000 | tf_op jit(solution)/shard_map/expert/pallas_call | solution.py:515
  56.7 0.2 collective-permute-start.16
  56.9 1.8 %collective-permute-done.16 = bf16[64,4096]{1,0:T(8,128)(2,1)S(1)} collective-permute-done((bf16[64,4096]{1,0:T(8,128)(2,1)S(1)}, bf16[64,4096]{1,0:T(8,128)(2,1)S(1)}, u32[]{:S(2)}, u32[]{:S(2)}) %collective-permute-start.16) | collective-permute-done | bytes 524320 | tf_op jit(solution)/shard_map/ppermute | solution.py:387
  58.7 0.1 convert_add_fusion
  58.9 0.5 collective-permute-start.17
  59.3 1.6 %own.7 = (f32[128,1024]{1,0:T(8,128)S(1)}, f32[8,128]{1,0:T(8,128)}) custom-call(s32[1]{0:T(128)} %bitcast.pos_ref, bf16[16,144,512]{2,1,0:T(8,128)(2,1)S(1)} %get-tuple-element.47.held, bf16[128,4096]{1,0:T(8,128)(2,1)S(1)} %copy-done, bf16[128,4096]{1,0:T(8,128)(2,1)S(1)} %copy-done.1, bf16[64,4096]{1,0:T(8,128)(2,1)S(1)} %get-tuple-element.67._), custom_call_target="tpu_custom_call" | custom-call | flops 2000000000 | bytes 8000000 | tf_op jit(solution)/shard_map/own/pallas_call | solution.py:472
  60.9 6.3 %collective-permute-done.17 = bf16[32,4096]{1,0:T(8,128)(2,1)S(1)} collective-permute-done((bf16[32,4096]{1,0:T(8,128)(2,1)S(1)}, bf16[32,4096]{1,0:T(8,128)(2,1)S(1)}, u32[]{:S(2)}, u32[]{:S(2)}) %collective-permute-start.17) | collective-permute-done | bytes 262176 | tf_op jit(solution)/shard_map/ppermute | solution.py:387
  67.4 1.5 %collective-permute-start.20 = (bf16[8,4096]{1,0:T(8,128)(2,1)S(1)}, bf16[8,4096]{1,0:T(8,128)(2,1)S(1)}, u32[]{:S(2)}, u32[]{:S(2)}) collective-permute-start(bf16[8,4096]{1,0:T(8,128)(2,1)S(1)} %get-tuple-element.71), channel_id=1, source_target_pairs={{0,4},{1,5},{2,6},{3,7},{4,8},{5,9},{6,10},{7,11},{8,12},{9,13},{1... | collective-permute-start | bytes 196616 | tf_op jit(solution)/shard_map/ppermute | solution.py:387
  68.9 1.3 %collective-permute-start.19 = (bf16[8,4096]{1,0:T(8,128)(2,1)S(1)}, bf16[8,4096]{1,0:T(8,128)(2,1)S(1)}, u32[]{:S(2)}, u32[]{:S(2)}) collective-permute-start(bf16[8,4096]{1,0:T(8,128)(2,1)S(1)} %get-tuple-element.72), channel_id=1, source_target_pairs={{0,8},{1,9},{2,10},{3,11},{4,12},{5,13},{6,14},{7,15},{8,0},{9,1},... | collective-permute-start | bytes 196616 | tf_op jit(solution)/shard_map/ppermute | solution.py:387
  70.2 1.1 %collective-permute-start.18 = (bf16[8,4096]{1,0:T(8,128)(2,1)S(1)}, bf16[8,4096]{1,0:T(8,128)(2,1)S(1)}, u32[]{:S(2)}, u32[]{:S(2)}) collective-permute-start(bf16[8,4096]{1,0:T(8,128)(2,1)S(1)} %get-tuple-element.73), channel_id=1, source_target_pairs={{0,12},{1,13},{2,14},{3,15},{4,0},{5,1},{6,2},{7,3},{8,4},{9,5},{1... | collective-permute-start | bytes 196616 | tf_op jit(solution)/shard_map/ppermute | solution.py:387
  71.3 1.6 %own.6 = (f32[128,1024]{1,0:T(8,128)S(1)}, f32[8,128]{1,0:T(8,128)}) custom-call(s32[1]{0:T(128)} %bitcast.pos_ref, bf16[16,144,512]{2,1,0:T(8,128)(2,1)S(1)} %get-tuple-element.47.held, bf16[128,4096]{1,0:T(8,128)(2,1)S(1)} %copy-done, bf16[128,4096]{1,0:T(8,128)(2,1)S(1)} %copy-done.1, bf16[64,4096]{1,0:T(8,128)(2,1)S(1)} %get-tuple-element.67._), custom_call_target="tpu_custom_call" | custom-call | flops 2000000000 | bytes 8000000 | tf_op jit(solution)/shard_map/own/pallas_call | solution.py:472
  72.9 1.1 %collective-permute-done.20.refs_7_ = bf16[8,4096]{1,0:T(8,128)(2,1)S(1)} collective-permute-done((bf16[8,4096]{1,0:T(8,128)(2,1)S(1)}, bf16[8,4096]{1,0:T(8,128)(2,1)S(1)}, u32[]{:S(2)}, u32[]{:S(2)}) %collective-permute-start.20) | collective-permute-done | bytes 65568 | tf_op jit(solution)/shard_map/ppermute | solution.py:387
  74.0 1.9 %collective-permute-done.19.refs_6_ = bf16[8,4096]{1,0:T(8,128)(2,1)S(1)} collective-permute-done((bf16[8,4096]{1,0:T(8,128)(2,1)S(1)}, bf16[8,4096]{1,0:T(8,128)(2,1)S(1)}, u32[]{:S(2)}, u32[]{:S(2)}) %collective-permute-start.19) | collective-permute-done | bytes 65568 | tf_op jit(solution)/shard_map/ppermute | solution.py:387
  75.9 1.9 %combine.1 = bf16[128,4096]{1,0:T(8,128)(2,1)} custom-call(s32[1]{0:T(128)} %bitcast.pos_ref, s32[4,128]{1,0:T(4,128)S(1)} %bitcast.6, f32[4,128]{1,0:T(4,128)S(1)} %bitcast.7, f32[128,1024]{1,0:T(8,128)S(1)} %get-tuple-element.49.refs_0_, f32[128,1024]{1,0:T(8,128)S(1)} %get-tuple-element.51.refs_1_, f32[128,1024]{1,0:T(8,128)S(1)} %get-tuple-element.68.refs_2_, ...), custom_call_target="tpu_custom_call" | custom-call | tf_op jit(solution)/shard_map/combine/pallas_call | solution.py:542
  (23 shorter events, 0.3 us)
Async XLA Ops:
  1.0 8.9 %collective-permute-start = (bf16[144,512]{1,0:T(8,128)(2,1)S(1)}, bf16[144,512]{1,0:T(8,128)(2,1)S(1)}, u32[]{:S(2)}, u32[]{:S(2)}) collective-permute-start(bf16[144,512]{1,0:T(8,128)(2,1)S(1)} %pack.1.refs_0_), channel_id=1, source_target_pairs={{0,4},{1,5},{2,6},{3,7},{4,8},{5,9},{6,10},{7,11},{8,12},{9,13},{1... | collective-permute-start | bytes 442376 | tf_op jit(solution)/shard_map/ppermute | solution.py:387
  4.1 6.5 %collective-permute-start.2 = (bf16[144,512]{1,0:T(8,128)(2,1)S(1)}, bf16[144,512]{1,0:T(8,128)(2,1)S(1)}, u32[]{:S(2)}, u32[]{:S(2)}) collective-permute-start(bf16[144,512]{1,0:T(8,128)(2,1)S(1)} %pack.1.refs_0_), channel_id=1, source_target_pairs={{0,2},{1,3},{2,0},{3,1},{4,6},{5,7},{6,4},{7,5},{8,10},{9,11},{10,... | collective-permute-start | bytes 442376 | tf_op jit(solution)/shard_map/ppermute | solution.py:387
  9.9 6.9 %collective-permute-start.1 = (bf16[144,512]{1,0:T(8,128)(2,1)S(1)}, bf16[144,512]{1,0:T(8,128)(2,1)S(1)}, u32[]{:S(2)}, u32[]{:S(2)}) collective-permute-start(bf16[144,512]{1,0:T(8,128)(2,1)S(1)} %collective-permute-done.refs_1_), channel_id=1, source_target_pairs={{0,4},{1,5},{2,6},{3,7},{4,8},{5,9},{6,10},{7,11},{8,12},{9,13},{1... | collective-permute-start | bytes 442376 | tf_op jit(solution)/shard_map/ppermute | solution.py:387
  9.9 8.3 %collective-permute-start.4 = (bf16[144,512]{1,0:T(8,128)(2,1)S(1)}, bf16[144,512]{1,0:T(8,128)(2,1)S(1)}, u32[]{:S(2)}, u32[]{:S(2)}) collective-permute-start(bf16[144,512]{1,0:T(8,128)(2,1)S(1)} %collective-permute-done.refs_1_), channel_id=1, source_target_pairs={{0,0},{1,1},{2,2},{3,3},{4,6},{5,7},{6,4},{7,5},{8,10},{9,11},{10,... | collective-permute-start | bytes 442376 | tf_op jit(solution)/shard_map/ppermute | solution.py:387
  16.9 1.4 %collective-permute-start.3 = (bf16[144,512]{1,0:T(8,128)(2,1)S(1)}, bf16[144,512]{1,0:T(8,128)(2,1)S(1)}, u32[]{:S(2)}, u32[]{:S(2)}) collective-permute-start(bf16[144,512]{1,0:T(8,128)(2,1)S(1)} %collective-permute-done.1.refs_2_), channel_id=1, source_target_pairs={{0,0},{1,1},{2,6},{3,7},{4,4},{5,5},{6,10},{7,11},{8,8},{9,9},{10,... | collective-permute-start | bytes 442376 | tf_op jit(solution)/shard_map/ppermute | solution.py:387
  17.5 1.5 %collective-permute-start.5 = (bf16[144,512]{1,0:T(8,128)(2,1)S(1)}, bf16[144,512]{1,0:T(8,128)(2,1)S(1)}, u32[]{:S(2)}, u32[]{:S(2)}) collective-permute-start(bf16[144,512]{1,0:T(8,128)(2,1)S(1)} %collective-permute-done.1.refs_2_), channel_id=1, source_target_pairs={{0,0},{1,1},{2,2},{3,3},{4,4},{5,5},{6,6},{7,7},{8,10},{9,11},{10,... | collective-permute-start | bytes 442376 | tf_op jit(solution)/shard_map/ppermute | solution.py:387
  18.2 0.8 %collective-permute-start.7 = (bf16[144,512]{1,0:T(8,128)(2,1)S(1)}, bf16[144,512]{1,0:T(8,128)(2,1)S(1)}, u32[]{:S(2)}, u32[]{:S(2)}) collective-permute-start(bf16[144,512]{1,0:T(8,128)(2,1)S(1)} %collective-permute-done.3.refs_3_), channel_id=1, source_target_pairs={{0,0},{1,1},{2,2},{3,3},{4,4},{5,5},{6,6},{7,7},{8,8},{9,9},{10,10... | collective-permute-start | bytes 442376 | tf_op jit(solution)/shard_map/ppermute | solution.py:387
  19.0 2.1 %collective-permute-start.6 = (bf16[576,512]{1,0:T(8,128)(2,1)S(1)}, bf16[576,512]{1,0:T(8,128)(2,1)S(1)}, u32[]{:S(2)}, u32[]{:S(2)}) collective-permute-start(bf16[576,512]{1,0:T(8,128)(2,1)S(1)} %pad_maximum_fusion), channel_id=1, source_target_pairs={{0,1},{1,0},{2,3},{3,2},{4,5},{5,4},{6,7},{7,6},{8,9},{9,8},{10,11... | collective-permute-start | bytes 1769480 | tf_op jit(solution)/shard_map/ppermute | solution.py:387
  19.1 4.1 %collective-permute-start.8 = (bf16[576,512]{1,0:T(8,128)(2,1)S(1)}, bf16[576,512]{1,0:T(8,128)(2,1)S(1)}, u32[]{:S(2)}, u32[]{:S(2)}) collective-permute-start(bf16[576,512]{1,0:T(8,128)(2,1)S(1)} %pad_maximum_fusion.1), channel_id=1, source_target_pairs={{0,1},{1,0},{2,3},{3,2},{4,5},{5,4},{6,7},{7,6},{8,9},{9,8},{10,11... | collective-permute-start | bytes 1769480 | tf_op jit(solution)/shard_map/ppermute | solution.py:387
  23.3 17.6 %copy-start = (bf16[128,4096]{1,0:T(8,128)(2,1)S(1)}, bf16[128,4096]{1,0:T(8,128)(2,1)}, u32[]{:S(2)}) copy-start(bf16[128,4096]{1,0:T(8,128)(2,1)} %q_ref.7) | copy-start | bytes 3145732
  23.3 17.6 %copy-start.1 = (bf16[128,4096]{1,0:T(8,128)(2,1)S(1)}, bf16[128,4096]{1,0:T(8,128)(2,1)}, u32[]{:S(2)}) copy-start(bf16[128,4096]{1,0:T(8,128)(2,1)} %x_ref.7) | copy-start | bytes 3145732
  26.5 18.3 %collective-permute-start.9 = (bf16[8,4096]{1,0:T(8,128)(2,1)S(1)}, bf16[8,4096]{1,0:T(8,128)(2,1)S(1)}, u32[]{:S(2)}, u32[]{:S(2)}) collective-permute-start(bf16[8,4096]{1,0:T(8,128)(2,1)S(1)} %get-tuple-element.52), channel_id=1, source_target_pairs={{0,4},{1,5},{2,6},{3,7},{4,8},{5,9},{6,10},{7,11},{8,12},{9,13},{1... | collective-permute-start | bytes 196616 | tf_op jit(solution)/shard_map/ppermute | solution.py:387
  28.2 17.1 %collective-permute-start.10 = (bf16[8,4096]{1,0:T(8,128)(2,1)S(1)}, bf16[8,4096]{1,0:T(8,128)(2,1)S(1)}, u32[]{:S(2)}, u32[]{:S(2)}) collective-permute-start(bf16[8,4096]{1,0:T(8,128)(2,1)S(1)} %get-tuple-element.53), channel_id=1, source_target_pairs={{0,8},{1,9},{2,10},{3,11},{4,12},{5,13},{6,14},{7,15},{8,0},{9,1},... | collective-permute-start | bytes 196616 | tf_op jit(solution)/shard_map/ppermute | solution.py:387
  40.2 5.5 %collective-permute-start.11 = (bf16[8,4096]{1,0:T(8,128)(2,1)S(1)}, bf16[8,4096]{1,0:T(8,128)(2,1)S(1)}, u32[]{:S(2)}, u32[]{:S(2)}) collective-permute-start(bf16[8,4096]{1,0:T(8,128)(2,1)S(1)} %get-tuple-element.54), channel_id=1, source_target_pairs={{0,12},{1,13},{2,14},{3,15},{4,0},{5,1},{6,2},{7,3},{8,4},{9,5},{1... | collective-permute-start | bytes 196616 | tf_op jit(solution)/shard_map/ppermute | solution.py:387
  40.2 5.5 %collective-permute-start.12 = (bf16[8,4096]{1,0:T(8,128)(2,1)S(1)}, bf16[8,4096]{1,0:T(8,128)(2,1)S(1)}, u32[]{:S(2)}, u32[]{:S(2)}) collective-permute-start(bf16[8,4096]{1,0:T(8,128)(2,1)S(1)} %get-tuple-element.48._.refs_0_), channel_id=1, source_target_pairs={{0,2},{1,3},{2,0},{3,1},{4,6},{5,7},{6,4},{7,5},{8,10},{9,11},{10,... | collective-permute-start | bytes 196616 | tf_op jit(solution)/shard_map/ppermute | solution.py:387
  45.7 7.4 %collective-permute-start.14 = (bf16[32,4096]{1,0:T(8,128)(2,1)S(1)}, bf16[32,4096]{1,0:T(8,128)(2,1)S(1)}, u32[]{:S(2)}, u32[]{:S(2)}) collective-permute-start(bf16[32,4096]{1,0:T(8,128)(2,1)S(1)} %pad_maximum_fusion.2), channel_id=1, source_target_pairs={{0,1},{1,0},{2,3},{3,2},{4,5},{5,4},{6,7},{7,6},{8,9},{9,8},{10,11... | collective-permute-start | bytes 786440 | tf_op jit(solution)/shard_map/ppermute | solution.py:387
  45.8 7.3 %collective-permute-start.13 = (bf16[24,4096]{1,0:T(8,128)(2,1)S(1)}, bf16[24,4096]{1,0:T(8,128)(2,1)S(1)}, u32[]{:S(2)}, u32[]{:S(2)}) collective-permute-start(bf16[24,4096]{1,0:T(8,128)(2,1)S(1)} %constant_dynamic-update-slice_fusion.refs_1_), channel_id=1, source_target_pairs={{0,2},{1,3},{2,0},{3,1},{4,6},{5,7},{6,4},{7,5},{8,10},{9,11},{10,... | collective-permute-start | bytes 589832 | tf_op jit(solution)/shard_map/ppermute | solution.py:387
  53.2 1.6 %collective-permute-start.15 = (bf16[32,4096]{1,0:T(8,128)(2,1)S(1)}, bf16[32,4096]{1,0:T(8,128)(2,1)S(1)}, u32[]{:S(2)}, u32[]{:S(2)}) collective-permute-start(bf16[32,4096]{1,0:T(8,128)(2,1)S(1)} %pad_maximum_fusion.3), channel_id=1, source_target_pairs={{0,1},{1,0},{2,3},{3,2},{4,5},{5,4},{6,7},{7,6},{8,9},{9,8},{10,11... | collective-permute-start | bytes 786440 | tf_op jit(solution)/shard_map/ppermute | solution.py:387
  56.7 2.0 %collective-permute-start.16 = (bf16[64,4096]{1,0:T(8,128)(2,1)S(1)}, bf16[64,4096]{1,0:T(8,128)(2,1)S(1)}, u32[]{:S(2)}, u32[]{:S(2)}) collective-permute-start(bf16[64,4096]{1,0:T(8,128)(2,1)S(1)} %get-tuple-element.70), channel_id=1, source_target_pairs={{0,1},{1,0},{2,3},{3,2},{4,5},{5,4},{6,7},{7,6},{8,9},{9,8},{10,11... | collective-permute-start | bytes 1572872 | tf_op jit(solution)/shard_map/ppermute | solution.py:387
  58.9 8.4 %collective-permute-start.17 = (bf16[32,4096]{1,0:T(8,128)(2,1)S(1)}, bf16[32,4096]{1,0:T(8,128)(2,1)S(1)}, u32[]{:S(2)}, u32[]{:S(2)}) collective-permute-start(bf16[32,4096]{1,0:T(8,128)(2,1)S(1)} %slice.35), channel_id=1, source_target_pairs={{0,2},{1,3},{2,0},{3,1},{4,6},{5,7},{6,4},{7,5},{8,10},{9,11},{10,... | collective-permute-start | bytes 786440 | tf_op jit(solution)/shard_map/ppermute | solution.py:387
  67.4 6.6 %collective-permute-start.20 = (bf16[8,4096]{1,0:T(8,128)(2,1)S(1)}, bf16[8,4096]{1,0:T(8,128)(2,1)S(1)}, u32[]{:S(2)}, u32[]{:S(2)}) collective-permute-start(bf16[8,4096]{1,0:T(8,128)(2,1)S(1)} %get-tuple-element.71), channel_id=1, source_target_pairs={{0,4},{1,5},{2,6},{3,7},{4,8},{5,9},{6,10},{7,11},{8,12},{9,13},{1... | collective-permute-start | bytes 196616 | tf_op jit(solution)/shard_map/ppermute | solution.py:387
  68.9 7.1 %collective-permute-start.19 = (bf16[8,4096]{1,0:T(8,128)(2,1)S(1)}, bf16[8,4096]{1,0:T(8,128)(2,1)S(1)}, u32[]{:S(2)}, u32[]{:S(2)}) collective-permute-start(bf16[8,4096]{1,0:T(8,128)(2,1)S(1)} %get-tuple-element.72), channel_id=1, source_target_pairs={{0,8},{1,9},{2,10},{3,11},{4,12},{5,13},{6,14},{7,15},{8,0},{9,1},... | collective-permute-start | bytes 196616 | tf_op jit(solution)/shard_map/ppermute | solution.py:387
  70.2 5.7 %copy-start.2 = (s32[128,4]{0,1:T(4,128)S(1)}, s32[128,4]{0,1:T(4,128)}, u32[]{:S(2)}) copy-start(s32[128,4]{0,1:T(4,128)} %param.17) | copy-start | bytes 6148
  70.2 5.7 %copy-start.3 = (f32[128,4]{0,1:T(4,128)S(1)}, f32[128,4]{0,1:T(4,128)}, u32[]{:S(2)}) copy-start(f32[128,4]{0,1:T(4,128)} %param.18) | copy-start | bytes 6148
  70.2 5.7 %collective-permute-start.18 = (bf16[8,4096]{1,0:T(8,128)(2,1)S(1)}, bf16[8,4096]{1,0:T(8,128)(2,1)S(1)}, u32[]{:S(2)}, u32[]{:S(2)}) collective-permute-start(bf16[8,4096]{1,0:T(8,128)(2,1)S(1)} %get-tuple-element.73), channel_id=1, source_target_pairs={{0,12},{1,13},{2,14},{3,15},{4,0},{5,1},{6,2},{7,3},{8,4},{9,5},{1... | collective-permute-start | bytes 196616 | tf_op jit(solution)/shard_map/ppermute | solution.py:387

commit v3 on v2

--- a/solution.py
+++ b/solution.py
@@ -13,7 +13,10 @@
 KV_HEADS = 2
 GROUP = QUERY_HEADS // KV_HEADS
 SHARDS = 4
+CAP = 6
 SLOTS = 8
+CUT = 4
+PIECE = CUT * CAP
 TILE = 128
 KEYS = 256
 KV_ROWS = TILE + 16
@@ -51,6 +54,28 @@
     )
     ranks = dot(wide.astype(BF16), before.astype(F32).astype(BF16))
     return members, ranks
+
+
+def one_hot(targets, count):
+    shape = (targets.shape[0], count) if targets.shape[1] == 1 else (count, targets.shape[1])
+    axis = 1 if targets.shape[1] == 1 else 0
+    places = lax.broadcasted_iota(jnp.int32, shape, axis).astype(F32)
+    return jnp.where(places == targets, 1.0, 0.0).astype(BF16)
+
+
+def split(x, size):
+    whole = jnp.floor((x + 0.5) / size)
+    return whole, x - whole * size
+
+
+def travel_row(x, senders, slots):
+    chunk, rest = split(x, senders * slots)
+    sender, slot = split(rest, slots)
+    return jnp.where(slot < CAP, sender * PIECE + chunk * CAP + slot, -1.0)
+
+
+def numbers(shape, axis):
+    return lax.broadcasted_iota(jnp.int32, shape, axis).astype(F32)
 
 
 def pack_kernel(docs_ref, keys_ref, values_ref, out_ref, docs, values, sems):
@@ -255,43 +280,49 @@
                         xs_ref[row : row + SLOTS, lane : lane + HEAD]
                         + done[h][k * TILE + g * SLOTS : k * TILE + (g + 1) * SLOTS]
                     )
+    width = state.shape[1] // CUT
+    order = one_hot(travel_row(numbers((1, CUT * SLOTS), 1), 1, SLOTS), PIECE)
     for k in range(planes):
         hidden = state[k * SLOTS : (k + 1) * SLOTS, :]
         mean = jnp.mean(hidden * hidden, axis=1, keepdims=True)
-        outs[k][...] = (hidden * lax.rsqrt(mean + 1e-06) * gain[...]).astype(BF16)
+        normed = hidden * lax.rsqrt(mean + 1e-06) * gain[...]
+        chunks = [normed[:, q * width : (q + 1) * width] for q in range(CUT)]
+        outs[k][...] = dot(order, jnp.concatenate(chunks, axis=0).astype(BF16)).astype(BF16)
 
 
 def expert_kernel(n, count, *refs):
     pieces = refs[:count]
     wg, wu, wd = refs[count : count + 3]
     keep_ref, send_ref, rows = refs[count + 4 :]
-    width = rows.shape[1]
-    total = n * SLOTS
-    out_rows = min(total, 16 * SLOTS)
+    step = pieces[0].shape[1]
+    senders = min(n, 16)
+    size, total = senders * PIECE, n * PIECE
     half = total // 2
-    step = 1024
-    for at in range(0, total, out_rows):
-        for col in range(0, width, step):
-            parts, first = [], 0
-            for piece in pieces:
-                size = piece.shape[0]
-                low, high = max(at - first, 0), min(at + out_rows - first, size)
-                if low < high:
-                    parts.append(piece[low:high, col : col + step].astype(F32))
-                first += size
-            rows[:, col : col + step] = jnp.concatenate(parts, axis=0).astype(BF16)
+    kept = senders * CAP
+    gather = one_hot(travel_row(numbers((size, 1), 0), senders, CAP), size)
+    spread = one_hot(travel_row(numbers((1, size), 1), senders, CAP), size)
+    for at in range(0, total, size):
+        parts, first = [], 0
+        for piece in pieces:
+            low, high = max(at - first, 0), min(at + size - first, piece.shape[0])
+            if low < high:
+                parts.append(piece[low:high, :].astype(F32))
+            first += piece.shape[0]
+        came = dot(gather, jnp.concatenate(parts, axis=0).astype(BF16)).astype(BF16)
+        for q in range(CUT):
+            rows[:, q * step : (q + 1) * step] = came[q * kept : (q + 1) * kept]
         gate = dot(rows[...], wg[...])
         up = dot(rows[...], wu[...])
         act = (gate / (1.0 + jnp.exp(-gate)) * up).astype(BF16)
-        for col in range(0, width, step):
-            part = dot(act, wd[:, col : col + step]).astype(BF16)
-            if out_rows > half:
-                keep_ref[:, col : col + step] = part[:half]
-                send_ref[:, col : col + step] = part[half:]
-            elif at < half:
-                keep_ref[at : at + out_rows, col : col + step] = part
-            else:
-                send_ref[at - half : at - half + out_rows, col : col + step] = part
+        parts = [dot(act, wd[:, q * step : (q + 1) * step]).astype(BF16) for q in range(CUT)]
+        out = dot(spread, jnp.concatenate(parts, axis=0)).astype(BF16)
+        if size > half:
+            keep_ref[...] = out[:half]
+            send_ref[...] = out[half:]
+        elif at < half:
+            keep_ref[at : at + size] = out
+        else:
+            send_ref[at - half : at - half + size] = out
 
 
 def own_kernel(n, part, loads, pos_ref, held, q_ref, x_ref, _, *refs):
@@ -341,10 +372,15 @@
     mix_high = mix.astype(BF16)
     mix_low = (mix - mix_high.astype(F32)).astype(BF16)
     size = halves[0].shape[1]
+    slots = planes * SLOTS
+    came = jnp.concatenate([p[...].astype(F32) for p in parts], axis=0).astype(BF16)
+    order = one_hot(travel_row(numbers((CUT * slots, 1), 0), planes, SLOTS), planes * PIECE)
+    came = dot(order, came).astype(BF16)
     for i, h in enumerate(halves):
-        columns = slice(i * size, (i + 1) * size)
-        rows = jnp.concatenate([p[:, columns].astype(F32) for p in parts], axis=0).astype(BF16)
-        out_ref[:, columns] = (h[...] + dot(mix_high, rows) + dot(mix_low, rows)).astype(BF16)
+        rows = came[i * slots : (i + 1) * slots]
+        out_ref[:, i * size : (i + 1) * size] = (
+            h[...] + dot(mix_high, rows) + dot(mix_low, rows)
+        ).astype(BF16)
 
 
 def pin(x):
@@ -426,7 +462,10 @@
                 any(needed(j, y, to) for to in (0, 1) for j in range(k + 1, far + 1))
                 for y in (0, 1)
             ]
-            pairs = [(s, (s + SHARDS) % n if used[s // 2 % 2] else s) for s in range(n)]
+            onward = [s + SHARDS if s + SHARDS < n else s % SHARDS + k * SHARDS for s in range(n)]
+            pairs = [
+                (s, onward[s] if used[s // 2 % 2] and s >= k * SHARDS else s) for s in range(n)
+            ]
             along.append(move(along[k], pairs))
         pairs = [(s, s ^ 2 if s >= k * SHARDS else s) for s in range(n)]
         across.append(move(along[k], pairs))
@@ -450,7 +489,7 @@
 
     *sent, held = pl.pallas_call(
         functools.partial(routed_kernel, n, late_senders),
-        out_shape=[jax.ShapeDtypeStruct((SLOTS, width), BF16)] * planes
+        out_shape=[jax.ShapeDtypeStruct((PIECE, width // CUT), BF16)] * planes
         + [held_shape],
         in_specs=[SMEM, HBM] + [VMEM] * 4 + [ANY] * len(late),
         out_specs=[VMEM] * (planes + 1),
@@ -511,13 +550,13 @@
     there, mate, late = lax.optimization_barrier((there, mate, late))
     pieces = here + there + [mate, move(jnp.concatenate(there, axis=0), flip_c)]
 
-    half = jax.ShapeDtypeStruct((n * SLOTS // 2, width), BF16)
+    half = jax.ShapeDtypeStruct((n * PIECE // 2, width // CUT), BF16)
     keep, send = pl.pallas_call(
         functools.partial(expert_kernel, n, len(pieces)),
         out_shape=[half, half],
         in_specs=[VMEM] * (len(pieces) + 3) + [ANY],
         out_specs=[VMEM, VMEM],
-        scratch_shapes=[pltpu.VMEM((16 * SLOTS, width), BF16)],
+        scratch_shapes=[pltpu.VMEM((min(n, 16) * CAP, width), BF16)],
         compiler_params=params(16),
         cost_estimate=pl.CostEstimate(
             flops=1_200_000_000, bytes_accessed=12_000_000, transcendentals=50_000
@@ -528,14 +567,14 @@
     halves += [own(part, keep)[0] for part in range(2, 4)]
 
     total = keep.astype(F32) + move(send, [(s, s ^ 1) for s in range(n)]).astype(F32)
-    quarter = n * SLOTS // 4
+    quarter = n * PIECE // 4
     other = move(total[quarter:].astype(BF16), [(s, s ^ 2) for s in range(n)])
     total = (total[:quarter] + other.astype(F32)).astype(BF16)
-    parts = [total[:SLOTS]]
+    parts = [total[:PIECE]]
     for k in range(1, planes):
         parts.append(
             move(
-                total[k * SLOTS : (k + 1) * SLOTS], [(s, (s - k * SHARDS) % n) for s in range(n)]
+                total[k * PIECE : (k + 1) * PIECE], [(s, (s - k * SHARDS) % n) for s in range(n)]
             )
         )
 

time: 78.8 us -> 76.4 us (0.970); the launches traced: 77.8 us -> 76.3 us
  waiting for transfers between devices: 29 us -> 16.2 us
  starting transfers between devices: 27.5 us -> 37.8 us
  Pallas kernels: 20.6 us -> 21.7 us
    ppermute x21, waiting for transfers between devices: 29 us -> 16.2 us  [move(): return lax.ppermute(value, 'expert', pairs)]
    ppermute x21, starting transfers between devices: 27.5 us -> 37.8 us  [move(): return lax.ppermute(value, 'expert', pairs)]
    pallas_call x1, Pallas kernels: 1.97 us -> 2.82 us  [local(): pl.pallas_call(functools.partial(expert_kernel, n, len(pieces)), out_shap...]
  transfers between devices with their start and end apart: 21 -> 21, of which waited for: 11 -> 10; matrix products, arithmetic and copies ran while one was open for 0% -> 0% of each run, Pallas kernels for 16% -> 17%
where the time goes in v3:
time: 76.4 us; the launch traced here: 76.3 us
  starting transfers between devices  37.8 us (49%)
  Pallas kernels  21.7 us (28%)
  waiting for transfers between devices  16.2 us (21%)
    ppermute x21, starting transfers between devices, move(): return lax.ppermute(value, 'expert', pairs)  37.8 us
    ppermute x21, waiting for transfers between devices, move(): return lax.ppermute(value, 'expert', pairs)  16.2 us
    pallas_call x4, Pallas kernels, own(): pl.pallas_call(functools.partial(own_kernel, n, part, len(sources)), out_...  8.23 us
    pallas_call x1, Pallas kernels, local(): pl.pallas_call(functools.partial(routed_kernel, n, late_senders), out_sha...  3.41 us
    pallas_call x1, Pallas kernels, local(): pl.pallas_call(functools.partial(expert_kernel, n, len(pieces)), out_shap...  2.82 us
    pallas_call x1, Pallas kernels, local(): pl.pallas_call(functools.partial(select_kernel, planes), out_shape=[jax.S...  2.21 us
    pallas_call x1, Pallas kernels, local(): pl.pallas_call(functools.partial(collect_kernel, n, early_senders), out_s...  2.2 us
    pallas_call x1, Pallas kernels, local(): pl.pallas_call(functools.partial(combine_kernel, planes), out_shape=jax.S...  1.88 us
  transfers between devices with their start and end apart: 21, of which 10 were waited for; matrix products, arithmetic and copies ran while one was open for 0% of the time, Pallas kernels for 17%

profile of v3, /device:TPU:0, one launch (start us, length us, event | category | flops | bytes accessed | tf_op | source)
XLA Modules:
  0.0 76.3 jit_solution(14296743364733803094)
XLA Ops:
  0.0 1.0 %pack.1.refs_0_ = bf16[144,512]{1,0:T(8,128)(2,1)S(1)} custom-call(s32[1,128]{1,0:T(1,128)} %bitcast.9, bf16[128,256]{1,0:T(8,128)(2,1)} %keys_ref.1, bf16[128,256]{1,0:T(8,128)(2,1)} %values_ref.1), custom_call_target="tpu_custom_call" | custom-call | tf_op jit(solution)/shard_map/pack/pallas_call | solution.py:408
  1.0 3.1 %collective-permute-start = (bf16[144,512]{1,0:T(8,128)(2,1)S(1)}, bf16[144,512]{1,0:T(8,128)(2,1)S(1)}, u32[]{:S(2)}, u32[]{:S(2)}) collective-permute-start(bf16[144,512]{1,0:T(8,128)(2,1)S(1)} %pack.1.refs_0_), channel_id=1, source_target_pairs={{0,4},{1,5},{2,6},{3,7},{4,8},{5,9},{6,10},{7,11},{8,12},{9,13},{1... | collective-permute-start | bytes 442376 | tf_op jit(solution)/shard_map/ppermute | solution.py:423
  4.1 1.5 %collective-permute-start.2 = (bf16[144,512]{1,0:T(8,128)(2,1)S(1)}, bf16[144,512]{1,0:T(8,128)(2,1)S(1)}, u32[]{:S(2)}, u32[]{:S(2)}) collective-permute-start(bf16[144,512]{1,0:T(8,128)(2,1)S(1)} %pack.1.refs_0_), channel_id=1, source_target_pairs={{0,2},{1,3},{2,0},{3,1},{4,6},{5,7},{6,4},{7,5},{8,10},{9,11},{10,... | collective-permute-start | bytes 442376 | tf_op jit(solution)/shard_map/ppermute | solution.py:423
  5.6 2.2 %select.1 = (bf16[2,256,512]{2,1,0:T(8,128)(2,1)S(1)}, f32[32,4096]{1,0:T(8,128)S(1)}, f32[8,512]{1,0:T(8,128)S(1)}) custom-call(s32[1]{0:T(128)} %bitcast.pos_ref, s32[4,128]{1,0:T(4,128)} %bitcast.5, s32[1,128]{1,0:T(1,128)} %bitcast.10, bf16[128,4096]{1,0:T(8,128)(2,1)} %q_ref.7, bf16[128,4096]{1,0:T(8,128)(2,1)} %x_ref.7), custom_call_target="tpu_custom_call" | custom-call | tf_op jit(solution)/shard_map/select/pallas_call | solution.py:432
  7.8 2.1 %collective-permute-done.refs_1_ = bf16[144,512]{1,0:T(8,128)(2,1)S(1)} collective-permute-done((bf16[144,512]{1,0:T(8,128)(2,1)S(1)}, bf16[144,512]{1,0:T(8,128)(2,1)S(1)}, u32[]{:S(2)}, u32[]{:S(2)}) %collective-permute-start) | collective-permute-done | bytes 147488 | tf_op jit(solution)/shard_map/ppermute | solution.py:423
  9.9 0.7 collective-permute-start.1
  10.6 0.7 collective-permute-start.4
  11.3 0.0 collective-permute-done.2.refs_4_
  11.3 0.7 collective-permute-start.3
  12.0 0.7 collective-permute-start.5
  12.7 0.0 collective-permute-done.4.refs_5_
  12.7 0.7 collective-permute-start.7
  13.4 0.1 collective-permute-start.6
  13.5 0.0 collective-permute-done.5.refs_6_
  13.6 0.5 collective-permute-start.8
  14.1 1.4 %collective-permute-done.6.refs_7_ = bf16[576,512]{1,0:T(8,128)(2,1)S(1)} collective-permute-done((bf16[576,512]{1,0:T(8,128)(2,1)S(1)}, bf16[576,512]{1,0:T(8,128)(2,1)S(1)}, u32[]{:S(2)}, u32[]{:S(2)}) %collective-permute-start.6) | collective-permute-done | bytes 589856 | tf_op jit(solution)/shard_map/ppermute | solution.py:423
  15.5 2.2 %collect.1._ = bf16[16,144,512]{2,1,0:T(8,128)(2,1)S(1)} custom-call(s32[1]{0:T(128)} %bitcast.pos_ref, bf16[144,512]{1,0:T(8,128)(2,1)S(1)} %pack.1.refs_0_, bf16[144,512]{1,0:T(8,128)(2,1)S(1)} %collective-permute-done.refs_1_, bf16[144,512]{1,0:T(8,128)(2,1)S(1)} %collective-permute-done.1.refs_2_, bf16[144,512]{1,0:T(8,128)(2,1)S(1)} %collective-permute-done.3.refs_3_, ...), custom_call_target="tpu_custom_call" | custom-call | tf_op jit(solution)/shard_map/collect/pallas_call | solution.py:480
  17.7 0.0 copy-start
  17.7 0.0 copy-start.1
  17.7 3.4 %routed.1 = (bf16[24,1024]{1,0:T(8,128)(2,1)S(1)}, bf16[24,1024]{1,0:T(8,128)(2,1)S(1)}, bf16[24,1024]{1,0:T(8,128)(2,1)S(1)}, bf16[24,1024]{1,0:T(8,128)(2,1)S(1)}, bf16[16,144,512]{2,1,0:T(8,128)(2,1)S(1)}) custom-call(s32[1]{0:T(128)} %bitcast.pos_ref, f32[1,4096]{1,0:T(1,128)} %bitcast.8, ...), custom_call_target="tpu_custom_call", output_to_operand_aliasing={{4}: (5, {})} | custom-call | tf_op jit(solution)/shard_map/routed/pallas_call | solution.py:490
  21.1 8.4 %collective-permute-start.9 = (bf16[24,1024]{1,0:T(8,128)(2,1)S(1)}, bf16[24,1024]{1,0:T(8,128)(2,1)S(1)}, u32[]{:S(2)}, u32[]{:S(2)}) collective-permute-start(bf16[24,1024]{1,0:T(8,128)(2,1)S(1)} %get-tuple-element.52), channel_id=1, source_target_pairs={{0,4},{1,5},{2,6},{3,7},{4,8},{5,9},{6,10},{7,11},{8,12},{9,13},{1... | collective-permute-start | bytes 147464 | tf_op jit(solution)/shard_map/ppermute | solution.py:423
  29.5 13.3 %collective-permute-start.10 = (bf16[24,1024]{1,0:T(8,128)(2,1)S(1)}, bf16[24,1024]{1,0:T(8,128)(2,1)S(1)}, u32[]{:S(2)}, u32[]{:S(2)}) collective-permute-start(bf16[24,1024]{1,0:T(8,128)(2,1)S(1)} %get-tuple-element.53), channel_id=1, source_target_pairs={{0,8},{1,9},{2,10},{3,11},{4,12},{5,13},{6,14},{7,15},{8,0},{9,1},... | collective-permute-start | bytes 147464 | tf_op jit(solution)/shard_map/ppermute | solution.py:423
  42.8 3.9 %own.4 = (f32[128,1024]{1,0:T(8,128)S(1)}, f32[8,128]{1,0:T(8,128)S(1)}, bf16[4096,384]{1,0:T(8,128)(2,1)S(1)}, bf16[4096,384]{1,0:T(8,128)(2,1)S(1)}, bf16[384,4096]{1,0:T(8,128)(2,1)S(1)}) custom-call(s32[1]{0:T(128)} %bitcast.pos_ref, bf16[16,144,512]{2,1,0:T(8,128)(2,1)S(1)} %get-tuple-element.47.held, bf16[128,4096]{1,0:T(8,128)(2,1)S(1)} %copy-done, ...), custom_call_target="tpu_custom_call" | custom-call | flops 2000000000 | bytes 8000000 | tf_op jit(solution)/shard_map/own/pallas_call | solution.py:511
  46.6 0.0 collective-permute-done.9
  46.7 0.1 collective-permute-done.10
  46.7 0.5 collective-permute-done.11
  47.2 0.0 collective-permute-done.12.refs_2_
  47.3 0.1 collective-permute-start.14
  47.4 1.5 %collective-permute-start.13 = (bf16[72,1024]{1,0:T(8,128)(2,1)S(1)}, bf16[72,1024]{1,0:T(8,128)(2,1)S(1)}, u32[]{:S(2)}, u32[]{:S(2)}) collective-permute-start(bf16[72,1024]{1,0:T(8,128)(2,1)S(1)} %constant_dynamic-update-slice_fusion.refs_1_), channel_id=1, source_target_pairs={{0,2},{1,3},{2,0},{3,1},{4,6},{5,7},{6,4},{7,5},{8,10},{9,11},{10,... | collective-permute-start | bytes 442376 | tf_op jit(solution)/shard_map/ppermute | solution.py:423
  48.9 1.2 %own.5 = (f32[128,1024]{1,0:T(8,128)S(1)}, f32[8,128]{1,0:T(8,128)S(1)}) custom-call(s32[1]{0:T(128)} %bitcast.pos_ref, bf16[16,144,512]{2,1,0:T(8,128)(2,1)S(1)} %get-tuple-element.47.held, bf16[128,4096]{1,0:T(8,128)(2,1)S(1)} %copy-done, bf16[128,4096]{1,0:T(8,128)(2,1)S(1)} %copy-done.1, f32[8,128]{1,0:T(8,128)S(1)} %get-tuple-element.50._), custom_call_target="tpu_custom_call" | custom-call | flops 2000000000 | bytes 8000000 | tf_op jit(solution)/shard_map/own/pallas_call | solution.py:511
  50.1 3.5 %collective-permute-done.13.refs_3_ = bf16[72,1024]{1,0:T(8,128)(2,1)S(1)} collective-permute-done((bf16[72,1024]{1,0:T(8,128)(2,1)S(1)}, bf16[72,1024]{1,0:T(8,128)(2,1)S(1)}, u32[]{:S(2)}, u32[]{:S(2)}) %collective-permute-start.13) | collective-permute-done | bytes 147488 | tf_op jit(solution)/shard_map/ppermute | solution.py:423
  53.7 0.1 collective-permute-start.15
  53.7 1.4 %collective-permute-done.15.refs_5_ = bf16[96,1024]{1,0:T(8,128)(2,1)S(1)} collective-permute-done((bf16[96,1024]{1,0:T(8,128)(2,1)S(1)}, bf16[96,1024]{1,0:T(8,128)(2,1)S(1)}, u32[]{:S(2)}, u32[]{:S(2)}) %collective-permute-start.15) | collective-permute-done | bytes 196640 | tf_op jit(solution)/shard_map/ppermute | solution.py:423
  55.2 2.8 %expert.1 = (bf16[192,1024]{1,0:T(8,128)(2,1)S(1)}, bf16[192,1024]{1,0:T(8,128)(2,1)S(1)}) custom-call(bf16[24,1024]{1,0:T(8,128)(2,1)S(1)} %get-tuple-element.48._.refs_0_, bf16[72,1024]{1,0:T(8,128)(2,1)S(1)} %constant_dynamic-update-slice_fusion.refs_1_, bf16[24,1024]{1,0:T(8,128)(2,1)S(1)} %collective-permute-done.12.refs_2_, ...), custom_call_target="tpu_custom_call" | custom-call | flops 1200000000 | bytes 12000000 | tf_op jit(solution)/shard_map/expert/pallas_call | solution.py:554
  58.0 0.2 collective-permute-start.16
  58.2 1.6 %collective-permute-done.16 = bf16[192,1024]{1,0:T(8,128)(2,1)S(1)} collective-permute-done((bf16[192,1024]{1,0:T(8,128)(2,1)S(1)}, bf16[192,1024]{1,0:T(8,128)(2,1)S(1)}, u32[]{:S(2)}, u32[]{:S(2)}) %collective-permute-start.16) | collective-permute-done | bytes 393248 | tf_op jit(solution)/shard_map/ppermute | solution.py:423
  59.8 0.1 convert_add_fusion
  59.9 1.5 %collective-permute-start.17 = (bf16[96,1024]{1,0:T(8,128)(2,1)S(1)}, bf16[96,1024]{1,0:T(8,128)(2,1)S(1)}, u32[]{:S(2)}, u32[]{:S(2)}) collective-permute-start(bf16[96,1024]{1,0:T(8,128)(2,1)S(1)} %slice.35), channel_id=1, source_target_pairs={{0,2},{1,3},{2,0},{3,1},{4,6},{5,7},{6,4},{7,5},{8,10},{9,11},{10,... | collective-permute-start | bytes 589832 | tf_op jit(solution)/shard_map/ppermute | solution.py:423
  61.4 1.6 %own.7 = (f32[128,1024]{1,0:T(8,128)S(1)}, f32[8,128]{1,0:T(8,128)}) custom-call(s32[1]{0:T(128)} %bitcast.pos_ref, bf16[16,144,512]{2,1,0:T(8,128)(2,1)S(1)} %get-tuple-element.47.held, bf16[128,4096]{1,0:T(8,128)(2,1)S(1)} %copy-done, bf16[128,4096]{1,0:T(8,128)(2,1)S(1)} %copy-done.1, bf16[192,1024]{1,0:T(8,128)(2,1)S(1)} %get-tuple-element.67._), custom_call_target="tpu_custom_call" | custom-call | flops 2000000000 | bytes 8000000 | tf_op jit(solution)/shard_map/own/pallas_call | solution.py:511
  63.0 3.9 %collective-permute-done.17 = bf16[96,1024]{1,0:T(8,128)(2,1)S(1)} collective-permute-done((bf16[96,1024]{1,0:T(8,128)(2,1)S(1)}, bf16[96,1024]{1,0:T(8,128)(2,1)S(1)}, u32[]{:S(2)}, u32[]{:S(2)}) %collective-permute-start.17) | collective-permute-done | bytes 196640 | tf_op jit(solution)/shard_map/ppermute | solution.py:423
  67.0 1.8 %collective-permute-start.20 = (bf16[24,1024]{1,0:T(8,128)(2,1)S(1)}, bf16[24,1024]{1,0:T(8,128)(2,1)S(1)}, u32[]{:S(2)}, u32[]{:S(2)}) collective-permute-start(bf16[24,1024]{1,0:T(8,128)(2,1)S(1)} %get-tuple-element.71), channel_id=1, source_target_pairs={{0,4},{1,5},{2,6},{3,7},{4,8},{5,9},{6,10},{7,11},{8,12},{9,13},{1... | collective-permute-start | bytes 147464 | tf_op jit(solution)/shard_map/ppermute | solution.py:423
  68.8 1.0 %collective-permute-start.19 = (bf16[24,1024]{1,0:T(8,128)(2,1)S(1)}, bf16[24,1024]{1,0:T(8,128)(2,1)S(1)}, u32[]{:S(2)}, u32[]{:S(2)}) collective-permute-start(bf16[24,1024]{1,0:T(8,128)(2,1)S(1)} %get-tuple-element.72), channel_id=1, source_target_pairs={{0,8},{1,9},{2,10},{3,11},{4,12},{5,13},{6,14},{7,15},{8,0},{9,1},... | collective-permute-start | bytes 147464 | tf_op jit(solution)/shard_map/ppermute | solution.py:423
  69.8 1.4 %collective-permute-start.18 = (bf16[24,1024]{1,0:T(8,128)(2,1)S(1)}, bf16[24,1024]{1,0:T(8,128)(2,1)S(1)}, u32[]{:S(2)}, u32[]{:S(2)}) collective-permute-start(bf16[24,1024]{1,0:T(8,128)(2,1)S(1)} %get-tuple-element.73), channel_id=1, source_target_pairs={{0,12},{1,13},{2,14},{3,15},{4,0},{5,1},{6,2},{7,3},{8,4},{9,5},{1... | collective-permute-start | bytes 147464 | tf_op jit(solution)/shard_map/ppermute | solution.py:423
  71.2 1.6 %own.6 = (f32[128,1024]{1,0:T(8,128)S(1)}, f32[8,128]{1,0:T(8,128)}) custom-call(s32[1]{0:T(128)} %bitcast.pos_ref, bf16[16,144,512]{2,1,0:T(8,128)(2,1)S(1)} %get-tuple-element.47.held, bf16[128,4096]{1,0:T(8,128)(2,1)S(1)} %copy-done, bf16[128,4096]{1,0:T(8,128)(2,1)S(1)} %copy-done.1, bf16[192,1024]{1,0:T(8,128)(2,1)S(1)} %get-tuple-element.67._), custom_call_target="tpu_custom_call" | custom-call | flops 2000000000 | bytes 8000000 | tf_op jit(solution)/shard_map/own/pallas_call | solution.py:511
  72.9 0.5 collective-permute-done.20.refs_7_
  73.4 1.1 %collective-permute-done.19.refs_6_ = bf16[24,1024]{1,0:T(8,128)(2,1)S(1)} collective-permute-done((bf16[24,1024]{1,0:T(8,128)(2,1)S(1)}, bf16[24,1024]{1,0:T(8,128)(2,1)S(1)}, u32[]{:S(2)}, u32[]{:S(2)}) %collective-permute-start.19) | collective-permute-done | bytes 49184 | tf_op jit(solution)/shard_map/ppermute | solution.py:423
  74.4 0.0 collective-permute-done.18.refs_5_
  74.5 1.9 %combine.1 = bf16[128,4096]{1,0:T(8,128)(2,1)} custom-call(s32[1]{0:T(128)} %bitcast.pos_ref, s32[4,128]{1,0:T(4,128)S(1)} %bitcast.6, f32[4,128]{1,0:T(4,128)S(1)} %bitcast.7, f32[128,1024]{1,0:T(8,128)S(1)} %get-tuple-element.49.refs_0_, f32[128,1024]{1,0:T(8,128)S(1)} %get-tuple-element.51.refs_1_, f32[128,1024]{1,0:T(8,128)S(1)} %get-tuple-element.68.refs_2_, ...), custom_call_target="tpu_custom_call" | custom-call | tf_op jit(solution)/shard_map/combine/pallas_call | solution.py:581
  (23 shorter events, 0.2 us)
Async XLA Ops:
  1.0 8.9 %collective-permute-start = (bf16[144,512]{1,0:T(8,128)(2,1)S(1)}, bf16[144,512]{1,0:T(8,128)(2,1)S(1)}, u32[]{:S(2)}, u32[]{:S(2)}) collective-permute-start(bf16[144,512]{1,0:T(8,128)(2,1)S(1)} %pack.1.refs_0_), channel_id=1, source_target_pairs={{0,4},{1,5},{2,6},{3,7},{4,8},{5,9},{6,10},{7,11},{8,12},{9,13},{1... | collective-permute-start | bytes 442376 | tf_op jit(solution)/shard_map/ppermute | solution.py:423
  4.1 7.2 %collective-permute-start.2 = (bf16[144,512]{1,0:T(8,128)(2,1)S(1)}, bf16[144,512]{1,0:T(8,128)(2,1)S(1)}, u32[]{:S(2)}, u32[]{:S(2)}) collective-permute-start(bf16[144,512]{1,0:T(8,128)(2,1)S(1)} %pack.1.refs_0_), channel_id=1, source_target_pairs={{0,2},{1,3},{2,0},{3,1},{4,6},{5,7},{6,4},{7,5},{8,10},{9,11},{10,... | collective-permute-start | bytes 442376 | tf_op jit(solution)/shard_map/ppermute | solution.py:423
  9.9 1.4 %collective-permute-start.1 = (bf16[144,512]{1,0:T(8,128)(2,1)S(1)}, bf16[144,512]{1,0:T(8,128)(2,1)S(1)}, u32[]{:S(2)}, u32[]{:S(2)}) collective-permute-start(bf16[144,512]{1,0:T(8,128)(2,1)S(1)} %collective-permute-done.refs_1_), channel_id=1, source_target_pairs={{0,0},{1,1},{2,2},{3,3},{4,8},{5,9},{6,10},{7,11},{8,12},{9,13},{1... | collective-permute-start | bytes 442376 | tf_op jit(solution)/shard_map/ppermute | solution.py:423
  10.6 2.1 %collective-permute-start.4 = (bf16[144,512]{1,0:T(8,128)(2,1)S(1)}, bf16[144,512]{1,0:T(8,128)(2,1)S(1)}, u32[]{:S(2)}, u32[]{:S(2)}) collective-permute-start(bf16[144,512]{1,0:T(8,128)(2,1)S(1)} %collective-permute-done.refs_1_), channel_id=1, source_target_pairs={{0,0},{1,1},{2,2},{3,3},{4,6},{5,7},{6,4},{7,5},{8,10},{9,11},{10,... | collective-permute-start | bytes 442376 | tf_op jit(solution)/shard_map/ppermute | solution.py:423
  11.3 1.4 %collective-permute-start.3 = (bf16[144,512]{1,0:T(8,128)(2,1)S(1)}, bf16[144,512]{1,0:T(8,128)(2,1)S(1)}, u32[]{:S(2)}, u32[]{:S(2)}) collective-permute-start(bf16[144,512]{1,0:T(8,128)(2,1)S(1)} %collective-permute-done.1.refs_2_), channel_id=1, source_target_pairs={{0,0},{1,1},{2,2},{3,3},{4,4},{5,5},{6,6},{7,7},{8,8},{9,9},{10,14... | collective-permute-start | bytes 442376 | tf_op jit(solution)/shard_map/ppermute | solution.py:423
  12.0 1.5 %collective-permute-start.5 = (bf16[144,512]{1,0:T(8,128)(2,1)S(1)}, bf16[144,512]{1,0:T(8,128)(2,1)S(1)}, u32[]{:S(2)}, u32[]{:S(2)}) collective-permute-start(bf16[144,512]{1,0:T(8,128)(2,1)S(1)} %collective-permute-done.1.refs_2_), channel_id=1, source_target_pairs={{0,0},{1,1},{2,2},{3,3},{4,4},{5,5},{6,6},{7,7},{8,10},{9,11},{10,... | collective-permute-start | bytes 442376 | tf_op jit(solution)/shard_map/ppermute | solution.py:423
  12.7 0.8 %collective-permute-start.7 = (bf16[144,512]{1,0:T(8,128)(2,1)S(1)}, bf16[144,512]{1,0:T(8,128)(2,1)S(1)}, u32[]{:S(2)}, u32[]{:S(2)}) collective-permute-start(bf16[144,512]{1,0:T(8,128)(2,1)S(1)} %collective-permute-done.3.refs_3_), channel_id=1, source_target_pairs={{0,0},{1,1},{2,2},{3,3},{4,4},{5,5},{6,6},{7,7},{8,8},{9,9},{10,10... | collective-permute-start | bytes 442376 | tf_op jit(solution)/shard_map/ppermute | solution.py:423
  13.4 2.1 %collective-permute-start.6 = (bf16[576,512]{1,0:T(8,128)(2,1)S(1)}, bf16[576,512]{1,0:T(8,128)(2,1)S(1)}, u32[]{:S(2)}, u32[]{:S(2)}) collective-permute-start(bf16[576,512]{1,0:T(8,128)(2,1)S(1)} %pad_maximum_fusion), channel_id=1, source_target_pairs={{0,1},{1,0},{2,3},{3,2},{4,5},{5,4},{6,7},{7,6},{8,9},{9,8},{10,11... | collective-permute-start | bytes 1769480 | tf_op jit(solution)/shard_map/ppermute | solution.py:423
  13.6 4.1 %collective-permute-start.8 = (bf16[576,512]{1,0:T(8,128)(2,1)S(1)}, bf16[576,512]{1,0:T(8,128)(2,1)S(1)}, u32[]{:S(2)}, u32[]{:S(2)}) collective-permute-start(bf16[576,512]{1,0:T(8,128)(2,1)S(1)} %pad_maximum_fusion.1), channel_id=1, source_target_pairs={{0,1},{1,0},{2,3},{3,2},{4,5},{5,4},{6,7},{7,6},{8,9},{9,8},{10,11... | collective-permute-start | bytes 1769480 | tf_op jit(solution)/shard_map/ppermute | solution.py:423
  17.7 25.1 %copy-start = (bf16[128,4096]{1,0:T(8,128)(2,1)S(1)}, bf16[128,4096]{1,0:T(8,128)(2,1)}, u32[]{:S(2)}) copy-start(bf16[128,4096]{1,0:T(8,128)(2,1)} %q_ref.7) | copy-start | bytes 3145732
  17.7 25.1 %copy-start.1 = (bf16[128,4096]{1,0:T(8,128)(2,1)S(1)}, bf16[128,4096]{1,0:T(8,128)(2,1)}, u32[]{:S(2)}) copy-start(bf16[128,4096]{1,0:T(8,128)(2,1)} %x_ref.7) | copy-start | bytes 3145732
  21.1 25.5 %collective-permute-start.9 = (bf16[24,1024]{1,0:T(8,128)(2,1)S(1)}, bf16[24,1024]{1,0:T(8,128)(2,1)S(1)}, u32[]{:S(2)}, u32[]{:S(2)}) collective-permute-start(bf16[24,1024]{1,0:T(8,128)(2,1)S(1)} %get-tuple-element.52), channel_id=1, source_target_pairs={{0,4},{1,5},{2,6},{3,7},{4,8},{5,9},{6,10},{7,11},{8,12},{9,13},{1... | collective-permute-start | bytes 147464 | tf_op jit(solution)/shard_map/ppermute | solution.py:423
  29.5 17.3 %collective-permute-start.10 = (bf16[24,1024]{1,0:T(8,128)(2,1)S(1)}, bf16[24,1024]{1,0:T(8,128)(2,1)S(1)}, u32[]{:S(2)}, u32[]{:S(2)}) collective-permute-start(bf16[24,1024]{1,0:T(8,128)(2,1)S(1)} %get-tuple-element.53), channel_id=1, source_target_pairs={{0,8},{1,9},{2,10},{3,11},{4,12},{5,13},{6,14},{7,15},{8,0},{9,1},... | collective-permute-start | bytes 147464 | tf_op jit(solution)/shard_map/ppermute | solution.py:423
  42.8 4.5 %collective-permute-start.11 = (bf16[24,1024]{1,0:T(8,128)(2,1)S(1)}, bf16[24,1024]{1,0:T(8,128)(2,1)S(1)}, u32[]{:S(2)}, u32[]{:S(2)}) collective-permute-start(bf16[24,1024]{1,0:T(8,128)(2,1)S(1)} %get-tuple-element.54), channel_id=1, source_target_pairs={{0,12},{1,13},{2,14},{3,15},{4,0},{5,1},{6,2},{7,3},{8,4},{9,5},{1... | collective-permute-start | bytes 147464 | tf_op jit(solution)/shard_map/ppermute | solution.py:423
  42.8 4.5 %collective-permute-start.12 = (bf16[24,1024]{1,0:T(8,128)(2,1)S(1)}, bf16[24,1024]{1,0:T(8,128)(2,1)S(1)}, u32[]{:S(2)}, u32[]{:S(2)}) collective-permute-start(bf16[24,1024]{1,0:T(8,128)(2,1)S(1)} %get-tuple-element.48._.refs_0_), channel_id=1, source_target_pairs={{0,2},{1,3},{2,0},{3,1},{4,6},{5,7},{6,4},{7,5},{8,10},{9,11},{10,... | collective-permute-start | bytes 147464 | tf_op jit(solution)/shard_map/ppermute | solution.py:423
  47.3 6.4 %collective-permute-start.14 = (bf16[96,1024]{1,0:T(8,128)(2,1)S(1)}, bf16[96,1024]{1,0:T(8,128)(2,1)S(1)}, u32[]{:S(2)}, u32[]{:S(2)}) collective-permute-start(bf16[96,1024]{1,0:T(8,128)(2,1)S(1)} %pad_maximum_fusion.2), channel_id=1, source_target_pairs={{0,1},{1,0},{2,3},{3,2},{4,5},{5,4},{6,7},{7,6},{8,9},{9,8},{10,11... | collective-permute-start | bytes 589832 | tf_op jit(solution)/shard_map/ppermute | solution.py:423
  47.4 6.3 %collective-permute-start.13 = (bf16[72,1024]{1,0:T(8,128)(2,1)S(1)}, bf16[72,1024]{1,0:T(8,128)(2,1)S(1)}, u32[]{:S(2)}, u32[]{:S(2)}) collective-permute-start(bf16[72,1024]{1,0:T(8,128)(2,1)S(1)} %constant_dynamic-update-slice_fusion.refs_1_), channel_id=1, source_target_pairs={{0,2},{1,3},{2,0},{3,1},{4,6},{5,7},{6,4},{7,5},{8,10},{9,11},{10,... | collective-permute-start | bytes 442376 | tf_op jit(solution)/shard_map/ppermute | solution.py:423
  53.7 1.5 %collective-permute-start.15 = (bf16[96,1024]{1,0:T(8,128)(2,1)S(1)}, bf16[96,1024]{1,0:T(8,128)(2,1)S(1)}, u32[]{:S(2)}, u32[]{:S(2)}) collective-permute-start(bf16[96,1024]{1,0:T(8,128)(2,1)S(1)} %pad_maximum_fusion.3), channel_id=1, source_target_pairs={{0,1},{1,0},{2,3},{3,2},{4,5},{5,4},{6,7},{7,6},{8,9},{9,8},{10,11... | collective-permute-start | bytes 589832 | tf_op jit(solution)/shard_map/ppermute | solution.py:423
  58.0 1.8 %collective-permute-start.16 = (bf16[192,1024]{1,0:T(8,128)(2,1)S(1)}, bf16[192,1024]{1,0:T(8,128)(2,1)S(1)}, u32[]{:S(2)}, u32[]{:S(2)}) collective-permute-start(bf16[192,1024]{1,0:T(8,128)(2,1)S(1)} %get-tuple-element.70), channel_id=1, source_target_pairs={{0,1},{1,0},{2,3},{3,2},{4,5},{5,4},{6,7},{7,6},{8,9},{9,8},{10,11... | collective-permute-start | bytes 1179656 | tf_op jit(solution)/shard_map/ppermute | solution.py:423
  59.9 7.0 %collective-permute-start.17 = (bf16[96,1024]{1,0:T(8,128)(2,1)S(1)}, bf16[96,1024]{1,0:T(8,128)(2,1)S(1)}, u32[]{:S(2)}, u32[]{:S(2)}) collective-permute-start(bf16[96,1024]{1,0:T(8,128)(2,1)S(1)} %slice.35), channel_id=1, source_target_pairs={{0,2},{1,3},{2,0},{3,1},{4,6},{5,7},{6,4},{7,5},{8,10},{9,11},{10,... | collective-permute-start | bytes 589832 | tf_op jit(solution)/shard_map/ppermute | solution.py:423
  67.0 6.3 %collective-permute-start.20 = (bf16[24,1024]{1,0:T(8,128)(2,1)S(1)}, bf16[24,1024]{1,0:T(8,128)(2,1)S(1)}, u32[]{:S(2)}, u32[]{:S(2)}) collective-permute-start(bf16[24,1024]{1,0:T(8,128)(2,1)S(1)} %get-tuple-element.71), channel_id=1, source_target_pairs={{0,4},{1,5},{2,6},{3,7},{4,8},{5,9},{6,10},{7,11},{8,12},{9,13},{1... | collective-permute-start | bytes 147464 | tf_op jit(solution)/shard_map/ppermute | solution.py:423
  68.8 5.6 %collective-permute-start.19 = (bf16[24,1024]{1,0:T(8,128)(2,1)S(1)}, bf16[24,1024]{1,0:T(8,128)(2,1)S(1)}, u32[]{:S(2)}, u32[]{:S(2)}) collective-permute-start(bf16[24,1024]{1,0:T(8,128)(2,1)S(1)} %get-tuple-element.72), channel_id=1, source_target_pairs={{0,8},{1,9},{2,10},{3,11},{4,12},{5,13},{6,14},{7,15},{8,0},{9,1},... | collective-permute-start | bytes 147464 | tf_op jit(solution)/shard_map/ppermute | solution.py:423
  69.8 4.6 %copy-start.2 = (s32[128,4]{0,1:T(4,128)S(1)}, s32[128,4]{0,1:T(4,128)}, u32[]{:S(2)}) copy-start(s32[128,4]{0,1:T(4,128)} %param.17) | copy-start | bytes 6148
  69.8 4.6 %copy-start.3 = (f32[128,4]{0,1:T(4,128)S(1)}, f32[128,4]{0,1:T(4,128)}, u32[]{:S(2)}) copy-start(f32[128,4]{0,1:T(4,128)} %param.18) | copy-start | bytes 6148
  69.8 4.6 %collective-permute-start.18 = (bf16[24,1024]{1,0:T(8,128)(2,1)S(1)}, bf16[24,1024]{1,0:T(8,128)(2,1)S(1)}, u32[]{:S(2)}, u32[]{:S(2)}) collective-permute-start(bf16[24,1024]{1,0:T(8,128)(2,1)S(1)} %get-tuple-element.73), channel_id=1, source_target_pairs={{0,12},{1,13},{2,14},{3,15},{4,0},{5,1},{6,2},{7,3},{8,4},{9,5},{1... | collective-permute-start | bytes 147464 | tf_op jit(solution)/shard_map/ppermute | solution.py:423

commit v4 on v3

--- a/solution.py
+++ b/solution.py
@@ -228,7 +228,8 @@
     planes = n // SHARDS
     z, y, c = pos // SHARDS, (pos // 2) % 2, pos % 2
     copies = []
-    for i, (piece, row, flip_c, flip_y, k) in enumerate(senders):
+    for i, (piece, row, flip_c, flip_y, passed) in enumerate(senders):
+        k = jnp.where(y == 0, passed[0], passed[1])
         sender = lax.rem(z - k + planes, planes) * SHARDS + (y ^ flip_y) * 2 + (c ^ flip_c)
         copy = pltpu.make_async_copy(
             pieces[piece].at[pl.ds(row, KV_ROWS)], held.at[sender], sems.at[i]
@@ -247,8 +248,8 @@
 def routed_kernel(n, senders, pos_ref, gain_ref, qs_ref, xs_ref, facts_ref, _, *refs):
     planes = n // SHARDS
     count = len(senders)
-    pieces, outs, held = refs[:2], refs[2 : 2 + planes], refs[2 + planes]
-    acc, bias, q_scr, state, gain, sems = refs[3 + planes :]
+    pieces, outs, held = refs[:4], refs[4 : 4 + planes], refs[4 + planes]
+    acc, bias, q_scr, state, gain, sems = refs[5 + planes :]
     pos = pos_ref[0]
     copies = place_pieces(n, senders, pos, pieces, held, sems)
     copies.append(pltpu.make_async_copy(gain_ref, gain, sems.at[count]))
@@ -451,31 +452,29 @@
 
     flip_y = [(s, s ^ 2) for s in range(n)]
     flip_c = [(s, s ^ 1) for s in range(n)]
-    along, across = [packed], []
-    for k in range(far + 1):
-        if k == 1:
-            along[1], q_rows = lax.optimization_barrier((along[1], q_rows))
-        if k > 1:
-            along[k], across[k - 2] = lax.optimization_barrier((along[k], across[k - 2]))
-        if k < far:
-            used = [
-                any(needed(j, y, to) for to in (0, 1) for j in range(k + 1, far + 1))
-                for y in (0, 1)
-            ]
-            onward = [s + SHARDS if s + SHARDS < n else s % SHARDS + k * SHARDS for s in range(n)]
-            pairs = [
-                (s, onward[s] if used[s // 2 % 2] and s >= k * SHARDS else s) for s in range(n)
-            ]
-            along.append(move(along[k], pairs))
-        pairs = [(s, s ^ 2 if s >= k * SHARDS else s) for s in range(n)]
-        across.append(move(along[k], pairs))
-    early = along + across[:-1] + [move(jnp.concatenate(along, axis=0), flip_c)]
-    late = [across[-1], move(jnp.concatenate(across, axis=0), flip_c)]
-    steps = range(far + 1)
-    early_senders = [(k, 0, 0, 0, k) for k in steps]
-    early_senders += [(far + 1 + k, 0, 0, 1, k) for k in steps[:-1]]
-    early_senders += [(2 * far + 1, k * KV_ROWS, 1, 0, k) for k in steps]
-    late_senders = [(0, 0, 0, 1, far)] + [(1, k * KV_ROWS, 1, 1, k) for k in steps]
+    along = [packed]
+    for k in range(1, far + 1):
+        used = [any(needed(k, y, to) for to in (0, 1)) for y in (0, 1)]
+        pairs = [(s, (s + k * SHARDS) % n if used[s // 2 % 2] else s) for s in range(n)]
+        along.append(move(packed, pairs))
+    along[1], q_rows = lax.optimization_barrier((along[1], q_rows))
+    shared = not needed(0, 1, 0) and not needed(far, 0, 1)
+    middle = range(1, far) if shared else range(far)
+    across = []
+    for k in middle:
+        if k == middle[1]:
+            along[k:], across = lax.optimization_barrier((along[k:], across))
+        across.append(move(along[k], [(s, s ^ 2 if s >= k * SHARDS else s) for s in range(n)]))
+    odd = (pos[0] & 2) != 0
+    final = move(jnp.where(odd, along[far], packed) if shared else along[far], flip_y)
+    early, late = along[:far] + across[:-1], [along[far], across[-1]]
+    sides = [(0, (k, k)) for k in range(far)] + [(1, (k, k)) for k in middle[:-1]]
+    late_sides = [(0, (far, far)), (1, (middle[-1],) * 2), (1, (far, 0 if shared else far))]
+    early.append(move(jnp.concatenate(early, axis=0), flip_c))
+    early_senders = [(i, 0, 0, *side) for i, side in enumerate(sides)]
+    early_senders += [(len(sides), i * KV_ROWS, 1, *side) for i, side in enumerate(sides)]
+    late_senders = [(i, 0, 0, *side) for i, side in enumerate(late_sides)]
+    late_senders += [(3, i * KV_ROWS, 1, *side) for i, side in enumerate(late_sides)]
     held_shape = jax.ShapeDtypeStruct((n, KV_ROWS, 4 * HEAD), BF16)
     held = pl.pallas_call(
         functools.partial(collect_kernel, n, early_senders),
@@ -484,9 +483,13 @@
         out_specs=VMEM,
         scratch_shapes=[pltpu.SemaphoreType.DMA((len(early_senders),))],
         compiler_params=params(small),
+        cost_estimate=pl.CostEstimate(flops=0, bytes_accessed=1000, transcendentals=0),
         name="collect",
     )(pos, *early)
 
+    final, held = lax.optimization_barrier((final, held))
+    late.append(final)
+    late.append(move(jnp.concatenate(late, axis=0), flip_c))
     *sent, held = pl.pallas_call(
         functools.partial(routed_kernel, n, late_senders),
         out_shape=[jax.ShapeDtypeStruct((PIECE, width // CUT), BF16)] * planes

time: 76.4 us -> 76.5 us (level)
  waiting for transfers between devices: 16.2 us -> 22.9 us
  starting transfers between devices: 37.8 us -> 31.9 us
    ppermute x21 -> x20, waiting for transfers between devices: 16.2 us -> 22.9 us  [move(): return lax.ppermute(value, 'expert', pairs)]
    ppermute x21 -> x20, starting transfers between devices: 37.8 us -> 31.9 us  [move(): return lax.ppermute(value, 'expert', pairs)]
  transfers between devices with their start and end apart: 21 -> 20, of which waited for: 10 -> 10; matrix products, arithmetic and copies ran while one was open for 0% -> 0% of each run, Pallas kernels for 17% -> 16%
where the time goes in v4:
time: 76.5 us; the launch traced here: 76.7 us
  starting transfers between devices  31.9 us (42%)
  waiting for transfers between devices  22.9 us (30%)
  Pallas kernels  21.3 us (28%)
    ppermute x20, starting transfers between devices, move(): return lax.ppermute(value, 'expert', pairs)  31.9 us
    ppermute x20, waiting for transfers between devices, move(): return lax.ppermute(value, 'expert', pairs)  22.9 us
    pallas_call x4, Pallas kernels, own(): pl.pallas_call(functools.partial(own_kernel, n, part, len(sources)), out_...  8.22 us
    pallas_call x1, Pallas kernels, local(): pl.pallas_call(functools.partial(routed_kernel, n, late_senders), out_sha...  3.55 us
    pallas_call x1, Pallas kernels, local(): pl.pallas_call(functools.partial(expert_kernel, n, len(pieces)), out_shap...  2.82 us
    pallas_call x1, Pallas kernels, local(): pl.pallas_call(functools.partial(select_kernel, planes), out_shape=[jax.S...  2.21 us
    pallas_call x1, Pallas kernels, local(): pl.pallas_call(functools.partial(combine_kernel, planes), out_shape=jax.S...  1.88 us
    pallas_call x1, Pallas kernels, local(): pl.pallas_call(functools.partial(collect_kernel, n, early_senders), out_s...  1.64 us
  transfers between devices with their start and end apart: 20, of which 10 were waited for; matrix products, arithmetic and copies ran while one was open for 0% of the time, Pallas kernels for 16%

profile of v4, /device:TPU:0, one launch (start us, length us, event | category | flops | bytes accessed | tf_op | source)
XLA Modules:
  0.0 76.7 jit_solution(3599008171527964600)
XLA Ops:
  0.0 1.0 %pack.1.refs_0_ = bf16[144,512]{1,0:T(8,128)(2,1)S(1)} custom-call(s32[1,128]{1,0:T(1,128)} %bitcast.9, bf16[128,256]{1,0:T(8,128)(2,1)} %keys_ref.1, bf16[128,256]{1,0:T(8,128)(2,1)} %values_ref.1), custom_call_target="tpu_custom_call" | custom-call | tf_op jit(solution)/shard_map/pack/pallas_call | solution.py:409
  1.0 3.1 %collective-permute-start = (bf16[144,512]{1,0:T(8,128)(2,1)S(1)}, bf16[144,512]{1,0:T(8,128)(2,1)S(1)}, u32[]{:S(2)}, u32[]{:S(2)}) collective-permute-start(bf16[144,512]{1,0:T(8,128)(2,1)S(1)} %pack.1.refs_0_), channel_id=1, source_target_pairs={{0,4},{1,5},{2,6},{3,7},{4,8},{5,9},{6,10},{7,11},{8,12},{9,13},{1... | collective-permute-start | bytes 442376 | tf_op jit(solution)/shard_map/ppermute | solution.py:424
  4.1 0.7 collective-permute-start.2
  4.7 2.7 %collective-permute-start.1 = (bf16[144,512]{1,0:T(8,128)(2,1)S(1)}, bf16[144,512]{1,0:T(8,128)(2,1)S(1)}, u32[]{:S(2)}, u32[]{:S(2)}) collective-permute-start(bf16[144,512]{1,0:T(8,128)(2,1)S(1)} %pack.1.refs_0_), channel_id=1, source_target_pairs={{0,8},{1,9},{2,10},{3,11},{4,12},{5,13},{6,14},{7,15},{8,0},{9,1},... | collective-permute-start | bytes 442376 | tf_op jit(solution)/shard_map/ppermute | solution.py:424
  7.4 2.2 %select.1 = (bf16[2,256,512]{2,1,0:T(8,128)(2,1)S(1)}, f32[32,4096]{1,0:T(8,128)S(1)}, f32[8,512]{1,0:T(8,128)S(1)}) custom-call(s32[1]{0:T(128)} %bitcast.pos_ref, s32[4,128]{1,0:T(4,128)} %bitcast.5, s32[1,128]{1,0:T(1,128)} %bitcast.10, bf16[128,4096]{1,0:T(8,128)(2,1)} %q_ref.7, bf16[128,4096]{1,0:T(8,128)(2,1)} %x_ref.7), custom_call_target="tpu_custom_call" | custom-call | tf_op jit(solution)/shard_map/select/pallas_call | solution.py:433
  9.6 1.3 %collective-permute-done.refs_1_ = bf16[144,512]{1,0:T(8,128)(2,1)S(1)} collective-permute-done((bf16[144,512]{1,0:T(8,128)(2,1)S(1)}, bf16[144,512]{1,0:T(8,128)(2,1)S(1)}, u32[]{:S(2)}, u32[]{:S(2)}) %collective-permute-start) | collective-permute-done | bytes 147488 | tf_op jit(solution)/shard_map/ppermute | solution.py:424
  10.9 0.7 collective-permute-start.3
  11.5 0.0 collective-permute-done.2.refs_0_
  11.5 4.7 %collective-permute-done.1.refs_2_ = bf16[144,512]{1,0:T(8,128)(2,1)S(1)} collective-permute-done((bf16[144,512]{1,0:T(8,128)(2,1)S(1)}, bf16[144,512]{1,0:T(8,128)(2,1)S(1)}, u32[]{:S(2)}, u32[]{:S(2)}) %collective-permute-start.1) | collective-permute-done | bytes 147488 | tf_op jit(solution)/shard_map/ppermute | solution.py:424
  16.3 0.1 collective-permute-start.5
  16.4 4.7 %collective-permute-start.4 = (bf16[144,512]{1,0:T(8,128)(2,1)S(1)}, bf16[144,512]{1,0:T(8,128)(2,1)S(1)}, u32[]{:S(2)}, u32[]{:S(2)}) collective-permute-start(bf16[144,512]{1,0:T(8,128)(2,1)S(1)} %broadcast_select_fusion), channel_id=1, source_target_pairs={{0,2},{1,3},{2,0},{3,1},{4,6},{5,7},{6,4},{7,5},{8,10},{9,11},{10,... | collective-permute-start | bytes 442376 | tf_op jit(solution)/shard_map/ppermute | solution.py:424
  21.2 0.7 collective-permute-start.6
  21.8 0.0 collective-permute-done.5.refs_4_
  21.8 1.6 %collect.1._ = bf16[16,144,512]{2,1,0:T(8,128)(2,1)S(1)} custom-call(s32[1]{0:T(128)} %bitcast.pos_ref, bf16[144,512]{1,0:T(8,128)(2,1)S(1)} %pack.1.refs_0_, bf16[144,512]{1,0:T(8,128)(2,1)S(1)} %collective-permute-done.refs_1_, bf16[144,512]{1,0:T(8,128)(2,1)S(1)} %collective-permute-done.1.refs_2_, bf16[144,512]{1,0:T(8,128)(2,1)S(1)} %collective-permute-done.3.refs_3_, ...), custom_call_target="tpu_custom_call" | custom-call | bytes 1000 | tf_op jit(solution)/shard_map/collect/pallas_call | solution.py:479
  23.5 2.2 %collective-permute-done.4.refs_2_ = bf16[144,512]{1,0:T(8,128)(2,1)S(1)} collective-permute-done((bf16[144,512]{1,0:T(8,128)(2,1)S(1)}, bf16[144,512]{1,0:T(8,128)(2,1)S(1)}, u32[]{:S(2)}, u32[]{:S(2)}) %collective-permute-start.4) | collective-permute-done | bytes 147488 | tf_op jit(solution)/shard_map/ppermute | solution.py:424
  25.7 0.0 copy-start
  25.7 0.0 copy-start.1
  25.7 0.1 collective-permute-start.7
  25.8 1.8 %collective-permute-done.7.refs_3_ = bf16[432,512]{1,0:T(8,128)(2,1)S(1)} collective-permute-done((bf16[432,512]{1,0:T(8,128)(2,1)S(1)}, bf16[432,512]{1,0:T(8,128)(2,1)S(1)}, u32[]{:S(2)}, u32[]{:S(2)}) %collective-permute-start.7) | collective-permute-done | bytes 442400 | tf_op jit(solution)/shard_map/ppermute | solution.py:424
  27.6 3.6 %routed.1 = (bf16[24,1024]{1,0:T(8,128)(2,1)S(1)}, bf16[24,1024]{1,0:T(8,128)(2,1)S(1)}, bf16[24,1024]{1,0:T(8,128)(2,1)S(1)}, bf16[24,1024]{1,0:T(8,128)(2,1)S(1)}, bf16[16,144,512]{2,1,0:T(8,128)(2,1)S(1)}) custom-call(s32[1]{0:T(128)} %bitcast.pos_ref, f32[1,4096]{1,0:T(1,128)} %bitcast.8, ...), custom_call_target="tpu_custom_call", output_to_operand_aliasing={{4}: (5, {})} | custom-call | tf_op jit(solution)/shard_map/routed/pallas_call | solution.py:493
  31.1 2.5 %collective-permute-start.8 = (bf16[24,1024]{1,0:T(8,128)(2,1)S(1)}, bf16[24,1024]{1,0:T(8,128)(2,1)S(1)}, u32[]{:S(2)}, u32[]{:S(2)}) collective-permute-start(bf16[24,1024]{1,0:T(8,128)(2,1)S(1)} %get-tuple-element.54), channel_id=1, source_target_pairs={{0,4},{1,5},{2,6},{3,7},{4,8},{5,9},{6,10},{7,11},{8,12},{9,13},{1... | collective-permute-start | bytes 147464 | tf_op jit(solution)/shard_map/ppermute | solution.py:424
  33.7 6.8 %collective-permute-start.9 = (bf16[24,1024]{1,0:T(8,128)(2,1)S(1)}, bf16[24,1024]{1,0:T(8,128)(2,1)S(1)}, u32[]{:S(2)}, u32[]{:S(2)}) collective-permute-start(bf16[24,1024]{1,0:T(8,128)(2,1)S(1)} %get-tuple-element.55), channel_id=1, source_target_pairs={{0,8},{1,9},{2,10},{3,11},{4,12},{5,13},{6,14},{7,15},{8,0},{9,1},... | collective-permute-start | bytes 147464 | tf_op jit(solution)/shard_map/ppermute | solution.py:424
  40.4 2.8 %collective-permute-start.10 = (bf16[24,1024]{1,0:T(8,128)(2,1)S(1)}, bf16[24,1024]{1,0:T(8,128)(2,1)S(1)}, u32[]{:S(2)}, u32[]{:S(2)}) collective-permute-start(bf16[24,1024]{1,0:T(8,128)(2,1)S(1)} %get-tuple-element.56), channel_id=1, source_target_pairs={{0,12},{1,13},{2,14},{3,15},{4,0},{5,1},{6,2},{7,3},{8,4},{9,5},{1... | collective-permute-start | bytes 147464 | tf_op jit(solution)/shard_map/ppermute | solution.py:424
  43.3 1.3 %collective-permute-start.11 = (bf16[24,1024]{1,0:T(8,128)(2,1)S(1)}, bf16[24,1024]{1,0:T(8,128)(2,1)S(1)}, u32[]{:S(2)}, u32[]{:S(2)}) collective-permute-start(bf16[24,1024]{1,0:T(8,128)(2,1)S(1)} %get-tuple-element.50._.refs_0_), channel_id=1, source_target_pairs={{0,2},{1,3},{2,0},{3,1},{4,6},{5,7},{6,4},{7,5},{8,10},{9,11},{10,... | collective-permute-start | bytes 147464 | tf_op jit(solution)/shard_map/ppermute | solution.py:424
  44.6 3.9 %own.4 = (f32[128,1024]{1,0:T(8,128)S(1)}, f32[8,128]{1,0:T(8,128)S(1)}, bf16[4096,384]{1,0:T(8,128)(2,1)S(1)}, bf16[4096,384]{1,0:T(8,128)(2,1)S(1)}, bf16[384,4096]{1,0:T(8,128)(2,1)S(1)}) custom-call(s32[1]{0:T(128)} %bitcast.pos_ref, bf16[16,144,512]{2,1,0:T(8,128)(2,1)S(1)} %get-tuple-element.49.held, bf16[128,4096]{1,0:T(8,128)(2,1)S(1)} %copy-done, ...), custom_call_target="tpu_custom_call" | custom-call | flops 2000000000 | bytes 8000000 | tf_op jit(solution)/shard_map/own/pallas_call | solution.py:514
  48.5 0.0 collective-permute-done.10
  48.5 0.0 collective-permute-done.11.refs_2_
  48.5 0.1 collective-permute-start.13
  48.6 0.8 %collective-permute-start.12 = (bf16[72,1024]{1,0:T(8,128)(2,1)S(1)}, bf16[72,1024]{1,0:T(8,128)(2,1)S(1)}, u32[]{:S(2)}, u32[]{:S(2)}) collective-permute-start(bf16[72,1024]{1,0:T(8,128)(2,1)S(1)} %constant_dynamic-update-slice_fusion.refs_1_), channel_id=1, source_target_pairs={{0,2},{1,3},{2,0},{3,1},{4,6},{5,7},{6,4},{7,5},{8,10},{9,11},{10,... | collective-permute-start | bytes 442376 | tf_op jit(solution)/shard_map/ppermute | solution.py:424
  49.4 1.2 %own.5 = (f32[128,1024]{1,0:T(8,128)S(1)}, f32[8,128]{1,0:T(8,128)S(1)}) custom-call(s32[1]{0:T(128)} %bitcast.pos_ref, bf16[16,144,512]{2,1,0:T(8,128)(2,1)S(1)} %get-tuple-element.49.held, bf16[128,4096]{1,0:T(8,128)(2,1)S(1)} %copy-done, bf16[128,4096]{1,0:T(8,128)(2,1)S(1)} %copy-done.1, f32[8,128]{1,0:T(8,128)S(1)} %get-tuple-element.52._), custom_call_target="tpu_custom_call" | custom-call | flops 2000000000 | bytes 8000000 | tf_op jit(solution)/shard_map/own/pallas_call | solution.py:514
  50.6 4.2 %collective-permute-done.12.refs_3_ = bf16[72,1024]{1,0:T(8,128)(2,1)S(1)} collective-permute-done((bf16[72,1024]{1,0:T(8,128)(2,1)S(1)}, bf16[72,1024]{1,0:T(8,128)(2,1)S(1)}, u32[]{:S(2)}, u32[]{:S(2)}) %collective-permute-start.12) | collective-permute-done | bytes 147488 | tf_op jit(solution)/shard_map/ppermute | solution.py:424
  54.9 0.0 collective-permute-done.13.refs_4_
  54.9 0.1 collective-permute-start.14
  55.0 1.4 %collective-permute-done.14.refs_5_ = bf16[96,1024]{1,0:T(8,128)(2,1)S(1)} collective-permute-done((bf16[96,1024]{1,0:T(8,128)(2,1)S(1)}, bf16[96,1024]{1,0:T(8,128)(2,1)S(1)}, u32[]{:S(2)}, u32[]{:S(2)}) %collective-permute-start.14) | collective-permute-done | bytes 196640 | tf_op jit(solution)/shard_map/ppermute | solution.py:424
  56.4 2.8 %expert.1 = (bf16[192,1024]{1,0:T(8,128)(2,1)S(1)}, bf16[192,1024]{1,0:T(8,128)(2,1)S(1)}) custom-call(bf16[24,1024]{1,0:T(8,128)(2,1)S(1)} %get-tuple-element.50._.refs_0_, bf16[72,1024]{1,0:T(8,128)(2,1)S(1)} %constant_dynamic-update-slice_fusion.refs_1_, bf16[24,1024]{1,0:T(8,128)(2,1)S(1)} %collective-permute-done.11.refs_2_, ...), custom_call_target="tpu_custom_call" | custom-call | flops 1200000000 | bytes 12000000 | tf_op jit(solution)/shard_map/expert/pallas_call | solution.py:557
  59.2 0.2 collective-permute-start.15
  59.4 1.6 %collective-permute-done.15 = bf16[192,1024]{1,0:T(8,128)(2,1)S(1)} collective-permute-done((bf16[192,1024]{1,0:T(8,128)(2,1)S(1)}, bf16[192,1024]{1,0:T(8,128)(2,1)S(1)}, u32[]{:S(2)}, u32[]{:S(2)}) %collective-permute-start.15) | collective-permute-done | bytes 393248 | tf_op jit(solution)/shard_map/ppermute | solution.py:424
  61.0 0.1 convert_add_fusion
  61.2 0.8 %collective-permute-start.16 = (bf16[96,1024]{1,0:T(8,128)(2,1)S(1)}, bf16[96,1024]{1,0:T(8,128)(2,1)S(1)}, u32[]{:S(2)}, u32[]{:S(2)}) collective-permute-start(bf16[96,1024]{1,0:T(8,128)(2,1)S(1)} %slice.35), channel_id=1, source_target_pairs={{0,2},{1,3},{2,0},{3,1},{4,6},{5,7},{6,4},{7,5},{8,10},{9,11},{10,... | collective-permute-start | bytes 589832 | tf_op jit(solution)/shard_map/ppermute | solution.py:424
  62.0 1.6 %own.7 = (f32[128,1024]{1,0:T(8,128)S(1)}, f32[8,128]{1,0:T(8,128)}) custom-call(s32[1]{0:T(128)} %bitcast.pos_ref, bf16[16,144,512]{2,1,0:T(8,128)(2,1)S(1)} %get-tuple-element.49.held, bf16[128,4096]{1,0:T(8,128)(2,1)S(1)} %copy-done, bf16[128,4096]{1,0:T(8,128)(2,1)S(1)} %copy-done.1, bf16[192,1024]{1,0:T(8,128)(2,1)S(1)} %get-tuple-element.69._), custom_call_target="tpu_custom_call" | custom-call | flops 2000000000 | bytes 8000000 | tf_op jit(solution)/shard_map/own/pallas_call | solution.py:514
  63.6 4.6 %collective-permute-done.16 = bf16[96,1024]{1,0:T(8,128)(2,1)S(1)} collective-permute-done((bf16[96,1024]{1,0:T(8,128)(2,1)S(1)}, bf16[96,1024]{1,0:T(8,128)(2,1)S(1)}, u32[]{:S(2)}, u32[]{:S(2)}) %collective-permute-start.16) | collective-permute-done | bytes 196640 | tf_op jit(solution)/shard_map/ppermute | solution.py:424
  68.3 0.1 collective-permute-start.19
  68.3 1.2 %collective-permute-start.18 = (bf16[24,1024]{1,0:T(8,128)(2,1)S(1)}, bf16[24,1024]{1,0:T(8,128)(2,1)S(1)}, u32[]{:S(2)}, u32[]{:S(2)}) collective-permute-start(bf16[24,1024]{1,0:T(8,128)(2,1)S(1)} %get-tuple-element.74), channel_id=1, source_target_pairs={{0,8},{1,9},{2,10},{3,11},{4,12},{5,13},{6,14},{7,15},{8,0},{9,1},... | collective-permute-start | bytes 147464 | tf_op jit(solution)/shard_map/ppermute | solution.py:424
  69.6 2.6 %collective-permute-start.17 = (bf16[24,1024]{1,0:T(8,128)(2,1)S(1)}, bf16[24,1024]{1,0:T(8,128)(2,1)S(1)}, u32[]{:S(2)}, u32[]{:S(2)}) collective-permute-start(bf16[24,1024]{1,0:T(8,128)(2,1)S(1)} %get-tuple-element.75), channel_id=1, source_target_pairs={{0,12},{1,13},{2,14},{3,15},{4,0},{5,1},{6,2},{7,3},{8,4},{9,5},{1... | collective-permute-start | bytes 147464 | tf_op jit(solution)/shard_map/ppermute | solution.py:424
  72.1 1.6 %own.6 = (f32[128,1024]{1,0:T(8,128)S(1)}, f32[8,128]{1,0:T(8,128)}) custom-call(s32[1]{0:T(128)} %bitcast.pos_ref, bf16[16,144,512]{2,1,0:T(8,128)(2,1)S(1)} %get-tuple-element.49.held, bf16[128,4096]{1,0:T(8,128)(2,1)S(1)} %copy-done, bf16[128,4096]{1,0:T(8,128)(2,1)S(1)} %copy-done.1, bf16[192,1024]{1,0:T(8,128)(2,1)S(1)} %get-tuple-element.69._), custom_call_target="tpu_custom_call" | custom-call | flops 2000000000 | bytes 8000000 | tf_op jit(solution)/shard_map/own/pallas_call | solution.py:514
  73.7 0.6 collective-permute-done.19.refs_7_
  74.3 0.5 collective-permute-done.17.refs_5_
  74.8 1.9 %combine.1 = bf16[128,4096]{1,0:T(8,128)(2,1)} custom-call(s32[1]{0:T(128)} %bitcast.pos_ref, s32[4,128]{1,0:T(4,128)S(1)} %bitcast.6, f32[4,128]{1,0:T(4,128)S(1)} %bitcast.7, f32[128,1024]{1,0:T(8,128)S(1)} %get-tuple-element.51.refs_0_, f32[128,1024]{1,0:T(8,128)S(1)} %get-tuple-element.53.refs_1_, f32[128,1024]{1,0:T(8,128)S(1)} %get-tuple-element.70.refs_2_, ...), custom_call_target="tpu_custom_call" | custom-call | tf_op jit(solution)/shard_map/combine/pallas_call | solution.py:584
  (22 shorter events, 0.2 us)
Async XLA Ops:
  1.0 9.9 %collective-permute-start = (bf16[144,512]{1,0:T(8,128)(2,1)S(1)}, bf16[144,512]{1,0:T(8,128)(2,1)S(1)}, u32[]{:S(2)}, u32[]{:S(2)}) collective-permute-start(bf16[144,512]{1,0:T(8,128)(2,1)S(1)} %pack.1.refs_0_), channel_id=1, source_target_pairs={{0,4},{1,5},{2,6},{3,7},{4,8},{5,9},{6,10},{7,11},{8,12},{9,13},{1... | collective-permute-start | bytes 442376 | tf_op jit(solution)/shard_map/ppermute | solution.py:424
  4.1 7.5 %collective-permute-start.2 = (bf16[144,512]{1,0:T(8,128)(2,1)S(1)}, bf16[144,512]{1,0:T(8,128)(2,1)S(1)}, u32[]{:S(2)}, u32[]{:S(2)}) collective-permute-start(bf16[144,512]{1,0:T(8,128)(2,1)S(1)} %pack.1.refs_0_), channel_id=1, source_target_pairs={{0,0},{1,1},{2,14},{3,15},{4,4},{5,5},{6,2},{7,3},{8,8},{9,9},{10,... | collective-permute-start | bytes 442376 | tf_op jit(solution)/shard_map/ppermute | solution.py:424
  4.7 11.5 %collective-permute-start.1 = (bf16[144,512]{1,0:T(8,128)(2,1)S(1)}, bf16[144,512]{1,0:T(8,128)(2,1)S(1)}, u32[]{:S(2)}, u32[]{:S(2)}) collective-permute-start(bf16[144,512]{1,0:T(8,128)(2,1)S(1)} %pack.1.refs_0_), channel_id=1, source_target_pairs={{0,8},{1,9},{2,10},{3,11},{4,12},{5,13},{6,14},{7,15},{8,0},{9,1},... | collective-permute-start | bytes 442376 | tf_op jit(solution)/shard_map/ppermute | solution.py:424
  10.9 5.4 %collective-permute-start.3 = (bf16[144,512]{1,0:T(8,128)(2,1)S(1)}, bf16[144,512]{1,0:T(8,128)(2,1)S(1)}, u32[]{:S(2)}, u32[]{:S(2)}) collective-permute-start(bf16[144,512]{1,0:T(8,128)(2,1)S(1)} %collective-permute-done.refs_1_), channel_id=1, source_target_pairs={{0,0},{1,1},{2,2},{3,3},{4,6},{5,7},{6,4},{7,5},{8,10},{9,11},{10,... | collective-permute-start | bytes 442376 | tf_op jit(solution)/shard_map/ppermute | solution.py:424
  16.3 5.5 %collective-permute-start.5 = (bf16[576,512]{1,0:T(8,128)(2,1)S(1)}, bf16[576,512]{1,0:T(8,128)(2,1)S(1)}, u32[]{:S(2)}, u32[]{:S(2)}) collective-permute-start(bf16[576,512]{1,0:T(8,128)(2,1)S(1)} %pad_maximum_fusion), channel_id=1, source_target_pairs={{0,1},{1,0},{2,3},{3,2},{4,5},{5,4},{6,7},{7,6},{8,9},{9,8},{10,11... | collective-permute-start | bytes 1769480 | tf_op jit(solution)/shard_map/ppermute | solution.py:424
  16.4 9.2 %collective-permute-start.4 = (bf16[144,512]{1,0:T(8,128)(2,1)S(1)}, bf16[144,512]{1,0:T(8,128)(2,1)S(1)}, u32[]{:S(2)}, u32[]{:S(2)}) collective-permute-start(bf16[144,512]{1,0:T(8,128)(2,1)S(1)} %broadcast_select_fusion), channel_id=1, source_target_pairs={{0,2},{1,3},{2,0},{3,1},{4,6},{5,7},{6,4},{7,5},{8,10},{9,11},{10,... | collective-permute-start | bytes 442376 | tf_op jit(solution)/shard_map/ppermute | solution.py:424
  21.2 4.5 %collective-permute-start.6 = (bf16[144,512]{1,0:T(8,128)(2,1)S(1)}, bf16[144,512]{1,0:T(8,128)(2,1)S(1)}, u32[]{:S(2)}, u32[]{:S(2)}) collective-permute-start(bf16[144,512]{1,0:T(8,128)(2,1)S(1)} %collective-permute-done.1.refs_2_), channel_id=1, source_target_pairs={{0,0},{1,1},{2,2},{3,3},{4,4},{5,5},{6,6},{7,7},{8,10},{9,11},{10,... | collective-permute-start | bytes 442376 | tf_op jit(solution)/shard_map/ppermute | solution.py:424
  25.7 18.9 %copy-start = (bf16[128,4096]{1,0:T(8,128)(2,1)S(1)}, bf16[128,4096]{1,0:T(8,128)(2,1)}, u32[]{:S(2)}) copy-start(bf16[128,4096]{1,0:T(8,128)(2,1)} %q_ref.7) | copy-start | bytes 3145732
  25.7 18.9 %copy-start.1 = (bf16[128,4096]{1,0:T(8,128)(2,1)S(1)}, bf16[128,4096]{1,0:T(8,128)(2,1)}, u32[]{:S(2)}) copy-start(bf16[128,4096]{1,0:T(8,128)(2,1)} %x_ref.7) | copy-start | bytes 3145732
  25.7 1.9 %collective-permute-start.7 = (bf16[432,512]{1,0:T(8,128)(2,1)S(1)}, bf16[432,512]{1,0:T(8,128)(2,1)S(1)}, u32[]{:S(2)}, u32[]{:S(2)}) collective-permute-start(bf16[432,512]{1,0:T(8,128)(2,1)S(1)} %pad_maximum_fusion.1), channel_id=1, source_target_pairs={{0,1},{1,0},{2,3},{3,2},{4,5},{5,4},{6,7},{7,6},{8,9},{9,8},{10,11... | collective-permute-start | bytes 1327112 | tf_op jit(solution)/shard_map/ppermute | solution.py:424
  31.1 17.3 %collective-permute-start.8 = (bf16[24,1024]{1,0:T(8,128)(2,1)S(1)}, bf16[24,1024]{1,0:T(8,128)(2,1)S(1)}, u32[]{:S(2)}, u32[]{:S(2)}) collective-permute-start(bf16[24,1024]{1,0:T(8,128)(2,1)S(1)} %get-tuple-element.54), channel_id=1, source_target_pairs={{0,4},{1,5},{2,6},{3,7},{4,8},{5,9},{6,10},{7,11},{8,12},{9,13},{1... | collective-permute-start | bytes 147464 | tf_op jit(solution)/shard_map/ppermute | solution.py:424
  33.7 14.8 %collective-permute-start.9 = (bf16[24,1024]{1,0:T(8,128)(2,1)S(1)}, bf16[24,1024]{1,0:T(8,128)(2,1)S(1)}, u32[]{:S(2)}, u32[]{:S(2)}) collective-permute-start(bf16[24,1024]{1,0:T(8,128)(2,1)S(1)} %get-tuple-element.55), channel_id=1, source_target_pairs={{0,8},{1,9},{2,10},{3,11},{4,12},{5,13},{6,14},{7,15},{8,0},{9,1},... | collective-permute-start | bytes 147464 | tf_op jit(solution)/shard_map/ppermute | solution.py:424
  40.4 8.0 %collective-permute-start.10 = (bf16[24,1024]{1,0:T(8,128)(2,1)S(1)}, bf16[24,1024]{1,0:T(8,128)(2,1)S(1)}, u32[]{:S(2)}, u32[]{:S(2)}) collective-permute-start(bf16[24,1024]{1,0:T(8,128)(2,1)S(1)} %get-tuple-element.56), channel_id=1, source_target_pairs={{0,12},{1,13},{2,14},{3,15},{4,0},{5,1},{6,2},{7,3},{8,4},{9,5},{1... | collective-permute-start | bytes 147464 | tf_op jit(solution)/shard_map/ppermute | solution.py:424
  43.3 5.2 %collective-permute-start.11 = (bf16[24,1024]{1,0:T(8,128)(2,1)S(1)}, bf16[24,1024]{1,0:T(8,128)(2,1)S(1)}, u32[]{:S(2)}, u32[]{:S(2)}) collective-permute-start(bf16[24,1024]{1,0:T(8,128)(2,1)S(1)} %get-tuple-element.50._.refs_0_), channel_id=1, source_target_pairs={{0,2},{1,3},{2,0},{3,1},{4,6},{5,7},{6,4},{7,5},{8,10},{9,11},{10,... | collective-permute-start | bytes 147464 | tf_op jit(solution)/shard_map/ppermute | solution.py:424
  48.5 6.4 %collective-permute-start.13 = (bf16[96,1024]{1,0:T(8,128)(2,1)S(1)}, bf16[96,1024]{1,0:T(8,128)(2,1)S(1)}, u32[]{:S(2)}, u32[]{:S(2)}) collective-permute-start(bf16[96,1024]{1,0:T(8,128)(2,1)S(1)} %pad_maximum_fusion.2), channel_id=1, source_target_pairs={{0,1},{1,0},{2,3},{3,2},{4,5},{5,4},{6,7},{7,6},{8,9},{9,8},{10,11... | collective-permute-start | bytes 589832 | tf_op jit(solution)/shard_map/ppermute | solution.py:424
  48.6 6.3 %collective-permute-start.12 = (bf16[72,1024]{1,0:T(8,128)(2,1)S(1)}, bf16[72,1024]{1,0:T(8,128)(2,1)S(1)}, u32[]{:S(2)}, u32[]{:S(2)}) collective-permute-start(bf16[72,1024]{1,0:T(8,128)(2,1)S(1)} %constant_dynamic-update-slice_fusion.refs_1_), channel_id=1, source_target_pairs={{0,2},{1,3},{2,0},{3,1},{4,6},{5,7},{6,4},{7,5},{8,10},{9,11},{10,... | collective-permute-start | bytes 442376 | tf_op jit(solution)/shard_map/ppermute | solution.py:424
  54.9 1.5 %collective-permute-start.14 = (bf16[96,1024]{1,0:T(8,128)(2,1)S(1)}, bf16[96,1024]{1,0:T(8,128)(2,1)S(1)}, u32[]{:S(2)}, u32[]{:S(2)}) collective-permute-start(bf16[96,1024]{1,0:T(8,128)(2,1)S(1)} %pad_maximum_fusion.3), channel_id=1, source_target_pairs={{0,1},{1,0},{2,3},{3,2},{4,5},{5,4},{6,7},{7,6},{8,9},{9,8},{10,11... | collective-permute-start | bytes 589832 | tf_op jit(solution)/shard_map/ppermute | solution.py:424
  59.2 1.8 %collective-permute-start.15 = (bf16[192,1024]{1,0:T(8,128)(2,1)S(1)}, bf16[192,1024]{1,0:T(8,128)(2,1)S(1)}, u32[]{:S(2)}, u32[]{:S(2)}) collective-permute-start(bf16[192,1024]{1,0:T(8,128)(2,1)S(1)} %get-tuple-element.72), channel_id=1, source_target_pairs={{0,1},{1,0},{2,3},{3,2},{4,5},{5,4},{6,7},{7,6},{8,9},{9,8},{10,11... | collective-permute-start | bytes 1179656 | tf_op jit(solution)/shard_map/ppermute | solution.py:424
  61.2 7.0 %collective-permute-start.16 = (bf16[96,1024]{1,0:T(8,128)(2,1)S(1)}, bf16[96,1024]{1,0:T(8,128)(2,1)S(1)}, u32[]{:S(2)}, u32[]{:S(2)}) collective-permute-start(bf16[96,1024]{1,0:T(8,128)(2,1)S(1)} %slice.35), channel_id=1, source_target_pairs={{0,2},{1,3},{2,0},{3,1},{4,6},{5,7},{6,4},{7,5},{8,10},{9,11},{10,... | collective-permute-start | bytes 589832 | tf_op jit(solution)/shard_map/ppermute | solution.py:424
  68.3 6.0 %collective-permute-start.19 = (bf16[24,1024]{1,0:T(8,128)(2,1)S(1)}, bf16[24,1024]{1,0:T(8,128)(2,1)S(1)}, u32[]{:S(2)}, u32[]{:S(2)}) collective-permute-start(bf16[24,1024]{1,0:T(8,128)(2,1)S(1)} %get-tuple-element.73), channel_id=1, source_target_pairs={{0,4},{1,5},{2,6},{3,7},{4,8},{5,9},{6,10},{7,11},{8,12},{9,13},{1... | collective-permute-start | bytes 147464 | tf_op jit(solution)/shard_map/ppermute | solution.py:424
  68.3 6.0 %collective-permute-start.18 = (bf16[24,1024]{1,0:T(8,128)(2,1)S(1)}, bf16[24,1024]{1,0:T(8,128)(2,1)S(1)}, u32[]{:S(2)}, u32[]{:S(2)}) collective-permute-start(bf16[24,1024]{1,0:T(8,128)(2,1)S(1)} %get-tuple-element.74), channel_id=1, source_target_pairs={{0,8},{1,9},{2,10},{3,11},{4,12},{5,13},{6,14},{7,15},{8,0},{9,1},... | collective-permute-start | bytes 147464 | tf_op jit(solution)/shard_map/ppermute | solution.py:424
  69.6 5.3 %copy-start.2 = (s32[128,4]{0,1:T(4,128)S(1)}, s32[128,4]{0,1:T(4,128)}, u32[]{:S(2)}) copy-start(s32[128,4]{0,1:T(4,128)} %param.17) | copy-start | bytes 6148
  69.6 5.3 %copy-start.3 = (f32[128,4]{0,1:T(4,128)S(1)}, f32[128,4]{0,1:T(4,128)}, u32[]{:S(2)}) copy-start(f32[128,4]{0,1:T(4,128)} %param.18) | copy-start | bytes 6148
  69.6 5.2 %collective-permute-start.17 = (bf16[24,1024]{1,0:T(8,128)(2,1)S(1)}, bf16[24,1024]{1,0:T(8,128)(2,1)S(1)}, u32[]{:S(2)}, u32[]{:S(2)}) collective-permute-start(bf16[24,1024]{1,0:T(8,128)(2,1)S(1)} %get-tuple-element.75), channel_id=1, source_target_pairs={{0,12},{1,13},{2,14},{3,15},{4,0},{5,1},{6,2},{7,3},{8,4},{9,5},{1... | collective-permute-start | bytes 147464 | tf_op jit(solution)/shard_map/ppermute | solution.py:424

commit v5 on v4

--- a/solution.py
+++ b/solution.py
@@ -102,18 +102,32 @@
 
 
 def select_kernel(planes, pos_ref, *refs):
-    sources, (qs_ref, xs_ref, facts_ref) = refs[:4], refs[4:7]
-    routes_ref, docs_ref, q_ref, x_ref, sems = refs[7:]
+    sources, (qs_ref, xs_ref, facts_ref, mix_ref, gather_ref, spread_ref) = refs[:5], refs[5:11]
+    routes_ref, docs_ref, q_ref, x_ref, gates_ref, sems = refs[11:]
     moves = [
         pltpu.make_async_copy(source, target, sems.at[i])
-        for i, (source, target) in enumerate(zip(sources, refs[7:11]))
+        for i, (source, target) in enumerate(zip(sources, refs[11:16]))
     ]
     for move in moves:
         move.start()
     for move in moves:
         move.wait()
     z = pos_ref[0] // SHARDS
-    members, ranks = slot_rows(routes_ref[...], [lax.rem(z + k, planes) for k in range(planes)])
+    experts = [lax.rem(z + k, planes) for k in range(planes)]
+    routes, gates = routes_ref[...], gates_ref[...]
+    members, ranks = slot_rows(routes, experts)
+    slot = lax.broadcasted_iota(jnp.int32, (SLOTS, TILE), 0).astype(F32)
+    mix = []
+    for k, e in enumerate(experts):
+        gate = jnp.sum(jnp.where(routes == e, gates, 0.0), axis=0, keepdims=True)
+        mix.append(jnp.where(ranks[k : k + 1] == slot, gate, 0.0))
+    mix = jnp.concatenate(mix, axis=0).T
+    mix_high = mix.astype(BF16)
+    mix_ref[:, : planes * SLOTS] = mix_high
+    mix_ref[:, planes * SLOTS :] = (mix - mix_high.astype(F32)).astype(BF16)
+    size = gather_ref.shape[0]
+    gather_ref[...] = one_hot(travel_row(numbers((size, 1), 0), size // PIECE, CAP), size)
+    spread_ref[...] = one_hot(travel_row(numbers((1, size), 1), size // PIECE, CAP), size)
     docs = docs_ref[...].astype(F32)
     lane_slot = (lax.broadcasted_iota(jnp.int32, (TILE, TILE), 0) % SLOTS).astype(F32)
     token = lax.broadcasted_iota(jnp.int32, (1, TILE), 1).astype(F32)
@@ -184,6 +198,11 @@
     return lax.fori_loop(clear, last, lambda kb, carried: step(kb, carried, False), state)
 
 
+def by_kv_head(heads):
+    groups = [(h, [a for a in heads if a // GROUP == h]) for h in range(KV_HEADS)]
+    return [(h, own) for h, own in groups if own]
+
+
 def keys_of(held, kb, h):
     keys = jnp.concatenate(
         [held[2 * kb + t, 0:TILE, h * HEAD : (h + 1) * HEAD] for t in range(2)], axis=0
@@ -199,29 +218,26 @@
     return jnp.concatenate([values, jnp.ones((EXTRA, KEYS), BF16)], axis=0)
 
 
-def flash(pos, held, q_ref, kv_heads, acc_ref, bias_ref, place, first):
-    lanes = place.shape[1]
-    chains = range(len(kv_heads))
-    for i in chains:
-        acc_ref[i] = jnp.zeros((HEAD + EXTRA, lanes), F32)
+def flash(pos, held, chains, bias_ref, place, first):
+    for _, _, acc in chains:
+        acc[...] = jnp.zeros(acc.shape, F32)
 
     def step(kb, tops, masked):
         out = []
-        for i in chains:
-            scores = dot(keys_of(held, kb, kv_heads[i]), q_ref[i])
+        for (queries, h, acc), old in zip(chains, tops):
+            scores = dot(keys_of(held, kb, h), queries[...])
             if masked:
-                scores = scores + bias_ref[...]
-            top = jnp.maximum(tops[i], jnp.max(scores, axis=0, keepdims=True))
+                copies = scores.shape[1] // bias_ref.shape[1]
+                scores = scores + jnp.concatenate([bias_ref[...]] * copies, axis=1)
+            top = jnp.maximum(old, jnp.max(scores, axis=0, keepdims=True))
             weights = jnp.exp2(scores - top).astype(BF16)
-            acc_ref[i] = acc_ref[i] * jnp.exp2(tops[i] - top) + dot(
-                values_of(held, kb, kv_heads[i]), weights
-            )
+            acc[...] = acc[...] * jnp.exp2(old - top) + dot(values_of(held, kb, h), weights)
             out.append(top)
         return tuple(out)
 
-    tops = tuple(jnp.full((1, lanes), LOW, F32) for _ in chains)
+    tops = tuple(jnp.full((1, acc.shape[1]), LOW, F32) for _, _, acc in chains)
     key_steps(pos, place, first, bias_ref, step, tops)
-    return [(acc_ref[i, 0:HEAD] / acc_ref[i, HEAD : HEAD + 1]).T for i in chains]
+    return [(acc[0:HEAD, :] / acc[HEAD : HEAD + 1, :]).T for _, _, acc in chains]
 
 
 def place_pieces(n, senders, pos, pieces, held, sems):
@@ -248,8 +264,8 @@
 def routed_kernel(n, senders, pos_ref, gain_ref, qs_ref, xs_ref, facts_ref, _, *refs):
     planes = n // SHARDS
     count = len(senders)
-    pieces, outs, held = refs[:4], refs[4 : 4 + planes], refs[4 + planes]
-    acc, bias, q_scr, state, gain, sems = refs[5 + planes :]
+    pieces, outs, held = refs[:3], refs[3 : 3 + planes], refs[3 + planes]
+    acc, bias, q_scr, state, gain, sems = refs[4 + planes :]
     pos = pos_ref[0]
     copies = place_pieces(n, senders, pos, pieces, held, sems)
     copies.append(pltpu.make_async_copy(gain_ref, gain, sems.at[count]))
@@ -265,9 +281,7 @@
         done = flash(
             pos,
             held,
-            q_scr,
-            range(KV_HEADS),
-            acc,
+            [(q_scr.at[h], h, acc.at[h]) for h in range(KV_HEADS)],
             bias,
             facts_ref[0:1, at] + base,
             starts_of(facts_ref[1:2, at], starts),
@@ -294,14 +308,12 @@
 def expert_kernel(n, count, *refs):
     pieces = refs[:count]
     wg, wu, wd = refs[count : count + 3]
-    keep_ref, send_ref, rows = refs[count + 4 :]
+    gather, spread, _, keep_ref, send_ref, rows = refs[count + 3 :]
     step = pieces[0].shape[1]
     senders = min(n, 16)
     size, total = senders * PIECE, n * PIECE
     half = total // 2
     kept = senders * CAP
-    gather = one_hot(travel_row(numbers((size, 1), 0), senders, CAP), size)
-    spread = one_hot(travel_row(numbers((1, size), 1), senders, CAP), size)
     for at in range(0, total, size):
         parts, first = [], 0
         for piece in pieces:
@@ -309,14 +321,14 @@
             if low < high:
                 parts.append(piece[low:high, :].astype(F32))
             first += piece.shape[0]
-        came = dot(gather, jnp.concatenate(parts, axis=0).astype(BF16)).astype(BF16)
+        came = dot(gather[...], jnp.concatenate(parts, axis=0).astype(BF16)).astype(BF16)
         for q in range(CUT):
             rows[:, q * step : (q + 1) * step] = came[q * kept : (q + 1) * kept]
         gate = dot(rows[...], wg[...])
         up = dot(rows[...], wu[...])
         act = (gate / (1.0 + jnp.exp(-gate)) * up).astype(BF16)
         parts = [dot(act, wd[:, q * step : (q + 1) * step]).astype(BF16) for q in range(CUT)]
-        out = dot(spread, jnp.concatenate(parts, axis=0)).astype(BF16)
+        out = dot(spread[...], jnp.concatenate(parts, axis=0)).astype(BF16)
         if size > half:
             keep_ref[...] = out[:half]
             send_ref[...] = out[half:]
@@ -326,10 +338,10 @@
             send_ref[at - half : at - half + size] = out
 
 
-def own_kernel(n, part, loads, pos_ref, held, q_ref, x_ref, _, *refs):
+def own_kernel(n, heads, loads, pos_ref, held, q_ref, x_ref, _, *refs):
     sources, (h_ref, done_ref) = refs[:loads], refs[loads : loads + 2]
     targets = refs[loads + 2 : 2 * loads + 2]
-    acc, bias, qt, sems = refs[2 * loads + 2 :]
+    bias, sems, *scratch = refs[2 * loads + 2 :]
     moves = [
         pltpu.make_async_copy(source.at[0], target, sems.at[i])
         for i, (source, target) in enumerate(zip(sources, targets))
@@ -341,47 +353,51 @@
     starts = doc_starts(n, pos, held)
     first = starts_of(held[pos, TILE:KV_ROWS, 0:HEAD].astype(F32)[0:1], starts)
     place = (pos * TILE + lax.broadcasted_iota(jnp.int32, (1, TILE), 1)).astype(F32)
-    for a in range(8):
-        terms = two_terms(q_ref[:, a * HEAD : (a + 1) * HEAD].astype(F32).T)
-        for i, term in enumerate(terms):
-            qt[0, i * HEAD : (i + 1) * HEAD, a * TILE : (a + 1) * TILE] = term
-    place = jnp.concatenate([place] * 8, axis=1)
-    first = jnp.concatenate([first] * 8, axis=1)
-    (done,) = flash(pos, held, qt, [part // 2], acc, bias, place, first)
-    for a in range(8):
-        lane = a * HEAD
-        h_ref[:, lane : lane + HEAD] = (
-            x_ref[:, lane : lane + HEAD].astype(F32) + done[a * TILE : (a + 1) * TILE]
+    chains = []
+    for i, (h, own) in enumerate(by_kv_head(heads)):
+        queries, acc = scratch[2 * i : 2 * i + 2]
+        chains.append((queries, h, acc))
+        for j, a in enumerate(own):
+            terms = two_terms(q_ref[:, a * HEAD : (a + 1) * HEAD].astype(F32).T)
+            for t, term in enumerate(terms):
+                queries[t * HEAD : (t + 1) * HEAD, j * TILE : (j + 1) * TILE] = term
+    done = jnp.concatenate(flash(pos, held, chains, bias, place, first), axis=0)
+    for j, a in enumerate(heads):
+        h_ref[:, j * HEAD : (j + 1) * HEAD] = (
+            x_ref[:, a * HEAD : (a + 1) * HEAD].astype(F32) + done[j * TILE : (j + 1) * TILE]
         )
     for move in moves:
         move.wait()
 
 
-def combine_kernel(planes, pos_ref, routes_ref, gates_ref, *refs):
-    halves, parts, out_ref = refs[:4], refs[4 : 4 + planes], refs[4 + planes]
-    z = pos_ref[0] // SHARDS
-    routes = routes_ref[...]
-    gates = gates_ref[...]
-    experts = [lax.rem(z + k, planes) for k in range(planes)]
-    members, ranks = slot_rows(routes, experts)
-    slot = lax.broadcasted_iota(jnp.int32, (SLOTS, TILE), 0).astype(F32)
-    mix = []
-    for k, e in enumerate(experts):
-        gate = jnp.sum(jnp.where(routes == e, gates, 0.0), axis=0, keepdims=True)
-        mix.append(jnp.where(ranks[k : k + 1] == slot, gate, 0.0))
-    mix = jnp.concatenate(mix, axis=0).T
-    mix_high = mix.astype(BF16)
-    mix_low = (mix - mix_high.astype(F32)).astype(BF16)
-    size = halves[0].shape[1]
+def combine_kernel(planes, widths, mix_ref, *refs):
+    count = len(widths)
+    halves, parts, out_ref = refs[:count], refs[count : count + planes], refs[count + planes]
+    buffer, sems = refs[count + planes + 1 :]
     slots = planes * SLOTS
     came = jnp.concatenate([p[...].astype(F32) for p in parts], axis=0).astype(BF16)
     order = one_hot(travel_row(numbers((CUT * slots, 1), 0), planes, SLOTS), planes * PIECE)
     came = dot(order, came).astype(BF16)
-    for i, h in enumerate(halves):
-        rows = came[i * slots : (i + 1) * slots]
-        out_ref[:, i * size : (i + 1) * size] = (
-            h[...] + dot(mix_high, rows) + dot(mix_low, rows)
-        ).astype(BF16)
+    size = buffer.shape[1] // CUT
+    moves = []
+    for q in range(CUT):
+        rows = came[q * slots : (q + 1) * slots]
+        part = dot(mix_ref[...], jnp.concatenate([rows, rows], axis=0))
+        at = 0
+        for h, width in zip(halves, widths):
+            low, high = max(at, q * size), min(at + width, (q + 1) * size)
+            if low < high:
+                buffer[:, low:high] = (
+                    h[:, low - at : high - at] + part[:, low - q * size : high - q * size]
+                ).astype(BF16)
+            at += width
+        columns = pl.ds(q * size, size)
+        moves.append(
+            pltpu.make_async_copy(buffer.at[:, columns], out_ref.at[:, columns], sems.at[q])
+        )
+        moves[-1].start()
+    for move in moves:
+        move.wait()
 
 
 def pin(x):
@@ -430,25 +446,30 @@
         return any(0 <= gap <= back for gap in gaps)
 
     far = max(k for k in range(planes) if any(needed(k, a, b) for a in (0, 1) for b in (0, 1)))
-    q_rows, x_rows, facts = pl.pallas_call(
+    size = min(n, 16) * PIECE
+    q_rows, x_rows, facts, mix, gather, spread = pl.pallas_call(
         functools.partial(select_kernel, planes),
         out_shape=[
             jax.ShapeDtypeStruct((KV_HEADS, 2 * HEAD, planes * TILE), BF16),
             jax.ShapeDtypeStruct((planes * SLOTS, width), F32),
             jax.ShapeDtypeStruct((8, planes * TILE), F32),
+            jax.ShapeDtypeStruct((tokens, 2 * planes * SLOTS), BF16),
+            jax.ShapeDtypeStruct((size, size), BF16),
+            jax.ShapeDtypeStruct((size, size), BF16),
         ],
-        in_specs=[SMEM] + [HBM] * 4,
-        out_specs=[VMEM] * 3,
+        in_specs=[SMEM] + [HBM] * 5,
+        out_specs=[VMEM] * 6,
         scratch_shapes=[
             pltpu.VMEM(routes_t.shape, jnp.int32),
             pltpu.VMEM(docs.shape, jnp.int32),
             pltpu.VMEM(queries.shape, BF16),
             pltpu.VMEM(resid.shape, BF16),
-            pltpu.SemaphoreType.DMA((4,)),
+            pltpu.VMEM(gates_t.shape, F32),
+            pltpu.SemaphoreType.DMA((5,)),
         ],
         compiler_params=params(small),
         name="select",
-    )(pos, pin(routes_t), pin(docs), pin(queries), pin(resid))
+    )(pos, *map(pin, (routes_t, docs, queries, resid, gates_t)))
 
     flip_y = [(s, s ^ 2) for s in range(n)]
     flip_c = [(s, s ^ 1) for s in range(n)]
@@ -467,14 +488,14 @@
         across.append(move(along[k], [(s, s ^ 2 if s >= k * SHARDS else s) for s in range(n)]))
     odd = (pos[0] & 2) != 0
     final = move(jnp.where(odd, along[far], packed) if shared else along[far], flip_y)
-    early, late = along[:far] + across[:-1], [along[far], across[-1]]
-    sides = [(0, (k, k)) for k in range(far)] + [(1, (k, k)) for k in middle[:-1]]
-    late_sides = [(0, (far, far)), (1, (middle[-1],) * 2), (1, (far, 0 if shared else far))]
+    early, late = along + across[:-1], [across[-1]]
+    sides = [(0, (k, k)) for k in range(far + 1)] + [(1, (k, k)) for k in middle[:-1]]
+    late_sides = [(1, (middle[-1],) * 2), (1, (far, 0 if shared else far))]
     early.append(move(jnp.concatenate(early, axis=0), flip_c))
     early_senders = [(i, 0, 0, *side) for i, side in enumerate(sides)]
     early_senders += [(len(sides), i * KV_ROWS, 1, *side) for i, side in enumerate(sides)]
     late_senders = [(i, 0, 0, *side) for i, side in enumerate(late_sides)]
-    late_senders += [(3, i * KV_ROWS, 1, *side) for i, side in enumerate(late_sides)]
+    late_senders += [(2, i * KV_ROWS, 1, *side) for i, side in enumerate(late_sides)]
     held_shape = jax.ShapeDtypeStruct((n, KV_ROWS, 4 * HEAD), BF16)
     held = pl.pallas_call(
         functools.partial(collect_kernel, n, early_senders),
@@ -509,27 +530,25 @@
         name="routed",
     )(pos, pin(norm_gain.reshape(1, width)), q_rows, x_rows, facts, held, *late)
 
-    def own(part, after, *sources):
-        columns = pl.BlockSpec((tokens, 8 * HEAD), lambda i: (0, part))
+    def own(heads, after, *sources):
+        lanes = [len(own) * TILE for _, own in by_kv_head(heads)]
         return pl.pallas_call(
-            functools.partial(own_kernel, n, part, len(sources)),
+            functools.partial(own_kernel, n, heads, len(sources)),
             out_shape=[
-                jax.ShapeDtypeStruct((tokens, 8 * HEAD), F32),
+                jax.ShapeDtypeStruct((tokens, len(heads) * HEAD), F32),
                 jax.ShapeDtypeStruct((8, TILE), F32),
             ]
             + [jax.ShapeDtypeStruct(w.shape[1:], BF16) for w in sources],
-            grid=(1,),
-            in_specs=[SMEM, VMEM, columns, columns, ANY] + [HBM] * len(sources),
-            out_specs=[
-                pl.BlockSpec((tokens, 8 * HEAD), lambda i: (0, 0)),
-                pl.BlockSpec((8, TILE), lambda i: (0, 0)),
-            ]
-            + [VMEM] * len(sources),
-            scratch_shapes=[
-                pltpu.VMEM((1, HEAD + EXTRA, 8 * TILE), F32),
-                pltpu.VMEM((KEYS, 8 * TILE), F32),
-                pltpu.VMEM((1, 2 * HEAD, 8 * TILE), BF16),
-                pltpu.SemaphoreType.DMA((3,)),
+            in_specs=[SMEM, VMEM, VMEM, VMEM, ANY] + [HBM] * len(sources),
+            out_specs=[VMEM] * (2 + len(sources)),
+            scratch_shapes=[pltpu.VMEM((KEYS, TILE), F32), pltpu.SemaphoreType.DMA((3,))]
+            + [
+                shape
+                for count in lanes
+                for shape in (
+                    pltpu.VMEM((2 * HEAD, count), BF16),
+                    pltpu.VMEM((HEAD + EXTRA, count), F32),
+                )
             ],
             compiler_params=params(small),
             cost_estimate=pl.CostEstimate(
@@ -538,8 +557,8 @@
             name="own",
         )(pos, held, queries, resid, after, *map(pin, sources))
 
-    half0, done, *weights = own(0, sent[0], w_gate, w_up, w_down)
-    half1, late = own(1, done)
+    half0, done, *weights = own(range(10), sent[0], w_gate, w_up, w_down)
+    half1, late = own(range(10, 21), done)
     halves = [half0, half1]
 
     come = [
@@ -557,7 +576,7 @@
     keep, send = pl.pallas_call(
         functools.partial(expert_kernel, n, len(pieces)),
         out_shape=[half, half],
-        in_specs=[VMEM] * (len(pieces) + 3) + [ANY],
+        in_specs=[VMEM] * (len(pieces) + 5) + [ANY],
         out_specs=[VMEM, VMEM],
         scratch_shapes=[pltpu.VMEM((min(n, 16) * CAP, width), BF16)],
         compiler_params=params(16),
@@ -565,13 +584,15 @@
             flops=1_200_000_000, bytes_accessed=12_000_000, transcendentals=50_000
         ),
         name="expert",
-    )(*pieces, *weights, late)
-
-    halves += [own(part, keep)[0] for part in range(2, 4)]
+    )(*pieces, *weights, gather, spread, late)
+
+    half2, done = own(range(21, QUERY_HEADS), keep)
+    halves.append(half2)
 
     total = keep.astype(F32) + move(send, [(s, s ^ 1) for s in range(n)]).astype(F32)
     quarter = n * PIECE // 4
     other = move(total[quarter:].astype(BF16), [(s, s ^ 2) for s in range(n)])
+    other, done = lax.optimization_barrier((other, done))
     total = (total[:quarter] + other.astype(F32)).astype(BF16)
     parts = [total[:PIECE]]
     for k in range(1, planes):
@@ -581,14 +602,16 @@
             )
         )
 
+    widths = [h.shape[1] for h in halves]
     return pl.pallas_call(
-        functools.partial(combine_kernel, planes),
+        functools.partial(combine_kernel, planes, widths),
         out_shape=jax.ShapeDtypeStruct((tokens, width), BF16),
-        in_specs=[SMEM] + [VMEM] * (6 + planes),
-        out_specs=VMEM,
+        in_specs=[VMEM] * (1 + len(halves) + planes),
+        out_specs=HBM,
+        scratch_shapes=[pltpu.VMEM((tokens, width), BF16), pltpu.SemaphoreType.DMA((CUT,))],
         compiler_params=params(small),
         name="combine",
-    )(pos, routes_t, gates_t, *halves, *parts)
+    )(mix, *halves, *parts)
 
 
 def solution(mesh):

time: 76.5 us -> 75.4 us (0.986); the launches traced: 76.7 us -> 74.8 us
  Pallas kernels: 21.3 us -> 19.8 us
  starting transfers between devices: 31.9 us -> 30.9 us
    pallas_call x5 -> x4, Pallas kernels: 10.1 us -> 8.48 us  [the longest x3 7.1 us: own(): pl.pallas_call(functools.partial(own_kernel, n, heads, len(sources)), out...]
    ppermute x20, starting transfers between devices: 31.9 us -> 30.9 us  [move(): return lax.ppermute(value, 'expert', pairs)]
  transfers between devices with their start and end apart: 20 -> 20, of which waited for: 10 -> 9; matrix products, arithmetic and copies ran while one was open for 0% -> 0% of each run, Pallas kernels for 16% -> 16%
where the time goes in v5:
time: 75.4 us; the launch traced here: 74.8 us
  starting transfers between devices  30.9 us (41%)
  waiting for transfers between devices  23.4 us (31%)
  Pallas kernels  19.8 us (26%)
    ppermute x20, starting transfers between devices, move(): return lax.ppermute(value, 'expert', pairs)  30.9 us
    ppermute x20, waiting for transfers between devices, move(): return lax.ppermute(value, 'expert', pairs)  23.4 us
    pallas_call x3, Pallas kernels, own(): pl.pallas_call(functools.partial(own_kernel, n, heads, len(sources)), out...  7.1 us
    pallas_call x1, Pallas kernels, local(): pl.pallas_call(functools.partial(routed_kernel, n, late_senders), out_sha...  3.15 us
    pallas_call x1, Pallas kernels, local(): pl.pallas_call(functools.partial(expert_kernel, n, len(pieces)), out_shap...  2.71 us
    pallas_call x1, Pallas kernels, local(): pl.pallas_call(functools.partial(select_kernel, planes), out_shape=[jax.S...  2.46 us
    pallas_call x1, Pallas kernels, local(): pl.pallas_call(functools.partial(collect_kernel, n, early_senders), out_s...  2.05 us
  transfers between devices with their start and end apart: 20, of which 9 were waited for; matrix products, arithmetic and copies ran while one was open for 0% of the time, Pallas kernels for 16%

profile of v5, /device:TPU:0, one launch (start us, length us, event | category | flops | bytes accessed | tf_op | source)
XLA Modules:
  0.0 74.8 jit_solution(7060989891497884945)
XLA Ops:
  0.0 1.0 %pack.1.refs_0_ = bf16[144,512]{1,0:T(8,128)(2,1)S(1)} custom-call(s32[1,128]{1,0:T(1,128)} %bitcast.8, bf16[128,256]{1,0:T(8,128)(2,1)} %keys_ref.1, bf16[128,256]{1,0:T(8,128)(2,1)} %values_ref.1), custom_call_target="tpu_custom_call" | custom-call | tf_op jit(solution)/shard_map/pack/pallas_call | solution.py:425
  1.0 3.1 %collective-permute-start = (bf16[144,512]{1,0:T(8,128)(2,1)S(1)}, bf16[144,512]{1,0:T(8,128)(2,1)S(1)}, u32[]{:S(2)}, u32[]{:S(2)}) collective-permute-start(bf16[144,512]{1,0:T(8,128)(2,1)S(1)} %pack.1.refs_0_), channel_id=1, source_target_pairs={{0,4},{1,5},{2,6},{3,7},{4,8},{5,9},{6,10},{7,11},{8,12},{9,13},{1... | collective-permute-start | bytes 442376 | tf_op jit(solution)/shard_map/ppermute | solution.py:440
  4.1 0.7 collective-permute-start.2
  4.7 2.7 %collective-permute-start.1 = (bf16[144,512]{1,0:T(8,128)(2,1)S(1)}, bf16[144,512]{1,0:T(8,128)(2,1)S(1)}, u32[]{:S(2)}, u32[]{:S(2)}) collective-permute-start(bf16[144,512]{1,0:T(8,128)(2,1)S(1)} %pack.1.refs_0_), channel_id=1, source_target_pairs={{0,8},{1,9},{2,10},{3,11},{4,12},{5,13},{6,14},{7,15},{8,0},{9,1},... | collective-permute-start | bytes 442376 | tf_op jit(solution)/shard_map/ppermute | solution.py:440
  7.4 2.5 %select.1 = (bf16[2,256,512]{2,1,0:T(8,128)(2,1)S(1)}, f32[32,4096]{1,0:T(8,128)S(1)}, f32[8,512]{1,0:T(8,128)S(1)}, bf16[128,64]{1,0:T(8,128)(2,1)S(1)}, bf16[3...) custom-call(s32[1]{0:T(128)} %bitcast.pos_ref, s32[4,128]{1,0:T(4,128)} %bitcast.6, s32[1,128]{1,0:T(1,128)} %bitcast.9, ...), custom_call_target="tpu_custom_call" | custom-call | tf_op jit(solution)/shard_map/select/pallas_call | solution.py:450
  9.8 1.0 %collective-permute-done.refs_1_ = bf16[144,512]{1,0:T(8,128)(2,1)S(1)} collective-permute-done((bf16[144,512]{1,0:T(8,128)(2,1)S(1)}, bf16[144,512]{1,0:T(8,128)(2,1)S(1)}, u32[]{:S(2)}, u32[]{:S(2)}) %collective-permute-start) | collective-permute-done | bytes 147488 | tf_op jit(solution)/shard_map/ppermute | solution.py:440
  10.9 0.7 collective-permute-start.3
  11.6 0.0 collective-permute-done.2.refs_3_
  11.6 4.7 %collective-permute-done.1.refs_2_ = bf16[144,512]{1,0:T(8,128)(2,1)S(1)} collective-permute-done((bf16[144,512]{1,0:T(8,128)(2,1)S(1)}, bf16[144,512]{1,0:T(8,128)(2,1)S(1)}, u32[]{:S(2)}, u32[]{:S(2)}) %collective-permute-start.1) | collective-permute-done | bytes 147488 | tf_op jit(solution)/shard_map/ppermute | solution.py:440
  16.3 0.1 collective-permute-start.5
  16.4 4.7 %collective-permute-start.4 = (bf16[144,512]{1,0:T(8,128)(2,1)S(1)}, bf16[144,512]{1,0:T(8,128)(2,1)S(1)}, u32[]{:S(2)}, u32[]{:S(2)}) collective-permute-start(bf16[144,512]{1,0:T(8,128)(2,1)S(1)} %get-tuple-element.82), channel_id=1, source_target_pairs={{0,2},{1,3},{2,0},{3,1},{4,6},{5,7},{6,4},{7,5},{8,10},{9,11},{10,... | collective-permute-start | bytes 442376 | tf_op jit(solution)/shard_map/ppermute | solution.py:440
  21.2 0.7 collective-permute-start.6
  21.8 0.0 collective-permute-done.5.refs_5_
  21.8 2.0 %collect.1._ = bf16[16,144,512]{2,1,0:T(8,128)(2,1)S(1)} custom-call(s32[1]{0:T(128)} %bitcast.pos_ref, bf16[144,512]{1,0:T(8,128)(2,1)S(1)} %pack.1.refs_0_, bf16[144,512]{1,0:T(8,128)(2,1)S(1)} %collective-permute-done.refs_1_, bf16[144,512]{1,0:T(8,128)(2,1)S(1)} %collective-permute-done.1.refs_2_, bf16[144,512]{1,0:T(8,128)(2,1)S(1)} %collective-permute-done.2.refs_3_, ...), custom_call_target="tpu_custom_call" | custom-call | bytes 1000 | tf_op jit(solution)/shard_map/collect/pallas_call | solution.py:500
  23.9 0.0 copy-start
  23.9 0.0 copy-start.1
  23.9 1.7 %collective-permute-done.4.refs_1_ = bf16[144,512]{1,0:T(8,128)(2,1)S(1)} collective-permute-done((bf16[144,512]{1,0:T(8,128)(2,1)S(1)}, bf16[144,512]{1,0:T(8,128)(2,1)S(1)}, u32[]{:S(2)}, u32[]{:S(2)}) %collective-permute-start.4) | collective-permute-done | bytes 147488 | tf_op jit(solution)/shard_map/ppermute | solution.py:440
  25.6 0.1 collective-permute-start.7
  25.7 1.6 %collective-permute-done.7.refs_2_ = bf16[288,512]{1,0:T(8,128)(2,1)S(1)} collective-permute-done((bf16[288,512]{1,0:T(8,128)(2,1)S(1)}, bf16[288,512]{1,0:T(8,128)(2,1)S(1)}, u32[]{:S(2)}, u32[]{:S(2)}) %collective-permute-start.7) | collective-permute-done | bytes 294944 | tf_op jit(solution)/shard_map/ppermute | solution.py:440
  27.3 3.1 %routed.1 = (bf16[24,1024]{1,0:T(8,128)(2,1)S(1)}, bf16[24,1024]{1,0:T(8,128)(2,1)S(1)}, bf16[24,1024]{1,0:T(8,128)(2,1)S(1)}, bf16[24,1024]{1,0:T(8,128)(2,1)S(1)}, bf16[16,144,512]{2,1,0:T(8,128)(2,1)S(1)}) custom-call(s32[1]{0:T(128)} %bitcast.pos_ref, f32[1,4096]{1,0:T(1,128)} %bitcast.5, ...), custom_call_target="tpu_custom_call", output_to_operand_aliasing={{4}: (5, {})} | custom-call | tf_op jit(solution)/shard_map/routed/pallas_call | solution.py:514
  30.4 2.6 %collective-permute-start.8 = (bf16[24,1024]{1,0:T(8,128)(2,1)S(1)}, bf16[24,1024]{1,0:T(8,128)(2,1)S(1)}, u32[]{:S(2)}, u32[]{:S(2)}) collective-permute-start(bf16[24,1024]{1,0:T(8,128)(2,1)S(1)} %get-tuple-element.57), channel_id=1, source_target_pairs={{0,4},{1,5},{2,6},{3,7},{4,8},{5,9},{6,10},{7,11},{8,12},{9,13},{1... | collective-permute-start | bytes 147464 | tf_op jit(solution)/shard_map/ppermute | solution.py:440
  33.0 6.9 %collective-permute-start.9 = (bf16[24,1024]{1,0:T(8,128)(2,1)S(1)}, bf16[24,1024]{1,0:T(8,128)(2,1)S(1)}, u32[]{:S(2)}, u32[]{:S(2)}) collective-permute-start(bf16[24,1024]{1,0:T(8,128)(2,1)S(1)} %get-tuple-element.58), channel_id=1, source_target_pairs={{0,8},{1,9},{2,10},{3,11},{4,12},{5,13},{6,14},{7,15},{8,0},{9,1},... | collective-permute-start | bytes 147464 | tf_op jit(solution)/shard_map/ppermute | solution.py:440
  39.9 1.1 %collective-permute-start.10 = (bf16[24,1024]{1,0:T(8,128)(2,1)S(1)}, bf16[24,1024]{1,0:T(8,128)(2,1)S(1)}, u32[]{:S(2)}, u32[]{:S(2)}) collective-permute-start(bf16[24,1024]{1,0:T(8,128)(2,1)S(1)} %get-tuple-element.59), channel_id=1, source_target_pairs={{0,12},{1,13},{2,14},{3,15},{4,0},{5,1},{6,2},{7,3},{8,4},{9,5},{1... | collective-permute-start | bytes 147464 | tf_op jit(solution)/shard_map/ppermute | solution.py:440
  41.0 1.3 %collective-permute-start.11 = (bf16[24,1024]{1,0:T(8,128)(2,1)S(1)}, bf16[24,1024]{1,0:T(8,128)(2,1)S(1)}, u32[]{:S(2)}, u32[]{:S(2)}) collective-permute-start(bf16[24,1024]{1,0:T(8,128)(2,1)S(1)} %get-tuple-element.53._.refs_0_), channel_id=1, source_target_pairs={{0,2},{1,3},{2,0},{3,1},{4,6},{5,7},{6,4},{7,5},{8,10},{9,11},{10,... | collective-permute-start | bytes 147464 | tf_op jit(solution)/shard_map/ppermute | solution.py:440
  42.3 3.9 %own.3 = (f32[128,1280]{1,0:T(8,128)S(1)}, f32[8,128]{1,0:T(8,128)S(1)}, bf16[4096,384]{1,0:T(8,128)(2,1)S(1)}, bf16[4096,384]{1,0:T(8,128)(2,1)S(1)}, bf16[384,4096]{1,0:T(8,128)(2,1)S(1)}) custom-call(s32[1]{0:T(128)} %bitcast.pos_ref, bf16[16,144,512]{2,1,0:T(8,128)(2,1)S(1)} %get-tuple-element.52.held, bf16[128,4096]{1,0:T(8,128)(2,1)S(1)} %copy-done, ...), custom_call_target="tpu_custom_call" | custom-call | flops 2000000000 | bytes 8000000 | tf_op jit(solution)/shard_map/own/pallas_call | solution.py:535
  46.2 0.0 collective-permute-done.10
  46.2 0.0 collective-permute-done.11.refs_2_
  46.2 0.1 collective-permute-start.13
  46.3 0.8 %collective-permute-start.12 = (bf16[72,1024]{1,0:T(8,128)(2,1)S(1)}, bf16[72,1024]{1,0:T(8,128)(2,1)S(1)}, u32[]{:S(2)}, u32[]{:S(2)}) collective-permute-start(bf16[72,1024]{1,0:T(8,128)(2,1)S(1)} %constant_dynamic-update-slice_fusion.5.refs_1_), channel_id=1, source_target_pairs={{0,2},{1,3},{2,0},{3,1},{4,6},{5,7},{6,4},{7,5},{8,10},{9,11},{10,... | collective-permute-start | bytes 442376 | tf_op jit(solution)/shard_map/ppermute | solution.py:440
  47.2 1.5 %own.4 = (f32[128,1408]{1,0:T(8,128)S(1)}, f32[8,128]{1,0:T(8,128)S(1)}) custom-call(s32[1]{0:T(128)} %bitcast.pos_ref, bf16[16,144,512]{2,1,0:T(8,128)(2,1)S(1)} %get-tuple-element.52.held, bf16[128,4096]{1,0:T(8,128)(2,1)S(1)} %copy-done, bf16[128,4096]{1,0:T(8,128)(2,1)S(1)} %copy-done.1, f32[8,128]{1,0:T(8,128)S(1)} %get-tuple-element.55._), custom_call_target="tpu_custom_call" | custom-call | flops 2000000000 | bytes 8000000 | tf_op jit(solution)/shard_map/own/pallas_call | solution.py:535
  48.7 3.9 %collective-permute-done.12.refs_3_ = bf16[72,1024]{1,0:T(8,128)(2,1)S(1)} collective-permute-done((bf16[72,1024]{1,0:T(8,128)(2,1)S(1)}, bf16[72,1024]{1,0:T(8,128)(2,1)S(1)}, u32[]{:S(2)}, u32[]{:S(2)}) %collective-permute-start.12) | collective-permute-done | bytes 147488 | tf_op jit(solution)/shard_map/ppermute | solution.py:440
  52.6 0.0 collective-permute-done.13.refs_4_
  52.6 0.1 collective-permute-start.14
  52.7 1.4 %collective-permute-done.14.refs_5_ = bf16[96,1024]{1,0:T(8,128)(2,1)S(1)} collective-permute-done((bf16[96,1024]{1,0:T(8,128)(2,1)S(1)}, bf16[96,1024]{1,0:T(8,128)(2,1)S(1)}, u32[]{:S(2)}, u32[]{:S(2)}) %collective-permute-start.14) | collective-permute-done | bytes 196640 | tf_op jit(solution)/shard_map/ppermute | solution.py:440
  54.1 2.7 %expert.1 = (bf16[192,1024]{1,0:T(8,128)(2,1)S(1)}, bf16[192,1024]{1,0:T(8,128)(2,1)S(1)}) custom-call(bf16[24,1024]{1,0:T(8,128)(2,1)S(1)} %get-tuple-element.53._.refs_0_, bf16[72,1024]{1,0:T(8,128)(2,1)S(1)} %constant_dynamic-update-slice_fusion.5.refs_1_, bf16[24,1024]{1,0:T(8,128)(2,1)S(1)} %collective-permute-done.11.refs_2_, ...), custom_call_target="tpu_custom_call" | custom-call | flops 1200000000 | bytes 12000000 | tf_op jit(solution)/shard_map/expert/pallas_call | solution.py:576
  56.8 0.2 collective-permute-start.15
  57.0 1.6 %collective-permute-done.15 = bf16[192,1024]{1,0:T(8,128)(2,1)S(1)} collective-permute-done((bf16[192,1024]{1,0:T(8,128)(2,1)S(1)}, bf16[192,1024]{1,0:T(8,128)(2,1)S(1)}, u32[]{:S(2)}, u32[]{:S(2)}) %collective-permute-start.15) | collective-permute-done | bytes 393248 | tf_op jit(solution)/shard_map/ppermute | solution.py:440
  58.6 0.1 convert_add_fusion
  58.8 0.8 %collective-permute-start.16 = (bf16[96,1024]{1,0:T(8,128)(2,1)S(1)}, bf16[96,1024]{1,0:T(8,128)(2,1)S(1)}, u32[]{:S(2)}, u32[]{:S(2)}) collective-permute-start(bf16[96,1024]{1,0:T(8,128)(2,1)S(1)} %slice.35), channel_id=1, source_target_pairs={{0,2},{1,3},{2,0},{3,1},{4,6},{5,7},{6,4},{7,5},{8,10},{9,11},{10,... | collective-permute-start | bytes 589832 | tf_op jit(solution)/shard_map/ppermute | solution.py:440
  59.6 6.2 %collective-permute-done.16 = bf16[96,1024]{1,0:T(8,128)(2,1)S(1)} collective-permute-done((bf16[96,1024]{1,0:T(8,128)(2,1)S(1)}, bf16[96,1024]{1,0:T(8,128)(2,1)S(1)}, u32[]{:S(2)}, u32[]{:S(2)}) %collective-permute-start.16) | collective-permute-done | bytes 196640 | tf_op jit(solution)/shard_map/ppermute | solution.py:440
  65.8 0.1 fusion
  65.9 2.1 %collective-permute-start.19 = (bf16[24,1024]{1,0:T(8,128)(2,1)S(1)}, bf16[24,1024]{1,0:T(8,128)(2,1)S(1)}, u32[]{:S(2)}, u32[]{:S(2)}) collective-permute-start(bf16[24,1024]{1,0:T(8,128)(2,1)S(1)} %get-tuple-element.77), channel_id=1, source_target_pairs={{0,4},{1,5},{2,6},{3,7},{4,8},{5,9},{6,10},{7,11},{8,12},{9,13},{1... | collective-permute-start | bytes 147464 | tf_op jit(solution)/shard_map/ppermute | solution.py:440
  67.9 0.0 collective-permute-start.18
  68.0 2.4 %collective-permute-start.17 = (bf16[24,1024]{1,0:T(8,128)(2,1)S(1)}, bf16[24,1024]{1,0:T(8,128)(2,1)S(1)}, u32[]{:S(2)}, u32[]{:S(2)}) collective-permute-start(bf16[24,1024]{1,0:T(8,128)(2,1)S(1)} %get-tuple-element.79), channel_id=1, source_target_pairs={{0,12},{1,13},{2,14},{3,15},{4,0},{5,1},{6,2},{7,3},{8,4},{9,5},{1... | collective-permute-start | bytes 147464 | tf_op jit(solution)/shard_map/ppermute | solution.py:440
  70.4 1.7 %own.5 = (f32[128,1408]{1,0:T(8,128)S(1)}, f32[8,128]{1,0:T(8,128)}) custom-call(s32[1]{0:T(128)} %bitcast.pos_ref, bf16[16,144,512]{2,1,0:T(8,128)(2,1)S(1)} %get-tuple-element.52.held, bf16[128,4096]{1,0:T(8,128)(2,1)S(1)} %copy-done, bf16[128,4096]{1,0:T(8,128)(2,1)S(1)} %copy-done.1, bf16[192,1024]{1,0:T(8,128)(2,1)S(1)} %get-tuple-element.74._), custom_call_target="tpu_custom_call" | custom-call | flops 2000000000 | bytes 8000000 | tf_op jit(solution)/shard_map/own/pallas_call | solution.py:535
  72.1 1.3 %collective-permute-done.18.refs_5_ = bf16[24,1024]{1,0:T(8,128)(2,1)S(1)} collective-permute-done((bf16[24,1024]{1,0:T(8,128)(2,1)S(1)}, bf16[24,1024]{1,0:T(8,128)(2,1)S(1)}, u32[]{:S(2)}, u32[]{:S(2)}) %collective-permute-start.18) | collective-permute-done | bytes 49184 | tf_op jit(solution)/shard_map/ppermute | solution.py:440
  73.4 0.0 collective-permute-done.17.refs_4_
  73.4 1.4 %combine.1 = bf16[128,4096]{1,0:T(8,128)(2,1)} custom-call(bf16[128,64]{1,0:T(8,128)(2,1)S(1)} %get-tuple-element.41.mix_ref, f32[128,1280]{1,0:T(8,128)S(1)} %get-tuple-element.54.refs_0_, f32[128,1408]{1,0:T(8,128)S(1)} %get-tuple-element.56.refs_1_, f32[128,1408]{1,0:T(8,128)S(1)} %get-tuple-element.75.refs_2_, ...), custom_call_target="tpu_custom_call" | custom-call | tf_op jit(solution)/shard_map/combine/pallas_call | solution.py:606
  (20 shorter events, 0.2 us)
Async XLA Ops:
  1.0 9.9 %collective-permute-start = (bf16[144,512]{1,0:T(8,128)(2,1)S(1)}, bf16[144,512]{1,0:T(8,128)(2,1)S(1)}, u32[]{:S(2)}, u32[]{:S(2)}) collective-permute-start(bf16[144,512]{1,0:T(8,128)(2,1)S(1)} %pack.1.refs_0_), channel_id=1, source_target_pairs={{0,4},{1,5},{2,6},{3,7},{4,8},{5,9},{6,10},{7,11},{8,12},{9,13},{1... | collective-permute-start | bytes 442376 | tf_op jit(solution)/shard_map/ppermute | solution.py:440
  4.1 7.5 %collective-permute-start.2 = (bf16[144,512]{1,0:T(8,128)(2,1)S(1)}, bf16[144,512]{1,0:T(8,128)(2,1)S(1)}, u32[]{:S(2)}, u32[]{:S(2)}) collective-permute-start(bf16[144,512]{1,0:T(8,128)(2,1)S(1)} %pack.1.refs_0_), channel_id=1, source_target_pairs={{0,0},{1,1},{2,14},{3,15},{4,4},{5,5},{6,2},{7,3},{8,8},{9,9},{10,... | collective-permute-start | bytes 442376 | tf_op jit(solution)/shard_map/ppermute | solution.py:440
  4.7 11.5 %collective-permute-start.1 = (bf16[144,512]{1,0:T(8,128)(2,1)S(1)}, bf16[144,512]{1,0:T(8,128)(2,1)S(1)}, u32[]{:S(2)}, u32[]{:S(2)}) collective-permute-start(bf16[144,512]{1,0:T(8,128)(2,1)S(1)} %pack.1.refs_0_), channel_id=1, source_target_pairs={{0,8},{1,9},{2,10},{3,11},{4,12},{5,13},{6,14},{7,15},{8,0},{9,1},... | collective-permute-start | bytes 442376 | tf_op jit(solution)/shard_map/ppermute | solution.py:440
  10.9 5.4 %collective-permute-start.3 = (bf16[144,512]{1,0:T(8,128)(2,1)S(1)}, bf16[144,512]{1,0:T(8,128)(2,1)S(1)}, u32[]{:S(2)}, u32[]{:S(2)}) collective-permute-start(bf16[144,512]{1,0:T(8,128)(2,1)S(1)} %collective-permute-done.refs_1_), channel_id=1, source_target_pairs={{0,0},{1,1},{2,2},{3,3},{4,6},{5,7},{6,4},{7,5},{8,10},{9,11},{10,... | collective-permute-start | bytes 442376 | tf_op jit(solution)/shard_map/ppermute | solution.py:440
  16.3 5.5 %collective-permute-start.5 = (bf16[720,512]{1,0:T(8,128)(2,1)S(1)}, bf16[720,512]{1,0:T(8,128)(2,1)S(1)}, u32[]{:S(2)}, u32[]{:S(2)}) collective-permute-start(bf16[720,512]{1,0:T(8,128)(2,1)S(1)} %constant_dynamic-update-slice_fusion), channel_id=1, source_target_pairs={{0,1},{1,0},{2,3},{3,2},{4,5},{5,4},{6,7},{7,6},{8,9},{9,8},{10,11... | collective-permute-start | bytes 2211848 | tf_op jit(solution)/shard_map/ppermute | solution.py:440
  16.4 9.2 %collective-permute-start.4 = (bf16[144,512]{1,0:T(8,128)(2,1)S(1)}, bf16[144,512]{1,0:T(8,128)(2,1)S(1)}, u32[]{:S(2)}, u32[]{:S(2)}) collective-permute-start(bf16[144,512]{1,0:T(8,128)(2,1)S(1)} %get-tuple-element.82), channel_id=1, source_target_pairs={{0,2},{1,3},{2,0},{3,1},{4,6},{5,7},{6,4},{7,5},{8,10},{9,11},{10,... | collective-permute-start | bytes 442376 | tf_op jit(solution)/shard_map/ppermute | solution.py:440
  21.2 4.4 %collective-permute-start.6 = (bf16[144,512]{1,0:T(8,128)(2,1)S(1)}, bf16[144,512]{1,0:T(8,128)(2,1)S(1)}, u32[]{:S(2)}, u32[]{:S(2)}) collective-permute-start(bf16[144,512]{1,0:T(8,128)(2,1)S(1)} %collective-permute-done.1.refs_2_), channel_id=1, source_target_pairs={{0,0},{1,1},{2,2},{3,3},{4,4},{5,5},{6,6},{7,7},{8,10},{9,11},{10,... | collective-permute-start | bytes 442376 | tf_op jit(solution)/shard_map/ppermute | solution.py:440
  23.9 18.4 %copy-start = (bf16[128,4096]{1,0:T(8,128)(2,1)S(1)}, bf16[128,4096]{1,0:T(8,128)(2,1)}, u32[]{:S(2)}) copy-start(bf16[128,4096]{1,0:T(8,128)(2,1)} %q_ref.5) | copy-start | bytes 3145732
  23.9 18.4 %copy-start.1 = (bf16[128,4096]{1,0:T(8,128)(2,1)S(1)}, bf16[128,4096]{1,0:T(8,128)(2,1)}, u32[]{:S(2)}) copy-start(bf16[128,4096]{1,0:T(8,128)(2,1)} %x_ref.5) | copy-start | bytes 3145732
  25.6 1.6 %collective-permute-start.7 = (bf16[288,512]{1,0:T(8,128)(2,1)S(1)}, bf16[288,512]{1,0:T(8,128)(2,1)S(1)}, u32[]{:S(2)}, u32[]{:S(2)}) collective-permute-start(bf16[288,512]{1,0:T(8,128)(2,1)S(1)} %pad_maximum_fusion), channel_id=1, source_target_pairs={{0,1},{1,0},{2,3},{3,2},{4,5},{5,4},{6,7},{7,6},{8,9},{9,8},{10,11... | collective-permute-start | bytes 884744 | tf_op jit(solution)/shard_map/ppermute | solution.py:440
  30.4 15.7 %collective-permute-start.8 = (bf16[24,1024]{1,0:T(8,128)(2,1)S(1)}, bf16[24,1024]{1,0:T(8,128)(2,1)S(1)}, u32[]{:S(2)}, u32[]{:S(2)}) collective-permute-start(bf16[24,1024]{1,0:T(8,128)(2,1)S(1)} %get-tuple-element.57), channel_id=1, source_target_pairs={{0,4},{1,5},{2,6},{3,7},{4,8},{5,9},{6,10},{7,11},{8,12},{9,13},{1... | collective-permute-start | bytes 147464 | tf_op jit(solution)/shard_map/ppermute | solution.py:440
  33.0 13.2 %collective-permute-start.9 = (bf16[24,1024]{1,0:T(8,128)(2,1)S(1)}, bf16[24,1024]{1,0:T(8,128)(2,1)S(1)}, u32[]{:S(2)}, u32[]{:S(2)}) collective-permute-start(bf16[24,1024]{1,0:T(8,128)(2,1)S(1)} %get-tuple-element.58), channel_id=1, source_target_pairs={{0,8},{1,9},{2,10},{3,11},{4,12},{5,13},{6,14},{7,15},{8,0},{9,1},... | collective-permute-start | bytes 147464 | tf_op jit(solution)/shard_map/ppermute | solution.py:440
  39.9 6.3 %collective-permute-start.10 = (bf16[24,1024]{1,0:T(8,128)(2,1)S(1)}, bf16[24,1024]{1,0:T(8,128)(2,1)S(1)}, u32[]{:S(2)}, u32[]{:S(2)}) collective-permute-start(bf16[24,1024]{1,0:T(8,128)(2,1)S(1)} %get-tuple-element.59), channel_id=1, source_target_pairs={{0,12},{1,13},{2,14},{3,15},{4,0},{5,1},{6,2},{7,3},{8,4},{9,5},{1... | collective-permute-start | bytes 147464 | tf_op jit(solution)/shard_map/ppermute | solution.py:440
  41.0 5.2 %collective-permute-start.11 = (bf16[24,1024]{1,0:T(8,128)(2,1)S(1)}, bf16[24,1024]{1,0:T(8,128)(2,1)S(1)}, u32[]{:S(2)}, u32[]{:S(2)}) collective-permute-start(bf16[24,1024]{1,0:T(8,128)(2,1)S(1)} %get-tuple-element.53._.refs_0_), channel_id=1, source_target_pairs={{0,2},{1,3},{2,0},{3,1},{4,6},{5,7},{6,4},{7,5},{8,10},{9,11},{10,... | collective-permute-start | bytes 147464 | tf_op jit(solution)/shard_map/ppermute | solution.py:440
  46.2 6.4 %collective-permute-start.13 = (bf16[96,1024]{1,0:T(8,128)(2,1)S(1)}, bf16[96,1024]{1,0:T(8,128)(2,1)S(1)}, u32[]{:S(2)}, u32[]{:S(2)}) collective-permute-start(bf16[96,1024]{1,0:T(8,128)(2,1)S(1)} %pad_maximum_fusion.1), channel_id=1, source_target_pairs={{0,1},{1,0},{2,3},{3,2},{4,5},{5,4},{6,7},{7,6},{8,9},{9,8},{10,11... | collective-permute-start | bytes 589832 | tf_op jit(solution)/shard_map/ppermute | solution.py:440
  46.3 6.3 %collective-permute-start.12 = (bf16[72,1024]{1,0:T(8,128)(2,1)S(1)}, bf16[72,1024]{1,0:T(8,128)(2,1)S(1)}, u32[]{:S(2)}, u32[]{:S(2)}) collective-permute-start(bf16[72,1024]{1,0:T(8,128)(2,1)S(1)} %constant_dynamic-update-slice_fusion.5.refs_1_), channel_id=1, source_target_pairs={{0,2},{1,3},{2,0},{3,1},{4,6},{5,7},{6,4},{7,5},{8,10},{9,11},{10,... | collective-permute-start | bytes 442376 | tf_op jit(solution)/shard_map/ppermute | solution.py:440
  52.6 1.5 %collective-permute-start.14 = (bf16[96,1024]{1,0:T(8,128)(2,1)S(1)}, bf16[96,1024]{1,0:T(8,128)(2,1)S(1)}, u32[]{:S(2)}, u32[]{:S(2)}) collective-permute-start(bf16[96,1024]{1,0:T(8,128)(2,1)S(1)} %pad_maximum_fusion.2), channel_id=1, source_target_pairs={{0,1},{1,0},{2,3},{3,2},{4,5},{5,4},{6,7},{7,6},{8,9},{9,8},{10,11... | collective-permute-start | bytes 589832 | tf_op jit(solution)/shard_map/ppermute | solution.py:440
  56.8 1.8 %collective-permute-start.15 = (bf16[192,1024]{1,0:T(8,128)(2,1)S(1)}, bf16[192,1024]{1,0:T(8,128)(2,1)S(1)}, u32[]{:S(2)}, u32[]{:S(2)}) collective-permute-start(bf16[192,1024]{1,0:T(8,128)(2,1)S(1)} %get-tuple-element.76), channel_id=1, source_target_pairs={{0,1},{1,0},{2,3},{3,2},{4,5},{5,4},{6,7},{7,6},{8,9},{9,8},{10,11... | collective-permute-start | bytes 1179656 | tf_op jit(solution)/shard_map/ppermute | solution.py:440
  58.8 7.0 %collective-permute-start.16 = (bf16[96,1024]{1,0:T(8,128)(2,1)S(1)}, bf16[96,1024]{1,0:T(8,128)(2,1)S(1)}, u32[]{:S(2)}, u32[]{:S(2)}) collective-permute-start(bf16[96,1024]{1,0:T(8,128)(2,1)S(1)} %slice.35), channel_id=1, source_target_pairs={{0,2},{1,3},{2,0},{3,1},{4,6},{5,7},{6,4},{7,5},{8,10},{9,11},{10,... | collective-permute-start | bytes 589832 | tf_op jit(solution)/shard_map/ppermute | solution.py:440
  65.9 6.2 %collective-permute-start.19 = (bf16[24,1024]{1,0:T(8,128)(2,1)S(1)}, bf16[24,1024]{1,0:T(8,128)(2,1)S(1)}, u32[]{:S(2)}, u32[]{:S(2)}) collective-permute-start(bf16[24,1024]{1,0:T(8,128)(2,1)S(1)} %get-tuple-element.77), channel_id=1, source_target_pairs={{0,4},{1,5},{2,6},{3,7},{4,8},{5,9},{6,10},{7,11},{8,12},{9,13},{1... | collective-permute-start | bytes 147464 | tf_op jit(solution)/shard_map/ppermute | solution.py:440
  67.9 5.5 %collective-permute-start.18 = (bf16[24,1024]{1,0:T(8,128)(2,1)S(1)}, bf16[24,1024]{1,0:T(8,128)(2,1)S(1)}, u32[]{:S(2)}, u32[]{:S(2)}) collective-permute-start(bf16[24,1024]{1,0:T(8,128)(2,1)S(1)} %get-tuple-element.78), channel_id=1, source_target_pairs={{0,8},{1,9},{2,10},{3,11},{4,12},{5,13},{6,14},{7,15},{8,0},{9,1},... | collective-permute-start | bytes 147464 | tf_op jit(solution)/shard_map/ppermute | solution.py:440
  68.0 5.4 %collective-permute-start.17 = (bf16[24,1024]{1,0:T(8,128)(2,1)S(1)}, bf16[24,1024]{1,0:T(8,128)(2,1)S(1)}, u32[]{:S(2)}, u32[]{:S(2)}) collective-permute-start(bf16[24,1024]{1,0:T(8,128)(2,1)S(1)} %get-tuple-element.79), channel_id=1, source_target_pairs={{0,12},{1,13},{2,14},{3,15},{4,0},{5,1},{6,2},{7,3},{8,4},{9,5},{1... | collective-permute-start | bytes 147464 | tf_op jit(solution)/shard_map/ppermute | solution.py:440

commit v6 on v5

--- a/solution.py
+++ b/solution.py
@@ -244,8 +244,7 @@
     planes = n // SHARDS
     z, y, c = pos // SHARDS, (pos // 2) % 2, pos % 2
     copies = []
-    for i, (piece, row, flip_c, flip_y, passed) in enumerate(senders):
-        k = jnp.where(y == 0, passed[0], passed[1])
+    for i, (piece, row, flip_c, flip_y, k) in enumerate(senders):
         sender = lax.rem(z - k + planes, planes) * SHARDS + (y ^ flip_y) * 2 + (c ^ flip_c)
         copy = pltpu.make_async_copy(
             pieces[piece].at[pl.ds(row, KV_ROWS)], held.at[sender], sems.at[i]
@@ -264,8 +263,8 @@
 def routed_kernel(n, senders, pos_ref, gain_ref, qs_ref, xs_ref, facts_ref, _, *refs):
     planes = n // SHARDS
     count = len(senders)
-    pieces, outs, held = refs[:3], refs[3 : 3 + planes], refs[3 + planes]
-    acc, bias, q_scr, state, gain, sems = refs[4 + planes :]
+    pieces, outs, held = refs[:2], refs[2 : 2 + planes], refs[2 + planes]
+    acc, bias, q_scr, state, gain, sems = refs[3 + planes :]
     pos = pos_ref[0]
     copies = place_pieces(n, senders, pos, pieces, held, sems)
     copies.append(pltpu.make_async_copy(gain_ref, gain, sems.at[count]))
@@ -372,8 +371,8 @@
 
 def combine_kernel(planes, widths, mix_ref, *refs):
     count = len(widths)
-    halves, parts, out_ref = refs[:count], refs[count : count + planes], refs[count + planes]
-    buffer, sems = refs[count + planes + 1 :]
+    halves, parts = refs[:count], refs[count : count + planes]
+    _, out_ref, buffer, sems = refs[count + planes :]
     slots = planes * SLOTS
     came = jnp.concatenate([p[...].astype(F32) for p in parts], axis=0).astype(BF16)
     order = one_hot(travel_row(numbers((CUT * slots, 1), 0), planes, SLOTS), planes * PIECE)
@@ -473,29 +472,25 @@
 
     flip_y = [(s, s ^ 2) for s in range(n)]
     flip_c = [(s, s ^ 1) for s in range(n)]
-    along = [packed]
-    for k in range(1, far + 1):
-        used = [any(needed(k, y, to) for to in (0, 1)) for y in (0, 1)]
-        pairs = [(s, (s + k * SHARDS) % n if used[s // 2 % 2] else s) for s in range(n)]
-        along.append(move(packed, pairs))
+    jump = {s: s + far * SHARDS - 2 for s in range(n - far * SHARDS) if s & 2}
+    jump.update({to: s for s, to in jump.items()})
+    jumped = move(packed, [(s, jump.get(s, s)) for s in range(n)])
+    along = [packed] + [
+        move(packed, [(s, (s + k * SHARDS) % n) for s in range(n)]) for k in range(1, far)
+    ]
     along[1], q_rows = lax.optimization_barrier((along[1], q_rows))
-    shared = not needed(0, 1, 0) and not needed(far, 0, 1)
-    middle = range(1, far) if shared else range(far)
     across = []
-    for k in middle:
-        if k == middle[1]:
-            along[k:], across = lax.optimization_barrier((along[k:], across))
+    for k in range(far):
+        if k > 1 and k == far - 1:
+            along[k], across = lax.optimization_barrier((along[k], across))
         across.append(move(along[k], [(s, s ^ 2 if s >= k * SHARDS else s) for s in range(n)]))
-    odd = (pos[0] & 2) != 0
-    final = move(jnp.where(odd, along[far], packed) if shared else along[far], flip_y)
-    early, late = along + across[:-1], [across[-1]]
-    sides = [(0, (k, k)) for k in range(far + 1)] + [(1, (k, k)) for k in middle[:-1]]
-    late_sides = [(1, (middle[-1],) * 2), (1, (far, 0 if shared else far))]
+    early, late = along + [jumped] + across[:-1], across[-1:]
+    sides = [(0, k) for k in range(far)] + [(1, far)] + [(1, k) for k in range(far - 1)]
     early.append(move(jnp.concatenate(early, axis=0), flip_c))
+    late.append(move(across[-1], flip_c))
     early_senders = [(i, 0, 0, *side) for i, side in enumerate(sides)]
     early_senders += [(len(sides), i * KV_ROWS, 1, *side) for i, side in enumerate(sides)]
-    late_senders = [(i, 0, 0, *side) for i, side in enumerate(late_sides)]
-    late_senders += [(2, i * KV_ROWS, 1, *side) for i, side in enumerate(late_sides)]
+    late_senders = [(flip, 0, flip, 1, far - 1) for flip in (0, 1)]
     held_shape = jax.ShapeDtypeStruct((n, KV_ROWS, 4 * HEAD), BF16)
     held = pl.pallas_call(
         functools.partial(collect_kernel, n, early_senders),
@@ -508,9 +503,6 @@
         name="collect",
     )(pos, *early)
 
-    final, held = lax.optimization_barrier((final, held))
-    late.append(final)
-    late.append(move(jnp.concatenate(late, axis=0), flip_c))
     *sent, held = pl.pallas_call(
         functools.partial(routed_kernel, n, late_senders),
         out_shape=[jax.ShapeDtypeStruct((PIECE, width // CUT), BF16)] * planes
@@ -606,12 +598,12 @@
     return pl.pallas_call(
         functools.partial(combine_kernel, planes, widths),
         out_shape=jax.ShapeDtypeStruct((tokens, width), BF16),
-        in_specs=[VMEM] * (1 + len(halves) + planes),
+        in_specs=[VMEM] * (1 + len(halves) + planes) + [ANY],
         out_specs=HBM,
         scratch_shapes=[pltpu.VMEM((tokens, width), BF16), pltpu.SemaphoreType.DMA((CUT,))],
         compiler_params=params(small),
         name="combine",
-    )(mix, *halves, *parts)
+    )(mix, *halves, *parts, done)
 
 
 def solution(mesh):

time: 75.4 us -> 74.1 us (0.983); the launches traced: 74.8 us -> 74.4 us
  no operation moved by 1% of the time
where the time goes in v6:
time: 74.1 us; the launch traced here: 74.4 us
  starting transfers between devices  31.6 us (43%)
  waiting for transfers between devices  22.7 us (31%)
  Pallas kernels  19.5 us (26%)
    ppermute x20, starting transfers between devices, move(): return lax.ppermute(value, 'expert', pairs)  31.6 us
    ppermute x20, waiting for transfers between devices, move(): return lax.ppermute(value, 'expert', pairs)  22.7 us
    pallas_call x3, Pallas kernels, own(): pl.pallas_call(functools.partial(own_kernel, n, heads, len(sources)), out...  6.75 us
    pallas_call x1, Pallas kernels, local(): pl.pallas_call(functools.partial(routed_kernel, n, late_senders), out_sha...  2.8 us
    pallas_call x1, Pallas kernels, local(): pl.pallas_call(functools.partial(expert_kernel, n, len(pieces)), out_shap...  2.7 us
    pallas_call x1, Pallas kernels, local(): pl.pallas_call(functools.partial(select_kernel, planes), out_shape=[jax.S...  2.46 us
    pallas_call x1, Pallas kernels, local(): pl.pallas_call(functools.partial(collect_kernel, n, early_senders), out_s...  2.4 us
  transfers between devices with their start and end apart: 20, of which 9 were waited for; matrix products, arithmetic and copies ran while one was open for 0% of the time, Pallas kernels for 16%

profile of v6, /device:TPU:0, one launch (start us, length us, event | category | flops | bytes accessed | tf_op | source)
XLA Modules:
  0.0 74.4 jit_solution(11204086057948792594)
XLA Ops:
  0.0 1.0 %pack.1.refs_0_ = bf16[144,512]{1,0:T(8,128)(2,1)S(1)} custom-call(s32[1,128]{1,0:T(1,128)} %bitcast.8, bf16[128,256]{1,0:T(8,128)(2,1)} %keys_ref.1, bf16[128,256]{1,0:T(8,128)(2,1)} %values_ref.1), custom_call_target="tpu_custom_call" | custom-call | tf_op jit(solution)/shard_map/pack/pallas_call | solution.py:424
  1.0 3.1 %collective-permute-start = (bf16[144,512]{1,0:T(8,128)(2,1)S(1)}, bf16[144,512]{1,0:T(8,128)(2,1)S(1)}, u32[]{:S(2)}, u32[]{:S(2)}) collective-permute-start(bf16[144,512]{1,0:T(8,128)(2,1)S(1)} %pack.1.refs_0_), channel_id=1, source_target_pairs={{0,4},{1,5},{2,6},{3,7},{4,8},{5,9},{6,10},{7,11},{8,12},{9,13},{1... | collective-permute-start | bytes 442376 | tf_op jit(solution)/shard_map/ppermute | solution.py:439
  4.1 0.7 collective-permute-start.4
  4.7 4.8 %collective-permute-start.2 = (bf16[144,512]{1,0:T(8,128)(2,1)S(1)}, bf16[144,512]{1,0:T(8,128)(2,1)S(1)}, u32[]{:S(2)}, u32[]{:S(2)}) collective-permute-start(bf16[144,512]{1,0:T(8,128)(2,1)S(1)} %pack.1.refs_0_), channel_id=1, source_target_pairs={{0,2},{1,3},{2,0},{3,1},{4,6},{5,7},{6,4},{7,5},{8,10},{9,11},{10,... | collective-permute-start | bytes 442376 | tf_op jit(solution)/shard_map/ppermute | solution.py:439
  9.5 0.0 collective-permute-start.1
  9.5 2.5 %select.1 = (bf16[2,256,512]{2,1,0:T(8,128)(2,1)S(1)}, f32[32,4096]{1,0:T(8,128)S(1)}, f32[8,512]{1,0:T(8,128)S(1)}, bf16[128,64]{1,0:T(8,128)(2,1)S(1)}, bf16[3...) custom-call(s32[1]{0:T(128)} %bitcast.pos_ref, s32[4,128]{1,0:T(4,128)} %bitcast.6, s32[1,128]{1,0:T(1,128)} %bitcast.9, ...), custom_call_target="tpu_custom_call" | custom-call | tf_op jit(solution)/shard_map/select/pallas_call | solution.py:449
  12.0 0.0 collective-permute-done.refs_1_
  12.0 0.7 collective-permute-start.3
  12.7 2.8 %collective-permute-done.2.refs_4_ = bf16[144,512]{1,0:T(8,128)(2,1)S(1)} collective-permute-done((bf16[144,512]{1,0:T(8,128)(2,1)S(1)}, bf16[144,512]{1,0:T(8,128)(2,1)S(1)}, u32[]{:S(2)}, u32[]{:S(2)}) %collective-permute-start.2) | collective-permute-done | bytes 147488 | tf_op jit(solution)/shard_map/ppermute | solution.py:439
  15.5 4.8 %collective-permute-done.1.refs_2_ = bf16[144,512]{1,0:T(8,128)(2,1)S(1)} collective-permute-done((bf16[144,512]{1,0:T(8,128)(2,1)S(1)}, bf16[144,512]{1,0:T(8,128)(2,1)S(1)}, u32[]{:S(2)}, u32[]{:S(2)}) %collective-permute-start.1) | collective-permute-done | bytes 147488 | tf_op jit(solution)/shard_map/ppermute | solution.py:439
  20.4 0.0 copy-start
  20.4 0.0 copy-start.1
  20.4 0.1 collective-permute-start.5
  20.5 0.8 %collective-permute-start.6 = (bf16[144,512]{1,0:T(8,128)(2,1)S(1)}, bf16[144,512]{1,0:T(8,128)(2,1)S(1)}, u32[]{:S(2)}, u32[]{:S(2)}) collective-permute-start(bf16[144,512]{1,0:T(8,128)(2,1)S(1)} %collective-permute-done.1.refs_2_), channel_id=1, source_target_pairs={{0,0},{1,1},{2,2},{3,3},{4,4},{5,5},{6,6},{7,7},{8,10},{9,11},{10,... | collective-permute-start | bytes 442376 | tf_op jit(solution)/shard_map/ppermute | solution.py:439
  21.3 0.6 collective-permute-start.7
  21.9 1.0 %collective-permute-done.5.refs_6_ = bf16[864,512]{1,0:T(8,128)(2,1)S(1)} collective-permute-done((bf16[864,512]{1,0:T(8,128)(2,1)S(1)}, bf16[864,512]{1,0:T(8,128)(2,1)S(1)}, u32[]{:S(2)}, u32[]{:S(2)}) %collective-permute-start.5) | collective-permute-done | bytes 884768 | tf_op jit(solution)/shard_map/ppermute | solution.py:439
  22.9 2.4 %collect.1._ = bf16[16,144,512]{2,1,0:T(8,128)(2,1)S(1)} custom-call(s32[1]{0:T(128)} %bitcast.pos_ref, bf16[144,512]{1,0:T(8,128)(2,1)S(1)} %pack.1.refs_0_, bf16[144,512]{1,0:T(8,128)(2,1)S(1)} %collective-permute-done.refs_1_, bf16[144,512]{1,0:T(8,128)(2,1)S(1)} %collective-permute-done.1.refs_2_, bf16[144,512]{1,0:T(8,128)(2,1)S(1)} %collective-permute-done.4.refs_3_, ...), custom_call_target="tpu_custom_call" | custom-call | bytes 1000 | tf_op jit(solution)/shard_map/collect/pallas_call | solution.py:495
  25.3 0.0 collective-permute-done.7.refs_1_
  25.3 2.8 %routed.1 = (bf16[24,1024]{1,0:T(8,128)(2,1)S(1)}, bf16[24,1024]{1,0:T(8,128)(2,1)S(1)}, bf16[24,1024]{1,0:T(8,128)(2,1)S(1)}, bf16[24,1024]{1,0:T(8,128)(2,1)S(1)}, bf16[16,144,512]{2,1,0:T(8,128)(2,1)S(1)}) custom-call(s32[1]{0:T(128)} %bitcast.pos_ref, f32[1,4096]{1,0:T(1,128)} %bitcast.5, ...), custom_call_target="tpu_custom_call", output_to_operand_aliasing={{4}: (5, {})} | custom-call | tf_op jit(solution)/shard_map/routed/pallas_call | solution.py:506
  28.2 2.3 %collective-permute-start.8 = (bf16[24,1024]{1,0:T(8,128)(2,1)S(1)}, bf16[24,1024]{1,0:T(8,128)(2,1)S(1)}, u32[]{:S(2)}, u32[]{:S(2)}) collective-permute-start(bf16[24,1024]{1,0:T(8,128)(2,1)S(1)} %get-tuple-element.56), channel_id=1, source_target_pairs={{0,4},{1,5},{2,6},{3,7},{4,8},{5,9},{6,10},{7,11},{8,12},{9,13},{1... | collective-permute-start | bytes 147464 | tf_op jit(solution)/shard_map/ppermute | solution.py:439
  30.4 8.5 %collective-permute-start.9 = (bf16[24,1024]{1,0:T(8,128)(2,1)S(1)}, bf16[24,1024]{1,0:T(8,128)(2,1)S(1)}, u32[]{:S(2)}, u32[]{:S(2)}) collective-permute-start(bf16[24,1024]{1,0:T(8,128)(2,1)S(1)} %get-tuple-element.57), channel_id=1, source_target_pairs={{0,8},{1,9},{2,10},{3,11},{4,12},{5,13},{6,14},{7,15},{8,0},{9,1},... | collective-permute-start | bytes 147464 | tf_op jit(solution)/shard_map/ppermute | solution.py:439
  38.9 2.8 %collective-permute-start.10 = (bf16[24,1024]{1,0:T(8,128)(2,1)S(1)}, bf16[24,1024]{1,0:T(8,128)(2,1)S(1)}, u32[]{:S(2)}, u32[]{:S(2)}) collective-permute-start(bf16[24,1024]{1,0:T(8,128)(2,1)S(1)} %get-tuple-element.58), channel_id=1, source_target_pairs={{0,12},{1,13},{2,14},{3,15},{4,0},{5,1},{6,2},{7,3},{8,4},{9,5},{1... | collective-permute-start | bytes 147464 | tf_op jit(solution)/shard_map/ppermute | solution.py:439
  41.8 1.1 %collective-permute-start.11 = (bf16[24,1024]{1,0:T(8,128)(2,1)S(1)}, bf16[24,1024]{1,0:T(8,128)(2,1)S(1)}, u32[]{:S(2)}, u32[]{:S(2)}) collective-permute-start(bf16[24,1024]{1,0:T(8,128)(2,1)S(1)} %get-tuple-element.52._.refs_0_), channel_id=1, source_target_pairs={{0,2},{1,3},{2,0},{3,1},{4,6},{5,7},{6,4},{7,5},{8,10},{9,11},{10,... | collective-permute-start | bytes 147464 | tf_op jit(solution)/shard_map/ppermute | solution.py:439
  42.9 3.9 %own.3 = (f32[128,1280]{1,0:T(8,128)S(1)}, f32[8,128]{1,0:T(8,128)S(1)}, bf16[4096,384]{1,0:T(8,128)(2,1)S(1)}, bf16[4096,384]{1,0:T(8,128)(2,1)S(1)}, bf16[384,4096]{1,0:T(8,128)(2,1)S(1)}) custom-call(s32[1]{0:T(128)} %bitcast.pos_ref, bf16[16,144,512]{2,1,0:T(8,128)(2,1)S(1)} %get-tuple-element.51.held, bf16[128,4096]{1,0:T(8,128)(2,1)S(1)} %copy-done, ...), custom_call_target="tpu_custom_call" | custom-call | flops 2000000000 | bytes 8000000 | tf_op jit(solution)/shard_map/own/pallas_call | solution.py:527
  46.7 0.0 collective-permute-done.8
  46.8 0.0 collective-permute-done.10
  46.8 0.0 collective-permute-done.11.refs_2_
  46.8 0.1 collective-permute-start.13
  46.9 1.0 %collective-permute-start.12 = (bf16[72,1024]{1,0:T(8,128)(2,1)S(1)}, bf16[72,1024]{1,0:T(8,128)(2,1)S(1)}, u32[]{:S(2)}, u32[]{:S(2)}) collective-permute-start(bf16[72,1024]{1,0:T(8,128)(2,1)S(1)} %constant_dynamic-update-slice_fusion.6.refs_1_), channel_id=1, source_target_pairs={{0,2},{1,3},{2,0},{3,1},{4,6},{5,7},{6,4},{7,5},{8,10},{9,11},{10,... | collective-permute-start | bytes 442376 | tf_op jit(solution)/shard_map/ppermute | solution.py:439
  47.9 1.5 %own.4 = (f32[128,1408]{1,0:T(8,128)S(1)}, f32[8,128]{1,0:T(8,128)S(1)}) custom-call(s32[1]{0:T(128)} %bitcast.pos_ref, bf16[16,144,512]{2,1,0:T(8,128)(2,1)S(1)} %get-tuple-element.51.held, bf16[128,4096]{1,0:T(8,128)(2,1)S(1)} %copy-done, bf16[128,4096]{1,0:T(8,128)(2,1)S(1)} %copy-done.1, f32[8,128]{1,0:T(8,128)S(1)} %get-tuple-element.54._), custom_call_target="tpu_custom_call" | custom-call | flops 2000000000 | bytes 8000000 | tf_op jit(solution)/shard_map/own/pallas_call | solution.py:527
  49.5 3.7 %collective-permute-done.12.refs_3_ = bf16[72,1024]{1,0:T(8,128)(2,1)S(1)} collective-permute-done((bf16[72,1024]{1,0:T(8,128)(2,1)S(1)}, bf16[72,1024]{1,0:T(8,128)(2,1)S(1)}, u32[]{:S(2)}, u32[]{:S(2)}) %collective-permute-start.12) | collective-permute-done | bytes 147488 | tf_op jit(solution)/shard_map/ppermute | solution.py:439
  53.2 0.0 collective-permute-done.13.refs_4_
  53.2 0.1 collective-permute-start.14
  53.3 1.4 %collective-permute-done.14.refs_5_ = bf16[96,1024]{1,0:T(8,128)(2,1)S(1)} collective-permute-done((bf16[96,1024]{1,0:T(8,128)(2,1)S(1)}, bf16[96,1024]{1,0:T(8,128)(2,1)S(1)}, u32[]{:S(2)}, u32[]{:S(2)}) %collective-permute-start.14) | collective-permute-done | bytes 196640 | tf_op jit(solution)/shard_map/ppermute | solution.py:439
  54.7 2.7 %expert.1 = (bf16[192,1024]{1,0:T(8,128)(2,1)S(1)}, bf16[192,1024]{1,0:T(8,128)(2,1)S(1)}) custom-call(bf16[24,1024]{1,0:T(8,128)(2,1)S(1)} %get-tuple-element.52._.refs_0_, bf16[72,1024]{1,0:T(8,128)(2,1)S(1)} %constant_dynamic-update-slice_fusion.6.refs_1_, bf16[24,1024]{1,0:T(8,128)(2,1)S(1)} %collective-permute-done.11.refs_2_, ...), custom_call_target="tpu_custom_call" | custom-call | flops 1200000000 | bytes 12000000 | tf_op jit(solution)/shard_map/expert/pallas_call | solution.py:568
  57.4 0.2 collective-permute-start.15
  57.6 1.6 %collective-permute-done.15 = bf16[192,1024]{1,0:T(8,128)(2,1)S(1)} collective-permute-done((bf16[192,1024]{1,0:T(8,128)(2,1)S(1)}, bf16[192,1024]{1,0:T(8,128)(2,1)S(1)}, u32[]{:S(2)}, u32[]{:S(2)}) %collective-permute-start.15) | collective-permute-done | bytes 393248 | tf_op jit(solution)/shard_map/ppermute | solution.py:439
  59.2 0.1 convert_add_fusion
  59.3 1.0 %collective-permute-start.16 = (bf16[96,1024]{1,0:T(8,128)(2,1)S(1)}, bf16[96,1024]{1,0:T(8,128)(2,1)S(1)}, u32[]{:S(2)}, u32[]{:S(2)}) collective-permute-start(bf16[96,1024]{1,0:T(8,128)(2,1)S(1)} %slice.35), channel_id=1, source_target_pairs={{0,2},{1,3},{2,0},{3,1},{4,6},{5,7},{6,4},{7,5},{8,10},{9,11},{10,... | collective-permute-start | bytes 589832 | tf_op jit(solution)/shard_map/ppermute | solution.py:439
  60.3 1.4 %own.5 = (f32[128,1408]{1,0:T(8,128)S(1)}, f32[8,128]{1,0:T(8,128)S(1)}) custom-call(s32[1]{0:T(128)} %bitcast.pos_ref, bf16[16,144,512]{2,1,0:T(8,128)(2,1)S(1)} %get-tuple-element.51.held, bf16[128,4096]{1,0:T(8,128)(2,1)S(1)} %copy-done, bf16[128,4096]{1,0:T(8,128)(2,1)S(1)} %copy-done.1, bf16[192,1024]{1,0:T(8,128)(2,1)S(1)} %get-tuple-element.73._), custom_call_target="tpu_custom_call" | custom-call | flops 2000000000 | bytes 8000000 | tf_op jit(solution)/shard_map/own/pallas_call | solution.py:527
  61.7 4.6 %collective-permute-done.16 = bf16[96,1024]{1,0:T(8,128)(2,1)S(1)} collective-permute-done((bf16[96,1024]{1,0:T(8,128)(2,1)S(1)}, bf16[96,1024]{1,0:T(8,128)(2,1)S(1)}, u32[]{:S(2)}, u32[]{:S(2)}) %collective-permute-start.16) | collective-permute-done | bytes 196640 | tf_op jit(solution)/shard_map/ppermute | solution.py:439
  66.4 0.1 collective-permute-start.19
  66.5 1.4 %collective-permute-start.18 = (bf16[24,1024]{1,0:T(8,128)(2,1)S(1)}, bf16[24,1024]{1,0:T(8,128)(2,1)S(1)}, u32[]{:S(2)}, u32[]{:S(2)}) collective-permute-start(bf16[24,1024]{1,0:T(8,128)(2,1)S(1)} %get-tuple-element.80), channel_id=1, source_target_pairs={{0,8},{1,9},{2,10},{3,11},{4,12},{5,13},{6,14},{7,15},{8,0},{9,1},... | collective-permute-start | bytes 147464 | tf_op jit(solution)/shard_map/ppermute | solution.py:439
  67.9 2.4 %collective-permute-start.17 = (bf16[24,1024]{1,0:T(8,128)(2,1)S(1)}, bf16[24,1024]{1,0:T(8,128)(2,1)S(1)}, u32[]{:S(2)}, u32[]{:S(2)}) collective-permute-start(bf16[24,1024]{1,0:T(8,128)(2,1)S(1)} %get-tuple-element.81), channel_id=1, source_target_pairs={{0,12},{1,13},{2,14},{3,15},{4,0},{5,1},{6,2},{7,3},{8,4},{9,5},{1... | collective-permute-start | bytes 147464 | tf_op jit(solution)/shard_map/ppermute | solution.py:439
  70.3 2.2 %collective-permute-done.19.refs_6_ = bf16[24,1024]{1,0:T(8,128)(2,1)S(1)} collective-permute-done((bf16[24,1024]{1,0:T(8,128)(2,1)S(1)}, bf16[24,1024]{1,0:T(8,128)(2,1)S(1)}, u32[]{:S(2)}, u32[]{:S(2)}) %collective-permute-start.19) | collective-permute-done | bytes 49184 | tf_op jit(solution)/shard_map/ppermute | solution.py:439
  72.5 0.0 collective-permute-done.18.refs_5_
  72.5 0.5 collective-permute-done.17.refs_4_
  73.0 1.4 %combine.1 = bf16[128,4096]{1,0:T(8,128)(2,1)} custom-call(bf16[128,64]{1,0:T(8,128)(2,1)S(1)} %get-tuple-element.42.mix_ref, f32[128,1280]{1,0:T(8,128)S(1)} %get-tuple-element.53.refs_0_, f32[128,1408]{1,0:T(8,128)S(1)} %get-tuple-element.55.refs_1_, f32[128,1408]{1,0:T(8,128)S(1)} %get-tuple-element.74.refs_2_, ...), custom_call_target="tpu_custom_call" | custom-call | tf_op jit(solution)/shard_map/combine/pallas_call | solution.py:598
  (20 shorter events, 0.2 us)
Async XLA Ops:
  1.0 11.0 %collective-permute-start = (bf16[144,512]{1,0:T(8,128)(2,1)S(1)}, bf16[144,512]{1,0:T(8,128)(2,1)S(1)}, u32[]{:S(2)}, u32[]{:S(2)}) collective-permute-start(bf16[144,512]{1,0:T(8,128)(2,1)S(1)} %pack.1.refs_0_), channel_id=1, source_target_pairs={{0,4},{1,5},{2,6},{3,7},{4,8},{5,9},{6,10},{7,11},{8,12},{9,13},{1... | collective-permute-start | bytes 442376 | tf_op jit(solution)/shard_map/ppermute | solution.py:439
  4.1 16.3 %collective-permute-start.4 = (bf16[144,512]{1,0:T(8,128)(2,1)S(1)}, bf16[144,512]{1,0:T(8,128)(2,1)S(1)}, u32[]{:S(2)}, u32[]{:S(2)}) collective-permute-start(bf16[144,512]{1,0:T(8,128)(2,1)S(1)} %pack.1.refs_0_), channel_id=1, source_target_pairs={{0,0},{1,1},{2,12},{3,13},{4,4},{5,5},{6,6},{7,7},{8,8},{9,9},{10,... | collective-permute-start | bytes 442376 | tf_op jit(solution)/shard_map/ppermute | solution.py:439
  4.7 10.8 %collective-permute-start.2 = (bf16[144,512]{1,0:T(8,128)(2,1)S(1)}, bf16[144,512]{1,0:T(8,128)(2,1)S(1)}, u32[]{:S(2)}, u32[]{:S(2)}) collective-permute-start(bf16[144,512]{1,0:T(8,128)(2,1)S(1)} %pack.1.refs_0_), channel_id=1, source_target_pairs={{0,2},{1,3},{2,0},{3,1},{4,6},{5,7},{6,4},{7,5},{8,10},{9,11},{10,... | collective-permute-start | bytes 442376 | tf_op jit(solution)/shard_map/ppermute | solution.py:439
  9.5 10.8 %collective-permute-start.1 = (bf16[144,512]{1,0:T(8,128)(2,1)S(1)}, bf16[144,512]{1,0:T(8,128)(2,1)S(1)}, u32[]{:S(2)}, u32[]{:S(2)}) collective-permute-start(bf16[144,512]{1,0:T(8,128)(2,1)S(1)} %pack.1.refs_0_), channel_id=1, source_target_pairs={{0,8},{1,9},{2,10},{3,11},{4,12},{5,13},{6,14},{7,15},{8,0},{9,1},... | collective-permute-start | bytes 442376 | tf_op jit(solution)/shard_map/ppermute | solution.py:439
  12.0 8.3 %collective-permute-start.3 = (bf16[144,512]{1,0:T(8,128)(2,1)S(1)}, bf16[144,512]{1,0:T(8,128)(2,1)S(1)}, u32[]{:S(2)}, u32[]{:S(2)}) collective-permute-start(bf16[144,512]{1,0:T(8,128)(2,1)S(1)} %collective-permute-done.refs_1_), channel_id=1, source_target_pairs={{0,0},{1,1},{2,2},{3,3},{4,6},{5,7},{6,4},{7,5},{8,10},{9,11},{10,... | collective-permute-start | bytes 442376 | tf_op jit(solution)/shard_map/ppermute | solution.py:439
  20.4 22.5 %copy-start = (bf16[128,4096]{1,0:T(8,128)(2,1)S(1)}, bf16[128,4096]{1,0:T(8,128)(2,1)}, u32[]{:S(2)}) copy-start(bf16[128,4096]{1,0:T(8,128)(2,1)} %q_ref.5) | copy-start | bytes 3145732
  20.4 22.4 %copy-start.1 = (bf16[128,4096]{1,0:T(8,128)(2,1)S(1)}, bf16[128,4096]{1,0:T(8,128)(2,1)}, u32[]{:S(2)}) copy-start(bf16[128,4096]{1,0:T(8,128)(2,1)} %x_ref.5) | copy-start | bytes 3145732
  20.4 2.5 %collective-permute-start.5 = (bf16[864,512]{1,0:T(8,128)(2,1)S(1)}, bf16[864,512]{1,0:T(8,128)(2,1)S(1)}, u32[]{:S(2)}, u32[]{:S(2)}) collective-permute-start(bf16[864,512]{1,0:T(8,128)(2,1)S(1)} %constant_dynamic-update-slice_fusion), channel_id=1, source_target_pairs={{0,1},{1,0},{2,3},{3,2},{4,5},{5,4},{6,7},{7,6},{8,9},{9,8},{10,11... | collective-permute-start | bytes 2654216 | tf_op jit(solution)/shard_map/ppermute | solution.py:439
  20.5 0.8 %collective-permute-start.6 = (bf16[144,512]{1,0:T(8,128)(2,1)S(1)}, bf16[144,512]{1,0:T(8,128)(2,1)S(1)}, u32[]{:S(2)}, u32[]{:S(2)}) collective-permute-start(bf16[144,512]{1,0:T(8,128)(2,1)S(1)} %collective-permute-done.1.refs_2_), channel_id=1, source_target_pairs={{0,0},{1,1},{2,2},{3,3},{4,4},{5,5},{6,6},{7,7},{8,10},{9,11},{10,... | collective-permute-start | bytes 442376 | tf_op jit(solution)/shard_map/ppermute | solution.py:439
  21.3 4.0 %collective-permute-start.7 = (bf16[144,512]{1,0:T(8,128)(2,1)S(1)}, bf16[144,512]{1,0:T(8,128)(2,1)S(1)}, u32[]{:S(2)}, u32[]{:S(2)}) collective-permute-start(bf16[144,512]{1,0:T(8,128)(2,1)S(1)} %collective-permute-done.6.refs_0_), channel_id=1, source_target_pairs={{0,1},{1,0},{2,3},{3,2},{4,5},{5,4},{6,7},{7,6},{8,9},{9,8},{10,11... | collective-permute-start | bytes 442376 | tf_op jit(solution)/shard_map/ppermute | solution.py:439
  28.2 18.6 %collective-permute-start.8 = (bf16[24,1024]{1,0:T(8,128)(2,1)S(1)}, bf16[24,1024]{1,0:T(8,128)(2,1)S(1)}, u32[]{:S(2)}, u32[]{:S(2)}) collective-permute-start(bf16[24,1024]{1,0:T(8,128)(2,1)S(1)} %get-tuple-element.56), channel_id=1, source_target_pairs={{0,4},{1,5},{2,6},{3,7},{4,8},{5,9},{6,10},{7,11},{8,12},{9,13},{1... | collective-permute-start | bytes 147464 | tf_op jit(solution)/shard_map/ppermute | solution.py:439
  30.4 16.3 %collective-permute-start.9 = (bf16[24,1024]{1,0:T(8,128)(2,1)S(1)}, bf16[24,1024]{1,0:T(8,128)(2,1)S(1)}, u32[]{:S(2)}, u32[]{:S(2)}) collective-permute-start(bf16[24,1024]{1,0:T(8,128)(2,1)S(1)} %get-tuple-element.57), channel_id=1, source_target_pairs={{0,8},{1,9},{2,10},{3,11},{4,12},{5,13},{6,14},{7,15},{8,0},{9,1},... | collective-permute-start | bytes 147464 | tf_op jit(solution)/shard_map/ppermute | solution.py:439
  38.9 7.8 %collective-permute-start.10 = (bf16[24,1024]{1,0:T(8,128)(2,1)S(1)}, bf16[24,1024]{1,0:T(8,128)(2,1)S(1)}, u32[]{:S(2)}, u32[]{:S(2)}) collective-permute-start(bf16[24,1024]{1,0:T(8,128)(2,1)S(1)} %get-tuple-element.58), channel_id=1, source_target_pairs={{0,12},{1,13},{2,14},{3,15},{4,0},{5,1},{6,2},{7,3},{8,4},{9,5},{1... | collective-permute-start | bytes 147464 | tf_op jit(solution)/shard_map/ppermute | solution.py:439
  41.8 5.0 %collective-permute-start.11 = (bf16[24,1024]{1,0:T(8,128)(2,1)S(1)}, bf16[24,1024]{1,0:T(8,128)(2,1)S(1)}, u32[]{:S(2)}, u32[]{:S(2)}) collective-permute-start(bf16[24,1024]{1,0:T(8,128)(2,1)S(1)} %get-tuple-element.52._.refs_0_), channel_id=1, source_target_pairs={{0,2},{1,3},{2,0},{3,1},{4,6},{5,7},{6,4},{7,5},{8,10},{9,11},{10,... | collective-permute-start | bytes 147464 | tf_op jit(solution)/shard_map/ppermute | solution.py:439
  46.8 6.4 %collective-permute-start.13 = (bf16[96,1024]{1,0:T(8,128)(2,1)S(1)}, bf16[96,1024]{1,0:T(8,128)(2,1)S(1)}, u32[]{:S(2)}, u32[]{:S(2)}) collective-permute-start(bf16[96,1024]{1,0:T(8,128)(2,1)S(1)} %pad_maximum_fusion), channel_id=1, source_target_pairs={{0,1},{1,0},{2,3},{3,2},{4,5},{5,4},{6,7},{7,6},{8,9},{9,8},{10,11... | collective-permute-start | bytes 589832 | tf_op jit(solution)/shard_map/ppermute | solution.py:439
  46.9 6.3 %collective-permute-start.12 = (bf16[72,1024]{1,0:T(8,128)(2,1)S(1)}, bf16[72,1024]{1,0:T(8,128)(2,1)S(1)}, u32[]{:S(2)}, u32[]{:S(2)}) collective-permute-start(bf16[72,1024]{1,0:T(8,128)(2,1)S(1)} %constant_dynamic-update-slice_fusion.6.refs_1_), channel_id=1, source_target_pairs={{0,2},{1,3},{2,0},{3,1},{4,6},{5,7},{6,4},{7,5},{8,10},{9,11},{10,... | collective-permute-start | bytes 442376 | tf_op jit(solution)/shard_map/ppermute | solution.py:439
  53.2 1.5 %collective-permute-start.14 = (bf16[96,1024]{1,0:T(8,128)(2,1)S(1)}, bf16[96,1024]{1,0:T(8,128)(2,1)S(1)}, u32[]{:S(2)}, u32[]{:S(2)}) collective-permute-start(bf16[96,1024]{1,0:T(8,128)(2,1)S(1)} %pad_maximum_fusion.1), channel_id=1, source_target_pairs={{0,1},{1,0},{2,3},{3,2},{4,5},{5,4},{6,7},{7,6},{8,9},{9,8},{10,11... | collective-permute-start | bytes 589832 | tf_op jit(solution)/shard_map/ppermute | solution.py:439
  57.4 1.8 %collective-permute-start.15 = (bf16[192,1024]{1,0:T(8,128)(2,1)S(1)}, bf16[192,1024]{1,0:T(8,128)(2,1)S(1)}, u32[]{:S(2)}, u32[]{:S(2)}) collective-permute-start(bf16[192,1024]{1,0:T(8,128)(2,1)S(1)} %get-tuple-element.75), channel_id=1, source_target_pairs={{0,1},{1,0},{2,3},{3,2},{4,5},{5,4},{6,7},{7,6},{8,9},{9,8},{10,11... | collective-permute-start | bytes 1179656 | tf_op jit(solution)/shard_map/ppermute | solution.py:439
  59.3 7.0 %collective-permute-start.16 = (bf16[96,1024]{1,0:T(8,128)(2,1)S(1)}, bf16[96,1024]{1,0:T(8,128)(2,1)S(1)}, u32[]{:S(2)}, u32[]{:S(2)}) collective-permute-start(bf16[96,1024]{1,0:T(8,128)(2,1)S(1)} %slice.35), channel_id=1, source_target_pairs={{0,2},{1,3},{2,0},{3,1},{4,6},{5,7},{6,4},{7,5},{8,10},{9,11},{10,... | collective-permute-start | bytes 589832 | tf_op jit(solution)/shard_map/ppermute | solution.py:439
  66.4 6.0 %collective-permute-start.19 = (bf16[24,1024]{1,0:T(8,128)(2,1)S(1)}, bf16[24,1024]{1,0:T(8,128)(2,1)S(1)}, u32[]{:S(2)}, u32[]{:S(2)}) collective-permute-start(bf16[24,1024]{1,0:T(8,128)(2,1)S(1)} %get-tuple-element.79), channel_id=1, source_target_pairs={{0,4},{1,5},{2,6},{3,7},{4,8},{5,9},{6,10},{7,11},{8,12},{9,13},{1... | collective-permute-start | bytes 147464 | tf_op jit(solution)/shard_map/ppermute | solution.py:439
  66.5 6.0 %collective-permute-start.18 = (bf16[24,1024]{1,0:T(8,128)(2,1)S(1)}, bf16[24,1024]{1,0:T(8,128)(2,1)S(1)}, u32[]{:S(2)}, u32[]{:S(2)}) collective-permute-start(bf16[24,1024]{1,0:T(8,128)(2,1)S(1)} %get-tuple-element.80), channel_id=1, source_target_pairs={{0,8},{1,9},{2,10},{3,11},{4,12},{5,13},{6,14},{7,15},{8,0},{9,1},... | collective-permute-start | bytes 147464 | tf_op jit(solution)/shard_map/ppermute | solution.py:439
  67.9 5.1 %collective-permute-start.17 = (bf16[24,1024]{1,0:T(8,128)(2,1)S(1)}, bf16[24,1024]{1,0:T(8,128)(2,1)S(1)}, u32[]{:S(2)}, u32[]{:S(2)}) collective-permute-start(bf16[24,1024]{1,0:T(8,128)(2,1)S(1)} %get-tuple-element.81), channel_id=1, source_target_pairs={{0,12},{1,13},{2,14},{3,15},{4,0},{5,1},{6,2},{7,3},{8,4},{9,5},{1... | collective-permute-start | bytes 147464 | tf_op jit(solution)/shard_map/ppermute | solution.py:439

commit v7 on v6

--- a/solution.py
+++ b/solution.py
@@ -103,7 +103,7 @@
 
 def select_kernel(planes, pos_ref, *refs):
     sources, (qs_ref, xs_ref, facts_ref, mix_ref, gather_ref, spread_ref) = refs[:5], refs[5:11]
-    routes_ref, docs_ref, q_ref, x_ref, gates_ref, sems = refs[11:]
+    routes_ref, docs_ref, q_ref, x_ref, gates_ref, stack, sems = refs[11:]
     moves = [
         pltpu.make_async_copy(source, target, sems.at[i])
         for i, (source, target) in enumerate(zip(sources, refs[11:16]))
@@ -129,32 +129,31 @@
     gather_ref[...] = one_hot(travel_row(numbers((size, 1), 0), size // PIECE, CAP), size)
     spread_ref[...] = one_hot(travel_row(numbers((1, size), 1), size // PIECE, CAP), size)
     docs = docs_ref[...].astype(F32)
-    lane_slot = (lax.broadcasted_iota(jnp.int32, (TILE, TILE), 0) % SLOTS).astype(F32)
     token = lax.broadcasted_iota(jnp.int32, (1, TILE), 1).astype(F32)
     facts = jnp.concatenate(
         [token, docs, jnp.ones((1, TILE), F32), jnp.zeros((5, TILE), F32)], axis=0
     ).astype(BF16)
     picks = [
-        jnp.where(ranks[k : k + 1] == lane_slot, members[k : k + 1], 0.0) for k in range(planes)
+        jnp.where(ranks[k : k + 1] == slot, members[k : k + 1], 0.0) for k in range(planes)
     ]
-    chooser = jnp.concatenate([p[:SLOTS] for p in picks], axis=0).astype(BF16)
+    rows = planes * CAP
+    plane, place = split(numbers((rows, 1), 0), CAP)
+    compact = one_hot(plane * SLOTS + place, planes * SLOTS)
+    chooser = dot(compact, jnp.concatenate(picks, axis=0).astype(BF16)).astype(BF16)
+    lane, _ = split(numbers((rows * GROUP, 1), 0), GROUP)
+    lane_pick = dot(one_hot(lane, rows), chooser).astype(BF16)
+    known = dot(facts, lane_pick, 1, 1)
+    facts_ref[...] = jnp.concatenate(
+        [known[0:1], known[1:2] + (1.0 - known[2:3]) * docs[:, 0:1], known[2:]], axis=0
+    )
     q_rows = dot(chooser, q_ref[...])
     xs_ref[...] = dot(chooser, x_ref[...])
-    for k in range(planes):
-        known = dot(facts, picks[k].astype(BF16), 1, 1)
-        facts_ref[:, k * TILE : (k + 1) * TILE] = jnp.concatenate(
-            [known[0:1], known[1:2] + (1.0 - known[2:3]) * docs[:, 0:1], known[2:]], axis=0
-        )
-        for h in range(KV_HEADS):
-            stack = jnp.concatenate(
-                [
-                    q_rows[k * SLOTS : (k + 1) * SLOTS, a * HEAD : (a + 1) * HEAD]
-                    for a in range(h * GROUP, (h + 1) * GROUP)
-                ],
-                axis=0,
-            )
-            for i, term in enumerate(two_terms(stack.T)):
-                qs_ref[h, i * HEAD : (i + 1) * HEAD, k * TILE : (k + 1) * TILE] = term
+    for h in range(KV_HEADS):
+        for g in range(GROUP):
+            a = h * GROUP + g
+            stack[pl.ds(g, rows, stride=GROUP), :] = q_rows[:, a * HEAD : (a + 1) * HEAD]
+        for i, term in enumerate(two_terms(stack[...].T)):
+            qs_ref[h, i * HEAD : (i + 1) * HEAD, :] = term
 
 
 def doc_starts(n, pos, held):
@@ -264,7 +263,7 @@
     planes = n // SHARDS
     count = len(senders)
     pieces, outs, held = refs[:2], refs[2 : 2 + planes], refs[2 + planes]
-    acc, bias, q_scr, state, gain, sems = refs[3 + planes :]
+    acc, bias, q_scr, stack, state, gain, sems = refs[3 + planes :]
     pos = pos_ref[0]
     copies = place_pieces(n, senders, pos, pieces, held, sems)
     copies.append(pltpu.make_async_copy(gain_ref, gain, sems.at[count]))
@@ -273,8 +272,14 @@
         copy.wait()
     starts = doc_starts(n, pos, held)
     lanes = q_scr.shape[2]
+    rows = lanes // GROUP
     base = (pos * TILE).astype(F32)
-    for part in range(planes * TILE // lanes):
+    width = state.shape[1] // CUT
+    row = numbers((CUT * rows, 1), 0)
+    plane, rest = split(row, PIECE)
+    chunk, slot = split(rest, CAP)
+    order = one_hot(chunk * rows + plane * CAP + slot, CUT * rows)
+    for part in range(xs_ref.shape[0] // rows):
         at = slice(part * lanes, (part + 1) * lanes)
         q_scr[...] = qs_ref[:, :, at]
         done = flash(
@@ -286,22 +291,20 @@
             starts_of(facts_ref[1:2, at], starts),
         )
         for h in range(KV_HEADS):
-            for k in range(lanes // TILE):
-                row = (part * (lanes // TILE) + k) * SLOTS
-                for g in range(GROUP):
-                    lane = (h * GROUP + g) * HEAD
-                    state[row : row + SLOTS, lane : lane + HEAD] = (
-                        xs_ref[row : row + SLOTS, lane : lane + HEAD]
-                        + done[h][k * TILE + g * SLOTS : k * TILE + (g + 1) * SLOTS]
-                    )
-    width = state.shape[1] // CUT
-    order = one_hot(travel_row(numbers((1, CUT * SLOTS), 1), 1, SLOTS), PIECE)
-    for k in range(planes):
-        hidden = state[k * SLOTS : (k + 1) * SLOTS, :]
+            stack[...] = done[h]
+            for g in range(GROUP):
+                lane = (h * GROUP + g) * HEAD
+                state[:, lane : lane + HEAD] = (
+                    xs_ref[part * rows : (part + 1) * rows, lane : lane + HEAD]
+                    + stack[pl.ds(g, rows, stride=GROUP), :]
+                )
+        hidden = state[...]
         mean = jnp.mean(hidden * hidden, axis=1, keepdims=True)
         normed = hidden * lax.rsqrt(mean + 1e-06) * gain[...]
         chunks = [normed[:, q * width : (q + 1) * width] for q in range(CUT)]
-        outs[k][...] = dot(order, jnp.concatenate(chunks, axis=0).astype(BF16)).astype(BF16)
+        sent = dot(order, jnp.concatenate(chunks, axis=0).astype(BF16))
+        for k in range(rows // CAP):
+            outs[part * (rows // CAP) + k][...] = sent[k * PIECE : (k + 1) * PIECE].astype(BF16)
 
 
 def expert_kernel(n, count, *refs):
@@ -449,9 +452,9 @@
     q_rows, x_rows, facts, mix, gather, spread = pl.pallas_call(
         functools.partial(select_kernel, planes),
         out_shape=[
-            jax.ShapeDtypeStruct((KV_HEADS, 2 * HEAD, planes * TILE), BF16),
-            jax.ShapeDtypeStruct((planes * SLOTS, width), F32),
-            jax.ShapeDtypeStruct((8, planes * TILE), F32),
+            jax.ShapeDtypeStruct((KV_HEADS, 2 * HEAD, planes * CAP * GROUP), BF16),
+            jax.ShapeDtypeStruct((planes * CAP, width), F32),
+            jax.ShapeDtypeStruct((8, planes * CAP * GROUP), F32),
             jax.ShapeDtypeStruct((tokens, 2 * planes * SLOTS), BF16),
             jax.ShapeDtypeStruct((size, size), BF16),
             jax.ShapeDtypeStruct((size, size), BF16),
@@ -464,6 +467,7 @@
             pltpu.VMEM(queries.shape, BF16),
             pltpu.VMEM(resid.shape, BF16),
             pltpu.VMEM(gates_t.shape, F32),
+            pltpu.VMEM((planes * CAP * GROUP, HEAD), F32),
             pltpu.SemaphoreType.DMA((5,)),
         ],
         compiler_params=params(small),
@@ -487,7 +491,6 @@
     early, late = along + [jumped] + across[:-1], across[-1:]
     sides = [(0, k) for k in range(far)] + [(1, far)] + [(1, k) for k in range(far - 1)]
     early.append(move(jnp.concatenate(early, axis=0), flip_c))
-    late.append(move(across[-1], flip_c))
     early_senders = [(i, 0, 0, *side) for i, side in enumerate(sides)]
     early_senders += [(len(sides), i * KV_ROWS, 1, *side) for i, side in enumerate(sides)]
     late_senders = [(flip, 0, flip, 1, far - 1) for flip in (0, 1)]
@@ -503,6 +506,9 @@
         name="collect",
     )(pos, *early)
 
+    lanes = min(planes, 4) * CAP * GROUP
+    late[0], held = lax.optimization_barrier((late[0], held))
+    late.append(move(late[0], flip_c))
     *sent, held = pl.pallas_call(
         functools.partial(routed_kernel, n, late_senders),
         out_shape=[jax.ShapeDtypeStruct((PIECE, width // CUT), BF16)] * planes
@@ -510,10 +516,11 @@
         in_specs=[SMEM, HBM] + [VMEM] * 4 + [ANY] * len(late),
         out_specs=[VMEM] * (planes + 1),
         scratch_shapes=[
-            pltpu.VMEM((KV_HEADS, HEAD + EXTRA, 4 * TILE), F32),
-            pltpu.VMEM((KEYS, 4 * TILE), F32),
-            pltpu.VMEM((KV_HEADS, 2 * HEAD, 4 * TILE), BF16),
-            pltpu.VMEM((planes * SLOTS, width), F32),
+            pltpu.VMEM((KV_HEADS, HEAD + EXTRA, lanes), F32),
+            pltpu.VMEM((KEYS, lanes), F32),
+            pltpu.VMEM((KV_HEADS, 2 * HEAD, lanes), BF16),
+            pltpu.VMEM((lanes, HEAD), F32),
+            pltpu.VMEM((lanes // GROUP, width), F32),
             pltpu.VMEM((1, width), F32),
             pltpu.SemaphoreType.DMA((len(late_senders) + 1,)),
         ],
@@ -550,7 +557,7 @@
         )(pos, held, queries, resid, after, *map(pin, sources))
 
     half0, done, *weights = own(range(10), sent[0], w_gate, w_up, w_down)
-    half1, late = own(range(10, 21), done)
+    half1, late = own(range(10, 18), done)
     halves = [half0, half1]
 
     come = [
@@ -578,7 +585,7 @@
         name="expert",
     )(*pieces, *weights, gather, spread, late)
 
-    half2, done = own(range(21, QUERY_HEADS), keep)
+    half2, done = own(range(18, QUERY_HEADS), keep)
     halves.append(half2)
 
     total = keep.astype(F32) + move(send, [(s, s ^ 1) for s in range(n)]).astype(F32)

time: 74.1 us -> 72.5 us (0.978); the launches traced: 74.4 us -> 71.8 us
  starting transfers between devices: 31.6 us -> 27 us
  waiting for transfers between devices: 22.7 us -> 24.8 us
    ppermute x20, starting transfers between devices: 31.6 us -> 27 us  [move(): return lax.ppermute(value, 'expert', pairs)]
    ppermute x20, waiting for transfers between devices: 22.7 us -> 24.8 us  [move(): return lax.ppermute(value, 'expert', pairs)]
  transfers between devices with their start and end apart: 20 -> 20, of which waited for: 9 -> 10; matrix products, arithmetic and copies ran while one was open for 0% -> 0% of each run, Pallas kernels for 16% -> 16%
where the time goes in v7:
time: 72.5 us; the launch traced here: 71.8 us
  starting transfers between devices  27 us (37%)
  waiting for transfers between devices  24.8 us (34%)
  Pallas kernels  19.4 us (27%)
    ppermute x20, starting transfers between devices, move(): return lax.ppermute(value, 'expert', pairs)  27 us
    ppermute x20, waiting for transfers between devices, move(): return lax.ppermute(value, 'expert', pairs)  24.8 us
    pallas_call x3, Pallas kernels, own(): pl.pallas_call(functools.partial(own_kernel, n, heads, len(sources)), out...  6.74 us
    pallas_call x1, Pallas kernels, local(): pl.pallas_call(functools.partial(expert_kernel, n, len(pieces)), out_shap...  2.71 us
    pallas_call x1, Pallas kernels, local(): pl.pallas_call(functools.partial(routed_kernel, n, late_senders), out_sha...  2.67 us
    pallas_call x1, Pallas kernels, local(): pl.pallas_call(functools.partial(select_kernel, planes), out_shape=[jax.S...  2.58 us
    pallas_call x1, Pallas kernels, local(): pl.pallas_call(functools.partial(collect_kernel, n, early_senders), out_s...  2.4 us
  transfers between devices with their start and end apart: 20, of which 10 were waited for; matrix products, arithmetic and copies ran while one was open for 0% of the time, Pallas kernels for 16%

profile of v7, /device:TPU:0, one launch (start us, length us, event | category | flops | bytes accessed | tf_op | source)
XLA Modules:
  0.0 71.8 jit_solution(9285183003628118177)
XLA Ops:
  0.0 1.0 %pack.1.refs_0_ = bf16[144,512]{1,0:T(8,128)(2,1)S(1)} custom-call(s32[1,128]{1,0:T(1,128)} %bitcast.8, bf16[128,256]{1,0:T(8,128)(2,1)} %keys_ref.1, bf16[128,256]{1,0:T(8,128)(2,1)} %values_ref.1), custom_call_target="tpu_custom_call" | custom-call | tf_op jit(solution)/shard_map/pack/pallas_call | solution.py:427
  1.0 3.1 %collective-permute-start = (bf16[144,512]{1,0:T(8,128)(2,1)S(1)}, bf16[144,512]{1,0:T(8,128)(2,1)S(1)}, u32[]{:S(2)}, u32[]{:S(2)}) collective-permute-start(bf16[144,512]{1,0:T(8,128)(2,1)S(1)} %pack.1.refs_0_), channel_id=1, source_target_pairs={{0,4},{1,5},{2,6},{3,7},{4,8},{5,9},{6,10},{7,11},{8,12},{9,13},{1... | collective-permute-start | bytes 442376 | tf_op jit(solution)/shard_map/ppermute | solution.py:442
  4.1 0.7 collective-permute-start.5
  4.7 4.8 %collective-permute-start.2 = (bf16[144,512]{1,0:T(8,128)(2,1)S(1)}, bf16[144,512]{1,0:T(8,128)(2,1)S(1)}, u32[]{:S(2)}, u32[]{:S(2)}) collective-permute-start(bf16[144,512]{1,0:T(8,128)(2,1)S(1)} %pack.1.refs_0_), channel_id=1, source_target_pairs={{0,2},{1,3},{2,0},{3,1},{4,6},{5,7},{6,4},{7,5},{8,10},{9,11},{10,... | collective-permute-start | bytes 442376 | tf_op jit(solution)/shard_map/ppermute | solution.py:442
  9.5 0.0 collective-permute-start.1
  9.5 2.6 %select.1 = (bf16[2,256,384]{2,1,0:T(8,128)(2,1)S(1)}, f32[24,4096]{1,0:T(8,128)S(1)}, f32[8,384]{1,0:T(8,128)S(1)}, bf16[128,64]{1,0:T(8,128)(2,1)S(1)}, bf16[3...) custom-call(s32[1]{0:T(128)} %bitcast.pos_ref, s32[4,128]{1,0:T(4,128)} %bitcast.6, s32[1,128]{1,0:T(1,128)} %bitcast.9, ...), custom_call_target="tpu_custom_call" | custom-call | tf_op jit(solution)/shard_map/select/pallas_call | solution.py:452
  12.1 0.0 collective-permute-done.refs_1_
  12.1 0.7 collective-permute-start.3
  12.9 2.7 %collective-permute-done.2.refs_4_ = bf16[144,512]{1,0:T(8,128)(2,1)S(1)} collective-permute-done((bf16[144,512]{1,0:T(8,128)(2,1)S(1)}, bf16[144,512]{1,0:T(8,128)(2,1)S(1)}, u32[]{:S(2)}, u32[]{:S(2)}) %collective-permute-start.2) | collective-permute-done | bytes 147488 | tf_op jit(solution)/shard_map/ppermute | solution.py:442
  15.5 4.8 %collective-permute-done.1.refs_2_ = bf16[144,512]{1,0:T(8,128)(2,1)S(1)} collective-permute-done((bf16[144,512]{1,0:T(8,128)(2,1)S(1)}, bf16[144,512]{1,0:T(8,128)(2,1)S(1)}, u32[]{:S(2)}, u32[]{:S(2)}) %collective-permute-start.1) | collective-permute-done | bytes 147488 | tf_op jit(solution)/shard_map/ppermute | solution.py:442
  20.3 0.0 collective-permute-done.3.refs_5_
  20.3 0.0 collective-permute-done.5.refs_3_
  20.4 0.0 copy-start
  20.4 0.0 copy-start.1
  20.4 0.1 collective-permute-start.6
  20.5 0.8 %collective-permute-start.4 = (bf16[144,512]{1,0:T(8,128)(2,1)S(1)}, bf16[144,512]{1,0:T(8,128)(2,1)S(1)}, u32[]{:S(2)}, u32[]{:S(2)}) collective-permute-start(bf16[144,512]{1,0:T(8,128)(2,1)S(1)} %collective-permute-done.1.refs_2_), channel_id=1, source_target_pairs={{0,0},{1,1},{2,2},{3,3},{4,4},{5,5},{6,6},{7,7},{8,10},{9,11},{10,... | collective-permute-start | bytes 442376 | tf_op jit(solution)/shard_map/ppermute | solution.py:442
  21.3 1.6 %collective-permute-done.6.refs_6_ = bf16[864,512]{1,0:T(8,128)(2,1)S(1)} collective-permute-done((bf16[864,512]{1,0:T(8,128)(2,1)S(1)}, bf16[864,512]{1,0:T(8,128)(2,1)S(1)}, u32[]{:S(2)}, u32[]{:S(2)}) %collective-permute-start.6) | collective-permute-done | bytes 884768 | tf_op jit(solution)/shard_map/ppermute | solution.py:442
  22.9 2.4 %collect.1._ = bf16[16,144,512]{2,1,0:T(8,128)(2,1)S(1)} custom-call(s32[1]{0:T(128)} %bitcast.pos_ref, bf16[144,512]{1,0:T(8,128)(2,1)S(1)} %pack.1.refs_0_, bf16[144,512]{1,0:T(8,128)(2,1)S(1)} %collective-permute-done.refs_1_, bf16[144,512]{1,0:T(8,128)(2,1)S(1)} %collective-permute-done.1.refs_2_, bf16[144,512]{1,0:T(8,128)(2,1)S(1)} %collective-permute-done.5.refs_3_, ...), custom_call_target="tpu_custom_call" | custom-call | bytes 1000 | tf_op jit(solution)/shard_map/collect/pallas_call | solution.py:498
  25.3 0.0 collective-permute-done.4.refs_0_
  25.3 0.2 collective-permute-start.7
  25.5 1.2 %collective-permute-done.7.refs_1_ = bf16[144,512]{1,0:T(8,128)(2,1)S(1)} collective-permute-done((bf16[144,512]{1,0:T(8,128)(2,1)S(1)}, bf16[144,512]{1,0:T(8,128)(2,1)S(1)}, u32[]{:S(2)}, u32[]{:S(2)}) %collective-permute-start.7) | collective-permute-done | bytes 147488 | tf_op jit(solution)/shard_map/ppermute | solution.py:442
  26.8 2.7 %routed.1 = (bf16[24,1024]{1,0:T(8,128)(2,1)S(1)}, bf16[24,1024]{1,0:T(8,128)(2,1)S(1)}, bf16[24,1024]{1,0:T(8,128)(2,1)S(1)}, bf16[24,1024]{1,0:T(8,128)(2,1)S(1)}, bf16[16,144,512]{2,1,0:T(8,128)(2,1)S(1)}) custom-call(s32[1]{0:T(128)} %bitcast.pos_ref, f32[1,4096]{1,0:T(1,128)} %bitcast.5, ...), custom_call_target="tpu_custom_call", output_to_operand_aliasing={{4}: (5, {})} | custom-call | tf_op jit(solution)/shard_map/routed/pallas_call | solution.py:512
  29.5 1.6 %collective-permute-start.8 = (bf16[24,1024]{1,0:T(8,128)(2,1)S(1)}, bf16[24,1024]{1,0:T(8,128)(2,1)S(1)}, u32[]{:S(2)}, u32[]{:S(2)}) collective-permute-start(bf16[24,1024]{1,0:T(8,128)(2,1)S(1)} %get-tuple-element.60), channel_id=1, source_target_pairs={{0,4},{1,5},{2,6},{3,7},{4,8},{5,9},{6,10},{7,11},{8,12},{9,13},{1... | collective-permute-start | bytes 147464 | tf_op jit(solution)/shard_map/ppermute | solution.py:442
  31.0 6.4 %collective-permute-start.9 = (bf16[24,1024]{1,0:T(8,128)(2,1)S(1)}, bf16[24,1024]{1,0:T(8,128)(2,1)S(1)}, u32[]{:S(2)}, u32[]{:S(2)}) collective-permute-start(bf16[24,1024]{1,0:T(8,128)(2,1)S(1)} %get-tuple-element.61), channel_id=1, source_target_pairs={{0,8},{1,9},{2,10},{3,11},{4,12},{5,13},{6,14},{7,15},{8,0},{9,1},... | collective-permute-start | bytes 147464 | tf_op jit(solution)/shard_map/ppermute | solution.py:442
  37.4 0.8 %collective-permute-start.10 = (bf16[24,1024]{1,0:T(8,128)(2,1)S(1)}, bf16[24,1024]{1,0:T(8,128)(2,1)S(1)}, u32[]{:S(2)}, u32[]{:S(2)}) collective-permute-start(bf16[24,1024]{1,0:T(8,128)(2,1)S(1)} %get-tuple-element.62), channel_id=1, source_target_pairs={{0,12},{1,13},{2,14},{3,15},{4,0},{5,1},{6,2},{7,3},{8,4},{9,5},{1... | collective-permute-start | bytes 147464 | tf_op jit(solution)/shard_map/ppermute | solution.py:442
  38.2 1.1 %collective-permute-start.11 = (bf16[24,1024]{1,0:T(8,128)(2,1)S(1)}, bf16[24,1024]{1,0:T(8,128)(2,1)S(1)}, u32[]{:S(2)}, u32[]{:S(2)}) collective-permute-start(bf16[24,1024]{1,0:T(8,128)(2,1)S(1)} %get-tuple-element.56._.refs_0_), channel_id=1, source_target_pairs={{0,2},{1,3},{2,0},{3,1},{4,6},{5,7},{6,4},{7,5},{8,10},{9,11},{10,... | collective-permute-start | bytes 147464 | tf_op jit(solution)/shard_map/ppermute | solution.py:442
  39.3 3.9 %own.3 = (f32[128,1280]{1,0:T(8,128)S(1)}, f32[8,128]{1,0:T(8,128)S(1)}, bf16[4096,384]{1,0:T(8,128)(2,1)S(1)}, bf16[4096,384]{1,0:T(8,128)(2,1)S(1)}, bf16[384,4096]{1,0:T(8,128)(2,1)S(1)}) custom-call(s32[1]{0:T(128)} %bitcast.pos_ref, bf16[16,144,512]{2,1,0:T(8,128)(2,1)S(1)} %get-tuple-element.55.held, bf16[128,4096]{1,0:T(8,128)(2,1)S(1)} %copy-done, ...), custom_call_target="tpu_custom_call" | custom-call | flops 2000000000 | bytes 8000000 | tf_op jit(solution)/shard_map/own/pallas_call | solution.py:534
  43.2 0.0 collective-permute-done.8
  43.2 0.0 collective-permute-done.9
  43.3 0.1 collective-permute-start.13
  43.4 1.0 %collective-permute-start.12 = (bf16[72,1024]{1,0:T(8,128)(2,1)S(1)}, bf16[72,1024]{1,0:T(8,128)(2,1)S(1)}, u32[]{:S(2)}, u32[]{:S(2)}) collective-permute-start(bf16[72,1024]{1,0:T(8,128)(2,1)S(1)} %constant_dynamic-update-slice_fusion.6.refs_1_), channel_id=1, source_target_pairs={{0,2},{1,3},{2,0},{3,1},{4,6},{5,7},{6,4},{7,5},{8,10},{9,11},{10,... | collective-permute-start | bytes 442376 | tf_op jit(solution)/shard_map/ppermute | solution.py:442
  44.4 1.4 %own.4 = (f32[128,1024]{1,0:T(8,128)S(1)}, f32[8,128]{1,0:T(8,128)S(1)}) custom-call(s32[1]{0:T(128)} %bitcast.pos_ref, bf16[16,144,512]{2,1,0:T(8,128)(2,1)S(1)} %get-tuple-element.55.held, bf16[128,4096]{1,0:T(8,128)(2,1)S(1)} %copy-done, bf16[128,4096]{1,0:T(8,128)(2,1)S(1)} %copy-done.1, f32[8,128]{1,0:T(8,128)S(1)} %get-tuple-element.58._), custom_call_target="tpu_custom_call" | custom-call | flops 2000000000 | bytes 8000000 | tf_op jit(solution)/shard_map/own/pallas_call | solution.py:534
  45.7 3.9 %collective-permute-done.12.refs_3_ = bf16[72,1024]{1,0:T(8,128)(2,1)S(1)} collective-permute-done((bf16[72,1024]{1,0:T(8,128)(2,1)S(1)}, bf16[72,1024]{1,0:T(8,128)(2,1)S(1)}, u32[]{:S(2)}, u32[]{:S(2)}) %collective-permute-start.12) | collective-permute-done | bytes 147488 | tf_op jit(solution)/shard_map/ppermute | solution.py:442
  49.6 0.1 collective-permute-start.14
  49.7 1.4 %collective-permute-done.14.refs_5_ = bf16[96,1024]{1,0:T(8,128)(2,1)S(1)} collective-permute-done((bf16[96,1024]{1,0:T(8,128)(2,1)S(1)}, bf16[96,1024]{1,0:T(8,128)(2,1)S(1)}, u32[]{:S(2)}, u32[]{:S(2)}) %collective-permute-start.14) | collective-permute-done | bytes 196640 | tf_op jit(solution)/shard_map/ppermute | solution.py:442
  51.2 2.7 %expert.1 = (bf16[192,1024]{1,0:T(8,128)(2,1)S(1)}, bf16[192,1024]{1,0:T(8,128)(2,1)S(1)}) custom-call(bf16[24,1024]{1,0:T(8,128)(2,1)S(1)} %get-tuple-element.56._.refs_0_, bf16[72,1024]{1,0:T(8,128)(2,1)S(1)} %constant_dynamic-update-slice_fusion.6.refs_1_, bf16[24,1024]{1,0:T(8,128)(2,1)S(1)} %collective-permute-done.11.refs_2_, ...), custom_call_target="tpu_custom_call" | custom-call | flops 1200000000 | bytes 12000000 | tf_op jit(solution)/shard_map/expert/pallas_call | solution.py:575
  53.9 0.2 collective-permute-start.15
  54.1 1.6 %collective-permute-done.15 = bf16[192,1024]{1,0:T(8,128)(2,1)S(1)} collective-permute-done((bf16[192,1024]{1,0:T(8,128)(2,1)S(1)}, bf16[192,1024]{1,0:T(8,128)(2,1)S(1)}, u32[]{:S(2)}, u32[]{:S(2)}) %collective-permute-start.15) | collective-permute-done | bytes 393248 | tf_op jit(solution)/shard_map/ppermute | solution.py:442
  55.7 0.1 convert_add_fusion
  55.8 1.0 %collective-permute-start.16 = (bf16[96,1024]{1,0:T(8,128)(2,1)S(1)}, bf16[96,1024]{1,0:T(8,128)(2,1)S(1)}, u32[]{:S(2)}, u32[]{:S(2)}) collective-permute-start(bf16[96,1024]{1,0:T(8,128)(2,1)S(1)} %slice.35), channel_id=1, source_target_pairs={{0,2},{1,3},{2,0},{3,1},{4,6},{5,7},{6,4},{7,5},{8,10},{9,11},{10,... | collective-permute-start | bytes 589832 | tf_op jit(solution)/shard_map/ppermute | solution.py:442
  56.8 1.5 %own.5 = (f32[128,1792]{1,0:T(8,128)S(1)}, f32[8,128]{1,0:T(8,128)S(1)}) custom-call(s32[1]{0:T(128)} %bitcast.pos_ref, bf16[16,144,512]{2,1,0:T(8,128)(2,1)S(1)} %get-tuple-element.55.held, bf16[128,4096]{1,0:T(8,128)(2,1)S(1)} %copy-done, bf16[128,4096]{1,0:T(8,128)(2,1)S(1)} %copy-done.1, bf16[192,1024]{1,0:T(8,128)(2,1)S(1)} %get-tuple-element.77._), custom_call_target="tpu_custom_call" | custom-call | flops 2000000000 | bytes 8000000 | tf_op jit(solution)/shard_map/own/pallas_call | solution.py:534
  58.3 4.5 %collective-permute-done.16 = bf16[96,1024]{1,0:T(8,128)(2,1)S(1)} collective-permute-done((bf16[96,1024]{1,0:T(8,128)(2,1)S(1)}, bf16[96,1024]{1,0:T(8,128)(2,1)S(1)}, u32[]{:S(2)}, u32[]{:S(2)}) %collective-permute-start.16) | collective-permute-done | bytes 196640 | tf_op jit(solution)/shard_map/ppermute | solution.py:442
  62.9 2.1 %collective-permute-start.19 = (bf16[24,1024]{1,0:T(8,128)(2,1)S(1)}, bf16[24,1024]{1,0:T(8,128)(2,1)S(1)}, u32[]{:S(2)}, u32[]{:S(2)}) collective-permute-start(bf16[24,1024]{1,0:T(8,128)(2,1)S(1)} %get-tuple-element.83), channel_id=1, source_target_pairs={{0,4},{1,5},{2,6},{3,7},{4,8},{5,9},{6,10},{7,11},{8,12},{9,13},{1... | collective-permute-start | bytes 147464 | tf_op jit(solution)/shard_map/ppermute | solution.py:442
  64.9 0.0 collective-permute-start.18
  65.0 2.4 %collective-permute-start.17 = (bf16[24,1024]{1,0:T(8,128)(2,1)S(1)}, bf16[24,1024]{1,0:T(8,128)(2,1)S(1)}, u32[]{:S(2)}, u32[]{:S(2)}) collective-permute-start(bf16[24,1024]{1,0:T(8,128)(2,1)S(1)} %get-tuple-element.85), channel_id=1, source_target_pairs={{0,12},{1,13},{2,14},{3,15},{4,0},{5,1},{6,2},{7,3},{8,4},{9,5},{1... | collective-permute-start | bytes 147464 | tf_op jit(solution)/shard_map/ppermute | solution.py:442
  67.4 1.7 %collective-permute-done.19.refs_6_ = bf16[24,1024]{1,0:T(8,128)(2,1)S(1)} collective-permute-done((bf16[24,1024]{1,0:T(8,128)(2,1)S(1)}, bf16[24,1024]{1,0:T(8,128)(2,1)S(1)}, u32[]{:S(2)}, u32[]{:S(2)}) %collective-permute-start.19) | collective-permute-done | bytes 49184 | tf_op jit(solution)/shard_map/ppermute | solution.py:442
  69.1 1.3 %collective-permute-done.18.refs_5_ = bf16[24,1024]{1,0:T(8,128)(2,1)S(1)} collective-permute-done((bf16[24,1024]{1,0:T(8,128)(2,1)S(1)}, bf16[24,1024]{1,0:T(8,128)(2,1)S(1)}, u32[]{:S(2)}, u32[]{:S(2)}) %collective-permute-start.18) | collective-permute-done | bytes 49184 | tf_op jit(solution)/shard_map/ppermute | solution.py:442
  70.4 1.4 %combine.1 = bf16[128,4096]{1,0:T(8,128)(2,1)} custom-call(bf16[128,64]{1,0:T(8,128)(2,1)S(1)} %get-tuple-element.44.mix_ref, f32[128,1280]{1,0:T(8,128)S(1)} %get-tuple-element.57.refs_0_, f32[128,1024]{1,0:T(8,128)S(1)} %get-tuple-element.59.refs_1_, f32[128,1792]{1,0:T(8,128)S(1)} %get-tuple-element.78.refs_2_, ...), custom_call_target="tpu_custom_call" | custom-call | tf_op jit(solution)/shard_map/combine/pallas_call | solution.py:605
  (20 shorter events, 0.2 us)
Async XLA Ops:
  1.0 11.2 %collective-permute-start = (bf16[144,512]{1,0:T(8,128)(2,1)S(1)}, bf16[144,512]{1,0:T(8,128)(2,1)S(1)}, u32[]{:S(2)}, u32[]{:S(2)}) collective-permute-start(bf16[144,512]{1,0:T(8,128)(2,1)S(1)} %pack.1.refs_0_), channel_id=1, source_target_pairs={{0,4},{1,5},{2,6},{3,7},{4,8},{5,9},{6,10},{7,11},{8,12},{9,13},{1... | collective-permute-start | bytes 442376 | tf_op jit(solution)/shard_map/ppermute | solution.py:442
  4.1 16.3 %collective-permute-start.5 = (bf16[144,512]{1,0:T(8,128)(2,1)S(1)}, bf16[144,512]{1,0:T(8,128)(2,1)S(1)}, u32[]{:S(2)}, u32[]{:S(2)}) collective-permute-start(bf16[144,512]{1,0:T(8,128)(2,1)S(1)} %pack.1.refs_0_), channel_id=1, source_target_pairs={{0,0},{1,1},{2,12},{3,13},{4,4},{5,5},{6,6},{7,7},{8,8},{9,9},{10,... | collective-permute-start | bytes 442376 | tf_op jit(solution)/shard_map/ppermute | solution.py:442
  4.7 10.8 %collective-permute-start.2 = (bf16[144,512]{1,0:T(8,128)(2,1)S(1)}, bf16[144,512]{1,0:T(8,128)(2,1)S(1)}, u32[]{:S(2)}, u32[]{:S(2)}) collective-permute-start(bf16[144,512]{1,0:T(8,128)(2,1)S(1)} %pack.1.refs_0_), channel_id=1, source_target_pairs={{0,2},{1,3},{2,0},{3,1},{4,6},{5,7},{6,4},{7,5},{8,10},{9,11},{10,... | collective-permute-start | bytes 442376 | tf_op jit(solution)/shard_map/ppermute | solution.py:442
  9.5 10.8 %collective-permute-start.1 = (bf16[144,512]{1,0:T(8,128)(2,1)S(1)}, bf16[144,512]{1,0:T(8,128)(2,1)S(1)}, u32[]{:S(2)}, u32[]{:S(2)}) collective-permute-start(bf16[144,512]{1,0:T(8,128)(2,1)S(1)} %pack.1.refs_0_), channel_id=1, source_target_pairs={{0,8},{1,9},{2,10},{3,11},{4,12},{5,13},{6,14},{7,15},{8,0},{9,1},... | collective-permute-start | bytes 442376 | tf_op jit(solution)/shard_map/ppermute | solution.py:442
  12.1 8.2 %collective-permute-start.3 = (bf16[144,512]{1,0:T(8,128)(2,1)S(1)}, bf16[144,512]{1,0:T(8,128)(2,1)S(1)}, u32[]{:S(2)}, u32[]{:S(2)}) collective-permute-start(bf16[144,512]{1,0:T(8,128)(2,1)S(1)} %collective-permute-done.refs_1_), channel_id=1, source_target_pairs={{0,0},{1,1},{2,2},{3,3},{4,6},{5,7},{6,4},{7,5},{8,10},{9,11},{10,... | collective-permute-start | bytes 442376 | tf_op jit(solution)/shard_map/ppermute | solution.py:442
  20.4 18.9 %copy-start = (bf16[128,4096]{1,0:T(8,128)(2,1)S(1)}, bf16[128,4096]{1,0:T(8,128)(2,1)}, u32[]{:S(2)}) copy-start(bf16[128,4096]{1,0:T(8,128)(2,1)} %q_ref.5) | copy-start | bytes 3145732
  20.4 18.9 %copy-start.1 = (bf16[128,4096]{1,0:T(8,128)(2,1)S(1)}, bf16[128,4096]{1,0:T(8,128)(2,1)}, u32[]{:S(2)}) copy-start(bf16[128,4096]{1,0:T(8,128)(2,1)} %x_ref.5) | copy-start | bytes 3145732
  20.4 2.5 %collective-permute-start.6 = (bf16[864,512]{1,0:T(8,128)(2,1)S(1)}, bf16[864,512]{1,0:T(8,128)(2,1)S(1)}, u32[]{:S(2)}, u32[]{:S(2)}) collective-permute-start(bf16[864,512]{1,0:T(8,128)(2,1)S(1)} %constant_dynamic-update-slice_fusion), channel_id=1, source_target_pairs={{0,1},{1,0},{2,3},{3,2},{4,5},{5,4},{6,7},{7,6},{8,9},{9,8},{10,11... | collective-permute-start | bytes 2654216 | tf_op jit(solution)/shard_map/ppermute | solution.py:442
  20.5 4.8 %collective-permute-start.4 = (bf16[144,512]{1,0:T(8,128)(2,1)S(1)}, bf16[144,512]{1,0:T(8,128)(2,1)S(1)}, u32[]{:S(2)}, u32[]{:S(2)}) collective-permute-start(bf16[144,512]{1,0:T(8,128)(2,1)S(1)} %collective-permute-done.1.refs_2_), channel_id=1, source_target_pairs={{0,0},{1,1},{2,2},{3,3},{4,4},{5,5},{6,6},{7,7},{8,10},{9,11},{10,... | collective-permute-start | bytes 442376 | tf_op jit(solution)/shard_map/ppermute | solution.py:442
  25.3 1.4 %collective-permute-start.7 = (bf16[144,512]{1,0:T(8,128)(2,1)S(1)}, bf16[144,512]{1,0:T(8,128)(2,1)S(1)}, u32[]{:S(2)}, u32[]{:S(2)}) collective-permute-start(bf16[144,512]{1,0:T(8,128)(2,1)S(1)} %collective-permute-done.4.refs_0_), channel_id=1, source_target_pairs={{0,1},{1,0},{2,3},{3,2},{4,5},{5,4},{6,7},{7,6},{8,9},{9,8},{10,11... | collective-permute-start | bytes 442376 | tf_op jit(solution)/shard_map/ppermute | solution.py:442
  29.5 13.7 %collective-permute-start.8 = (bf16[24,1024]{1,0:T(8,128)(2,1)S(1)}, bf16[24,1024]{1,0:T(8,128)(2,1)S(1)}, u32[]{:S(2)}, u32[]{:S(2)}) collective-permute-start(bf16[24,1024]{1,0:T(8,128)(2,1)S(1)} %get-tuple-element.60), channel_id=1, source_target_pairs={{0,4},{1,5},{2,6},{3,7},{4,8},{5,9},{6,10},{7,11},{8,12},{9,13},{1... | collective-permute-start | bytes 147464 | tf_op jit(solution)/shard_map/ppermute | solution.py:442
  31.0 12.2 %collective-permute-start.9 = (bf16[24,1024]{1,0:T(8,128)(2,1)S(1)}, bf16[24,1024]{1,0:T(8,128)(2,1)S(1)}, u32[]{:S(2)}, u32[]{:S(2)}) collective-permute-start(bf16[24,1024]{1,0:T(8,128)(2,1)S(1)} %get-tuple-element.61), channel_id=1, source_target_pairs={{0,8},{1,9},{2,10},{3,11},{4,12},{5,13},{6,14},{7,15},{8,0},{9,1},... | collective-permute-start | bytes 147464 | tf_op jit(solution)/shard_map/ppermute | solution.py:442
  37.4 5.8 %collective-permute-start.10 = (bf16[24,1024]{1,0:T(8,128)(2,1)S(1)}, bf16[24,1024]{1,0:T(8,128)(2,1)S(1)}, u32[]{:S(2)}, u32[]{:S(2)}) collective-permute-start(bf16[24,1024]{1,0:T(8,128)(2,1)S(1)} %get-tuple-element.62), channel_id=1, source_target_pairs={{0,12},{1,13},{2,14},{3,15},{4,0},{5,1},{6,2},{7,3},{8,4},{9,5},{1... | collective-permute-start | bytes 147464 | tf_op jit(solution)/shard_map/ppermute | solution.py:442
  38.2 5.0 %collective-permute-start.11 = (bf16[24,1024]{1,0:T(8,128)(2,1)S(1)}, bf16[24,1024]{1,0:T(8,128)(2,1)S(1)}, u32[]{:S(2)}, u32[]{:S(2)}) collective-permute-start(bf16[24,1024]{1,0:T(8,128)(2,1)S(1)} %get-tuple-element.56._.refs_0_), channel_id=1, source_target_pairs={{0,2},{1,3},{2,0},{3,1},{4,6},{5,7},{6,4},{7,5},{8,10},{9,11},{10,... | collective-permute-start | bytes 147464 | tf_op jit(solution)/shard_map/ppermute | solution.py:442
  43.3 6.4 %collective-permute-start.13 = (bf16[96,1024]{1,0:T(8,128)(2,1)S(1)}, bf16[96,1024]{1,0:T(8,128)(2,1)S(1)}, u32[]{:S(2)}, u32[]{:S(2)}) collective-permute-start(bf16[96,1024]{1,0:T(8,128)(2,1)S(1)} %pad_maximum_fusion), channel_id=1, source_target_pairs={{0,1},{1,0},{2,3},{3,2},{4,5},{5,4},{6,7},{7,6},{8,9},{9,8},{10,11... | collective-permute-start | bytes 589832 | tf_op jit(solution)/shard_map/ppermute | solution.py:442
  43.4 6.3 %collective-permute-start.12 = (bf16[72,1024]{1,0:T(8,128)(2,1)S(1)}, bf16[72,1024]{1,0:T(8,128)(2,1)S(1)}, u32[]{:S(2)}, u32[]{:S(2)}) collective-permute-start(bf16[72,1024]{1,0:T(8,128)(2,1)S(1)} %constant_dynamic-update-slice_fusion.6.refs_1_), channel_id=1, source_target_pairs={{0,2},{1,3},{2,0},{3,1},{4,6},{5,7},{6,4},{7,5},{8,10},{9,11},{10,... | collective-permute-start | bytes 442376 | tf_op jit(solution)/shard_map/ppermute | solution.py:442
  49.6 1.5 %collective-permute-start.14 = (bf16[96,1024]{1,0:T(8,128)(2,1)S(1)}, bf16[96,1024]{1,0:T(8,128)(2,1)S(1)}, u32[]{:S(2)}, u32[]{:S(2)}) collective-permute-start(bf16[96,1024]{1,0:T(8,128)(2,1)S(1)} %pad_maximum_fusion.1), channel_id=1, source_target_pairs={{0,1},{1,0},{2,3},{3,2},{4,5},{5,4},{6,7},{7,6},{8,9},{9,8},{10,11... | collective-permute-start | bytes 589832 | tf_op jit(solution)/shard_map/ppermute | solution.py:442
  53.9 1.8 %collective-permute-start.15 = (bf16[192,1024]{1,0:T(8,128)(2,1)S(1)}, bf16[192,1024]{1,0:T(8,128)(2,1)S(1)}, u32[]{:S(2)}, u32[]{:S(2)}) collective-permute-start(bf16[192,1024]{1,0:T(8,128)(2,1)S(1)} %get-tuple-element.79), channel_id=1, source_target_pairs={{0,1},{1,0},{2,3},{3,2},{4,5},{5,4},{6,7},{7,6},{8,9},{9,8},{10,11... | collective-permute-start | bytes 1179656 | tf_op jit(solution)/shard_map/ppermute | solution.py:442
  55.8 7.0 %collective-permute-start.16 = (bf16[96,1024]{1,0:T(8,128)(2,1)S(1)}, bf16[96,1024]{1,0:T(8,128)(2,1)S(1)}, u32[]{:S(2)}, u32[]{:S(2)}) collective-permute-start(bf16[96,1024]{1,0:T(8,128)(2,1)S(1)} %slice.35), channel_id=1, source_target_pairs={{0,2},{1,3},{2,0},{3,1},{4,6},{5,7},{6,4},{7,5},{8,10},{9,11},{10,... | collective-permute-start | bytes 589832 | tf_op jit(solution)/shard_map/ppermute | solution.py:442
  62.9 6.2 %collective-permute-start.19 = (bf16[24,1024]{1,0:T(8,128)(2,1)S(1)}, bf16[24,1024]{1,0:T(8,128)(2,1)S(1)}, u32[]{:S(2)}, u32[]{:S(2)}) collective-permute-start(bf16[24,1024]{1,0:T(8,128)(2,1)S(1)} %get-tuple-element.83), channel_id=1, source_target_pairs={{0,4},{1,5},{2,6},{3,7},{4,8},{5,9},{6,10},{7,11},{8,12},{9,13},{1... | collective-permute-start | bytes 147464 | tf_op jit(solution)/shard_map/ppermute | solution.py:442
  64.9 5.5 %collective-permute-start.18 = (bf16[24,1024]{1,0:T(8,128)(2,1)S(1)}, bf16[24,1024]{1,0:T(8,128)(2,1)S(1)}, u32[]{:S(2)}, u32[]{:S(2)}) collective-permute-start(bf16[24,1024]{1,0:T(8,128)(2,1)S(1)} %get-tuple-element.84), channel_id=1, source_target_pairs={{0,8},{1,9},{2,10},{3,11},{4,12},{5,13},{6,14},{7,15},{8,0},{9,1},... | collective-permute-start | bytes 147464 | tf_op jit(solution)/shard_map/ppermute | solution.py:442
  65.0 5.5 %collective-permute-start.17 = (bf16[24,1024]{1,0:T(8,128)(2,1)S(1)}, bf16[24,1024]{1,0:T(8,128)(2,1)S(1)}, u32[]{:S(2)}, u32[]{:S(2)}) collective-permute-start(bf16[24,1024]{1,0:T(8,128)(2,1)S(1)} %get-tuple-element.85), channel_id=1, source_target_pairs={{0,12},{1,13},{2,14},{3,15},{4,0},{5,1},{6,2},{7,3},{8,4},{9,5},{1... | collective-permute-start | bytes 147464 | tf_op jit(solution)/shard_map/ppermute | solution.py:442

commit v8 on v7

--- a/solution.py
+++ b/solution.py
@@ -448,7 +448,7 @@
         return any(0 <= gap <= back for gap in gaps)
 
     far = max(k for k in range(planes) if any(needed(k, a, b) for a in (0, 1) for b in (0, 1)))
-    size = min(n, 16) * PIECE
+    size = min(n // 2, 16) * PIECE
     q_rows, x_rows, facts, mix, gather, spread = pl.pallas_call(
         functools.partial(select_kernel, planes),
         out_shape=[
@@ -479,13 +479,19 @@
     jump = {s: s + far * SHARDS - 2 for s in range(n - far * SHARDS) if s & 2}
     jump.update({to: s for s, to in jump.items()})
     jumped = move(packed, [(s, jump.get(s, s)) for s in range(n)])
-    along = [packed] + [
-        move(packed, [(s, (s + k * SHARDS) % n) for s in range(n)]) for k in range(1, far)
-    ]
-    along[1], q_rows = lax.optimization_barrier((along[1], q_rows))
+    along = [packed]
+    for k in range(1, far):
+        below = (k - 1) * SHARDS
+        pairs = [
+            (s, s if s < below else s + SHARDS if s + SHARDS < n else s % SHARDS + below)
+            for s in range(n)
+        ]
+        along.append(move(along[-1], pairs))
     across = []
     for k in range(far):
-        if k > 1 and k == far - 1:
+        if k == 1:
+            along[1], q_rows = lax.optimization_barrier((along[1], q_rows))
+        elif k == far - 1:
             along[k], across = lax.optimization_barrier((along[k], across))
         across.append(move(along[k], [(s, s ^ 2 if s >= k * SHARDS else s) for s in range(n)]))
     early, late = along + [jumped] + across[:-1], across[-1:]
@@ -557,7 +563,7 @@
         )(pos, held, queries, resid, after, *map(pin, sources))
 
     half0, done, *weights = own(range(10), sent[0], w_gate, w_up, w_down)
-    half1, late = own(range(10, 18), done)
+    half1, late = own(range(10, GROUP), done)
     halves = [half0, half1]
 
     come = [
@@ -568,31 +574,33 @@
     here = [sent[0], jnp.concatenate(come, axis=0)]
     there = [next_door, move(here[1], flip_y)]
     mate = move(jnp.concatenate(here, axis=0), flip_c)
-    there, mate, late = lax.optimization_barrier((there, mate, late))
-    pieces = here + there + [mate, move(jnp.concatenate(there, axis=0), flip_c)]
-
-    half = jax.ShapeDtypeStruct((n * PIECE // 2, width // CUT), BF16)
-    keep, send = pl.pallas_call(
-        functools.partial(expert_kernel, n, len(pieces)),
-        out_shape=[half, half],
-        in_specs=[VMEM] * (len(pieces) + 5) + [ANY],
-        out_specs=[VMEM, VMEM],
-        scratch_shapes=[pltpu.VMEM((min(n, 16) * CAP, width), BF16)],
-        compiler_params=params(16),
-        cost_estimate=pl.CostEstimate(
-            flops=1_200_000_000, bytes_accessed=12_000_000, transcendentals=50_000
-        ),
-        name="expert",
-    )(*pieces, *weights, gather, spread, late)
-
-    half2, done = own(range(18, QUERY_HEADS), keep)
+    half = jax.ShapeDtypeStruct((n * PIECE // 4, width // CUT), BF16)
+
+    def expert(pieces, after):
+        return pl.pallas_call(
+            functools.partial(expert_kernel, n // 2, len(pieces)),
+            out_shape=[half, half],
+            in_specs=[VMEM] * (len(pieces) + 5) + [ANY],
+            out_specs=[VMEM, VMEM],
+            scratch_shapes=[pltpu.VMEM((min(n // 2, 16) * CAP, width), BF16)],
+            compiler_params=params(16),
+            cost_estimate=pl.CostEstimate(
+                flops=600_000_000, bytes_accessed=2_000_000, transcendentals=20_000
+            ),
+            name="expert",
+        )(*pieces, *weights, gather, spread, after)
+
+    keep, send = expert(here + [mate], done)
+    there, late, keep = lax.optimization_barrier((there, late, keep))
+    mine = keep.astype(F32) + move(send, flip_c).astype(F32)
+    mate = move(jnp.concatenate(there, axis=0), flip_c)
+    keep, send = expert(there + [mate], late)
+    half2, done = own(range(GROUP, QUERY_HEADS), keep)
     halves.append(half2)
-
-    total = keep.astype(F32) + move(send, [(s, s ^ 1) for s in range(n)]).astype(F32)
-    quarter = n * PIECE // 4
-    other = move(total[quarter:].astype(BF16), [(s, s ^ 2) for s in range(n)])
+    theirs = keep.astype(F32) + move(send, flip_c).astype(F32)
+    other = move(theirs.astype(BF16), flip_y)
     other, done = lax.optimization_barrier((other, done))
-    total = (total[:quarter] + other.astype(F32)).astype(BF16)
+    total = (mine + other.astype(F32)).astype(BF16)
     parts = [total[:PIECE]]
     for k in range(1, planes):
         parts.append(

time: 72.5 us -> 72.1 us (level)
  waiting for transfers between devices: 24.8 us -> 17.1 us
  starting transfers between devices: 27 us -> 33.8 us
  Pallas kernels: 19.4 us -> 20.6 us
    ppermute x20 -> x21, waiting for transfers between devices: 24.8 us -> 17.1 us  [move(): return lax.ppermute(value, 'expert', pairs)]
    ppermute x20 -> x21, starting transfers between devices: 27 us -> 33.8 us  [move(): return lax.ppermute(value, 'expert', pairs)]
    pallas_call x1 -> x2, Pallas kernels: 2.71 us -> 4.04 us  [expert(): pl.pallas_call(functools.partial(expert_kernel, n // 2, len(pieces)), out...]
  transfers between devices with their start and end apart: 20 -> 21, of which waited for: 10 -> 9; matrix products, arithmetic and copies ran while one was open for 0% -> 0% of each run, Pallas kernels for 16% -> 19%
where the time goes in v8:
time: 72.1 us
  starting transfers between devices  33.8 us (47%)
  Pallas kernels  20.6 us (29%)
  waiting for transfers between devices  17.1 us (24%)
    ppermute x21, starting transfers between devices, move(): return lax.ppermute(value, 'expert', pairs)  33.8 us
    ppermute x21, waiting for transfers between devices, move(): return lax.ppermute(value, 'expert', pairs)  17.1 us
    pallas_call x3, Pallas kernels, own(): pl.pallas_call(functools.partial(own_kernel, n, heads, len(sources)), out...  6.64 us
    pallas_call x2, Pallas kernels, expert(): pl.pallas_call(functools.partial(expert_kernel, n // 2, len(pieces)), out...  4.04 us
    pallas_call x1, Pallas kernels, local(): pl.pallas_call(functools.partial(routed_kernel, n, late_senders), out_sha...  2.67 us
    pallas_call x1, Pallas kernels, local(): pl.pallas_call(functools.partial(select_kernel, planes), out_shape=[jax.S...  2.49 us
    pallas_call x1, Pallas kernels, local(): pl.pallas_call(functools.partial(collect_kernel, n, early_senders), out_s...  2.4 us
  transfers between devices with their start and end apart: 21, of which 9 were waited for; matrix products, arithmetic and copies ran while one was open for 0% of the time, Pallas kernels for 19%

profile of v8, /device:TPU:0, one launch (start us, length us, event | category | flops | bytes accessed | tf_op | source)
XLA Modules:
  0.0 72.1 jit_solution(4952392711117974090)
XLA Ops:
  0.0 1.0 %pack.1.refs_0_ = bf16[144,512]{1,0:T(8,128)(2,1)S(1)} custom-call(s32[1,128]{1,0:T(1,128)} %bitcast.8, bf16[128,256]{1,0:T(8,128)(2,1)} %keys_ref.1, bf16[128,256]{1,0:T(8,128)(2,1)} %values_ref.1), custom_call_target="tpu_custom_call" | custom-call | tf_op jit(solution)/shard_map/pack/pallas_call | solution.py:427
  1.0 3.1 %collective-permute-start = (bf16[144,512]{1,0:T(8,128)(2,1)S(1)}, bf16[144,512]{1,0:T(8,128)(2,1)S(1)}, u32[]{:S(2)}, u32[]{:S(2)}) collective-permute-start(bf16[144,512]{1,0:T(8,128)(2,1)S(1)} %pack.1.refs_0_), channel_id=1, source_target_pairs={{0,4},{1,5},{2,6},{3,7},{4,8},{5,9},{6,10},{7,11},{8,12},{9,13},{1... | collective-permute-start | bytes 442376 | tf_op jit(solution)/shard_map/ppermute | solution.py:442
  4.1 0.7 collective-permute-start.5
  4.7 4.8 %collective-permute-start.2 = (bf16[144,512]{1,0:T(8,128)(2,1)S(1)}, bf16[144,512]{1,0:T(8,128)(2,1)S(1)}, u32[]{:S(2)}, u32[]{:S(2)}) collective-permute-start(bf16[144,512]{1,0:T(8,128)(2,1)S(1)} %pack.1.refs_0_), channel_id=1, source_target_pairs={{0,2},{1,3},{2,0},{3,1},{4,6},{5,7},{6,4},{7,5},{8,10},{9,11},{10,... | collective-permute-start | bytes 442376 | tf_op jit(solution)/shard_map/ppermute | solution.py:442
  9.5 2.5 %select.1 = (bf16[2,256,384]{2,1,0:T(8,128)(2,1)S(1)}, f32[24,4096]{1,0:T(8,128)S(1)}, f32[8,384]{1,0:T(8,128)S(1)}, bf16[128,64]{1,0:T(8,128)(2,1)S(1)}, bf16[1...) custom-call(s32[1]{0:T(128)} %bitcast.pos_ref, s32[4,128]{1,0:T(4,128)} %bitcast.6, s32[1,128]{1,0:T(1,128)} %bitcast.9, ...), custom_call_target="tpu_custom_call" | custom-call | tf_op jit(solution)/shard_map/select/pallas_call | solution.py:452
  12.1 0.7 collective-permute-start.3
  12.7 0.7 collective-permute-start.1
  13.4 2.1 %collective-permute-done.2.refs_4_ = bf16[144,512]{1,0:T(8,128)(2,1)S(1)} collective-permute-done((bf16[144,512]{1,0:T(8,128)(2,1)S(1)}, bf16[144,512]{1,0:T(8,128)(2,1)S(1)}, u32[]{:S(2)}, u32[]{:S(2)}) %collective-permute-start.2) | collective-permute-done | bytes 147488 | tf_op jit(solution)/shard_map/ppermute | solution.py:442
  15.6 0.0 collective-permute-done.5.refs_3_
  15.6 0.0 copy-start
  15.6 0.0 copy-start.1
  15.6 0.1 collective-permute-start.6
  15.7 0.8 %collective-permute-start.4 = (bf16[144,512]{1,0:T(8,128)(2,1)S(1)}, bf16[144,512]{1,0:T(8,128)(2,1)S(1)}, u32[]{:S(2)}, u32[]{:S(2)}) collective-permute-start(bf16[144,512]{1,0:T(8,128)(2,1)S(1)} %collective-permute-done.1.refs_2_), channel_id=1, source_target_pairs={{0,0},{1,1},{2,2},{3,3},{4,4},{5,5},{6,6},{7,7},{8,10},{9,11},{10,... | collective-permute-start | bytes 442376 | tf_op jit(solution)/shard_map/ppermute | solution.py:442
  16.5 1.6 %collective-permute-done.6.refs_6_ = bf16[864,512]{1,0:T(8,128)(2,1)S(1)} collective-permute-done((bf16[864,512]{1,0:T(8,128)(2,1)S(1)}, bf16[864,512]{1,0:T(8,128)(2,1)S(1)}, u32[]{:S(2)}, u32[]{:S(2)}) %collective-permute-start.6) | collective-permute-done | bytes 884768 | tf_op jit(solution)/shard_map/ppermute | solution.py:442
  18.1 2.4 %collect.1._ = bf16[16,144,512]{2,1,0:T(8,128)(2,1)S(1)} custom-call(s32[1]{0:T(128)} %bitcast.pos_ref, bf16[144,512]{1,0:T(8,128)(2,1)S(1)} %pack.1.refs_0_, bf16[144,512]{1,0:T(8,128)(2,1)S(1)} %collective-permute-done.refs_1_, bf16[144,512]{1,0:T(8,128)(2,1)S(1)} %collective-permute-done.1.refs_2_, bf16[144,512]{1,0:T(8,128)(2,1)S(1)} %collective-permute-done.5.refs_3_, ...), custom_call_target="tpu_custom_call" | custom-call | bytes 1000 | tf_op jit(solution)/shard_map/collect/pallas_call | solution.py:504
  20.5 0.0 collective-permute-done.4.refs_0_
  20.6 0.2 collective-permute-start.7
  20.8 1.2 %collective-permute-done.7.refs_1_ = bf16[144,512]{1,0:T(8,128)(2,1)S(1)} collective-permute-done((bf16[144,512]{1,0:T(8,128)(2,1)S(1)}, bf16[144,512]{1,0:T(8,128)(2,1)S(1)}, u32[]{:S(2)}, u32[]{:S(2)}) %collective-permute-start.7) | collective-permute-done | bytes 147488 | tf_op jit(solution)/shard_map/ppermute | solution.py:442
  22.0 2.7 %routed.1 = (bf16[24,1024]{1,0:T(8,128)(2,1)S(1)}, bf16[24,1024]{1,0:T(8,128)(2,1)S(1)}, bf16[24,1024]{1,0:T(8,128)(2,1)S(1)}, bf16[24,1024]{1,0:T(8,128)(2,1)S(1)}, bf16[16,144,512]{2,1,0:T(8,128)(2,1)S(1)}) custom-call(s32[1]{0:T(128)} %bitcast.pos_ref, f32[1,4096]{1,0:T(1,128)} %bitcast.5, ...), custom_call_target="tpu_custom_call", output_to_operand_aliasing={{4}: (5, {})} | custom-call | tf_op jit(solution)/shard_map/routed/pallas_call | solution.py:518
  24.7 8.9 %collective-permute-start.8 = (bf16[24,1024]{1,0:T(8,128)(2,1)S(1)}, bf16[24,1024]{1,0:T(8,128)(2,1)S(1)}, u32[]{:S(2)}, u32[]{:S(2)}) collective-permute-start(bf16[24,1024]{1,0:T(8,128)(2,1)S(1)} %get-tuple-element.63), channel_id=1, source_target_pairs={{0,4},{1,5},{2,6},{3,7},{4,8},{5,9},{6,10},{7,11},{8,12},{9,13},{1... | collective-permute-start | bytes 147464 | tf_op jit(solution)/shard_map/ppermute | solution.py:442
  33.5 6.0 %collective-permute-start.9 = (bf16[24,1024]{1,0:T(8,128)(2,1)S(1)}, bf16[24,1024]{1,0:T(8,128)(2,1)S(1)}, u32[]{:S(2)}, u32[]{:S(2)}) collective-permute-start(bf16[24,1024]{1,0:T(8,128)(2,1)S(1)} %get-tuple-element.64), channel_id=1, source_target_pairs={{0,8},{1,9},{2,10},{3,11},{4,12},{5,13},{6,14},{7,15},{8,0},{9,1},... | collective-permute-start | bytes 147464 | tf_op jit(solution)/shard_map/ppermute | solution.py:442
  39.6 1.1 %collective-permute-start.11 = (bf16[24,1024]{1,0:T(8,128)(2,1)S(1)}, bf16[24,1024]{1,0:T(8,128)(2,1)S(1)}, u32[]{:S(2)}, u32[]{:S(2)}) collective-permute-start(bf16[24,1024]{1,0:T(8,128)(2,1)S(1)} %get-tuple-element.59._.refs_0_), channel_id=1, source_target_pairs={{0,2},{1,3},{2,0},{3,1},{4,6},{5,7},{6,4},{7,5},{8,10},{9,11},{10,... | collective-permute-start | bytes 147464 | tf_op jit(solution)/shard_map/ppermute | solution.py:442
  40.6 3.9 %own.3 = (f32[128,1280]{1,0:T(8,128)S(1)}, f32[8,128]{1,0:T(8,128)S(1)}, bf16[4096,384]{1,0:T(8,128)(2,1)S(1)}, bf16[4096,384]{1,0:T(8,128)(2,1)S(1)}, bf16[384,4096]{1,0:T(8,128)(2,1)S(1)}) custom-call(s32[1]{0:T(128)} %bitcast.pos_ref, bf16[16,144,512]{2,1,0:T(8,128)(2,1)S(1)} %get-tuple-element.58.held, bf16[128,4096]{1,0:T(8,128)(2,1)S(1)} %copy-done, ...), custom_call_target="tpu_custom_call" | custom-call | flops 2000000000 | bytes 8000000 | tf_op jit(solution)/shard_map/own/pallas_call | solution.py:540
  44.5 0.0 collective-permute-done.8
  44.5 0.0 collective-permute-done.11.refs_0_
  44.6 0.1 collective-permute-start.13
  44.7 1.0 %collective-permute-start.12 = (bf16[72,1024]{1,0:T(8,128)(2,1)S(1)}, bf16[72,1024]{1,0:T(8,128)(2,1)S(1)}, u32[]{:S(2)}, u32[]{:S(2)}) collective-permute-start(bf16[72,1024]{1,0:T(8,128)(2,1)S(1)} %constant_dynamic-update-slice_fusion.6.refs_1_), channel_id=1, source_target_pairs={{0,2},{1,3},{2,0},{3,1},{4,6},{5,7},{6,4},{7,5},{8,10},{9,11},{10,... | collective-permute-start | bytes 442376 | tf_op jit(solution)/shard_map/ppermute | solution.py:442
  45.7 1.0 %own.4 = (f32[128,768]{1,0:T(8,128)S(1)}, f32[8,128]{1,0:T(8,128)S(1)}) custom-call(s32[1]{0:T(128)} %bitcast.pos_ref, bf16[16,144,512]{2,1,0:T(8,128)(2,1)S(1)} %get-tuple-element.58.held, bf16[128,4096]{1,0:T(8,128)(2,1)S(1)} %copy-done, bf16[128,4096]{1,0:T(8,128)(2,1)S(1)} %copy-done.1, f32[8,128]{1,0:T(8,128)S(1)} %get-tuple-element.76._.refs_8_), custom_call_target="tpu_custom_call" | custom-call | flops 2000000000 | bytes 8000000 | tf_op jit(solution)/shard_map/own/pallas_call | solution.py:540
  46.8 0.0 collective-permute-done.13.refs_2_
  46.8 2.0 %expert.2 = (bf16[96,1024]{1,0:T(8,128)(2,1)S(1)}, bf16[96,1024]{1,0:T(8,128)(2,1)S(1)}) custom-call(bf16[24,1024]{1,0:T(8,128)(2,1)S(1)} %get-tuple-element.59._.refs_0_, bf16[72,1024]{1,0:T(8,128)(2,1)S(1)} %constant_dynamic-update-slice_fusion.6.refs_1_, bf16[96,1024]{1,0:T(8,128)(2,1)S(1)} %collective-permute-done.13.refs_2_, ...), custom_call_target="tpu_custom_call" | custom-call | flops 600000000 | bytes 2000000 | tf_op jit(solution)/shard_map/expert/pallas_call | solution.py:580
  48.8 2.1 %collective-permute-done.12.refs_1_ = bf16[72,1024]{1,0:T(8,128)(2,1)S(1)} collective-permute-done((bf16[72,1024]{1,0:T(8,128)(2,1)S(1)}, bf16[72,1024]{1,0:T(8,128)(2,1)S(1)}, u32[]{:S(2)}, u32[]{:S(2)}) %collective-permute-start.12) | collective-permute-done | bytes 147488 | tf_op jit(solution)/shard_map/ppermute | solution.py:442
  50.9 0.1 collective-permute-start.14
  51.0 1.4 %collective-permute-done.14.refs_2_ = bf16[96,1024]{1,0:T(8,128)(2,1)S(1)} collective-permute-done((bf16[96,1024]{1,0:T(8,128)(2,1)S(1)}, bf16[96,1024]{1,0:T(8,128)(2,1)S(1)}, u32[]{:S(2)}, u32[]{:S(2)}) %collective-permute-start.14) | collective-permute-done | bytes 196640 | tf_op jit(solution)/shard_map/ppermute | solution.py:442
  52.5 2.0 %expert.3 = (bf16[96,1024]{1,0:T(8,128)(2,1)S(1)}, bf16[96,1024]{1,0:T(8,128)(2,1)S(1)}) custom-call(bf16[24,1024]{1,0:T(8,128)(2,1)S(1)} %collective-permute-done.11.refs_0_, bf16[72,1024]{1,0:T(8,128)(2,1)S(1)} %collective-permute-done.12.refs_1_, bf16[96,1024]{1,0:T(8,128)(2,1)S(1)} %collective-permute-done.14.refs_2_, ...), custom_call_target="tpu_custom_call" | custom-call | flops 600000000 | bytes 2000000 | tf_op jit(solution)/shard_map/expert/pallas_call | solution.py:580
  54.5 0.2 collective-permute-start.16
  54.7 1.3 %collective-permute-done.16 = bf16[96,1024]{1,0:T(8,128)(2,1)S(1)} collective-permute-done((bf16[96,1024]{1,0:T(8,128)(2,1)S(1)}, bf16[96,1024]{1,0:T(8,128)(2,1)S(1)}, u32[]{:S(2)}, u32[]{:S(2)}) %collective-permute-start.16) | collective-permute-done | bytes 196640 | tf_op jit(solution)/shard_map/ppermute | solution.py:442
  56.0 1.0 %collective-permute-start.17 = (bf16[96,1024]{1,0:T(8,128)(2,1)S(1)}, bf16[96,1024]{1,0:T(8,128)(2,1)S(1)}, u32[]{:S(2)}, u32[]{:S(2)}) collective-permute-start(bf16[96,1024]{1,0:T(8,128)(2,1)S(1)} %add_convert_fusion.1), channel_id=1, source_target_pairs={{0,2},{1,3},{2,0},{3,1},{4,6},{5,7},{6,4},{7,5},{8,10},{9,11},{10,... | collective-permute-start | bytes 589832 | tf_op jit(solution)/shard_map/ppermute | solution.py:442
  57.1 0.0 collective-permute-start.15
  57.1 1.7 %own.5 = (f32[128,2048]{1,0:T(8,128)S(1)}, f32[8,128]{1,0:T(8,128)S(1)}) custom-call(s32[1]{0:T(128)} %bitcast.pos_ref, bf16[16,144,512]{2,1,0:T(8,128)(2,1)S(1)} %get-tuple-element.58.held, bf16[128,4096]{1,0:T(8,128)(2,1)S(1)} %copy-done, bf16[128,4096]{1,0:T(8,128)(2,1)S(1)} %copy-done.1, bf16[96,1024]{1,0:T(8,128)(2,1)S(1)} %get-tuple-element.81._), custom_call_target="tpu_custom_call" | custom-call | flops 2000000000 | bytes 8000000 | tf_op jit(solution)/shard_map/own/pallas_call | solution.py:540
  58.8 4.2 %collective-permute-done.17 = bf16[96,1024]{1,0:T(8,128)(2,1)S(1)} collective-permute-done((bf16[96,1024]{1,0:T(8,128)(2,1)S(1)}, bf16[96,1024]{1,0:T(8,128)(2,1)S(1)}, u32[]{:S(2)}, u32[]{:S(2)}) %collective-permute-start.17) | collective-permute-done | bytes 196640 | tf_op jit(solution)/shard_map/ppermute | solution.py:442
  63.0 0.0 collective-permute-done.15
  63.1 0.1 add_convert_fusion
  63.2 2.1 %collective-permute-start.20 = (bf16[24,1024]{1,0:T(8,128)(2,1)S(1)}, bf16[24,1024]{1,0:T(8,128)(2,1)S(1)}, u32[]{:S(2)}, u32[]{:S(2)}) collective-permute-start(bf16[24,1024]{1,0:T(8,128)(2,1)S(1)} %get-tuple-element.89), channel_id=1, source_target_pairs={{0,4},{1,5},{2,6},{3,7},{4,8},{5,9},{6,10},{7,11},{8,12},{9,13},{1... | collective-permute-start | bytes 147464 | tf_op jit(solution)/shard_map/ppermute | solution.py:442
  65.2 0.2 collective-permute-start.19
  65.5 2.2 %collective-permute-start.18 = (bf16[24,1024]{1,0:T(8,128)(2,1)S(1)}, bf16[24,1024]{1,0:T(8,128)(2,1)S(1)}, u32[]{:S(2)}, u32[]{:S(2)}) collective-permute-start(bf16[24,1024]{1,0:T(8,128)(2,1)S(1)} %get-tuple-element.91), channel_id=1, source_target_pairs={{0,12},{1,13},{2,14},{3,15},{4,0},{5,1},{6,2},{7,3},{8,4},{9,5},{1... | collective-permute-start | bytes 147464 | tf_op jit(solution)/shard_map/ppermute | solution.py:442
  67.7 1.7 %collective-permute-done.20.refs_6_ = bf16[24,1024]{1,0:T(8,128)(2,1)S(1)} collective-permute-done((bf16[24,1024]{1,0:T(8,128)(2,1)S(1)}, bf16[24,1024]{1,0:T(8,128)(2,1)S(1)}, u32[]{:S(2)}, u32[]{:S(2)}) %collective-permute-start.20) | collective-permute-done | bytes 49184 | tf_op jit(solution)/shard_map/ppermute | solution.py:442
  69.4 1.4 %collective-permute-done.19.refs_5_ = bf16[24,1024]{1,0:T(8,128)(2,1)S(1)} collective-permute-done((bf16[24,1024]{1,0:T(8,128)(2,1)S(1)}, bf16[24,1024]{1,0:T(8,128)(2,1)S(1)}, u32[]{:S(2)}, u32[]{:S(2)}) %collective-permute-start.19) | collective-permute-done | bytes 49184 | tf_op jit(solution)/shard_map/ppermute | solution.py:442
  70.7 1.4 %combine.1 = bf16[128,4096]{1,0:T(8,128)(2,1)} custom-call(bf16[128,64]{1,0:T(8,128)(2,1)S(1)} %get-tuple-element.47.mix_ref, f32[128,1280]{1,0:T(8,128)S(1)} %get-tuple-element.60.refs_0_, f32[128,768]{1,0:T(8,128)S(1)} %get-tuple-element.62.refs_1_, f32[128,2048]{1,0:T(8,128)S(1)} %get-tuple-element.82.refs_2_, ...), custom_call_target="tpu_custom_call" | custom-call | tf_op jit(solution)/shard_map/combine/pallas_call | solution.py:613
  (22 shorter events, 0.2 us)
Async XLA Ops:
  1.0 11.1 %collective-permute-start = (bf16[144,512]{1,0:T(8,128)(2,1)S(1)}, bf16[144,512]{1,0:T(8,128)(2,1)S(1)}, u32[]{:S(2)}, u32[]{:S(2)}) collective-permute-start(bf16[144,512]{1,0:T(8,128)(2,1)S(1)} %pack.1.refs_0_), channel_id=1, source_target_pairs={{0,4},{1,5},{2,6},{3,7},{4,8},{5,9},{6,10},{7,11},{8,12},{9,13},{1... | collective-permute-start | bytes 442376 | tf_op jit(solution)/shard_map/ppermute | solution.py:442
  4.1 11.5 %collective-permute-start.5 = (bf16[144,512]{1,0:T(8,128)(2,1)S(1)}, bf16[144,512]{1,0:T(8,128)(2,1)S(1)}, u32[]{:S(2)}, u32[]{:S(2)}) collective-permute-start(bf16[144,512]{1,0:T(8,128)(2,1)S(1)} %pack.1.refs_0_), channel_id=1, source_target_pairs={{0,0},{1,1},{2,12},{3,13},{4,4},{5,5},{6,6},{7,7},{8,8},{9,9},{10,... | collective-permute-start | bytes 442376 | tf_op jit(solution)/shard_map/ppermute | solution.py:442
  4.7 10.8 %collective-permute-start.2 = (bf16[144,512]{1,0:T(8,128)(2,1)S(1)}, bf16[144,512]{1,0:T(8,128)(2,1)S(1)}, u32[]{:S(2)}, u32[]{:S(2)}) collective-permute-start(bf16[144,512]{1,0:T(8,128)(2,1)S(1)} %pack.1.refs_0_), channel_id=1, source_target_pairs={{0,2},{1,3},{2,0},{3,1},{4,6},{5,7},{6,4},{7,5},{8,10},{9,11},{10,... | collective-permute-start | bytes 442376 | tf_op jit(solution)/shard_map/ppermute | solution.py:442
  12.1 3.5 %collective-permute-start.3 = (bf16[144,512]{1,0:T(8,128)(2,1)S(1)}, bf16[144,512]{1,0:T(8,128)(2,1)S(1)}, u32[]{:S(2)}, u32[]{:S(2)}) collective-permute-start(bf16[144,512]{1,0:T(8,128)(2,1)S(1)} %collective-permute-done.refs_1_), channel_id=1, source_target_pairs={{0,0},{1,1},{2,2},{3,3},{4,6},{5,7},{6,4},{7,5},{8,10},{9,11},{10,... | collective-permute-start | bytes 442376 | tf_op jit(solution)/shard_map/ppermute | solution.py:442
  12.7 2.8 %collective-permute-start.1 = (bf16[144,512]{1,0:T(8,128)(2,1)S(1)}, bf16[144,512]{1,0:T(8,128)(2,1)S(1)}, u32[]{:S(2)}, u32[]{:S(2)}) collective-permute-start(bf16[144,512]{1,0:T(8,128)(2,1)S(1)} %collective-permute-done.refs_1_), channel_id=1, source_target_pairs={{0,0},{1,1},{2,2},{3,3},{4,8},{5,9},{6,10},{7,11},{8,12},{9,13},{1... | collective-permute-start | bytes 442376 | tf_op jit(solution)/shard_map/ppermute | solution.py:442
  15.6 25.0 %copy-start = (bf16[128,4096]{1,0:T(8,128)(2,1)S(1)}, bf16[128,4096]{1,0:T(8,128)(2,1)}, u32[]{:S(2)}) copy-start(bf16[128,4096]{1,0:T(8,128)(2,1)} %q_ref.5) | copy-start | bytes 3145732
  15.6 25.0 %copy-start.1 = (bf16[128,4096]{1,0:T(8,128)(2,1)S(1)}, bf16[128,4096]{1,0:T(8,128)(2,1)}, u32[]{:S(2)}) copy-start(bf16[128,4096]{1,0:T(8,128)(2,1)} %x_ref.5) | copy-start | bytes 3145732
  15.6 2.5 %collective-permute-start.6 = (bf16[864,512]{1,0:T(8,128)(2,1)S(1)}, bf16[864,512]{1,0:T(8,128)(2,1)S(1)}, u32[]{:S(2)}, u32[]{:S(2)}) collective-permute-start(bf16[864,512]{1,0:T(8,128)(2,1)S(1)} %constant_dynamic-update-slice_fusion), channel_id=1, source_target_pairs={{0,1},{1,0},{2,3},{3,2},{4,5},{5,4},{6,7},{7,6},{8,9},{9,8},{10,11... | collective-permute-start | bytes 2654216 | tf_op jit(solution)/shard_map/ppermute | solution.py:442
  15.7 4.8 %collective-permute-start.4 = (bf16[144,512]{1,0:T(8,128)(2,1)S(1)}, bf16[144,512]{1,0:T(8,128)(2,1)S(1)}, u32[]{:S(2)}, u32[]{:S(2)}) collective-permute-start(bf16[144,512]{1,0:T(8,128)(2,1)S(1)} %collective-permute-done.1.refs_2_), channel_id=1, source_target_pairs={{0,0},{1,1},{2,2},{3,3},{4,4},{5,5},{6,6},{7,7},{8,10},{9,11},{10,... | collective-permute-start | bytes 442376 | tf_op jit(solution)/shard_map/ppermute | solution.py:442
  20.6 1.4 %collective-permute-start.7 = (bf16[144,512]{1,0:T(8,128)(2,1)S(1)}, bf16[144,512]{1,0:T(8,128)(2,1)S(1)}, u32[]{:S(2)}, u32[]{:S(2)}) collective-permute-start(bf16[144,512]{1,0:T(8,128)(2,1)S(1)} %collective-permute-done.4.refs_0_), channel_id=1, source_target_pairs={{0,1},{1,0},{2,3},{3,2},{4,5},{5,4},{6,7},{7,6},{8,9},{9,8},{10,11... | collective-permute-start | bytes 442376 | tf_op jit(solution)/shard_map/ppermute | solution.py:442
  24.7 19.8 %collective-permute-start.8 = (bf16[24,1024]{1,0:T(8,128)(2,1)S(1)}, bf16[24,1024]{1,0:T(8,128)(2,1)S(1)}, u32[]{:S(2)}, u32[]{:S(2)}) collective-permute-start(bf16[24,1024]{1,0:T(8,128)(2,1)S(1)} %get-tuple-element.63), channel_id=1, source_target_pairs={{0,4},{1,5},{2,6},{3,7},{4,8},{5,9},{6,10},{7,11},{8,12},{9,13},{1... | collective-permute-start | bytes 147464 | tf_op jit(solution)/shard_map/ppermute | solution.py:442
  33.5 11.0 %collective-permute-start.9 = (bf16[24,1024]{1,0:T(8,128)(2,1)S(1)}, bf16[24,1024]{1,0:T(8,128)(2,1)S(1)}, u32[]{:S(2)}, u32[]{:S(2)}) collective-permute-start(bf16[24,1024]{1,0:T(8,128)(2,1)S(1)} %get-tuple-element.64), channel_id=1, source_target_pairs={{0,8},{1,9},{2,10},{3,11},{4,12},{5,13},{6,14},{7,15},{8,0},{9,1},... | collective-permute-start | bytes 147464 | tf_op jit(solution)/shard_map/ppermute | solution.py:442
  39.6 4.9 %collective-permute-start.10 = (bf16[24,1024]{1,0:T(8,128)(2,1)S(1)}, bf16[24,1024]{1,0:T(8,128)(2,1)S(1)}, u32[]{:S(2)}, u32[]{:S(2)}) collective-permute-start(bf16[24,1024]{1,0:T(8,128)(2,1)S(1)} %get-tuple-element.65), channel_id=1, source_target_pairs={{0,12},{1,13},{2,14},{3,15},{4,0},{5,1},{6,2},{7,3},{8,4},{9,5},{1... | collective-permute-start | bytes 147464 | tf_op jit(solution)/shard_map/ppermute | solution.py:442
  39.6 5.0 %collective-permute-start.11 = (bf16[24,1024]{1,0:T(8,128)(2,1)S(1)}, bf16[24,1024]{1,0:T(8,128)(2,1)S(1)}, u32[]{:S(2)}, u32[]{:S(2)}) collective-permute-start(bf16[24,1024]{1,0:T(8,128)(2,1)S(1)} %get-tuple-element.59._.refs_0_), channel_id=1, source_target_pairs={{0,2},{1,3},{2,0},{3,1},{4,6},{5,7},{6,4},{7,5},{8,10},{9,11},{10,... | collective-permute-start | bytes 147464 | tf_op jit(solution)/shard_map/ppermute | solution.py:442
  44.6 2.2 %collective-permute-start.13 = (bf16[96,1024]{1,0:T(8,128)(2,1)S(1)}, bf16[96,1024]{1,0:T(8,128)(2,1)S(1)}, u32[]{:S(2)}, u32[]{:S(2)}) collective-permute-start(bf16[96,1024]{1,0:T(8,128)(2,1)S(1)} %pad_maximum_fusion), channel_id=1, source_target_pairs={{0,1},{1,0},{2,3},{3,2},{4,5},{5,4},{6,7},{7,6},{8,9},{9,8},{10,11... | collective-permute-start | bytes 589832 | tf_op jit(solution)/shard_map/ppermute | solution.py:442
  44.7 6.3 %collective-permute-start.12 = (bf16[72,1024]{1,0:T(8,128)(2,1)S(1)}, bf16[72,1024]{1,0:T(8,128)(2,1)S(1)}, u32[]{:S(2)}, u32[]{:S(2)}) collective-permute-start(bf16[72,1024]{1,0:T(8,128)(2,1)S(1)} %constant_dynamic-update-slice_fusion.6.refs_1_), channel_id=1, source_target_pairs={{0,2},{1,3},{2,0},{3,1},{4,6},{5,7},{6,4},{7,5},{8,10},{9,11},{10,... | collective-permute-start | bytes 442376 | tf_op jit(solution)/shard_map/ppermute | solution.py:442
  50.9 1.5 %collective-permute-start.14 = (bf16[96,1024]{1,0:T(8,128)(2,1)S(1)}, bf16[96,1024]{1,0:T(8,128)(2,1)S(1)}, u32[]{:S(2)}, u32[]{:S(2)}) collective-permute-start(bf16[96,1024]{1,0:T(8,128)(2,1)S(1)} %pad_maximum_fusion.1), channel_id=1, source_target_pairs={{0,1},{1,0},{2,3},{3,2},{4,5},{5,4},{6,7},{7,6},{8,9},{9,8},{10,11... | collective-permute-start | bytes 589832 | tf_op jit(solution)/shard_map/ppermute | solution.py:442
  54.5 1.5 %collective-permute-start.16 = (bf16[96,1024]{1,0:T(8,128)(2,1)S(1)}, bf16[96,1024]{1,0:T(8,128)(2,1)S(1)}, u32[]{:S(2)}, u32[]{:S(2)}) collective-permute-start(bf16[96,1024]{1,0:T(8,128)(2,1)S(1)} %get-tuple-element.85), channel_id=1, source_target_pairs={{0,1},{1,0},{2,3},{3,2},{4,5},{5,4},{6,7},{7,6},{8,9},{9,8},{10,11... | collective-permute-start | bytes 589832 | tf_op jit(solution)/shard_map/ppermute | solution.py:442
  56.0 7.0 %collective-permute-start.17 = (bf16[96,1024]{1,0:T(8,128)(2,1)S(1)}, bf16[96,1024]{1,0:T(8,128)(2,1)S(1)}, u32[]{:S(2)}, u32[]{:S(2)}) collective-permute-start(bf16[96,1024]{1,0:T(8,128)(2,1)S(1)} %add_convert_fusion.1), channel_id=1, source_target_pairs={{0,2},{1,3},{2,0},{3,1},{4,6},{5,7},{6,4},{7,5},{8,10},{9,11},{10,... | collective-permute-start | bytes 589832 | tf_op jit(solution)/shard_map/ppermute | solution.py:442
  57.1 6.0 %collective-permute-start.15 = (bf16[96,1024]{1,0:T(8,128)(2,1)S(1)}, bf16[96,1024]{1,0:T(8,128)(2,1)S(1)}, u32[]{:S(2)}, u32[]{:S(2)}) collective-permute-start(bf16[96,1024]{1,0:T(8,128)(2,1)S(1)} %get-tuple-element.84), channel_id=1, source_target_pairs={{0,1},{1,0},{2,3},{3,2},{4,5},{5,4},{6,7},{7,6},{8,9},{9,8},{10,11... | collective-permute-start | bytes 589832 | tf_op jit(solution)/shard_map/ppermute | solution.py:442
  63.2 6.2 %collective-permute-start.20 = (bf16[24,1024]{1,0:T(8,128)(2,1)S(1)}, bf16[24,1024]{1,0:T(8,128)(2,1)S(1)}, u32[]{:S(2)}, u32[]{:S(2)}) collective-permute-start(bf16[24,1024]{1,0:T(8,128)(2,1)S(1)} %get-tuple-element.89), channel_id=1, source_target_pairs={{0,4},{1,5},{2,6},{3,7},{4,8},{5,9},{6,10},{7,11},{8,12},{9,13},{1... | collective-permute-start | bytes 147464 | tf_op jit(solution)/shard_map/ppermute | solution.py:442
  65.2 5.5 %collective-permute-start.19 = (bf16[24,1024]{1,0:T(8,128)(2,1)S(1)}, bf16[24,1024]{1,0:T(8,128)(2,1)S(1)}, u32[]{:S(2)}, u32[]{:S(2)}) collective-permute-start(bf16[24,1024]{1,0:T(8,128)(2,1)S(1)} %get-tuple-element.90), channel_id=1, source_target_pairs={{0,8},{1,9},{2,10},{3,11},{4,12},{5,13},{6,14},{7,15},{8,0},{9,1},... | collective-permute-start | bytes 147464 | tf_op jit(solution)/shard_map/ppermute | solution.py:442
  65.5 5.3 %collective-permute-start.18 = (bf16[24,1024]{1,0:T(8,128)(2,1)S(1)}, bf16[24,1024]{1,0:T(8,128)(2,1)S(1)}, u32[]{:S(2)}, u32[]{:S(2)}) collective-permute-start(bf16[24,1024]{1,0:T(8,128)(2,1)S(1)} %get-tuple-element.91), channel_id=1, source_target_pairs={{0,12},{1,13},{2,14},{3,15},{4,0},{5,1},{6,2},{7,3},{8,4},{9,5},{1... | collective-permute-start | bytes 147464 | tf_op jit(solution)/shard_map/ppermute | solution.py:442

commit v9 on v8

--- a/solution.py
+++ b/solution.py
@@ -479,19 +479,13 @@
     jump = {s: s + far * SHARDS - 2 for s in range(n - far * SHARDS) if s & 2}
     jump.update({to: s for s, to in jump.items()})
     jumped = move(packed, [(s, jump.get(s, s)) for s in range(n)])
-    along = [packed]
-    for k in range(1, far):
-        below = (k - 1) * SHARDS
-        pairs = [
-            (s, s if s < below else s + SHARDS if s + SHARDS < n else s % SHARDS + below)
-            for s in range(n)
-        ]
-        along.append(move(along[-1], pairs))
+    along = [packed] + [
+        move(packed, [(s, (s + k * SHARDS) % n) for s in range(n)]) for k in range(1, far)
+    ]
+    along[1], q_rows = lax.optimization_barrier((along[1], q_rows))
     across = []
     for k in range(far):
-        if k == 1:
-            along[1], q_rows = lax.optimization_barrier((along[1], q_rows))
-        elif k == far - 1:
+        if k > 1 and k == far - 1:
             along[k], across = lax.optimization_barrier((along[k], across))
         across.append(move(along[k], [(s, s ^ 2 if s >= k * SHARDS else s) for s in range(n)]))
     early, late = along + [jumped] + across[:-1], across[-1:]

time: 72.1 us -> 71.4 us (level)
  starting transfers between devices: 33.8 us -> 26.8 us
  waiting for transfers between devices: 17.1 us -> 22.8 us
    ppermute x21, starting transfers between devices: 33.8 us -> 26.8 us  [move(): return lax.ppermute(value, 'expert', pairs)]
    ppermute x21, waiting for transfers between devices: 17.1 us -> 22.8 us  [move(): return lax.ppermute(value, 'expert', pairs)]
  transfers between devices with their start and end apart: 21 -> 21, of which waited for: 9 -> 10; matrix products, arithmetic and copies ran while one was open for 0% -> 0% of each run, Pallas kernels for 19% -> 19%
where the time goes in v9:
time: 71.4 us; the launch traced here: 70.8 us
  starting transfers between devices  26.8 us (38%)
  waiting for transfers between devices  22.8 us (32%)
  Pallas kernels  20.6 us (29%)
    ppermute x21, starting transfers between devices, move(): return lax.ppermute(value, 'expert', pairs)  26.8 us
    ppermute x21, waiting for transfers between devices, move(): return lax.ppermute(value, 'expert', pairs)  22.8 us
    pallas_call x3, Pallas kernels, own(): pl.pallas_call(functools.partial(own_kernel, n, heads, len(sources)), out...  6.64 us
    pallas_call x2, Pallas kernels, expert(): pl.pallas_call(functools.partial(expert_kernel, n // 2, len(pieces)), out...  4.03 us
    pallas_call x1, Pallas kernels, local(): pl.pallas_call(functools.partial(routed_kernel, n, late_senders), out_sha...  2.67 us
    pallas_call x1, Pallas kernels, local(): pl.pallas_call(functools.partial(select_kernel, planes), out_shape=[jax.S...  2.49 us
    pallas_call x1, Pallas kernels, local(): pl.pallas_call(functools.partial(collect_kernel, n, early_senders), out_s...  2.4 us
  transfers between devices with their start and end apart: 21, of which 10 were waited for; matrix products, arithmetic and copies ran while one was open for 0% of the time, Pallas kernels for 19%

profile of v9, /device:TPU:0, one launch (start us, length us, event | category | flops | bytes accessed | tf_op | source)
XLA Modules:
  0.0 70.8 jit_solution(602247265296912571)
XLA Ops:
  0.0 1.0 %pack.1.refs_0_ = bf16[144,512]{1,0:T(8,128)(2,1)S(1)} custom-call(s32[1,128]{1,0:T(1,128)} %bitcast.8, bf16[128,256]{1,0:T(8,128)(2,1)} %keys_ref.1, bf16[128,256]{1,0:T(8,128)(2,1)} %values_ref.1), custom_call_target="tpu_custom_call" | custom-call | tf_op jit(solution)/shard_map/pack/pallas_call | solution.py:427
  1.0 3.1 %collective-permute-start = (bf16[144,512]{1,0:T(8,128)(2,1)S(1)}, bf16[144,512]{1,0:T(8,128)(2,1)S(1)}, u32[]{:S(2)}, u32[]{:S(2)}) collective-permute-start(bf16[144,512]{1,0:T(8,128)(2,1)S(1)} %pack.1.refs_0_), channel_id=1, source_target_pairs={{0,4},{1,5},{2,6},{3,7},{4,8},{5,9},{6,10},{7,11},{8,12},{9,13},{1... | collective-permute-start | bytes 442376 | tf_op jit(solution)/shard_map/ppermute | solution.py:442
  4.1 0.7 collective-permute-start.5
  4.7 4.8 %collective-permute-start.2 = (bf16[144,512]{1,0:T(8,128)(2,1)S(1)}, bf16[144,512]{1,0:T(8,128)(2,1)S(1)}, u32[]{:S(2)}, u32[]{:S(2)}) collective-permute-start(bf16[144,512]{1,0:T(8,128)(2,1)S(1)} %pack.1.refs_0_), channel_id=1, source_target_pairs={{0,2},{1,3},{2,0},{3,1},{4,6},{5,7},{6,4},{7,5},{8,10},{9,11},{10,... | collective-permute-start | bytes 442376 | tf_op jit(solution)/shard_map/ppermute | solution.py:442
  9.5 0.0 collective-permute-start.1
  9.5 2.5 %select.1 = (bf16[2,256,384]{2,1,0:T(8,128)(2,1)S(1)}, f32[24,4096]{1,0:T(8,128)S(1)}, f32[8,384]{1,0:T(8,128)S(1)}, bf16[128,64]{1,0:T(8,128)(2,1)S(1)}, bf16[1...) custom-call(s32[1]{0:T(128)} %bitcast.pos_ref, s32[4,128]{1,0:T(4,128)} %bitcast.6, s32[1,128]{1,0:T(1,128)} %bitcast.9, ...), custom_call_target="tpu_custom_call" | custom-call | tf_op jit(solution)/shard_map/select/pallas_call | solution.py:452
  12.0 0.0 collective-permute-done.refs_1_
  12.1 0.7 collective-permute-start.3
  12.8 2.8 %collective-permute-done.2.refs_4_ = bf16[144,512]{1,0:T(8,128)(2,1)S(1)} collective-permute-done((bf16[144,512]{1,0:T(8,128)(2,1)S(1)}, bf16[144,512]{1,0:T(8,128)(2,1)S(1)}, u32[]{:S(2)}, u32[]{:S(2)}) %collective-permute-start.2) | collective-permute-done | bytes 147488 | tf_op jit(solution)/shard_map/ppermute | solution.py:442
  15.5 4.8 %collective-permute-done.1.refs_2_ = bf16[144,512]{1,0:T(8,128)(2,1)S(1)} collective-permute-done((bf16[144,512]{1,0:T(8,128)(2,1)S(1)}, bf16[144,512]{1,0:T(8,128)(2,1)S(1)}, u32[]{:S(2)}, u32[]{:S(2)}) %collective-permute-start.1) | collective-permute-done | bytes 147488 | tf_op jit(solution)/shard_map/ppermute | solution.py:442
  20.3 0.0 collective-permute-done.3.refs_5_
  20.4 0.0 copy-start
  20.4 0.0 copy-start.1
  20.4 0.1 collective-permute-start.6
  20.5 0.8 %collective-permute-start.4 = (bf16[144,512]{1,0:T(8,128)(2,1)S(1)}, bf16[144,512]{1,0:T(8,128)(2,1)S(1)}, u32[]{:S(2)}, u32[]{:S(2)}) collective-permute-start(bf16[144,512]{1,0:T(8,128)(2,1)S(1)} %collective-permute-done.1.refs_2_), channel_id=1, source_target_pairs={{0,0},{1,1},{2,2},{3,3},{4,4},{5,5},{6,6},{7,7},{8,10},{9,11},{10,... | collective-permute-start | bytes 442376 | tf_op jit(solution)/shard_map/ppermute | solution.py:442
  21.3 1.6 %collective-permute-done.6.refs_6_ = bf16[864,512]{1,0:T(8,128)(2,1)S(1)} collective-permute-done((bf16[864,512]{1,0:T(8,128)(2,1)S(1)}, bf16[864,512]{1,0:T(8,128)(2,1)S(1)}, u32[]{:S(2)}, u32[]{:S(2)}) %collective-permute-start.6) | collective-permute-done | bytes 884768 | tf_op jit(solution)/shard_map/ppermute | solution.py:442
  22.9 2.4 %collect.1._ = bf16[16,144,512]{2,1,0:T(8,128)(2,1)S(1)} custom-call(s32[1]{0:T(128)} %bitcast.pos_ref, bf16[144,512]{1,0:T(8,128)(2,1)S(1)} %pack.1.refs_0_, bf16[144,512]{1,0:T(8,128)(2,1)S(1)} %collective-permute-done.refs_1_, bf16[144,512]{1,0:T(8,128)(2,1)S(1)} %collective-permute-done.1.refs_2_, bf16[144,512]{1,0:T(8,128)(2,1)S(1)} %collective-permute-done.5.refs_3_, ...), custom_call_target="tpu_custom_call" | custom-call | bytes 1000 | tf_op jit(solution)/shard_map/collect/pallas_call | solution.py:498
  25.3 0.2 collective-permute-start.7
  25.5 1.2 %collective-permute-done.7.refs_1_ = bf16[144,512]{1,0:T(8,128)(2,1)S(1)} collective-permute-done((bf16[144,512]{1,0:T(8,128)(2,1)S(1)}, bf16[144,512]{1,0:T(8,128)(2,1)S(1)}, u32[]{:S(2)}, u32[]{:S(2)}) %collective-permute-start.7) | collective-permute-done | bytes 147488 | tf_op jit(solution)/shard_map/ppermute | solution.py:442
  26.8 2.7 %routed.1 = (bf16[24,1024]{1,0:T(8,128)(2,1)S(1)}, bf16[24,1024]{1,0:T(8,128)(2,1)S(1)}, bf16[24,1024]{1,0:T(8,128)(2,1)S(1)}, bf16[24,1024]{1,0:T(8,128)(2,1)S(1)}, bf16[16,144,512]{2,1,0:T(8,128)(2,1)S(1)}) custom-call(s32[1]{0:T(128)} %bitcast.pos_ref, f32[1,4096]{1,0:T(1,128)} %bitcast.5, ...), custom_call_target="tpu_custom_call", output_to_operand_aliasing={{4}: (5, {})} | custom-call | tf_op jit(solution)/shard_map/routed/pallas_call | solution.py:512
  29.5 1.5 %collective-permute-start.8 = (bf16[24,1024]{1,0:T(8,128)(2,1)S(1)}, bf16[24,1024]{1,0:T(8,128)(2,1)S(1)}, u32[]{:S(2)}, u32[]{:S(2)}) collective-permute-start(bf16[24,1024]{1,0:T(8,128)(2,1)S(1)} %get-tuple-element.63), channel_id=1, source_target_pairs={{0,4},{1,5},{2,6},{3,7},{4,8},{5,9},{6,10},{7,11},{8,12},{9,13},{1... | collective-permute-start | bytes 147464 | tf_op jit(solution)/shard_map/ppermute | solution.py:442
  30.9 6.5 %collective-permute-start.9 = (bf16[24,1024]{1,0:T(8,128)(2,1)S(1)}, bf16[24,1024]{1,0:T(8,128)(2,1)S(1)}, u32[]{:S(2)}, u32[]{:S(2)}) collective-permute-start(bf16[24,1024]{1,0:T(8,128)(2,1)S(1)} %get-tuple-element.64), channel_id=1, source_target_pairs={{0,8},{1,9},{2,10},{3,11},{4,12},{5,13},{6,14},{7,15},{8,0},{9,1},... | collective-permute-start | bytes 147464 | tf_op jit(solution)/shard_map/ppermute | solution.py:442
  37.4 0.7 collective-permute-start.10
  38.1 1.2 %collective-permute-start.11 = (bf16[24,1024]{1,0:T(8,128)(2,1)S(1)}, bf16[24,1024]{1,0:T(8,128)(2,1)S(1)}, u32[]{:S(2)}, u32[]{:S(2)}) collective-permute-start(bf16[24,1024]{1,0:T(8,128)(2,1)S(1)} %get-tuple-element.59._.refs_0_), channel_id=1, source_target_pairs={{0,2},{1,3},{2,0},{3,1},{4,6},{5,7},{6,4},{7,5},{8,10},{9,11},{10,... | collective-permute-start | bytes 147464 | tf_op jit(solution)/shard_map/ppermute | solution.py:442
  39.3 3.9 %own.3 = (f32[128,1280]{1,0:T(8,128)S(1)}, f32[8,128]{1,0:T(8,128)S(1)}, bf16[4096,384]{1,0:T(8,128)(2,1)S(1)}, bf16[4096,384]{1,0:T(8,128)(2,1)S(1)}, bf16[384,4096]{1,0:T(8,128)(2,1)S(1)}) custom-call(s32[1]{0:T(128)} %bitcast.pos_ref, bf16[16,144,512]{2,1,0:T(8,128)(2,1)S(1)} %get-tuple-element.58.held, bf16[128,4096]{1,0:T(8,128)(2,1)S(1)} %copy-done, ...), custom_call_target="tpu_custom_call" | custom-call | flops 2000000000 | bytes 8000000 | tf_op jit(solution)/shard_map/own/pallas_call | solution.py:534
  43.2 0.0 collective-permute-done.8
  43.2 0.0 collective-permute-done.11.refs_0_
  43.3 0.1 collective-permute-start.13
  43.4 0.9 %collective-permute-start.12 = (bf16[72,1024]{1,0:T(8,128)(2,1)S(1)}, bf16[72,1024]{1,0:T(8,128)(2,1)S(1)}, u32[]{:S(2)}, u32[]{:S(2)}) collective-permute-start(bf16[72,1024]{1,0:T(8,128)(2,1)S(1)} %constant_dynamic-update-slice_fusion.6.refs_1_), channel_id=1, source_target_pairs={{0,2},{1,3},{2,0},{3,1},{4,6},{5,7},{6,4},{7,5},{8,10},{9,11},{10,... | collective-permute-start | bytes 442376 | tf_op jit(solution)/shard_map/ppermute | solution.py:442
  44.3 1.0 %own.4 = (f32[128,768]{1,0:T(8,128)S(1)}, f32[8,128]{1,0:T(8,128)S(1)}) custom-call(s32[1]{0:T(128)} %bitcast.pos_ref, bf16[16,144,512]{2,1,0:T(8,128)(2,1)S(1)} %get-tuple-element.58.held, bf16[128,4096]{1,0:T(8,128)(2,1)S(1)} %copy-done, bf16[128,4096]{1,0:T(8,128)(2,1)S(1)} %copy-done.1, f32[8,128]{1,0:T(8,128)S(1)} %get-tuple-element.76._.refs_8_), custom_call_target="tpu_custom_call" | custom-call | flops 2000000000 | bytes 8000000 | tf_op jit(solution)/shard_map/own/pallas_call | solution.py:534
  45.3 2.0 %expert.2 = (bf16[96,1024]{1,0:T(8,128)(2,1)S(1)}, bf16[96,1024]{1,0:T(8,128)(2,1)S(1)}) custom-call(bf16[24,1024]{1,0:T(8,128)(2,1)S(1)} %get-tuple-element.59._.refs_0_, bf16[72,1024]{1,0:T(8,128)(2,1)S(1)} %constant_dynamic-update-slice_fusion.6.refs_1_, bf16[96,1024]{1,0:T(8,128)(2,1)S(1)} %collective-permute-done.13.refs_2_, ...), custom_call_target="tpu_custom_call" | custom-call | flops 600000000 | bytes 2000000 | tf_op jit(solution)/shard_map/expert/pallas_call | solution.py:574
  47.3 2.3 %collective-permute-done.12.refs_1_ = bf16[72,1024]{1,0:T(8,128)(2,1)S(1)} collective-permute-done((bf16[72,1024]{1,0:T(8,128)(2,1)S(1)}, bf16[72,1024]{1,0:T(8,128)(2,1)S(1)}, u32[]{:S(2)}, u32[]{:S(2)}) %collective-permute-start.12) | collective-permute-done | bytes 147488 | tf_op jit(solution)/shard_map/ppermute | solution.py:442
  49.6 0.1 collective-permute-start.14
  49.7 1.4 %collective-permute-done.14.refs_2_ = bf16[96,1024]{1,0:T(8,128)(2,1)S(1)} collective-permute-done((bf16[96,1024]{1,0:T(8,128)(2,1)S(1)}, bf16[96,1024]{1,0:T(8,128)(2,1)S(1)}, u32[]{:S(2)}, u32[]{:S(2)}) %collective-permute-start.14) | collective-permute-done | bytes 196640 | tf_op jit(solution)/shard_map/ppermute | solution.py:442
  51.1 2.0 %expert.3 = (bf16[96,1024]{1,0:T(8,128)(2,1)S(1)}, bf16[96,1024]{1,0:T(8,128)(2,1)S(1)}) custom-call(bf16[24,1024]{1,0:T(8,128)(2,1)S(1)} %collective-permute-done.11.refs_0_, bf16[72,1024]{1,0:T(8,128)(2,1)S(1)} %collective-permute-done.12.refs_1_, bf16[96,1024]{1,0:T(8,128)(2,1)S(1)} %collective-permute-done.14.refs_2_, ...), custom_call_target="tpu_custom_call" | custom-call | flops 600000000 | bytes 2000000 | tf_op jit(solution)/shard_map/expert/pallas_call | solution.py:574
  53.2 0.2 collective-permute-start.16
  53.4 1.3 %collective-permute-done.16 = bf16[96,1024]{1,0:T(8,128)(2,1)S(1)} collective-permute-done((bf16[96,1024]{1,0:T(8,128)(2,1)S(1)}, bf16[96,1024]{1,0:T(8,128)(2,1)S(1)}, u32[]{:S(2)}, u32[]{:S(2)}) %collective-permute-start.16) | collective-permute-done | bytes 196640 | tf_op jit(solution)/shard_map/ppermute | solution.py:442
  54.7 0.9 %collective-permute-start.17 = (bf16[96,1024]{1,0:T(8,128)(2,1)S(1)}, bf16[96,1024]{1,0:T(8,128)(2,1)S(1)}, u32[]{:S(2)}, u32[]{:S(2)}) collective-permute-start(bf16[96,1024]{1,0:T(8,128)(2,1)S(1)} %add_convert_fusion.1), channel_id=1, source_target_pairs={{0,2},{1,3},{2,0},{3,1},{4,6},{5,7},{6,4},{7,5},{8,10},{9,11},{10,... | collective-permute-start | bytes 589832 | tf_op jit(solution)/shard_map/ppermute | solution.py:442
  55.6 1.7 %own.5 = (f32[128,2048]{1,0:T(8,128)S(1)}, f32[8,128]{1,0:T(8,128)S(1)}) custom-call(s32[1]{0:T(128)} %bitcast.pos_ref, bf16[16,144,512]{2,1,0:T(8,128)(2,1)S(1)} %get-tuple-element.58.held, bf16[128,4096]{1,0:T(8,128)(2,1)S(1)} %copy-done, bf16[128,4096]{1,0:T(8,128)(2,1)S(1)} %copy-done.1, bf16[96,1024]{1,0:T(8,128)(2,1)S(1)} %get-tuple-element.81._), custom_call_target="tpu_custom_call" | custom-call | flops 2000000000 | bytes 8000000 | tf_op jit(solution)/shard_map/own/pallas_call | solution.py:534
  57.4 4.4 %collective-permute-done.17 = bf16[96,1024]{1,0:T(8,128)(2,1)S(1)} collective-permute-done((bf16[96,1024]{1,0:T(8,128)(2,1)S(1)}, bf16[96,1024]{1,0:T(8,128)(2,1)S(1)}, u32[]{:S(2)}, u32[]{:S(2)}) %collective-permute-start.17) | collective-permute-done | bytes 196640 | tf_op jit(solution)/shard_map/ppermute | solution.py:442
  61.7 0.1 add_convert_fusion
  61.9 2.1 %collective-permute-start.20 = (bf16[24,1024]{1,0:T(8,128)(2,1)S(1)}, bf16[24,1024]{1,0:T(8,128)(2,1)S(1)}, u32[]{:S(2)}, u32[]{:S(2)}) collective-permute-start(bf16[24,1024]{1,0:T(8,128)(2,1)S(1)} %get-tuple-element.89), channel_id=1, source_target_pairs={{0,4},{1,5},{2,6},{3,7},{4,8},{5,9},{6,10},{7,11},{8,12},{9,13},{1... | collective-permute-start | bytes 147464 | tf_op jit(solution)/shard_map/ppermute | solution.py:442
  63.9 0.0 collective-permute-start.19
  63.9 2.4 %collective-permute-start.18 = (bf16[24,1024]{1,0:T(8,128)(2,1)S(1)}, bf16[24,1024]{1,0:T(8,128)(2,1)S(1)}, u32[]{:S(2)}, u32[]{:S(2)}) collective-permute-start(bf16[24,1024]{1,0:T(8,128)(2,1)S(1)} %get-tuple-element.91), channel_id=1, source_target_pairs={{0,12},{1,13},{2,14},{3,15},{4,0},{5,1},{6,2},{7,3},{8,4},{9,5},{1... | collective-permute-start | bytes 147464 | tf_op jit(solution)/shard_map/ppermute | solution.py:442
  66.4 1.7 %collective-permute-done.20.refs_6_ = bf16[24,1024]{1,0:T(8,128)(2,1)S(1)} collective-permute-done((bf16[24,1024]{1,0:T(8,128)(2,1)S(1)}, bf16[24,1024]{1,0:T(8,128)(2,1)S(1)}, u32[]{:S(2)}, u32[]{:S(2)}) %collective-permute-start.20) | collective-permute-done | bytes 49184 | tf_op jit(solution)/shard_map/ppermute | solution.py:442
  68.1 1.4 %collective-permute-done.19.refs_5_ = bf16[24,1024]{1,0:T(8,128)(2,1)S(1)} collective-permute-done((bf16[24,1024]{1,0:T(8,128)(2,1)S(1)}, bf16[24,1024]{1,0:T(8,128)(2,1)S(1)}, u32[]{:S(2)}, u32[]{:S(2)}) %collective-permute-start.19) | collective-permute-done | bytes 49184 | tf_op jit(solution)/shard_map/ppermute | solution.py:442
  69.4 0.0 collective-permute-done.18.refs_4_
  69.4 1.4 %combine.1 = bf16[128,4096]{1,0:T(8,128)(2,1)} custom-call(bf16[128,64]{1,0:T(8,128)(2,1)S(1)} %get-tuple-element.47.mix_ref, f32[128,1280]{1,0:T(8,128)S(1)} %get-tuple-element.60.refs_0_, f32[128,768]{1,0:T(8,128)S(1)} %get-tuple-element.62.refs_1_, f32[128,2048]{1,0:T(8,128)S(1)} %get-tuple-element.82.refs_2_, ...), custom_call_target="tpu_custom_call" | custom-call | tf_op jit(solution)/shard_map/combine/pallas_call | solution.py:607
  (22 shorter events, 0.2 us)
Async XLA Ops:
  1.0 11.1 %collective-permute-start = (bf16[144,512]{1,0:T(8,128)(2,1)S(1)}, bf16[144,512]{1,0:T(8,128)(2,1)S(1)}, u32[]{:S(2)}, u32[]{:S(2)}) collective-permute-start(bf16[144,512]{1,0:T(8,128)(2,1)S(1)} %pack.1.refs_0_), channel_id=1, source_target_pairs={{0,4},{1,5},{2,6},{3,7},{4,8},{5,9},{6,10},{7,11},{8,12},{9,13},{1... | collective-permute-start | bytes 442376 | tf_op jit(solution)/shard_map/ppermute | solution.py:442
  4.1 16.3 %collective-permute-start.5 = (bf16[144,512]{1,0:T(8,128)(2,1)S(1)}, bf16[144,512]{1,0:T(8,128)(2,1)S(1)}, u32[]{:S(2)}, u32[]{:S(2)}) collective-permute-start(bf16[144,512]{1,0:T(8,128)(2,1)S(1)} %pack.1.refs_0_), channel_id=1, source_target_pairs={{0,0},{1,1},{2,12},{3,13},{4,4},{5,5},{6,6},{7,7},{8,8},{9,9},{10,... | collective-permute-start | bytes 442376 | tf_op jit(solution)/shard_map/ppermute | solution.py:442
  4.7 10.8 %collective-permute-start.2 = (bf16[144,512]{1,0:T(8,128)(2,1)S(1)}, bf16[144,512]{1,0:T(8,128)(2,1)S(1)}, u32[]{:S(2)}, u32[]{:S(2)}) collective-permute-start(bf16[144,512]{1,0:T(8,128)(2,1)S(1)} %pack.1.refs_0_), channel_id=1, source_target_pairs={{0,2},{1,3},{2,0},{3,1},{4,6},{5,7},{6,4},{7,5},{8,10},{9,11},{10,... | collective-permute-start | bytes 442376 | tf_op jit(solution)/shard_map/ppermute | solution.py:442
  9.5 10.8 %collective-permute-start.1 = (bf16[144,512]{1,0:T(8,128)(2,1)S(1)}, bf16[144,512]{1,0:T(8,128)(2,1)S(1)}, u32[]{:S(2)}, u32[]{:S(2)}) collective-permute-start(bf16[144,512]{1,0:T(8,128)(2,1)S(1)} %pack.1.refs_0_), channel_id=1, source_target_pairs={{0,8},{1,9},{2,10},{3,11},{4,12},{5,13},{6,14},{7,15},{8,0},{9,1},... | collective-permute-start | bytes 442376 | tf_op jit(solution)/shard_map/ppermute | solution.py:442
  12.1 8.3 %collective-permute-start.3 = (bf16[144,512]{1,0:T(8,128)(2,1)S(1)}, bf16[144,512]{1,0:T(8,128)(2,1)S(1)}, u32[]{:S(2)}, u32[]{:S(2)}) collective-permute-start(bf16[144,512]{1,0:T(8,128)(2,1)S(1)} %collective-permute-done.refs_1_), channel_id=1, source_target_pairs={{0,0},{1,1},{2,2},{3,3},{4,6},{5,7},{6,4},{7,5},{8,10},{9,11},{10,... | collective-permute-start | bytes 442376 | tf_op jit(solution)/shard_map/ppermute | solution.py:442
  20.4 18.9 %copy-start = (bf16[128,4096]{1,0:T(8,128)(2,1)S(1)}, bf16[128,4096]{1,0:T(8,128)(2,1)}, u32[]{:S(2)}) copy-start(bf16[128,4096]{1,0:T(8,128)(2,1)} %q_ref.5) | copy-start | bytes 3145732
  20.4 18.9 %copy-start.1 = (bf16[128,4096]{1,0:T(8,128)(2,1)S(1)}, bf16[128,4096]{1,0:T(8,128)(2,1)}, u32[]{:S(2)}) copy-start(bf16[128,4096]{1,0:T(8,128)(2,1)} %x_ref.5) | copy-start | bytes 3145732
  20.4 2.5 %collective-permute-start.6 = (bf16[864,512]{1,0:T(8,128)(2,1)S(1)}, bf16[864,512]{1,0:T(8,128)(2,1)S(1)}, u32[]{:S(2)}, u32[]{:S(2)}) collective-permute-start(bf16[864,512]{1,0:T(8,128)(2,1)S(1)} %constant_dynamic-update-slice_fusion), channel_id=1, source_target_pairs={{0,1},{1,0},{2,3},{3,2},{4,5},{5,4},{6,7},{7,6},{8,9},{9,8},{10,11... | collective-permute-start | bytes 2654216 | tf_op jit(solution)/shard_map/ppermute | solution.py:442
  20.5 4.8 %collective-permute-start.4 = (bf16[144,512]{1,0:T(8,128)(2,1)S(1)}, bf16[144,512]{1,0:T(8,128)(2,1)S(1)}, u32[]{:S(2)}, u32[]{:S(2)}) collective-permute-start(bf16[144,512]{1,0:T(8,128)(2,1)S(1)} %collective-permute-done.1.refs_2_), channel_id=1, source_target_pairs={{0,0},{1,1},{2,2},{3,3},{4,4},{5,5},{6,6},{7,7},{8,10},{9,11},{10,... | collective-permute-start | bytes 442376 | tf_op jit(solution)/shard_map/ppermute | solution.py:442
  25.3 1.4 %collective-permute-start.7 = (bf16[144,512]{1,0:T(8,128)(2,1)S(1)}, bf16[144,512]{1,0:T(8,128)(2,1)S(1)}, u32[]{:S(2)}, u32[]{:S(2)}) collective-permute-start(bf16[144,512]{1,0:T(8,128)(2,1)S(1)} %collective-permute-done.4.refs_0_), channel_id=1, source_target_pairs={{0,1},{1,0},{2,3},{3,2},{4,5},{5,4},{6,7},{7,6},{8,9},{9,8},{10,11... | collective-permute-start | bytes 442376 | tf_op jit(solution)/shard_map/ppermute | solution.py:442
  29.5 13.7 %collective-permute-start.8 = (bf16[24,1024]{1,0:T(8,128)(2,1)S(1)}, bf16[24,1024]{1,0:T(8,128)(2,1)S(1)}, u32[]{:S(2)}, u32[]{:S(2)}) collective-permute-start(bf16[24,1024]{1,0:T(8,128)(2,1)S(1)} %get-tuple-element.63), channel_id=1, source_target_pairs={{0,4},{1,5},{2,6},{3,7},{4,8},{5,9},{6,10},{7,11},{8,12},{9,13},{1... | collective-permute-start | bytes 147464 | tf_op jit(solution)/shard_map/ppermute | solution.py:442
  30.9 12.3 %collective-permute-start.9 = (bf16[24,1024]{1,0:T(8,128)(2,1)S(1)}, bf16[24,1024]{1,0:T(8,128)(2,1)S(1)}, u32[]{:S(2)}, u32[]{:S(2)}) collective-permute-start(bf16[24,1024]{1,0:T(8,128)(2,1)S(1)} %get-tuple-element.64), channel_id=1, source_target_pairs={{0,8},{1,9},{2,10},{3,11},{4,12},{5,13},{6,14},{7,15},{8,0},{9,1},... | collective-permute-start | bytes 147464 | tf_op jit(solution)/shard_map/ppermute | solution.py:442
  37.4 5.8 %collective-permute-start.10 = (bf16[24,1024]{1,0:T(8,128)(2,1)S(1)}, bf16[24,1024]{1,0:T(8,128)(2,1)S(1)}, u32[]{:S(2)}, u32[]{:S(2)}) collective-permute-start(bf16[24,1024]{1,0:T(8,128)(2,1)S(1)} %get-tuple-element.65), channel_id=1, source_target_pairs={{0,12},{1,13},{2,14},{3,15},{4,0},{5,1},{6,2},{7,3},{8,4},{9,5},{1... | collective-permute-start | bytes 147464 | tf_op jit(solution)/shard_map/ppermute | solution.py:442
  38.1 5.1 %collective-permute-start.11 = (bf16[24,1024]{1,0:T(8,128)(2,1)S(1)}, bf16[24,1024]{1,0:T(8,128)(2,1)S(1)}, u32[]{:S(2)}, u32[]{:S(2)}) collective-permute-start(bf16[24,1024]{1,0:T(8,128)(2,1)S(1)} %get-tuple-element.59._.refs_0_), channel_id=1, source_target_pairs={{0,2},{1,3},{2,0},{3,1},{4,6},{5,7},{6,4},{7,5},{8,10},{9,11},{10,... | collective-permute-start | bytes 147464 | tf_op jit(solution)/shard_map/ppermute | solution.py:442
  43.3 2.0 %collective-permute-start.13 = (bf16[96,1024]{1,0:T(8,128)(2,1)S(1)}, bf16[96,1024]{1,0:T(8,128)(2,1)S(1)}, u32[]{:S(2)}, u32[]{:S(2)}) collective-permute-start(bf16[96,1024]{1,0:T(8,128)(2,1)S(1)} %pad_maximum_fusion), channel_id=1, source_target_pairs={{0,1},{1,0},{2,3},{3,2},{4,5},{5,4},{6,7},{7,6},{8,9},{9,8},{10,11... | collective-permute-start | bytes 589832 | tf_op jit(solution)/shard_map/ppermute | solution.py:442
  43.4 6.3 %collective-permute-start.12 = (bf16[72,1024]{1,0:T(8,128)(2,1)S(1)}, bf16[72,1024]{1,0:T(8,128)(2,1)S(1)}, u32[]{:S(2)}, u32[]{:S(2)}) collective-permute-start(bf16[72,1024]{1,0:T(8,128)(2,1)S(1)} %constant_dynamic-update-slice_fusion.6.refs_1_), channel_id=1, source_target_pairs={{0,2},{1,3},{2,0},{3,1},{4,6},{5,7},{6,4},{7,5},{8,10},{9,11},{10,... | collective-permute-start | bytes 442376 | tf_op jit(solution)/shard_map/ppermute | solution.py:442
  49.6 1.5 %collective-permute-start.14 = (bf16[96,1024]{1,0:T(8,128)(2,1)S(1)}, bf16[96,1024]{1,0:T(8,128)(2,1)S(1)}, u32[]{:S(2)}, u32[]{:S(2)}) collective-permute-start(bf16[96,1024]{1,0:T(8,128)(2,1)S(1)} %pad_maximum_fusion.1), channel_id=1, source_target_pairs={{0,1},{1,0},{2,3},{3,2},{4,5},{5,4},{6,7},{7,6},{8,9},{9,8},{10,11... | collective-permute-start | bytes 589832 | tf_op jit(solution)/shard_map/ppermute | solution.py:442
  53.2 1.5 %collective-permute-start.16 = (bf16[96,1024]{1,0:T(8,128)(2,1)S(1)}, bf16[96,1024]{1,0:T(8,128)(2,1)S(1)}, u32[]{:S(2)}, u32[]{:S(2)}) collective-permute-start(bf16[96,1024]{1,0:T(8,128)(2,1)S(1)} %get-tuple-element.85), channel_id=1, source_target_pairs={{0,1},{1,0},{2,3},{3,2},{4,5},{5,4},{6,7},{7,6},{8,9},{9,8},{10,11... | collective-permute-start | bytes 589832 | tf_op jit(solution)/shard_map/ppermute | solution.py:442
  54.7 7.0 %collective-permute-start.17 = (bf16[96,1024]{1,0:T(8,128)(2,1)S(1)}, bf16[96,1024]{1,0:T(8,128)(2,1)S(1)}, u32[]{:S(2)}, u32[]{:S(2)}) collective-permute-start(bf16[96,1024]{1,0:T(8,128)(2,1)S(1)} %add_convert_fusion.1), channel_id=1, source_target_pairs={{0,2},{1,3},{2,0},{3,1},{4,6},{5,7},{6,4},{7,5},{8,10},{9,11},{10,... | collective-permute-start | bytes 589832 | tf_op jit(solution)/shard_map/ppermute | solution.py:442
  55.6 6.1 %collective-permute-start.15 = (bf16[96,1024]{1,0:T(8,128)(2,1)S(1)}, bf16[96,1024]{1,0:T(8,128)(2,1)S(1)}, u32[]{:S(2)}, u32[]{:S(2)}) collective-permute-start(bf16[96,1024]{1,0:T(8,128)(2,1)S(1)} %get-tuple-element.84), channel_id=1, source_target_pairs={{0,1},{1,0},{2,3},{3,2},{4,5},{5,4},{6,7},{7,6},{8,9},{9,8},{10,11... | collective-permute-start | bytes 589832 | tf_op jit(solution)/shard_map/ppermute | solution.py:442
  61.9 6.2 %collective-permute-start.20 = (bf16[24,1024]{1,0:T(8,128)(2,1)S(1)}, bf16[24,1024]{1,0:T(8,128)(2,1)S(1)}, u32[]{:S(2)}, u32[]{:S(2)}) collective-permute-start(bf16[24,1024]{1,0:T(8,128)(2,1)S(1)} %get-tuple-element.89), channel_id=1, source_target_pairs={{0,4},{1,5},{2,6},{3,7},{4,8},{5,9},{6,10},{7,11},{8,12},{9,13},{1... | collective-permute-start | bytes 147464 | tf_op jit(solution)/shard_map/ppermute | solution.py:442
  63.9 5.5 %collective-permute-start.19 = (bf16[24,1024]{1,0:T(8,128)(2,1)S(1)}, bf16[24,1024]{1,0:T(8,128)(2,1)S(1)}, u32[]{:S(2)}, u32[]{:S(2)}) collective-permute-start(bf16[24,1024]{1,0:T(8,128)(2,1)S(1)} %get-tuple-element.90), channel_id=1, source_target_pairs={{0,8},{1,9},{2,10},{3,11},{4,12},{5,13},{6,14},{7,15},{8,0},{9,1},... | collective-permute-start | bytes 147464 | tf_op jit(solution)/shard_map/ppermute | solution.py:442
  63.9 5.5 %collective-permute-start.18 = (bf16[24,1024]{1,0:T(8,128)(2,1)S(1)}, bf16[24,1024]{1,0:T(8,128)(2,1)S(1)}, u32[]{:S(2)}, u32[]{:S(2)}) collective-permute-start(bf16[24,1024]{1,0:T(8,128)(2,1)S(1)} %get-tuple-element.91), channel_id=1, source_target_pairs={{0,12},{1,13},{2,14},{3,15},{4,0},{5,1},{6,2},{7,3},{8,4},{9,5},{1... | collective-permute-start | bytes 147464 | tf_op jit(solution)/shard_map/ppermute | solution.py:442

commit v10 on v9

--- a/solution.py
+++ b/solution.py
@@ -18,7 +18,8 @@
 CUT = 4
 PIECE = CUT * CAP
 TILE = 128
-KEYS = 256
+KEYS = 512
+STEP = KEYS // TILE
 KV_ROWS = TILE + 16
 SCALE = math.log2(math.e) / math.sqrt(HEAD)
 LOW = -1e30
@@ -184,7 +185,7 @@
 
 def key_steps(pos, place, first, bias_ref, step, state):
     low = jnp.min(first).astype(jnp.int32) // KEYS
-    last = pos // (KEYS // TILE)
+    last = pos // STEP
     clear = jnp.minimum((jnp.max(first).astype(jnp.int32) + KEYS - 1) // KEYS, last)
 
     def edge(j, carried):
@@ -204,7 +205,7 @@
 
 def keys_of(held, kb, h):
     keys = jnp.concatenate(
-        [held[2 * kb + t, 0:TILE, h * HEAD : (h + 1) * HEAD] for t in range(2)], axis=0
+        [held[STEP * kb + t, 0:TILE, h * HEAD : (h + 1) * HEAD] for t in range(STEP)], axis=0
     )
     return jnp.concatenate([keys, keys], axis=1)
 
@@ -212,7 +213,7 @@
 def values_of(held, kb, h):
     at = (KV_HEADS + h) * HEAD
     values = jnp.concatenate(
-        [held[2 * kb + t, 0:TILE, at : at + HEAD] for t in range(2)], axis=1
+        [held[STEP * kb + t, 0:TILE, at : at + HEAD] for t in range(STEP)], axis=1
     )
     return jnp.concatenate([values, jnp.ones((EXTRA, KEYS), BF16)], axis=0)
 
@@ -493,6 +494,7 @@
     early.append(move(jnp.concatenate(early, axis=0), flip_c))
     early_senders = [(i, 0, 0, *side) for i, side in enumerate(sides)]
     early_senders += [(len(sides), i * KV_ROWS, 1, *side) for i, side in enumerate(sides)]
+    early_senders += [(0, 0, flip, 0, far) for flip in (0, 1)]
     late_senders = [(flip, 0, flip, 1, far - 1) for flip in (0, 1)]
     held_shape = jax.ShapeDtypeStruct((n, KV_ROWS, 4 * HEAD), BF16)
     held = pl.pallas_call(

time: 71.4 us -> 70.9 us (level)
  waiting for transfers between devices: 22.8 us -> 20.3 us
  Pallas kernels: 20.6 us -> 22.3 us
    ppermute x21, waiting for transfers between devices: 22.8 us -> 20.3 us  [move(): return lax.ppermute(value, 'expert', pairs)]
    pallas_call x3, Pallas kernels: 6.64 us -> 7.59 us  [own(): pl.pallas_call(functools.partial(own_kernel, n, heads, len(sources)), out...]
  transfers between devices with their start and end apart: 21 -> 21, of which waited for: 10 -> 10; matrix products, arithmetic and copies ran while one was open for 0% -> 0% of each run, Pallas kernels for 19% -> 21%
where the time goes in v10:
time: 70.9 us; the launch traced here: 70.5 us
  starting transfers between devices  27.2 us (38%)
  Pallas kernels  22.3 us (31%)
  waiting for transfers between devices  20.3 us (29%)
    ppermute x21, starting transfers between devices, move(): return lax.ppermute(value, 'expert', pairs)  27.2 us
    ppermute x21, waiting for transfers between devices, move(): return lax.ppermute(value, 'expert', pairs)  20.3 us
    pallas_call x3, Pallas kernels, own(): pl.pallas_call(functools.partial(own_kernel, n, heads, len(sources)), out...  7.59 us
    pallas_call x2, Pallas kernels, expert(): pl.pallas_call(functools.partial(expert_kernel, n // 2, len(pieces)), out...  4.07 us
    pallas_call x1, Pallas kernels, local(): pl.pallas_call(functools.partial(routed_kernel, n, late_senders), out_sha...  2.95 us
    pallas_call x1, Pallas kernels, local(): pl.pallas_call(functools.partial(collect_kernel, n, early_senders), out_s...  2.88 us
    pallas_call x1, Pallas kernels, local(): pl.pallas_call(functools.partial(select_kernel, planes), out_shape=[jax.S...  2.49 us
  transfers between devices with their start and end apart: 21, of which 10 were waited for; matrix products, arithmetic and copies ran while one was open for 0% of the time, Pallas kernels for 21%

profile of v10, /device:TPU:0, one launch (start us, length us, event | category | flops | bytes accessed | tf_op | source)
XLA Modules:
  0.0 70.5 jit_solution(14645838197976474266)
XLA Ops:
  0.0 1.0 %pack.1.refs_0_ = bf16[144,512]{1,0:T(8,128)(2,1)S(1)} custom-call(s32[1,128]{1,0:T(1,128)} %bitcast.8, bf16[128,256]{1,0:T(8,128)(2,1)} %keys_ref.1, bf16[128,256]{1,0:T(8,128)(2,1)} %values_ref.1), custom_call_target="tpu_custom_call" | custom-call | tf_op jit(solution)/shard_map/pack/pallas_call | solution.py:428
  1.0 3.1 %collective-permute-start = (bf16[144,512]{1,0:T(8,128)(2,1)S(1)}, bf16[144,512]{1,0:T(8,128)(2,1)S(1)}, u32[]{:S(2)}, u32[]{:S(2)}) collective-permute-start(bf16[144,512]{1,0:T(8,128)(2,1)S(1)} %pack.1.refs_0_), channel_id=1, source_target_pairs={{0,4},{1,5},{2,6},{3,7},{4,8},{5,9},{6,10},{7,11},{8,12},{9,13},{1... | collective-permute-start | bytes 442376 | tf_op jit(solution)/shard_map/ppermute | solution.py:443
  4.1 0.7 collective-permute-start.5
  4.7 4.8 %collective-permute-start.2 = (bf16[144,512]{1,0:T(8,128)(2,1)S(1)}, bf16[144,512]{1,0:T(8,128)(2,1)S(1)}, u32[]{:S(2)}, u32[]{:S(2)}) collective-permute-start(bf16[144,512]{1,0:T(8,128)(2,1)S(1)} %pack.1.refs_0_), channel_id=1, source_target_pairs={{0,2},{1,3},{2,0},{3,1},{4,6},{5,7},{6,4},{7,5},{8,10},{9,11},{10,... | collective-permute-start | bytes 442376 | tf_op jit(solution)/shard_map/ppermute | solution.py:443
  9.5 0.0 collective-permute-start.1
  9.5 2.5 %select.1 = (bf16[2,256,384]{2,1,0:T(8,128)(2,1)S(1)}, f32[24,4096]{1,0:T(8,128)S(1)}, f32[8,384]{1,0:T(8,128)S(1)}, bf16[128,64]{1,0:T(8,128)(2,1)S(1)}, bf16[1...) custom-call(s32[1]{0:T(128)} %bitcast.pos_ref, s32[4,128]{1,0:T(4,128)} %bitcast.6, s32[1,128]{1,0:T(1,128)} %bitcast.9, ...), custom_call_target="tpu_custom_call" | custom-call | tf_op jit(solution)/shard_map/select/pallas_call | solution.py:453
  12.0 0.0 collective-permute-done.refs_1_
  12.1 0.7 collective-permute-start.3
  12.8 2.8 %collective-permute-done.2.refs_4_ = bf16[144,512]{1,0:T(8,128)(2,1)S(1)} collective-permute-done((bf16[144,512]{1,0:T(8,128)(2,1)S(1)}, bf16[144,512]{1,0:T(8,128)(2,1)S(1)}, u32[]{:S(2)}, u32[]{:S(2)}) %collective-permute-start.2) | collective-permute-done | bytes 147488 | tf_op jit(solution)/shard_map/ppermute | solution.py:443
  15.5 4.8 %collective-permute-done.1.refs_2_ = bf16[144,512]{1,0:T(8,128)(2,1)S(1)} collective-permute-done((bf16[144,512]{1,0:T(8,128)(2,1)S(1)}, bf16[144,512]{1,0:T(8,128)(2,1)S(1)}, u32[]{:S(2)}, u32[]{:S(2)}) %collective-permute-start.1) | collective-permute-done | bytes 147488 | tf_op jit(solution)/shard_map/ppermute | solution.py:443
  20.3 0.0 collective-permute-done.3.refs_5_
  20.4 0.0 copy-start
  20.4 0.0 copy-start.1
  20.4 0.1 collective-permute-start.6
  20.5 0.8 %collective-permute-start.4 = (bf16[144,512]{1,0:T(8,128)(2,1)S(1)}, bf16[144,512]{1,0:T(8,128)(2,1)S(1)}, u32[]{:S(2)}, u32[]{:S(2)}) collective-permute-start(bf16[144,512]{1,0:T(8,128)(2,1)S(1)} %collective-permute-done.1.refs_2_), channel_id=1, source_target_pairs={{0,0},{1,1},{2,2},{3,3},{4,4},{5,5},{6,6},{7,7},{8,10},{9,11},{10,... | collective-permute-start | bytes 442376 | tf_op jit(solution)/shard_map/ppermute | solution.py:443
  21.3 1.6 %collective-permute-done.6.refs_6_ = bf16[864,512]{1,0:T(8,128)(2,1)S(1)} collective-permute-done((bf16[864,512]{1,0:T(8,128)(2,1)S(1)}, bf16[864,512]{1,0:T(8,128)(2,1)S(1)}, u32[]{:S(2)}, u32[]{:S(2)}) %collective-permute-start.6) | collective-permute-done | bytes 884768 | tf_op jit(solution)/shard_map/ppermute | solution.py:443
  22.9 2.9 %collect.1._ = bf16[16,144,512]{2,1,0:T(8,128)(2,1)S(1)} custom-call(s32[1]{0:T(128)} %bitcast.pos_ref, bf16[144,512]{1,0:T(8,128)(2,1)S(1)} %pack.1.refs_0_, bf16[144,512]{1,0:T(8,128)(2,1)S(1)} %collective-permute-done.refs_1_, bf16[144,512]{1,0:T(8,128)(2,1)S(1)} %collective-permute-done.1.refs_2_, bf16[144,512]{1,0:T(8,128)(2,1)S(1)} %collective-permute-done.5.refs_3_, ...), custom_call_target="tpu_custom_call" | custom-call | bytes 1000 | tf_op jit(solution)/shard_map/collect/pallas_call | solution.py:500
  25.8 0.0 collective-permute-done.4.refs_0_
  25.8 0.2 collective-permute-start.7
  26.0 1.2 %collective-permute-done.7.refs_1_ = bf16[144,512]{1,0:T(8,128)(2,1)S(1)} collective-permute-done((bf16[144,512]{1,0:T(8,128)(2,1)S(1)}, bf16[144,512]{1,0:T(8,128)(2,1)S(1)}, u32[]{:S(2)}, u32[]{:S(2)}) %collective-permute-start.7) | collective-permute-done | bytes 147488 | tf_op jit(solution)/shard_map/ppermute | solution.py:443
  27.3 3.0 %routed.1 = (bf16[24,1024]{1,0:T(8,128)(2,1)S(1)}, bf16[24,1024]{1,0:T(8,128)(2,1)S(1)}, bf16[24,1024]{1,0:T(8,128)(2,1)S(1)}, bf16[24,1024]{1,0:T(8,128)(2,1)S(1)}, bf16[16,144,512]{2,1,0:T(8,128)(2,1)S(1)}) custom-call(s32[1]{0:T(128)} %bitcast.pos_ref, f32[1,4096]{1,0:T(1,128)} %bitcast.5, ...), custom_call_target="tpu_custom_call", output_to_operand_aliasing={{4}: (5, {})} | custom-call | tf_op jit(solution)/shard_map/routed/pallas_call | solution.py:514
  30.2 1.8 %collective-permute-start.8 = (bf16[24,1024]{1,0:T(8,128)(2,1)S(1)}, bf16[24,1024]{1,0:T(8,128)(2,1)S(1)}, u32[]{:S(2)}, u32[]{:S(2)}) collective-permute-start(bf16[24,1024]{1,0:T(8,128)(2,1)S(1)} %get-tuple-element.63), channel_id=1, source_target_pairs={{0,4},{1,5},{2,6},{3,7},{4,8},{5,9},{6,10},{7,11},{8,12},{9,13},{1... | collective-permute-start | bytes 147464 | tf_op jit(solution)/shard_map/ppermute | solution.py:443
  32.0 5.5 %collective-permute-start.9 = (bf16[24,1024]{1,0:T(8,128)(2,1)S(1)}, bf16[24,1024]{1,0:T(8,128)(2,1)S(1)}, u32[]{:S(2)}, u32[]{:S(2)}) collective-permute-start(bf16[24,1024]{1,0:T(8,128)(2,1)S(1)} %get-tuple-element.64), channel_id=1, source_target_pairs={{0,8},{1,9},{2,10},{3,11},{4,12},{5,13},{6,14},{7,15},{8,0},{9,1},... | collective-permute-start | bytes 147464 | tf_op jit(solution)/shard_map/ppermute | solution.py:443
  37.5 1.2 %collective-permute-start.10 = (bf16[24,1024]{1,0:T(8,128)(2,1)S(1)}, bf16[24,1024]{1,0:T(8,128)(2,1)S(1)}, u32[]{:S(2)}, u32[]{:S(2)}) collective-permute-start(bf16[24,1024]{1,0:T(8,128)(2,1)S(1)} %get-tuple-element.65), channel_id=1, source_target_pairs={{0,12},{1,13},{2,14},{3,15},{4,0},{5,1},{6,2},{7,3},{8,4},{9,5},{1... | collective-permute-start | bytes 147464 | tf_op jit(solution)/shard_map/ppermute | solution.py:443
  38.7 0.3 collective-permute-start.11
  39.0 3.9 %own.3 = (f32[128,1280]{1,0:T(8,128)S(1)}, f32[8,128]{1,0:T(8,128)S(1)}, bf16[4096,384]{1,0:T(8,128)(2,1)S(1)}, bf16[4096,384]{1,0:T(8,128)(2,1)S(1)}, bf16[384,4096]{1,0:T(8,128)(2,1)S(1)}) custom-call(s32[1]{0:T(128)} %bitcast.pos_ref, bf16[16,144,512]{2,1,0:T(8,128)(2,1)S(1)} %get-tuple-element.58.held, bf16[128,4096]{1,0:T(8,128)(2,1)S(1)} %copy-done, ...), custom_call_target="tpu_custom_call" | custom-call | flops 2000000000 | bytes 8000000 | tf_op jit(solution)/shard_map/own/pallas_call | solution.py:536
  42.8 0.0 collective-permute-done.8
  42.9 0.0 collective-permute-done.10
  42.9 0.1 collective-permute-start.13
  43.0 1.8 %collective-permute-start.12 = (bf16[72,1024]{1,0:T(8,128)(2,1)S(1)}, bf16[72,1024]{1,0:T(8,128)(2,1)S(1)}, u32[]{:S(2)}, u32[]{:S(2)}) collective-permute-start(bf16[72,1024]{1,0:T(8,128)(2,1)S(1)} %constant_dynamic-update-slice_fusion.6.refs_1_), channel_id=1, source_target_pairs={{0,2},{1,3},{2,0},{3,1},{4,6},{5,7},{6,4},{7,5},{8,10},{9,11},{10,... | collective-permute-start | bytes 442376 | tf_op jit(solution)/shard_map/ppermute | solution.py:443
  44.8 1.4 %own.4 = (f32[128,768]{1,0:T(8,128)S(1)}, f32[8,128]{1,0:T(8,128)S(1)}) custom-call(s32[1]{0:T(128)} %bitcast.pos_ref, bf16[16,144,512]{2,1,0:T(8,128)(2,1)S(1)} %get-tuple-element.58.held, bf16[128,4096]{1,0:T(8,128)(2,1)S(1)} %copy-done, bf16[128,4096]{1,0:T(8,128)(2,1)S(1)} %copy-done.1, f32[8,128]{1,0:T(8,128)S(1)} %get-tuple-element.76._.refs_8_), custom_call_target="tpu_custom_call" | custom-call | flops 2000000000 | bytes 8000000 | tf_op jit(solution)/shard_map/own/pallas_call | solution.py:536
  46.2 2.1 %expert.2 = (bf16[96,1024]{1,0:T(8,128)(2,1)S(1)}, bf16[96,1024]{1,0:T(8,128)(2,1)S(1)}) custom-call(bf16[24,1024]{1,0:T(8,128)(2,1)S(1)} %get-tuple-element.59._.refs_0_, bf16[72,1024]{1,0:T(8,128)(2,1)S(1)} %constant_dynamic-update-slice_fusion.6.refs_1_, bf16[96,1024]{1,0:T(8,128)(2,1)S(1)} %collective-permute-done.13.refs_2_, ...), custom_call_target="tpu_custom_call" | custom-call | flops 600000000 | bytes 2000000 | tf_op jit(solution)/shard_map/expert/pallas_call | solution.py:576
  48.3 1.0 %collective-permute-done.12.refs_1_ = bf16[72,1024]{1,0:T(8,128)(2,1)S(1)} collective-permute-done((bf16[72,1024]{1,0:T(8,128)(2,1)S(1)}, bf16[72,1024]{1,0:T(8,128)(2,1)S(1)}, u32[]{:S(2)}, u32[]{:S(2)}) %collective-permute-start.12) | collective-permute-done | bytes 147488 | tf_op jit(solution)/shard_map/ppermute | solution.py:443
  49.3 0.1 collective-permute-start.14
  49.4 1.4 %collective-permute-done.14.refs_2_ = bf16[96,1024]{1,0:T(8,128)(2,1)S(1)} collective-permute-done((bf16[96,1024]{1,0:T(8,128)(2,1)S(1)}, bf16[96,1024]{1,0:T(8,128)(2,1)S(1)}, u32[]{:S(2)}, u32[]{:S(2)}) %collective-permute-start.14) | collective-permute-done | bytes 196640 | tf_op jit(solution)/shard_map/ppermute | solution.py:443
  50.8 2.0 %expert.3 = (bf16[96,1024]{1,0:T(8,128)(2,1)S(1)}, bf16[96,1024]{1,0:T(8,128)(2,1)S(1)}) custom-call(bf16[24,1024]{1,0:T(8,128)(2,1)S(1)} %collective-permute-done.11.refs_0_, bf16[72,1024]{1,0:T(8,128)(2,1)S(1)} %collective-permute-done.12.refs_1_, bf16[96,1024]{1,0:T(8,128)(2,1)S(1)} %collective-permute-done.14.refs_2_, ...), custom_call_target="tpu_custom_call" | custom-call | flops 600000000 | bytes 2000000 | tf_op jit(solution)/shard_map/expert/pallas_call | solution.py:576
  52.8 0.2 collective-permute-start.16
  53.0 1.3 %collective-permute-done.16 = bf16[96,1024]{1,0:T(8,128)(2,1)S(1)} collective-permute-done((bf16[96,1024]{1,0:T(8,128)(2,1)S(1)}, bf16[96,1024]{1,0:T(8,128)(2,1)S(1)}, u32[]{:S(2)}, u32[]{:S(2)}) %collective-permute-start.16) | collective-permute-done | bytes 196640 | tf_op jit(solution)/shard_map/ppermute | solution.py:443
  54.4 1.8 %collective-permute-start.17 = (bf16[96,1024]{1,0:T(8,128)(2,1)S(1)}, bf16[96,1024]{1,0:T(8,128)(2,1)S(1)}, u32[]{:S(2)}, u32[]{:S(2)}) collective-permute-start(bf16[96,1024]{1,0:T(8,128)(2,1)S(1)} %add_convert_fusion.1), channel_id=1, source_target_pairs={{0,2},{1,3},{2,0},{3,1},{4,6},{5,7},{6,4},{7,5},{8,10},{9,11},{10,... | collective-permute-start | bytes 589832 | tf_op jit(solution)/shard_map/ppermute | solution.py:443
  56.2 2.3 %own.5 = (f32[128,2048]{1,0:T(8,128)S(1)}, f32[8,128]{1,0:T(8,128)S(1)}) custom-call(s32[1]{0:T(128)} %bitcast.pos_ref, bf16[16,144,512]{2,1,0:T(8,128)(2,1)S(1)} %get-tuple-element.58.held, bf16[128,4096]{1,0:T(8,128)(2,1)S(1)} %copy-done, bf16[128,4096]{1,0:T(8,128)(2,1)S(1)} %copy-done.1, bf16[96,1024]{1,0:T(8,128)(2,1)S(1)} %get-tuple-element.81._), custom_call_target="tpu_custom_call" | custom-call | flops 2000000000 | bytes 8000000 | tf_op jit(solution)/shard_map/own/pallas_call | solution.py:536
  58.5 2.9 %collective-permute-done.17 = bf16[96,1024]{1,0:T(8,128)(2,1)S(1)} collective-permute-done((bf16[96,1024]{1,0:T(8,128)(2,1)S(1)}, bf16[96,1024]{1,0:T(8,128)(2,1)S(1)}, u32[]{:S(2)}, u32[]{:S(2)}) %collective-permute-start.17) | collective-permute-done | bytes 196640 | tf_op jit(solution)/shard_map/ppermute | solution.py:443
  61.4 0.1 add_convert_fusion
  61.5 1.7 %collective-permute-start.20 = (bf16[24,1024]{1,0:T(8,128)(2,1)S(1)}, bf16[24,1024]{1,0:T(8,128)(2,1)S(1)}, u32[]{:S(2)}, u32[]{:S(2)}) collective-permute-start(bf16[24,1024]{1,0:T(8,128)(2,1)S(1)} %get-tuple-element.89), channel_id=1, source_target_pairs={{0,4},{1,5},{2,6},{3,7},{4,8},{5,9},{6,10},{7,11},{8,12},{9,13},{1... | collective-permute-start | bytes 147464 | tf_op jit(solution)/shard_map/ppermute | solution.py:443
  63.2 0.6 collective-permute-start.19
  63.8 1.9 %collective-permute-start.18 = (bf16[24,1024]{1,0:T(8,128)(2,1)S(1)}, bf16[24,1024]{1,0:T(8,128)(2,1)S(1)}, u32[]{:S(2)}, u32[]{:S(2)}) collective-permute-start(bf16[24,1024]{1,0:T(8,128)(2,1)S(1)} %get-tuple-element.91), channel_id=1, source_target_pairs={{0,12},{1,13},{2,14},{3,15},{4,0},{5,1},{6,2},{7,3},{8,4},{9,5},{1... | collective-permute-start | bytes 147464 | tf_op jit(solution)/shard_map/ppermute | solution.py:443
  65.7 2.3 %collective-permute-done.20.refs_6_ = bf16[24,1024]{1,0:T(8,128)(2,1)S(1)} collective-permute-done((bf16[24,1024]{1,0:T(8,128)(2,1)S(1)}, bf16[24,1024]{1,0:T(8,128)(2,1)S(1)}, u32[]{:S(2)}, u32[]{:S(2)}) %collective-permute-start.20) | collective-permute-done | bytes 49184 | tf_op jit(solution)/shard_map/ppermute | solution.py:443
  68.0 1.0 %collective-permute-done.19.refs_5_ = bf16[24,1024]{1,0:T(8,128)(2,1)S(1)} collective-permute-done((bf16[24,1024]{1,0:T(8,128)(2,1)S(1)}, bf16[24,1024]{1,0:T(8,128)(2,1)S(1)}, u32[]{:S(2)}, u32[]{:S(2)}) %collective-permute-start.19) | collective-permute-done | bytes 49184 | tf_op jit(solution)/shard_map/ppermute | solution.py:443
  68.9 1.4 %combine.1 = bf16[128,4096]{1,0:T(8,128)(2,1)} custom-call(bf16[128,64]{1,0:T(8,128)(2,1)S(1)} %get-tuple-element.47.mix_ref, f32[128,1280]{1,0:T(8,128)S(1)} %get-tuple-element.60.refs_0_, f32[128,768]{1,0:T(8,128)S(1)} %get-tuple-element.62.refs_1_, f32[128,2048]{1,0:T(8,128)S(1)} %get-tuple-element.82.refs_2_, ...), custom_call_target="tpu_custom_call" | custom-call | tf_op jit(solution)/shard_map/combine/pallas_call | solution.py:609
  (22 shorter events, 0.2 us)
Async XLA Ops:
  1.0 11.1 %collective-permute-start = (bf16[144,512]{1,0:T(8,128)(2,1)S(1)}, bf16[144,512]{1,0:T(8,128)(2,1)S(1)}, u32[]{:S(2)}, u32[]{:S(2)}) collective-permute-start(bf16[144,512]{1,0:T(8,128)(2,1)S(1)} %pack.1.refs_0_), channel_id=1, source_target_pairs={{0,4},{1,5},{2,6},{3,7},{4,8},{5,9},{6,10},{7,11},{8,12},{9,13},{1... | collective-permute-start | bytes 442376 | tf_op jit(solution)/shard_map/ppermute | solution.py:443
  4.1 16.3 %collective-permute-start.5 = (bf16[144,512]{1,0:T(8,128)(2,1)S(1)}, bf16[144,512]{1,0:T(8,128)(2,1)S(1)}, u32[]{:S(2)}, u32[]{:S(2)}) collective-permute-start(bf16[144,512]{1,0:T(8,128)(2,1)S(1)} %pack.1.refs_0_), channel_id=1, source_target_pairs={{0,0},{1,1},{2,12},{3,13},{4,4},{5,5},{6,6},{7,7},{8,8},{9,9},{10,... | collective-permute-start | bytes 442376 | tf_op jit(solution)/shard_map/ppermute | solution.py:443
  4.7 10.8 %collective-permute-start.2 = (bf16[144,512]{1,0:T(8,128)(2,1)S(1)}, bf16[144,512]{1,0:T(8,128)(2,1)S(1)}, u32[]{:S(2)}, u32[]{:S(2)}) collective-permute-start(bf16[144,512]{1,0:T(8,128)(2,1)S(1)} %pack.1.refs_0_), channel_id=1, source_target_pairs={{0,2},{1,3},{2,0},{3,1},{4,6},{5,7},{6,4},{7,5},{8,10},{9,11},{10,... | collective-permute-start | bytes 442376 | tf_op jit(solution)/shard_map/ppermute | solution.py:443
  9.5 10.8 %collective-permute-start.1 = (bf16[144,512]{1,0:T(8,128)(2,1)S(1)}, bf16[144,512]{1,0:T(8,128)(2,1)S(1)}, u32[]{:S(2)}, u32[]{:S(2)}) collective-permute-start(bf16[144,512]{1,0:T(8,128)(2,1)S(1)} %pack.1.refs_0_), channel_id=1, source_target_pairs={{0,8},{1,9},{2,10},{3,11},{4,12},{5,13},{6,14},{7,15},{8,0},{9,1},... | collective-permute-start | bytes 442376 | tf_op jit(solution)/shard_map/ppermute | solution.py:443
  12.1 8.3 %collective-permute-start.3 = (bf16[144,512]{1,0:T(8,128)(2,1)S(1)}, bf16[144,512]{1,0:T(8,128)(2,1)S(1)}, u32[]{:S(2)}, u32[]{:S(2)}) collective-permute-start(bf16[144,512]{1,0:T(8,128)(2,1)S(1)} %collective-permute-done.refs_1_), channel_id=1, source_target_pairs={{0,0},{1,1},{2,2},{3,3},{4,6},{5,7},{6,4},{7,5},{8,10},{9,11},{10,... | collective-permute-start | bytes 442376 | tf_op jit(solution)/shard_map/ppermute | solution.py:443
  20.4 18.6 %copy-start = (bf16[128,4096]{1,0:T(8,128)(2,1)S(1)}, bf16[128,4096]{1,0:T(8,128)(2,1)}, u32[]{:S(2)}) copy-start(bf16[128,4096]{1,0:T(8,128)(2,1)} %q_ref.5) | copy-start | bytes 3145732
  20.4 18.5 %copy-start.1 = (bf16[128,4096]{1,0:T(8,128)(2,1)S(1)}, bf16[128,4096]{1,0:T(8,128)(2,1)}, u32[]{:S(2)}) copy-start(bf16[128,4096]{1,0:T(8,128)(2,1)} %x_ref.5) | copy-start | bytes 3145732
  20.4 2.5 %collective-permute-start.6 = (bf16[864,512]{1,0:T(8,128)(2,1)S(1)}, bf16[864,512]{1,0:T(8,128)(2,1)S(1)}, u32[]{:S(2)}, u32[]{:S(2)}) collective-permute-start(bf16[864,512]{1,0:T(8,128)(2,1)S(1)} %constant_dynamic-update-slice_fusion), channel_id=1, source_target_pairs={{0,1},{1,0},{2,3},{3,2},{4,5},{5,4},{6,7},{7,6},{8,9},{9,8},{10,11... | collective-permute-start | bytes 2654216 | tf_op jit(solution)/shard_map/ppermute | solution.py:443
  20.5 5.3 %collective-permute-start.4 = (bf16[144,512]{1,0:T(8,128)(2,1)S(1)}, bf16[144,512]{1,0:T(8,128)(2,1)S(1)}, u32[]{:S(2)}, u32[]{:S(2)}) collective-permute-start(bf16[144,512]{1,0:T(8,128)(2,1)S(1)} %collective-permute-done.1.refs_2_), channel_id=1, source_target_pairs={{0,0},{1,1},{2,2},{3,3},{4,4},{5,5},{6,6},{7,7},{8,10},{9,11},{10,... | collective-permute-start | bytes 442376 | tf_op jit(solution)/shard_map/ppermute | solution.py:443
  25.8 1.4 %collective-permute-start.7 = (bf16[144,512]{1,0:T(8,128)(2,1)S(1)}, bf16[144,512]{1,0:T(8,128)(2,1)S(1)}, u32[]{:S(2)}, u32[]{:S(2)}) collective-permute-start(bf16[144,512]{1,0:T(8,128)(2,1)S(1)} %collective-permute-done.4.refs_0_), channel_id=1, source_target_pairs={{0,1},{1,0},{2,3},{3,2},{4,5},{5,4},{6,7},{7,6},{8,9},{9,8},{10,11... | collective-permute-start | bytes 442376 | tf_op jit(solution)/shard_map/ppermute | solution.py:443
  30.2 12.6 %collective-permute-start.8 = (bf16[24,1024]{1,0:T(8,128)(2,1)S(1)}, bf16[24,1024]{1,0:T(8,128)(2,1)S(1)}, u32[]{:S(2)}, u32[]{:S(2)}) collective-permute-start(bf16[24,1024]{1,0:T(8,128)(2,1)S(1)} %get-tuple-element.63), channel_id=1, source_target_pairs={{0,4},{1,5},{2,6},{3,7},{4,8},{5,9},{6,10},{7,11},{8,12},{9,13},{1... | collective-permute-start | bytes 147464 | tf_op jit(solution)/shard_map/ppermute | solution.py:443
  32.0 10.9 %collective-permute-start.9 = (bf16[24,1024]{1,0:T(8,128)(2,1)S(1)}, bf16[24,1024]{1,0:T(8,128)(2,1)S(1)}, u32[]{:S(2)}, u32[]{:S(2)}) collective-permute-start(bf16[24,1024]{1,0:T(8,128)(2,1)S(1)} %get-tuple-element.64), channel_id=1, source_target_pairs={{0,8},{1,9},{2,10},{3,11},{4,12},{5,13},{6,14},{7,15},{8,0},{9,1},... | collective-permute-start | bytes 147464 | tf_op jit(solution)/shard_map/ppermute | solution.py:443
  37.5 5.3 %collective-permute-start.10 = (bf16[24,1024]{1,0:T(8,128)(2,1)S(1)}, bf16[24,1024]{1,0:T(8,128)(2,1)S(1)}, u32[]{:S(2)}, u32[]{:S(2)}) collective-permute-start(bf16[24,1024]{1,0:T(8,128)(2,1)S(1)} %get-tuple-element.65), channel_id=1, source_target_pairs={{0,12},{1,13},{2,14},{3,15},{4,0},{5,1},{6,2},{7,3},{8,4},{9,5},{1... | collective-permute-start | bytes 147464 | tf_op jit(solution)/shard_map/ppermute | solution.py:443
  38.7 4.2 %collective-permute-start.11 = (bf16[24,1024]{1,0:T(8,128)(2,1)S(1)}, bf16[24,1024]{1,0:T(8,128)(2,1)S(1)}, u32[]{:S(2)}, u32[]{:S(2)}) collective-permute-start(bf16[24,1024]{1,0:T(8,128)(2,1)S(1)} %get-tuple-element.59._.refs_0_), channel_id=1, source_target_pairs={{0,2},{1,3},{2,0},{3,1},{4,6},{5,7},{6,4},{7,5},{8,10},{9,11},{10,... | collective-permute-start | bytes 147464 | tf_op jit(solution)/shard_map/ppermute | solution.py:443
  42.9 3.3 %collective-permute-start.13 = (bf16[96,1024]{1,0:T(8,128)(2,1)S(1)}, bf16[96,1024]{1,0:T(8,128)(2,1)S(1)}, u32[]{:S(2)}, u32[]{:S(2)}) collective-permute-start(bf16[96,1024]{1,0:T(8,128)(2,1)S(1)} %pad_maximum_fusion), channel_id=1, source_target_pairs={{0,1},{1,0},{2,3},{3,2},{4,5},{5,4},{6,7},{7,6},{8,9},{9,8},{10,11... | collective-permute-start | bytes 589832 | tf_op jit(solution)/shard_map/ppermute | solution.py:443
  43.0 6.3 %collective-permute-start.12 = (bf16[72,1024]{1,0:T(8,128)(2,1)S(1)}, bf16[72,1024]{1,0:T(8,128)(2,1)S(1)}, u32[]{:S(2)}, u32[]{:S(2)}) collective-permute-start(bf16[72,1024]{1,0:T(8,128)(2,1)S(1)} %constant_dynamic-update-slice_fusion.6.refs_1_), channel_id=1, source_target_pairs={{0,2},{1,3},{2,0},{3,1},{4,6},{5,7},{6,4},{7,5},{8,10},{9,11},{10,... | collective-permute-start | bytes 442376 | tf_op jit(solution)/shard_map/ppermute | solution.py:443
  49.3 1.5 %collective-permute-start.14 = (bf16[96,1024]{1,0:T(8,128)(2,1)S(1)}, bf16[96,1024]{1,0:T(8,128)(2,1)S(1)}, u32[]{:S(2)}, u32[]{:S(2)}) collective-permute-start(bf16[96,1024]{1,0:T(8,128)(2,1)S(1)} %pad_maximum_fusion.1), channel_id=1, source_target_pairs={{0,1},{1,0},{2,3},{3,2},{4,5},{5,4},{6,7},{7,6},{8,9},{9,8},{10,11... | collective-permute-start | bytes 589832 | tf_op jit(solution)/shard_map/ppermute | solution.py:443
  52.8 1.5 %collective-permute-start.16 = (bf16[96,1024]{1,0:T(8,128)(2,1)S(1)}, bf16[96,1024]{1,0:T(8,128)(2,1)S(1)}, u32[]{:S(2)}, u32[]{:S(2)}) collective-permute-start(bf16[96,1024]{1,0:T(8,128)(2,1)S(1)} %get-tuple-element.85), channel_id=1, source_target_pairs={{0,1},{1,0},{2,3},{3,2},{4,5},{5,4},{6,7},{7,6},{8,9},{9,8},{10,11... | collective-permute-start | bytes 589832 | tf_op jit(solution)/shard_map/ppermute | solution.py:443
  54.4 7.0 %collective-permute-start.17 = (bf16[96,1024]{1,0:T(8,128)(2,1)S(1)}, bf16[96,1024]{1,0:T(8,128)(2,1)S(1)}, u32[]{:S(2)}, u32[]{:S(2)}) collective-permute-start(bf16[96,1024]{1,0:T(8,128)(2,1)S(1)} %add_convert_fusion.1), channel_id=1, source_target_pairs={{0,2},{1,3},{2,0},{3,1},{4,6},{5,7},{6,4},{7,5},{8,10},{9,11},{10,... | collective-permute-start | bytes 589832 | tf_op jit(solution)/shard_map/ppermute | solution.py:443
  56.2 5.2 %collective-permute-start.15 = (bf16[96,1024]{1,0:T(8,128)(2,1)S(1)}, bf16[96,1024]{1,0:T(8,128)(2,1)S(1)}, u32[]{:S(2)}, u32[]{:S(2)}) collective-permute-start(bf16[96,1024]{1,0:T(8,128)(2,1)S(1)} %get-tuple-element.84), channel_id=1, source_target_pairs={{0,1},{1,0},{2,3},{3,2},{4,5},{5,4},{6,7},{7,6},{8,9},{9,8},{10,11... | collective-permute-start | bytes 589832 | tf_op jit(solution)/shard_map/ppermute | solution.py:443
  61.5 6.4 %collective-permute-start.20 = (bf16[24,1024]{1,0:T(8,128)(2,1)S(1)}, bf16[24,1024]{1,0:T(8,128)(2,1)S(1)}, u32[]{:S(2)}, u32[]{:S(2)}) collective-permute-start(bf16[24,1024]{1,0:T(8,128)(2,1)S(1)} %get-tuple-element.89), channel_id=1, source_target_pairs={{0,4},{1,5},{2,6},{3,7},{4,8},{5,9},{6,10},{7,11},{8,12},{9,13},{1... | collective-permute-start | bytes 147464 | tf_op jit(solution)/shard_map/ppermute | solution.py:443
  63.2 5.7 %collective-permute-start.19 = (bf16[24,1024]{1,0:T(8,128)(2,1)S(1)}, bf16[24,1024]{1,0:T(8,128)(2,1)S(1)}, u32[]{:S(2)}, u32[]{:S(2)}) collective-permute-start(bf16[24,1024]{1,0:T(8,128)(2,1)S(1)} %get-tuple-element.90), channel_id=1, source_target_pairs={{0,8},{1,9},{2,10},{3,11},{4,12},{5,13},{6,14},{7,15},{8,0},{9,1},... | collective-permute-start | bytes 147464 | tf_op jit(solution)/shard_map/ppermute | solution.py:443
  63.8 5.1 %collective-permute-start.18 = (bf16[24,1024]{1,0:T(8,128)(2,1)S(1)}, bf16[24,1024]{1,0:T(8,128)(2,1)S(1)}, u32[]{:S(2)}, u32[]{:S(2)}) collective-permute-start(bf16[24,1024]{1,0:T(8,128)(2,1)S(1)} %get-tuple-element.91), channel_id=1, source_target_pairs={{0,12},{1,13},{2,14},{3,15},{4,0},{5,1},{6,2},{7,3},{8,4},{9,5},{1... | collective-permute-start | bytes 147464 | tf_op jit(solution)/shard_map/ppermute | solution.py:443

commit v11 on v10

--- a/solution.py
+++ b/solution.py
@@ -119,9 +119,10 @@
     members, ranks = slot_rows(routes, experts)
     slot = lax.broadcasted_iota(jnp.int32, (SLOTS, TILE), 0).astype(F32)
     mix = []
-    for k, e in enumerate(experts):
+    _, places = slot_rows(routes, list(range(planes)))
+    for e in range(planes):
         gate = jnp.sum(jnp.where(routes == e, gates, 0.0), axis=0, keepdims=True)
-        mix.append(jnp.where(ranks[k : k + 1] == slot, gate, 0.0))
+        mix.append(jnp.where(places[e : e + 1] == slot, gate, 0.0))
     mix = jnp.concatenate(mix, axis=0).T
     mix_high = mix.astype(BF16)
     mix_ref[:, : planes * SLOTS] = mix_high
@@ -375,12 +376,11 @@
 
 def combine_kernel(planes, widths, mix_ref, *refs):
     count = len(widths)
-    halves, parts = refs[:count], refs[count : count + planes]
-    _, out_ref, buffer, sems = refs[count + planes :]
+    halves = refs[:count]
+    part_ref, _, out_ref, buffer, sems = refs[count:]
     slots = planes * SLOTS
-    came = jnp.concatenate([p[...].astype(F32) for p in parts], axis=0).astype(BF16)
     order = one_hot(travel_row(numbers((CUT * slots, 1), 0), planes, SLOTS), planes * PIECE)
-    came = dot(order, came).astype(BF16)
+    came = dot(order, part_ref[...]).astype(BF16)
     size = buffer.shape[1] // CUT
     moves = []
     for q in range(CUT):
@@ -597,19 +597,19 @@
     other = move(theirs.astype(BF16), flip_y)
     other, done = lax.optimization_barrier((other, done))
     total = (mine + other.astype(F32)).astype(BF16)
-    parts = [total[:PIECE]]
-    for k in range(1, planes):
-        parts.append(
-            move(
-                total[k * PIECE : (k + 1) * PIECE], [(s, (s - k * SHARDS) % n) for s in range(n)]
-            )
-        )
+    z = pos[0] // SHARDS
+    total = total.reshape(planes, PIECE, width // CUT)
+    order = lax.rem(z - jnp.arange(planes) + planes, planes)
+    total = total.at[order].get(mode="promise_in_bounds")
+    lines = [[k * SHARDS + j for k in range(planes)] for j in range(SHARDS)]
+    came = lax.all_to_all(total, "expert", 0, 0, axis_index_groups=lines, tiled=True)
+    parts = [came.reshape(planes * PIECE, width // CUT)]
 
     widths = [h.shape[1] for h in halves]
     return pl.pallas_call(
         functools.partial(combine_kernel, planes, widths),
         out_shape=jax.ShapeDtypeStruct((tokens, width), BF16),
-        in_specs=[VMEM] * (1 + len(halves) + planes) + [ANY],
+        in_specs=[VMEM] * (2 + len(halves)) + [ANY],
         out_specs=HBM,
         scratch_shapes=[pltpu.VMEM((tokens, width), BF16), pltpu.SemaphoreType.DMA((CUT,))],
         compiler_params=params(small),

time: 70.9 us -> 90.3 us (1.27)
  blocking collectives: 0 us -> 13.3 us
  local copies, waits for them, and re-layouts: 0.12 us -> 13 us
  waiting for transfers between devices: 20.3 us -> 13 us
  other arithmetic: 0.16 us -> 1.2 us
    all_to_all x0 -> x1, blocking collectives: none -> 13.3 us  [local(): lax.all_to_all(total, 'expert', 0, 0, axis_index_groups=lines, tiled=True)]
    unnamed x11 -> x51, local copies, waits for them, and re-layouts: 0.08 us -> 12.4 us
    ppermute x21 -> x18, waiting for transfers between devices: 20.3 us -> 13 us  [move(): return lax.ppermute(value, 'expert', pairs)]
    convert_element_type x1, other arithmetic: 0.05 us -> 1.07 us  [local(): other = move(theirs.astype(BF16), flip_y)]
    ppermute x21 -> x18, starting transfers between devices: 27.2 us -> 26.5 us  [move(): return lax.ppermute(value, 'expert', pairs)]
  transfers between devices with their start and end apart: 21 -> 18, of which waited for: 10 -> 7; matrix products, arithmetic and copies ran while one was open for 0% -> 2% of each run, Pallas kernels for 21% -> 16%
where the time goes in v11:
time: 90.3 us; the launch traced here: 90.1 us
  starting transfers between devices  26.5 us (29%)
  Pallas kernels  22.7 us (25%)
  blocking collectives  13.3 us (15%)
  local copies, waits for them, and re-layouts  13 us (14%)
  waiting for transfers between devices  13 us (14%)
  other arithmetic  1.2 us (1%)
    ppermute x18, starting transfers between devices, move(): return lax.ppermute(value, 'expert', pairs)  26.5 us
    all_to_all x1, blocking collectives, local(): lax.all_to_all(total, 'expert', 0, 0, axis_index_groups=lines, tiled=True)  13.3 us
    ppermute x18, waiting for transfers between devices, move(): return lax.ppermute(value, 'expert', pairs)  13 us
    unnamed x51, local copies, waits for them, and re-layouts  12.4 us
    pallas_call x3, Pallas kernels, own(): pl.pallas_call(functools.partial(own_kernel, n, heads, len(sources)), out...  7.57 us
    pallas_call x2, Pallas kernels, expert(): pl.pallas_call(functools.partial(expert_kernel, n // 2, len(pieces)), out...  4.69 us
    pallas_call x1, Pallas kernels, local(): pl.pallas_call(functools.partial(routed_kernel, n, late_senders), out_sha...  2.93 us
    pallas_call x1, Pallas kernels, local(): pl.pallas_call(functools.partial(collect_kernel, n, early_senders), out_s...  2.68 us
  transfers between devices with their start and end apart: 18, of which 7 were waited for; matrix products, arithmetic and copies ran while one was open for 2% of the time, Pallas kernels for 16%

profile of v11, /device:TPU:0, one launch (start us, length us, event | category | flops | bytes accessed | tf_op | source)
XLA Modules:
  0.0 90.1 jit_solution(3092443551420961369)
XLA Ops:
  0.0 1.0 %pack.1.refs_0_ = bf16[144,512]{1,0:T(8,128)(2,1)S(1)} custom-call(s32[1,128]{1,0:T(1,128)} %bitcast.14, bf16[128,256]{1,0:T(8,128)(2,1)} %keys_ref.1, bf16[128,256]{1,0:T(8,128)(2,1)} %values_ref.1), custom_call_target="tpu_custom_call" | custom-call | tf_op jit(solution)/shard_map/pack/pallas_call | solution.py:428
  1.0 3.1 %collective-permute-start = (bf16[144,512]{1,0:T(8,128)(2,1)S(1)}, bf16[144,512]{1,0:T(8,128)(2,1)S(1)}, u32[]{:S(2)}, u32[]{:S(2)}) collective-permute-start(bf16[144,512]{1,0:T(8,128)(2,1)S(1)} %pack.1.refs_0_), channel_id=1, source_target_pairs={{0,4},{1,5},{2,6},{3,7},{4,8},{5,9},{6,10},{7,11},{8,12},{9,13},{1... | collective-permute-start | bytes 442376 | tf_op jit(solution)/shard_map/ppermute | solution.py:443
  4.1 2.6 %collective-permute-start.1 = (bf16[144,512]{1,0:T(8,128)(2,1)S(1)}, bf16[144,512]{1,0:T(8,128)(2,1)}, u32[]{:S(2)}, u32[]{:S(2)}) collective-permute-start(bf16[144,512]{1,0:T(8,128)(2,1)S(1)} %pack.1.refs_0_), channel_id=1, source_target_pairs={{0,8},{1,9},{2,10},{3,11},{4,12},{5,13},{6,14},{7,15},{8,0},{9,1},... | collective-permute-start | bytes 442376 | tf_op jit(solution)/shard_map/ppermute | solution.py:443
  6.7 1.5 %collective-permute-start.2 = (bf16[144,512]{1,0:T(8,128)(2,1)S(1)}, bf16[144,512]{1,0:T(8,128)(2,1)S(1)}, u32[]{:S(2)}, u32[]{:S(2)}) collective-permute-start(bf16[144,512]{1,0:T(8,128)(2,1)S(1)} %pack.1.refs_0_), channel_id=1, source_target_pairs={{0,2},{1,3},{2,0},{3,1},{4,6},{5,7},{6,4},{7,5},{8,10},{9,11},{10,... | collective-permute-start | bytes 442376 | tf_op jit(solution)/shard_map/ppermute | solution.py:443
  8.2 0.7 collective-permute-start.5
  8.8 2.5 %select.21 = (bf16[2,256,384]{2,1,0:T(8,128)(2,1)S(1)}, f32[24,4096]{1,0:T(8,128)S(1)}, f32[8,384]{1,0:T(8,128)S(1)}, bf16[128,64]{1,0:T(8,128)(2,1)S(1)}, bf16[...) custom-call(s32[1]{0:T(128)} %bitcast.pos_ref, s32[4,128]{1,0:T(4,128)} %bitcast.12, s32[1,128]{1,0:T(1,128)} %bitcast.15, ...), custom_call_target="tpu_custom_call" | custom-call | tf_op jit(solution)/shard_map/select/pallas_call | solution.py:453
  11.4 0.7 collective-permute-start.3
  12.1 7.4 %collective-permute-done.1.refs_2_ = bf16[144,512]{1,0:T(8,128)(2,1)} collective-permute-done((bf16[144,512]{1,0:T(8,128)(2,1)S(1)}, bf16[144,512]{1,0:T(8,128)(2,1)}, u32[]{:S(2)}, u32[]{:S(2)}) %collective-permute-start.1) | collective-permute-done | bytes 147488 | tf_op jit(solution)/shard_map/ppermute | solution.py:443
  19.5 1.0 %constant_dynamic-update-slice_fusion.3 = bf16[864,512]{1,0:T(8,128)(2,1)S(1)} fusion(bf16[864,512]{1,0:T(8,128)(2,1)S(1)} %constant_dynamic-update-slice_fusion.4, bf16[144,512]{1,0:T(8,128)(2,1)} %collective-permute-done.1.refs_2_), kind=kLoop, calls=%fused_computation.8 | loop fusion | bytes 294912
  20.7 1.7 %collective-permute-start.4 = (bf16[144,512]{1,0:T(8,128)(2,1)}, bf16[144,512]{1,0:T(8,128)(2,1)S(1)}, u32[]{:S(2)}, u32[]{:S(2)}) collective-permute-start(bf16[144,512]{1,0:T(8,128)(2,1)} %collective-permute-done.1.refs_2_), channel_id=1, source_target_pairs={{0,0},{1,1},{2,2},{3,3},{4,4},{5,5},{6,6},{7,7},{8,10},{9,11},{10,... | collective-permute-start | bytes 442376 | tf_op jit(solution)/shard_map/ppermute | solution.py:443
  22.4 0.7 collective-permute-done.6.refs_6_
  23.1 0.9 %copy-done.8 = bf16[144,512]{1,0:T(8,128)(2,1)S(1)} copy-done((bf16[144,512]{1,0:T(8,128)(2,1)S(1)}, bf16[144,512]{1,0:T(8,128)(2,1)}, u32[]{:S(2)}) %copy-start.8) | copy-done | bytes 147480
  24.0 0.9 %copy-done.10 = bf16[144,512]{1,0:T(8,128)(2,1)S(1)} copy-done((bf16[144,512]{1,0:T(8,128)(2,1)S(1)}, bf16[144,512]{1,0:T(8,128)(2,1)}, u32[]{:S(2)}) %copy-start.10) | copy-done | bytes 147480
  24.9 0.9 %copy-done.12 = bf16[144,512]{1,0:T(8,128)(2,1)S(1)} copy-done((bf16[144,512]{1,0:T(8,128)(2,1)S(1)}, bf16[144,512]{1,0:T(8,128)(2,1)}, u32[]{:S(2)}) %copy-start.12) | copy-done | bytes 147480
  25.8 2.7 %collect.1._ = bf16[16,144,512]{2,1,0:T(8,128)(2,1)S(1)} custom-call(s32[1]{0:T(128)} %bitcast.pos_ref, bf16[144,512]{1,0:T(8,128)(2,1)S(1)} %pack.1.refs_0_, bf16[144,512]{1,0:T(8,128)(2,1)S(1)} %copy-done.8, bf16[144,512]{1,0:T(8,128)(2,1)} %collective-permute-done.1.refs_2_, bf16[144,512]{1,0:T(8,128)(2,1)S(1)} %copy-done.12, ...), custom_call_target="tpu_custom_call" | custom-call | bytes 1000 | tf_op jit(solution)/shard_map/collect/pallas_call | solution.py:500
  28.5 0.2 collective-permute-start.7
  28.8 1.2 %collective-permute-done.7.refs_1_ = bf16[144,512]{1,0:T(8,128)(2,1)S(1)} collective-permute-done((bf16[144,512]{1,0:T(8,128)(2,1)S(1)}, bf16[144,512]{1,0:T(8,128)(2,1)S(1)}, u32[]{:S(2)}, u32[]{:S(2)}) %collective-permute-start.7) | collective-permute-done | bytes 147488 | tf_op jit(solution)/shard_map/ppermute | solution.py:443
  30.0 2.9 %routed.1 = (bf16[24,1024]{1,0:T(8,128)(2,1)S(1)}, bf16[24,1024]{1,0:T(8,128)(2,1)S(1)}, bf16[24,1024]{1,0:T(8,128)(2,1)S(1)}, bf16[24,1024]{1,0:T(8,128)(2,1)S(1)}, bf16[16,144,512]{2,1,0:T(8,128)(2,1)S(1)}) custom-call(s32[1]{0:T(128)} %bitcast.pos_ref, f32[1,4096]{1,0:T(1,128)} %bitcast.11, ...), custom_call_target="tpu_custom_call", output_to_operand_aliasing={{4}: (5, {})} | custom-call | tf_op jit(solution)/shard_map/routed/pallas_call | solution.py:514
  32.9 4.1 %collective-permute-start.8 = (bf16[24,1024]{1,0:T(8,128)(2,1)S(1)}, bf16[24,1024]{1,0:T(8,128)(2,1)S(1)}, u32[]{:S(2)}, u32[]{:S(2)}) collective-permute-start(bf16[24,1024]{1,0:T(8,128)(2,1)S(1)} %get-tuple-element.63), channel_id=1, source_target_pairs={{0,4},{1,5},{2,6},{3,7},{4,8},{5,9},{6,10},{7,11},{8,12},{9,13},{1... | collective-permute-start | bytes 147464 | tf_op jit(solution)/shard_map/ppermute | solution.py:443
  37.0 4.9 %collective-permute-start.9 = (bf16[24,1024]{1,0:T(8,128)(2,1)S(1)}, bf16[24,1024]{1,0:T(8,128)(2,1)S(1)}, u32[]{:S(2)}, u32[]{:S(2)}) collective-permute-start(bf16[24,1024]{1,0:T(8,128)(2,1)S(1)} %get-tuple-element.64), channel_id=1, source_target_pairs={{0,8},{1,9},{2,10},{3,11},{4,12},{5,13},{6,14},{7,15},{8,0},{9,1},... | collective-permute-start | bytes 147464 | tf_op jit(solution)/shard_map/ppermute | solution.py:443
  41.9 2.8 %collective-permute-start.10 = (bf16[24,1024]{1,0:T(8,128)(2,1)S(1)}, bf16[24,1024]{1,0:T(8,128)(2,1)S(1)}, u32[]{:S(2)}, u32[]{:S(2)}) collective-permute-start(bf16[24,1024]{1,0:T(8,128)(2,1)S(1)} %get-tuple-element.65), channel_id=1, source_target_pairs={{0,12},{1,13},{2,14},{3,15},{4,0},{5,1},{6,2},{7,3},{8,4},{9,5},{1... | collective-permute-start | bytes 147464 | tf_op jit(solution)/shard_map/ppermute | solution.py:443
  44.7 0.7 collective-permute-start.11
  45.5 3.9 %own.3 = (f32[128,1280]{1,0:T(8,128)S(1)}, f32[8,128]{1,0:T(8,128)S(1)}, bf16[4096,384]{1,0:T(8,128)(2,1)S(1)}, bf16[4096,384]{1,0:T(8,128)(2,1)S(1)}, bf16[384,4096]{1,0:T(8,128)(2,1)S(1)}) custom-call(s32[1]{0:T(128)} %bitcast.pos_ref, bf16[16,144,512]{2,1,0:T(8,128)(2,1)S(1)} %get-tuple-element.58.held, bf16[128,4096]{1,0:T(8,128)(2,1)S(1)} %copy-done, ...), custom_call_target="tpu_custom_call" | custom-call | flops 2000000000 | bytes 8000000 | tf_op jit(solution)/shard_map/own/pallas_call | solution.py:536
  49.4 0.8 copy-done.5
  50.4 1.3 %collective-permute-start.12 = (bf16[72,1024]{1,0:T(8,128)(2,1)S(1)}, bf16[72,1024]{1,0:T(8,128)(2,1)S(1)}, u32[]{:S(2)}, u32[]{:S(2)}) collective-permute-start(bf16[72,1024]{1,0:T(8,128)(2,1)S(1)} %constant_dynamic-update-slice_fusion.6.refs_1_), channel_id=1, source_target_pairs={{0,2},{1,3},{2,0},{3,1},{4,6},{5,7},{6,4},{7,5},{8,10},{9,11},{10,... | collective-permute-start | bytes 442376 | tf_op jit(solution)/shard_map/ppermute | solution.py:443
  51.7 1.4 %own.4 = (f32[128,768]{1,0:T(8,128)S(1)}, f32[8,128]{1,0:T(8,128)S(1)}) custom-call(s32[1]{0:T(128)} %bitcast.pos_ref, bf16[16,144,512]{2,1,0:T(8,128)(2,1)S(1)} %get-tuple-element.58.held, bf16[128,4096]{1,0:T(8,128)(2,1)S(1)} %copy-done, bf16[128,4096]{1,0:T(8,128)(2,1)S(1)} %copy-done.1, f32[8,128]{1,0:T(8,128)S(1)} %get-tuple-element.76._.refs_8_), custom_call_target="tpu_custom_call" | custom-call | flops 2000000000 | bytes 8000000 | tf_op jit(solution)/shard_map/own/pallas_call | solution.py:536
  53.1 2.0 %expert.2 = (bf16[96,1024]{1,0:T(8,128)(2,1)S(1)}, bf16[96,1024]{1,0:T(8,128)(2,1)S(1)}) custom-call(bf16[24,1024]{1,0:T(8,128)(2,1)S(1)} %get-tuple-element.59._.refs_0_, bf16[72,1024]{1,0:T(8,128)(2,1)S(1)} %constant_dynamic-update-slice_fusion.6.refs_1_, bf16[96,1024]{1,0:T(8,128)(2,1)S(1)} %collective-permute-done.13.refs_2_, ...), custom_call_target="tpu_custom_call" | custom-call | flops 600000000 | bytes 2000000 | tf_op jit(solution)/shard_map/expert/pallas_call | solution.py:576
  55.2 0.7 copy-done.15
  55.9 0.8 collective-permute-done.12.refs_1_
  56.7 1.4 %collective-permute-done.14.refs_2_ = bf16[96,1024]{1,0:T(8,128)(2,1)S(1)} collective-permute-done((bf16[96,1024]{1,0:T(8,128)(2,1)S(1)}, bf16[96,1024]{1,0:T(8,128)(2,1)S(1)}, u32[]{:S(2)}, u32[]{:S(2)}) %collective-permute-start.14) | collective-permute-done | bytes 196640 | tf_op jit(solution)/shard_map/ppermute | solution.py:443
  58.1 2.7 %expert.3 = (bf16[96,1024]{1,0:T(8,128)(2,1)S(1)}, bf16[96,1024]{1,0:T(8,128)(2,1)}) custom-call(bf16[24,1024]{1,0:T(8,128)(2,1)S(1)} %collective-permute-done.11.refs_0_, bf16[72,1024]{1,0:T(8,128)(2,1)S(1)} %collective-permute-done.12.refs_1_, bf16[96,1024]{1,0:T(8,128)(2,1)S(1)} %collective-permute-done.14.refs_2_, ...), custom_call_target="tpu_custom_call" | custom-call | flops 600000000 | bytes 2000000 | tf_op jit(solution)/shard_map/expert/pallas_call | solution.py:576
  60.8 0.7 copy-done.17
  61.5 0.1 collective-permute-start.16
  61.6 0.4 collective-permute-start.15
  62.1 1.2 %collective-permute-done.16 = bf16[96,1024]{1,0:T(8,128)(2,1)} collective-permute-done((bf16[96,1024]{1,0:T(8,128)(2,1)}, bf16[96,1024]{1,0:T(8,128)(2,1)}, u32[]{:S(2)}, u32[]{:S(2)}) %collective-permute-start.16) | collective-permute-done | bytes 196640 | tf_op jit(solution)/shard_map/ppermute | solution.py:443
  63.3 1.1 %add_convert_fusion.1 = bf16[96,1024]{1,0:T(8,128)(2,1)S(1)} fusion(bf16[96,1024]{1,0:T(8,128)(2,1)} %collective-permute-done.16, bf16[96,1024]{1,0:T(8,128)(2,1)} %copy-done.17), kind=kLoop, calls=%fused_computation.2 | loop fusion | flops 393216 | bytes 589824 | tf_op jit(solution)/shard_map/convert_element_type | solution.py:597
  64.3 1.3 %collective-permute-start.17 = (bf16[96,1024]{1,0:T(8,128)(2,1)S(1)}, bf16[96,1024]{1,0:T(8,128)(2,1)S(1)}, u32[]{:S(2)}, u32[]{:S(2)}) collective-permute-start(bf16[96,1024]{1,0:T(8,128)(2,1)S(1)} %add_convert_fusion.1), channel_id=1, source_target_pairs={{0,2},{1,3},{2,0},{3,1},{4,6},{5,7},{6,4},{7,5},{8,10},{9,11},{10,... | collective-permute-start | bytes 589832 | tf_op jit(solution)/shard_map/ppermute | solution.py:443
  65.7 1.2 %copy-done.2 = bf16[128,4096]{1,0:T(8,128)(2,1)S(1)} copy-done((bf16[128,4096]{1,0:T(8,128)(2,1)S(1)}, bf16[128,4096]{1,0:T(8,128)(2,1)}, u32[]{:S(2)}) %copy-start.2) | copy-done | bytes 1048600
  66.9 0.9 %copy-done.18 = bf16[96,1024]{1,0:T(8,128)(2,1)S(1)} copy-done((bf16[96,1024]{1,0:T(8,128)(2,1)S(1)}, bf16[96,1024]{1,0:T(8,128)(2,1)}, u32[]{:S(2)}) %copy-start.18) | copy-done | bytes 196632
  67.9 2.3 %own.5 = (f32[128,2048]{1,0:T(8,128)S(1)}, f32[8,128]{1,0:T(8,128)S(1)}) custom-call(s32[1]{0:T(128)} %bitcast.pos_ref, bf16[16,144,512]{2,1,0:T(8,128)(2,1)S(1)} %get-tuple-element.58.held, bf16[128,4096]{1,0:T(8,128)(2,1)S(1)} %copy-done, bf16[128,4096]{1,0:T(8,128)(2,1)S(1)} %copy-done.2, bf16[96,1024]{1,0:T(8,128)(2,1)S(1)} %copy-done.18), custom_call_target="tpu_custom_call" | custom-call | flops 2000000000 | bytes 8000000 | tf_op jit(solution)/shard_map/own/pallas_call | solution.py:536
  70.2 1.0 %copy-done.3 = f32[128,2048]{1,0:T(8,128)} copy-done((f32[128,2048]{1,0:T(8,128)}, f32[128,2048]{1,0:T(8,128)S(1)}, u32[]{:S(2)}) %copy-start.3) | copy-done | bytes 1048600
  71.2 0.2 collective-permute-done.17
  71.5 0.6 gather_fusion
  72.0 13.3 %all_to_all.5 = bf16[4,24,1024]{2,1,0:T(8,128)(2,1)S(1)} all-to-all(bf16[4,24,1024]{2,1,0:T(8,128)(2,1)S(1)} %gather_fusion), channel_id=1, replica_groups={{0,4,8,12},{1,5,9,13},{2,6,10,14},{3,7,11,15},{16,20,24,28},{17,21,25,2..., dimensions={0} | all-to-all | bytes 393216 | tf_op jit(solution)/shard_map/all_to_all | solution.py:605
  85.3 1.2 %copy-done.4 = f32[128,2048]{1,0:T(8,128)S(1)} copy-done((f32[128,2048]{1,0:T(8,128)S(1)}, f32[128,2048]{1,0:T(8,128)}, u32[]{:S(2)}) %copy-start.4) | copy-done | bytes 1048600
  86.5 1.1 %copy-done.6 = f32[128,1280]{1,0:T(8,128)S(1)} copy-done((f32[128,1280]{1,0:T(8,128)S(1)}, f32[128,1280]{1,0:T(8,128)}, u32[]{:S(2)}) %copy-start.6) | copy-done | bytes 655384
  87.6 1.0 %copy-done.14 = f32[128,768]{1,0:T(8,128)S(1)} copy-done((f32[128,768]{1,0:T(8,128)S(1)}, f32[128,768]{1,0:T(8,128)}, u32[]{:S(2)}) %copy-start.14) | copy-done | bytes 393240
  88.6 1.4 %combine.1 = bf16[128,4096]{1,0:T(8,128)(2,1)} custom-call(bf16[128,64]{1,0:T(8,128)(2,1)S(1)} %copy-done.20, f32[128,1280]{1,0:T(8,128)S(1)} %copy-done.6, f32[128,768]{1,0:T(8,128)S(1)} %copy-done.14, f32[128,2048]{1,0:T(8,128)S(1)} %copy-done.4, bf16[96,1024]{1,0:T(8,128)(2,1)S(1)} %bitcast.9, f32[8,128]{1,0:T(8,128)S(1)} %get-tuple-element.88.refs_4_), custom_call_target="tpu_custom_call" | custom-call | tf_op jit(solution)/shard_map/combine/pallas_call | solution.py:609
  (59 shorter events, 0.5 us)
Async XLA Ops:
  1.0 10.4 %collective-permute-start = (bf16[144,512]{1,0:T(8,128)(2,1)S(1)}, bf16[144,512]{1,0:T(8,128)(2,1)S(1)}, u32[]{:S(2)}, u32[]{:S(2)}) collective-permute-start(bf16[144,512]{1,0:T(8,128)(2,1)S(1)} %pack.1.refs_0_), channel_id=1, source_target_pairs={{0,4},{1,5},{2,6},{3,7},{4,8},{5,9},{6,10},{7,11},{8,12},{9,13},{1... | collective-permute-start | bytes 442376 | tf_op jit(solution)/shard_map/ppermute | solution.py:443
  4.1 15.5 %collective-permute-start.1 = (bf16[144,512]{1,0:T(8,128)(2,1)S(1)}, bf16[144,512]{1,0:T(8,128)(2,1)}, u32[]{:S(2)}, u32[]{:S(2)}) collective-permute-start(bf16[144,512]{1,0:T(8,128)(2,1)S(1)} %pack.1.refs_0_), channel_id=1, source_target_pairs={{0,8},{1,9},{2,10},{3,11},{4,12},{5,13},{6,14},{7,15},{8,0},{9,1},... | collective-permute-start | bytes 442376 | tf_op jit(solution)/shard_map/ppermute | solution.py:443
  6.7 12.9 %collective-permute-start.2 = (bf16[144,512]{1,0:T(8,128)(2,1)S(1)}, bf16[144,512]{1,0:T(8,128)(2,1)S(1)}, u32[]{:S(2)}, u32[]{:S(2)}) collective-permute-start(bf16[144,512]{1,0:T(8,128)(2,1)S(1)} %pack.1.refs_0_), channel_id=1, source_target_pairs={{0,2},{1,3},{2,0},{3,1},{4,6},{5,7},{6,4},{7,5},{8,10},{9,11},{10,... | collective-permute-start | bytes 442376 | tf_op jit(solution)/shard_map/ppermute | solution.py:443
  8.2 12.3 %collective-permute-start.5 = (bf16[144,512]{1,0:T(8,128)(2,1)S(1)}, bf16[144,512]{1,0:T(8,128)(2,1)S(1)}, u32[]{:S(2)}, u32[]{:S(2)}) collective-permute-start(bf16[144,512]{1,0:T(8,128)(2,1)S(1)} %pack.1.refs_0_), channel_id=1, source_target_pairs={{0,0},{1,1},{2,12},{3,13},{4,4},{5,5},{6,6},{7,7},{8,8},{9,9},{10,... | collective-permute-start | bytes 442376 | tf_op jit(solution)/shard_map/ppermute | solution.py:443
  11.3 9.2 %copy-start.19 = (bf16[128,64]{1,0:T(8,128)(2,1)}, bf16[128,64]{1,0:T(8,128)(2,1)S(1)}, u32[]{:S(2)}) copy-start(bf16[128,64]{1,0:T(8,128)(2,1)S(1)} %get-tuple-element.47.mix_ref) | copy-start | bytes 49156
  11.4 11.0 %copy-start.7 = (bf16[144,512]{1,0:T(8,128)(2,1)}, bf16[144,512]{1,0:T(8,128)(2,1)S(1)}, u32[]{:S(2)}) copy-start(bf16[144,512]{1,0:T(8,128)(2,1)S(1)} %collective-permute-done.refs_1_) | copy-start | bytes 442372
  11.4 8.1 %collective-permute-start.3 = (bf16[144,512]{1,0:T(8,128)(2,1)S(1)}, bf16[144,512]{1,0:T(8,128)(2,1)S(1)}, u32[]{:S(2)}, u32[]{:S(2)}) collective-permute-start(bf16[144,512]{1,0:T(8,128)(2,1)S(1)} %collective-permute-done.refs_1_), channel_id=1, source_target_pairs={{0,0},{1,1},{2,2},{3,3},{4,6},{5,7},{6,4},{7,5},{8,10},{9,11},{10,... | collective-permute-start | bytes 442376 | tf_op jit(solution)/shard_map/ppermute | solution.py:443
  19.5 2.9 %copy-start.9 = (bf16[144,512]{1,0:T(8,128)(2,1)}, bf16[144,512]{1,0:T(8,128)(2,1)S(1)}, u32[]{:S(2)}) copy-start(bf16[144,512]{1,0:T(8,128)(2,1)S(1)} %collective-permute-done.2.refs_4_) | copy-start | bytes 442372
  20.5 1.9 %copy-start.11 = (bf16[144,512]{1,0:T(8,128)(2,1)}, bf16[144,512]{1,0:T(8,128)(2,1)S(1)}, u32[]{:S(2)}) copy-start(bf16[144,512]{1,0:T(8,128)(2,1)S(1)} %collective-permute-done.5.refs_3_) | copy-start | bytes 442372
  20.6 24.9 %copy-start = (bf16[128,4096]{1,0:T(8,128)(2,1)S(1)}, bf16[128,4096]{1,0:T(8,128)(2,1)}, u32[]{:S(2)}) copy-start(bf16[128,4096]{1,0:T(8,128)(2,1)} %q_ref.5) | copy-start | bytes 3145732
  20.6 24.9 %copy-start.1 = (bf16[128,4096]{1,0:T(8,128)(2,1)S(1)}, bf16[128,4096]{1,0:T(8,128)(2,1)}, u32[]{:S(2)}) copy-start(bf16[128,4096]{1,0:T(8,128)(2,1)} %x_ref.5) | copy-start | bytes 3145732
  20.6 2.5 %collective-permute-start.6 = (bf16[864,512]{1,0:T(8,128)(2,1)S(1)}, bf16[864,512]{1,0:T(8,128)(2,1)S(1)}, u32[]{:S(2)}, u32[]{:S(2)}) collective-permute-start(bf16[864,512]{1,0:T(8,128)(2,1)S(1)} %constant_dynamic-update-slice_fusion), channel_id=1, source_target_pairs={{0,1},{1,0},{2,3},{3,2},{4,5},{5,4},{6,7},{7,6},{8,9},{9,8},{10,11... | collective-permute-start | bytes 2654216 | tf_op jit(solution)/shard_map/ppermute | solution.py:443
  20.7 7.8 %collective-permute-start.4 = (bf16[144,512]{1,0:T(8,128)(2,1)}, bf16[144,512]{1,0:T(8,128)(2,1)S(1)}, u32[]{:S(2)}, u32[]{:S(2)}) collective-permute-start(bf16[144,512]{1,0:T(8,128)(2,1)} %collective-permute-done.1.refs_2_), channel_id=1, source_target_pairs={{0,0},{1,1},{2,2},{3,3},{4,4},{5,5},{6,6},{7,7},{8,10},{9,11},{10,... | collective-permute-start | bytes 442376 | tf_op jit(solution)/shard_map/ppermute | solution.py:443
  23.1 0.9 %copy-start.8 = (bf16[144,512]{1,0:T(8,128)(2,1)S(1)}, bf16[144,512]{1,0:T(8,128)(2,1)}, u32[]{:S(2)}) copy-start(bf16[144,512]{1,0:T(8,128)(2,1)} %copy-done.7) | copy-start | bytes 442372
  24.0 0.9 %copy-start.10 = (bf16[144,512]{1,0:T(8,128)(2,1)S(1)}, bf16[144,512]{1,0:T(8,128)(2,1)}, u32[]{:S(2)}) copy-start(bf16[144,512]{1,0:T(8,128)(2,1)} %copy-done.9) | copy-start | bytes 442372
  24.9 0.9 %copy-start.12 = (bf16[144,512]{1,0:T(8,128)(2,1)S(1)}, bf16[144,512]{1,0:T(8,128)(2,1)}, u32[]{:S(2)}) copy-start(bf16[144,512]{1,0:T(8,128)(2,1)} %copy-done.11) | copy-start | bytes 442372
  28.5 1.4 %collective-permute-start.7 = (bf16[144,512]{1,0:T(8,128)(2,1)S(1)}, bf16[144,512]{1,0:T(8,128)(2,1)S(1)}, u32[]{:S(2)}, u32[]{:S(2)}) collective-permute-start(bf16[144,512]{1,0:T(8,128)(2,1)S(1)} %collective-permute-done.4.refs_0_), channel_id=1, source_target_pairs={{0,1},{1,0},{2,3},{3,2},{4,5},{5,4},{6,7},{7,6},{8,9},{9,8},{10,11... | collective-permute-start | bytes 442376 | tf_op jit(solution)/shard_map/ppermute | solution.py:443
  32.9 17.3 %collective-permute-start.8 = (bf16[24,1024]{1,0:T(8,128)(2,1)S(1)}, bf16[24,1024]{1,0:T(8,128)(2,1)S(1)}, u32[]{:S(2)}, u32[]{:S(2)}) collective-permute-start(bf16[24,1024]{1,0:T(8,128)(2,1)S(1)} %get-tuple-element.63), channel_id=1, source_target_pairs={{0,4},{1,5},{2,6},{3,7},{4,8},{5,9},{6,10},{7,11},{8,12},{9,13},{1... | collective-permute-start | bytes 147464 | tf_op jit(solution)/shard_map/ppermute | solution.py:443
  37.0 13.2 %collective-permute-start.9 = (bf16[24,1024]{1,0:T(8,128)(2,1)S(1)}, bf16[24,1024]{1,0:T(8,128)(2,1)S(1)}, u32[]{:S(2)}, u32[]{:S(2)}) collective-permute-start(bf16[24,1024]{1,0:T(8,128)(2,1)S(1)} %get-tuple-element.64), channel_id=1, source_target_pairs={{0,8},{1,9},{2,10},{3,11},{4,12},{5,13},{6,14},{7,15},{8,0},{9,1},... | collective-permute-start | bytes 147464 | tf_op jit(solution)/shard_map/ppermute | solution.py:443
  41.9 8.3 %collective-permute-start.10 = (bf16[24,1024]{1,0:T(8,128)(2,1)S(1)}, bf16[24,1024]{1,0:T(8,128)(2,1)S(1)}, u32[]{:S(2)}, u32[]{:S(2)}) collective-permute-start(bf16[24,1024]{1,0:T(8,128)(2,1)S(1)} %get-tuple-element.65), channel_id=1, source_target_pairs={{0,12},{1,13},{2,14},{3,15},{4,0},{5,1},{6,2},{7,3},{8,4},{9,5},{1... | collective-permute-start | bytes 147464 | tf_op jit(solution)/shard_map/ppermute | solution.py:443
  44.7 5.5 %collective-permute-start.11 = (bf16[24,1024]{1,0:T(8,128)(2,1)S(1)}, bf16[24,1024]{1,0:T(8,128)(2,1)S(1)}, u32[]{:S(2)}, u32[]{:S(2)}) collective-permute-start(bf16[24,1024]{1,0:T(8,128)(2,1)S(1)} %get-tuple-element.59._.refs_0_), channel_id=1, source_target_pairs={{0,2},{1,3},{2,0},{3,1},{4,6},{5,7},{6,4},{7,5},{8,10},{9,11},{10,... | collective-permute-start | bytes 147464 | tf_op jit(solution)/shard_map/ppermute | solution.py:443
  49.4 0.8 copy-start.5
  50.3 2.9 %collective-permute-start.13 = (bf16[96,1024]{1,0:T(8,128)(2,1)S(1)}, bf16[96,1024]{1,0:T(8,128)(2,1)S(1)}, u32[]{:S(2)}, u32[]{:S(2)}) collective-permute-start(bf16[96,1024]{1,0:T(8,128)(2,1)S(1)} %pad_maximum_fusion), channel_id=1, source_target_pairs={{0,1},{1,0},{2,3},{3,2},{4,5},{5,4},{6,7},{7,6},{8,9},{9,8},{10,11... | collective-permute-start | bytes 589832 | tf_op jit(solution)/shard_map/ppermute | solution.py:443
  50.4 6.3 %collective-permute-start.12 = (bf16[72,1024]{1,0:T(8,128)(2,1)S(1)}, bf16[72,1024]{1,0:T(8,128)(2,1)S(1)}, u32[]{:S(2)}, u32[]{:S(2)}) collective-permute-start(bf16[72,1024]{1,0:T(8,128)(2,1)S(1)} %constant_dynamic-update-slice_fusion.6.refs_1_), channel_id=1, source_target_pairs={{0,2},{1,3},{2,0},{3,1},{4,6},{5,7},{6,4},{7,5},{8,10},{9,11},{10,... | collective-permute-start | bytes 442376 | tf_op jit(solution)/shard_map/ppermute | solution.py:443
  53.1 2.0 %copy-start.13 = (f32[128,768]{1,0:T(8,128)}, f32[128,768]{1,0:T(8,128)S(1)}, u32[]{:S(2)}) copy-start(f32[128,768]{1,0:T(8,128)S(1)} %get-tuple-element.62.refs_1_) | copy-start | bytes 1179652
  55.2 0.7 copy-start.15
  55.9 0.9 copy-start.21
  56.6 1.5 %collective-permute-start.14 = (bf16[96,1024]{1,0:T(8,128)(2,1)S(1)}, bf16[96,1024]{1,0:T(8,128)(2,1)S(1)}, u32[]{:S(2)}, u32[]{:S(2)}) collective-permute-start(bf16[96,1024]{1,0:T(8,128)(2,1)S(1)} %pad_maximum_fusion.1), channel_id=1, source_target_pairs={{0,1},{1,0},{2,3},{3,2},{4,5},{5,4},{6,7},{7,6},{8,9},{9,8},{10,11... | collective-permute-start | bytes 589832 | tf_op jit(solution)/shard_map/ppermute | solution.py:443
  60.8 0.7 copy-start.17
  61.5 1.8 %collective-permute-start.16 = (bf16[96,1024]{1,0:T(8,128)(2,1)}, bf16[96,1024]{1,0:T(8,128)(2,1)}, u32[]{:S(2)}, u32[]{:S(2)}) collective-permute-start(bf16[96,1024]{1,0:T(8,128)(2,1)} %get-tuple-element.85), channel_id=1, source_target_pairs={{0,1},{1,0},{2,3},{3,2},{4,5},{5,4},{6,7},{7,6},{8,9},{9,8},{10,11... | collective-permute-start | bytes 589832 | tf_op jit(solution)/shard_map/ppermute | solution.py:443
  61.6 9.7 %collective-permute-start.15 = (bf16[96,1024]{1,0:T(8,128)(2,1)}, bf16[96,1024]{1,0:T(8,128)(2,1)S(1)}, u32[]{:S(2)}, u32[]{:S(2)}) collective-permute-start(bf16[96,1024]{1,0:T(8,128)(2,1)} %copy-done.21), channel_id=1, source_target_pairs={{0,1},{1,0},{2,3},{3,2},{4,5},{5,4},{6,7},{7,6},{8,9},{9,8},{10,11... | collective-permute-start | bytes 589832 | tf_op jit(solution)/shard_map/ppermute | solution.py:443
  64.3 7.0 %collective-permute-start.17 = (bf16[96,1024]{1,0:T(8,128)(2,1)S(1)}, bf16[96,1024]{1,0:T(8,128)(2,1)S(1)}, u32[]{:S(2)}, u32[]{:S(2)}) collective-permute-start(bf16[96,1024]{1,0:T(8,128)(2,1)S(1)} %add_convert_fusion.1), channel_id=1, source_target_pairs={{0,2},{1,3},{2,0},{3,1},{4,6},{5,7},{6,4},{7,5},{8,10},{9,11},{10,... | collective-permute-start | bytes 589832 | tf_op jit(solution)/shard_map/ppermute | solution.py:443
  65.7 1.2 %copy-start.2 = (bf16[128,4096]{1,0:T(8,128)(2,1)S(1)}, bf16[128,4096]{1,0:T(8,128)(2,1)}, u32[]{:S(2)}) copy-start(bf16[128,4096]{1,0:T(8,128)(2,1)} %x_ref.5) | copy-start | bytes 3145732
  66.9 0.9 %copy-start.18 = (bf16[96,1024]{1,0:T(8,128)(2,1)S(1)}, bf16[96,1024]{1,0:T(8,128)(2,1)}, u32[]{:S(2)}) copy-start(bf16[96,1024]{1,0:T(8,128)(2,1)} %copy-done.17) | copy-start | bytes 589828
  67.9 3.5 %copy-start.16 = (bf16[96,1024]{1,0:T(8,128)(2,1)S(1)}, bf16[96,1024]{1,0:T(8,128)(2,1)}, u32[]{:S(2)}) copy-start(bf16[96,1024]{1,0:T(8,128)(2,1)} %copy-done.15) | copy-start | bytes 589828
  67.9 17.4 %copy-start.20 = (bf16[128,64]{1,0:T(8,128)(2,1)S(1)}, bf16[128,64]{1,0:T(8,128)(2,1)}, u32[]{:S(2)}) copy-start(bf16[128,64]{1,0:T(8,128)(2,1)} %copy-done.19) | copy-start | bytes 49156
  70.2 1.0 %copy-start.3 = (f32[128,2048]{1,0:T(8,128)}, f32[128,2048]{1,0:T(8,128)S(1)}, u32[]{:S(2)}) copy-start(f32[128,2048]{1,0:T(8,128)S(1)} %get-tuple-element.82.refs_2_) | copy-start | bytes 3145732
  85.3 1.2 %copy-start.4 = (f32[128,2048]{1,0:T(8,128)S(1)}, f32[128,2048]{1,0:T(8,128)}, u32[]{:S(2)}) copy-start(f32[128,2048]{1,0:T(8,128)} %copy-done.3) | copy-start | bytes 3145732
  86.5 1.1 %copy-start.6 = (f32[128,1280]{1,0:T(8,128)S(1)}, f32[128,1280]{1,0:T(8,128)}, u32[]{:S(2)}) copy-start(f32[128,1280]{1,0:T(8,128)} %copy-done.5) | copy-start | bytes 1966084
  87.6 1.0 %copy-start.14 = (f32[128,768]{1,0:T(8,128)S(1)}, f32[128,768]{1,0:T(8,128)}, u32[]{:S(2)}) copy-start(f32[128,768]{1,0:T(8,128)} %copy-done.13) | copy-start | bytes 1179652

commit v12 on v10

--- a/solution.py
+++ b/solution.py
@@ -153,8 +153,7 @@
         for g in range(GROUP):
             a = h * GROUP + g
             stack[pl.ds(g, rows, stride=GROUP), :] = q_rows[:, a * HEAD : (a + 1) * HEAD]
-        for i, term in enumerate(two_terms(stack[...].T)):
-            qs_ref[h, i * HEAD : (i + 1) * HEAD, :] = term
+        qs_ref[h] = stack[...].T.astype(BF16)
 
 
 def doc_starts(n, pos, held):
@@ -177,12 +176,6 @@
     return first
 
 
-def two_terms(x):
-    scaled = x.astype(F32) * SCALE
-    high = scaled.astype(BF16)
-    return high, (scaled - high.astype(F32)).astype(BF16)
-
-
 def key_steps(pos, place, first, bias_ref, step, state):
     low = jnp.min(first).astype(jnp.int32) // KEYS
     last = pos // STEP
@@ -203,11 +196,11 @@
     return [(h, own) for h, own in groups if own]
 
 
-def keys_of(held, kb, h):
-    keys = jnp.concatenate(
-        [held[STEP * kb + t, 0:TILE, h * HEAD : (h + 1) * HEAD] for t in range(STEP)], axis=0
+def keys_of(held, kb, heads):
+    low, high = heads[0] * HEAD, (heads[-1] + 1) * HEAD
+    return jnp.concatenate(
+        [held[STEP * kb + t, 0:TILE, low:high] for t in range(STEP)], axis=0
     )
-    return jnp.concatenate([keys, keys], axis=1)
 
 
 def values_of(held, kb, h):
@@ -224,14 +217,19 @@
 
     def step(kb, tops, masked):
         out = []
-        for (queries, h, acc), old in zip(chains, tops):
-            scores = dot(keys_of(held, kb, h), queries[...])
+        for (queries, heads, acc), old in zip(chains, tops):
+            scores = dot(keys_of(held, kb, heads), queries[...])
             if masked:
                 copies = scores.shape[1] // bias_ref.shape[1]
                 scores = scores + jnp.concatenate([bias_ref[...]] * copies, axis=1)
             top = jnp.maximum(old, jnp.max(scores, axis=0, keepdims=True))
-            weights = jnp.exp2(scores - top).astype(BF16)
-            acc[...] = acc[...] * jnp.exp2(old - top) + dot(values_of(held, kb, h), weights)
+            weights = jnp.exp2((scores - top) * SCALE).astype(BF16)
+            share = weights.shape[1] // len(heads)
+            added = [
+                dot(values_of(held, kb, h), weights[:, i * share : (i + 1) * share])
+                for i, h in enumerate(heads)
+            ]
+            acc[...] = acc[...] * jnp.exp2((old - top) * SCALE) + jnp.concatenate(added, axis=1)
             out.append(top)
         return tuple(out)
 
@@ -272,7 +270,8 @@
     for copy in copies:
         copy.wait()
     starts = doc_starts(n, pos, held)
-    lanes = q_scr.shape[2]
+    lanes = q_scr.shape[1] // KV_HEADS
+    q_scr[...] = jnp.zeros(q_scr.shape, BF16)
     rows = lanes // GROUP
     base = (pos * TILE).astype(F32)
     width = state.shape[1] // CUT
@@ -282,17 +281,18 @@
     order = one_hot(chunk * rows + plane * CAP + slot, CUT * rows)
     for part in range(xs_ref.shape[0] // rows):
         at = slice(part * lanes, (part + 1) * lanes)
-        q_scr[...] = qs_ref[:, :, at]
-        done = flash(
+        for h in range(KV_HEADS):
+            q_scr[h * HEAD : (h + 1) * HEAD, h * lanes : (h + 1) * lanes] = qs_ref[h, :, at]
+        (done,) = flash(
             pos,
             held,
-            [(q_scr.at[h], h, acc.at[h]) for h in range(KV_HEADS)],
+            [(q_scr, list(range(KV_HEADS)), acc)],
             bias,
             facts_ref[0:1, at] + base,
             starts_of(facts_ref[1:2, at], starts),
         )
         for h in range(KV_HEADS):
-            stack[...] = done[h]
+            stack[...] = done[h * lanes : (h + 1) * lanes]
             for g in range(GROUP):
                 lane = (h * GROUP + g) * HEAD
                 state[:, lane : lane + HEAD] = (
@@ -359,11 +359,10 @@
     chains = []
     for i, (h, own) in enumerate(by_kv_head(heads)):
         queries, acc = scratch[2 * i : 2 * i + 2]
-        chains.append((queries, h, acc))
+        chains.append((queries, [h], acc))
         for j, a in enumerate(own):
-            terms = two_terms(q_ref[:, a * HEAD : (a + 1) * HEAD].astype(F32).T)
-            for t, term in enumerate(terms):
-                queries[t * HEAD : (t + 1) * HEAD, j * TILE : (j + 1) * TILE] = term
+            rows = q_ref[:, a * HEAD : (a + 1) * HEAD].astype(F32)
+            queries[:, j * TILE : (j + 1) * TILE] = rows.T.astype(BF16)
     done = jnp.concatenate(flash(pos, held, chains, bias, place, first), axis=0)
     for j, a in enumerate(heads):
         h_ref[:, j * HEAD : (j + 1) * HEAD] = (
@@ -453,7 +452,7 @@
     q_rows, x_rows, facts, mix, gather, spread = pl.pallas_call(
         functools.partial(select_kernel, planes),
         out_shape=[
-            jax.ShapeDtypeStruct((KV_HEADS, 2 * HEAD, planes * CAP * GROUP), BF16),
+            jax.ShapeDtypeStruct((KV_HEADS, HEAD, planes * CAP * GROUP), BF16),
             jax.ShapeDtypeStruct((planes * CAP, width), F32),
             jax.ShapeDtypeStruct((8, planes * CAP * GROUP), F32),
             jax.ShapeDtypeStruct((tokens, 2 * planes * SLOTS), BF16),
@@ -518,9 +517,9 @@
         in_specs=[SMEM, HBM] + [VMEM] * 4 + [ANY] * len(late),
         out_specs=[VMEM] * (planes + 1),
         scratch_shapes=[
-            pltpu.VMEM((KV_HEADS, HEAD + EXTRA, lanes), F32),
+            pltpu.VMEM((HEAD + EXTRA, KV_HEADS * lanes), F32),
             pltpu.VMEM((KEYS, lanes), F32),
-            pltpu.VMEM((KV_HEADS, 2 * HEAD, lanes), BF16),
+            pltpu.VMEM((KV_HEADS * HEAD, KV_HEADS * lanes), BF16),
             pltpu.VMEM((lanes, HEAD), F32),
             pltpu.VMEM((lanes // GROUP, width), F32),
             pltpu.VMEM((1, width), F32),
@@ -547,7 +546,7 @@
                 shape
                 for count in lanes
                 for shape in (
-                    pltpu.VMEM((2 * HEAD, count), BF16),
+                    pltpu.VMEM((HEAD, count), BF16),
                     pltpu.VMEM((HEAD + EXTRA, count), F32),
                 )
             ],

time: 70.9 us -> 70.3 us (level)
  transfers between devices with their start and end apart: 21 -> 21, of which waited for: 10 -> 11; matrix products, arithmetic and copies ran while one was open for 0% -> 0% of each run, Pallas kernels for 21% -> 22%
where the time goes in v12:
time: 70.3 us; the launch traced here: 70 us
  starting transfers between devices  27.2 us (39%)
  Pallas kernels  22.3 us (32%)
  waiting for transfers between devices  19.7 us (28%)
    ppermute x21, starting transfers between devices, move(): return lax.ppermute(value, 'expert', pairs)  27.2 us
    ppermute x21, waiting for transfers between devices, move(): return lax.ppermute(value, 'expert', pairs)  19.7 us
    pallas_call x3, Pallas kernels, own(): pl.pallas_call(functools.partial(own_kernel, n, heads, len(sources)), out...  7.76 us
    pallas_call x2, Pallas kernels, expert(): pl.pallas_call(functools.partial(expert_kernel, n // 2, len(pieces)), out...  4.07 us
    pallas_call x1, Pallas kernels, local(): pl.pallas_call(functools.partial(collect_kernel, n, early_senders), out_s...  2.88 us
    pallas_call x1, Pallas kernels, local(): pl.pallas_call(functools.partial(routed_kernel, n, late_senders), out_sha...  2.76 us
    pallas_call x1, Pallas kernels, local(): pl.pallas_call(functools.partial(select_kernel, planes), out_shape=[jax.S...  2.49 us
  transfers between devices with their start and end apart: 21, of which 11 were waited for; matrix products, arithmetic and copies ran while one was open for 0% of the time, Pallas kernels for 22%

profile of v12, /device:TPU:0, one launch (start us, length us, event | category | flops | bytes accessed | tf_op | source)
XLA Modules:
  0.0 70.0 jit_solution(8760976909166840089)
XLA Ops:
  0.0 1.0 %pack.1.refs_0_ = bf16[144,512]{1,0:T(8,128)(2,1)S(1)} custom-call(s32[1,128]{1,0:T(1,128)} %bitcast.8, bf16[128,256]{1,0:T(8,128)(2,1)} %keys_ref.1, bf16[128,256]{1,0:T(8,128)(2,1)} %values_ref.1), custom_call_target="tpu_custom_call" | custom-call | tf_op jit(solution)/shard_map/pack/pallas_call | solution.py:427
  1.0 3.1 %collective-permute-start = (bf16[144,512]{1,0:T(8,128)(2,1)S(1)}, bf16[144,512]{1,0:T(8,128)(2,1)S(1)}, u32[]{:S(2)}, u32[]{:S(2)}) collective-permute-start(bf16[144,512]{1,0:T(8,128)(2,1)S(1)} %pack.1.refs_0_), channel_id=1, source_target_pairs={{0,4},{1,5},{2,6},{3,7},{4,8},{5,9},{6,10},{7,11},{8,12},{9,13},{1... | collective-permute-start | bytes 442376 | tf_op jit(solution)/shard_map/ppermute | solution.py:442
  4.1 0.7 collective-permute-start.5
  4.7 4.8 %collective-permute-start.2 = (bf16[144,512]{1,0:T(8,128)(2,1)S(1)}, bf16[144,512]{1,0:T(8,128)(2,1)S(1)}, u32[]{:S(2)}, u32[]{:S(2)}) collective-permute-start(bf16[144,512]{1,0:T(8,128)(2,1)S(1)} %pack.1.refs_0_), channel_id=1, source_target_pairs={{0,2},{1,3},{2,0},{3,1},{4,6},{5,7},{6,4},{7,5},{8,10},{9,11},{10,... | collective-permute-start | bytes 442376 | tf_op jit(solution)/shard_map/ppermute | solution.py:442
  9.5 0.0 collective-permute-start.1
  9.5 2.5 %select.1 = (bf16[2,128,384]{2,1,0:T(8,128)(2,1)S(1)}, f32[24,4096]{1,0:T(8,128)S(1)}, f32[8,384]{1,0:T(8,128)S(1)}, bf16[128,64]{1,0:T(8,128)(2,1)S(1)}, bf16[1...) custom-call(s32[1]{0:T(128)} %bitcast.pos_ref, s32[4,128]{1,0:T(4,128)} %bitcast.6, s32[1,128]{1,0:T(1,128)} %bitcast.9, ...), custom_call_target="tpu_custom_call" | custom-call | tf_op jit(solution)/shard_map/select/pallas_call | solution.py:452
  12.0 0.0 collective-permute-done.refs_1_
  12.1 0.7 collective-permute-start.3
  12.8 2.8 %collective-permute-done.2.refs_4_ = bf16[144,512]{1,0:T(8,128)(2,1)S(1)} collective-permute-done((bf16[144,512]{1,0:T(8,128)(2,1)S(1)}, bf16[144,512]{1,0:T(8,128)(2,1)S(1)}, u32[]{:S(2)}, u32[]{:S(2)}) %collective-permute-start.2) | collective-permute-done | bytes 147488 | tf_op jit(solution)/shard_map/ppermute | solution.py:442
  15.5 4.8 %collective-permute-done.1.refs_2_ = bf16[144,512]{1,0:T(8,128)(2,1)S(1)} collective-permute-done((bf16[144,512]{1,0:T(8,128)(2,1)S(1)}, bf16[144,512]{1,0:T(8,128)(2,1)S(1)}, u32[]{:S(2)}, u32[]{:S(2)}) %collective-permute-start.1) | collective-permute-done | bytes 147488 | tf_op jit(solution)/shard_map/ppermute | solution.py:442
  20.4 0.0 copy-start
  20.4 0.0 copy-start.1
  20.4 0.1 collective-permute-start.6
  20.5 0.8 %collective-permute-start.4 = (bf16[144,512]{1,0:T(8,128)(2,1)S(1)}, bf16[144,512]{1,0:T(8,128)(2,1)S(1)}, u32[]{:S(2)}, u32[]{:S(2)}) collective-permute-start(bf16[144,512]{1,0:T(8,128)(2,1)S(1)} %collective-permute-done.1.refs_2_), channel_id=1, source_target_pairs={{0,0},{1,1},{2,2},{3,3},{4,4},{5,5},{6,6},{7,7},{8,10},{9,11},{10,... | collective-permute-start | bytes 442376 | tf_op jit(solution)/shard_map/ppermute | solution.py:442
  21.3 1.6 %collective-permute-done.6.refs_6_ = bf16[864,512]{1,0:T(8,128)(2,1)S(1)} collective-permute-done((bf16[864,512]{1,0:T(8,128)(2,1)S(1)}, bf16[864,512]{1,0:T(8,128)(2,1)S(1)}, u32[]{:S(2)}, u32[]{:S(2)}) %collective-permute-start.6) | collective-permute-done | bytes 884768 | tf_op jit(solution)/shard_map/ppermute | solution.py:442
  22.9 2.9 %collect.1._ = bf16[16,144,512]{2,1,0:T(8,128)(2,1)S(1)} custom-call(s32[1]{0:T(128)} %bitcast.pos_ref, bf16[144,512]{1,0:T(8,128)(2,1)S(1)} %pack.1.refs_0_, bf16[144,512]{1,0:T(8,128)(2,1)S(1)} %collective-permute-done.refs_1_, bf16[144,512]{1,0:T(8,128)(2,1)S(1)} %collective-permute-done.1.refs_2_, bf16[144,512]{1,0:T(8,128)(2,1)S(1)} %collective-permute-done.5.refs_3_, ...), custom_call_target="tpu_custom_call" | custom-call | bytes 1000 | tf_op jit(solution)/shard_map/collect/pallas_call | solution.py:499
  25.8 0.0 collective-permute-done.4.refs_0_
  25.8 0.2 collective-permute-start.7
  26.0 1.2 %collective-permute-done.7.refs_1_ = bf16[144,512]{1,0:T(8,128)(2,1)S(1)} collective-permute-done((bf16[144,512]{1,0:T(8,128)(2,1)S(1)}, bf16[144,512]{1,0:T(8,128)(2,1)S(1)}, u32[]{:S(2)}, u32[]{:S(2)}) %collective-permute-start.7) | collective-permute-done | bytes 147488 | tf_op jit(solution)/shard_map/ppermute | solution.py:442
  27.3 2.8 %routed.1 = (bf16[24,1024]{1,0:T(8,128)(2,1)S(1)}, bf16[24,1024]{1,0:T(8,128)(2,1)S(1)}, bf16[24,1024]{1,0:T(8,128)(2,1)S(1)}, bf16[24,1024]{1,0:T(8,128)(2,1)S(1)}, bf16[16,144,512]{2,1,0:T(8,128)(2,1)S(1)}) custom-call(s32[1]{0:T(128)} %bitcast.pos_ref, f32[1,4096]{1,0:T(1,128)} %bitcast.5, ...), custom_call_target="tpu_custom_call", output_to_operand_aliasing={{4}: (5, {})} | custom-call | tf_op jit(solution)/shard_map/routed/pallas_call | solution.py:513
  30.0 1.5 %collective-permute-start.8 = (bf16[24,1024]{1,0:T(8,128)(2,1)S(1)}, bf16[24,1024]{1,0:T(8,128)(2,1)S(1)}, u32[]{:S(2)}, u32[]{:S(2)}) collective-permute-start(bf16[24,1024]{1,0:T(8,128)(2,1)S(1)} %get-tuple-element.63), channel_id=1, source_target_pairs={{0,4},{1,5},{2,6},{3,7},{4,8},{5,9},{6,10},{7,11},{8,12},{9,13},{1... | collective-permute-start | bytes 147464 | tf_op jit(solution)/shard_map/ppermute | solution.py:442
  31.5 4.7 %collective-permute-start.9 = (bf16[24,1024]{1,0:T(8,128)(2,1)S(1)}, bf16[24,1024]{1,0:T(8,128)(2,1)S(1)}, u32[]{:S(2)}, u32[]{:S(2)}) collective-permute-start(bf16[24,1024]{1,0:T(8,128)(2,1)S(1)} %get-tuple-element.64), channel_id=1, source_target_pairs={{0,8},{1,9},{2,10},{3,11},{4,12},{5,13},{6,14},{7,15},{8,0},{9,1},... | collective-permute-start | bytes 147464 | tf_op jit(solution)/shard_map/ppermute | solution.py:442
  36.2 2.8 %collective-permute-start.10 = (bf16[24,1024]{1,0:T(8,128)(2,1)S(1)}, bf16[24,1024]{1,0:T(8,128)(2,1)S(1)}, u32[]{:S(2)}, u32[]{:S(2)}) collective-permute-start(bf16[24,1024]{1,0:T(8,128)(2,1)S(1)} %get-tuple-element.65), channel_id=1, source_target_pairs={{0,12},{1,13},{2,14},{3,15},{4,0},{5,1},{6,2},{7,3},{8,4},{9,5},{1... | collective-permute-start | bytes 147464 | tf_op jit(solution)/shard_map/ppermute | solution.py:442
  39.1 3.9 %own.3 = (f32[128,1280]{1,0:T(8,128)S(1)}, f32[8,128]{1,0:T(8,128)S(1)}, bf16[4096,384]{1,0:T(8,128)(2,1)S(1)}, bf16[4096,384]{1,0:T(8,128)(2,1)S(1)}, bf16[384,4096]{1,0:T(8,128)(2,1)S(1)}) custom-call(s32[1]{0:T(128)} %bitcast.pos_ref, bf16[16,144,512]{2,1,0:T(8,128)(2,1)S(1)} %get-tuple-element.58.held, bf16[128,4096]{1,0:T(8,128)(2,1)S(1)} %copy-done, ...), custom_call_target="tpu_custom_call" | custom-call | flops 2000000000 | bytes 8000000 | tf_op jit(solution)/shard_map/own/pallas_call | solution.py:535
  43.0 0.0 collective-permute-done.10
  43.0 0.2 collective-permute-done.11.refs_0_
  43.2 0.1 collective-permute-start.13
  43.3 1.9 %collective-permute-start.12 = (bf16[72,1024]{1,0:T(8,128)(2,1)S(1)}, bf16[72,1024]{1,0:T(8,128)(2,1)S(1)}, u32[]{:S(2)}, u32[]{:S(2)}) collective-permute-start(bf16[72,1024]{1,0:T(8,128)(2,1)S(1)} %constant_dynamic-update-slice_fusion.6.refs_1_), channel_id=1, source_target_pairs={{0,2},{1,3},{2,0},{3,1},{4,6},{5,7},{6,4},{7,5},{8,10},{9,11},{10,... | collective-permute-start | bytes 442376 | tf_op jit(solution)/shard_map/ppermute | solution.py:442
  45.2 1.4 %own.4 = (f32[128,768]{1,0:T(8,128)S(1)}, f32[8,128]{1,0:T(8,128)S(1)}) custom-call(s32[1]{0:T(128)} %bitcast.pos_ref, bf16[16,144,512]{2,1,0:T(8,128)(2,1)S(1)} %get-tuple-element.58.held, bf16[128,4096]{1,0:T(8,128)(2,1)S(1)} %copy-done, bf16[128,4096]{1,0:T(8,128)(2,1)S(1)} %copy-done.1, f32[8,128]{1,0:T(8,128)S(1)} %get-tuple-element.76._.refs_8_), custom_call_target="tpu_custom_call" | custom-call | flops 2000000000 | bytes 8000000 | tf_op jit(solution)/shard_map/own/pallas_call | solution.py:535
  46.7 2.0 %expert.2 = (bf16[96,1024]{1,0:T(8,128)(2,1)S(1)}, bf16[96,1024]{1,0:T(8,128)(2,1)S(1)}) custom-call(bf16[24,1024]{1,0:T(8,128)(2,1)S(1)} %get-tuple-element.59._.refs_0_, bf16[72,1024]{1,0:T(8,128)(2,1)S(1)} %constant_dynamic-update-slice_fusion.6.refs_1_, bf16[96,1024]{1,0:T(8,128)(2,1)S(1)} %collective-permute-done.13.refs_2_, ...), custom_call_target="tpu_custom_call" | custom-call | flops 600000000 | bytes 2000000 | tf_op jit(solution)/shard_map/expert/pallas_call | solution.py:575
  48.7 0.9 %collective-permute-done.12.refs_1_ = bf16[72,1024]{1,0:T(8,128)(2,1)S(1)} collective-permute-done((bf16[72,1024]{1,0:T(8,128)(2,1)S(1)}, bf16[72,1024]{1,0:T(8,128)(2,1)S(1)}, u32[]{:S(2)}, u32[]{:S(2)}) %collective-permute-start.12) | collective-permute-done | bytes 147488 | tf_op jit(solution)/shard_map/ppermute | solution.py:442
  49.6 0.1 collective-permute-start.14
  49.7 1.4 %collective-permute-done.14.refs_2_ = bf16[96,1024]{1,0:T(8,128)(2,1)S(1)} collective-permute-done((bf16[96,1024]{1,0:T(8,128)(2,1)S(1)}, bf16[96,1024]{1,0:T(8,128)(2,1)S(1)}, u32[]{:S(2)}, u32[]{:S(2)}) %collective-permute-start.14) | collective-permute-done | bytes 196640 | tf_op jit(solution)/shard_map/ppermute | solution.py:442
  51.2 2.0 %expert.3 = (bf16[96,1024]{1,0:T(8,128)(2,1)S(1)}, bf16[96,1024]{1,0:T(8,128)(2,1)S(1)}) custom-call(bf16[24,1024]{1,0:T(8,128)(2,1)S(1)} %collective-permute-done.11.refs_0_, bf16[72,1024]{1,0:T(8,128)(2,1)S(1)} %collective-permute-done.12.refs_1_, bf16[96,1024]{1,0:T(8,128)(2,1)S(1)} %collective-permute-done.14.refs_2_, ...), custom_call_target="tpu_custom_call" | custom-call | flops 600000000 | bytes 2000000 | tf_op jit(solution)/shard_map/expert/pallas_call | solution.py:575
  53.2 0.2 collective-permute-start.16
  53.4 1.3 %collective-permute-done.16 = bf16[96,1024]{1,0:T(8,128)(2,1)S(1)} collective-permute-done((bf16[96,1024]{1,0:T(8,128)(2,1)S(1)}, bf16[96,1024]{1,0:T(8,128)(2,1)S(1)}, u32[]{:S(2)}, u32[]{:S(2)}) %collective-permute-start.16) | collective-permute-done | bytes 196640 | tf_op jit(solution)/shard_map/ppermute | solution.py:442
  54.8 1.8 %collective-permute-start.17 = (bf16[96,1024]{1,0:T(8,128)(2,1)S(1)}, bf16[96,1024]{1,0:T(8,128)(2,1)S(1)}, u32[]{:S(2)}, u32[]{:S(2)}) collective-permute-start(bf16[96,1024]{1,0:T(8,128)(2,1)S(1)} %add_convert_fusion.1), channel_id=1, source_target_pairs={{0,2},{1,3},{2,0},{3,1},{4,6},{5,7},{6,4},{7,5},{8,10},{9,11},{10,... | collective-permute-start | bytes 589832 | tf_op jit(solution)/shard_map/ppermute | solution.py:442
  56.6 0.0 collective-permute-start.15
  56.6 2.5 %own.5 = (f32[128,2048]{1,0:T(8,128)S(1)}, f32[8,128]{1,0:T(8,128)S(1)}) custom-call(s32[1]{0:T(128)} %bitcast.pos_ref, bf16[16,144,512]{2,1,0:T(8,128)(2,1)S(1)} %get-tuple-element.58.held, bf16[128,4096]{1,0:T(8,128)(2,1)S(1)} %copy-done, bf16[128,4096]{1,0:T(8,128)(2,1)S(1)} %copy-done.1, bf16[96,1024]{1,0:T(8,128)(2,1)S(1)} %get-tuple-element.81._), custom_call_target="tpu_custom_call" | custom-call | flops 2000000000 | bytes 8000000 | tf_op jit(solution)/shard_map/own/pallas_call | solution.py:535
  59.0 2.8 %collective-permute-done.17 = bf16[96,1024]{1,0:T(8,128)(2,1)S(1)} collective-permute-done((bf16[96,1024]{1,0:T(8,128)(2,1)S(1)}, bf16[96,1024]{1,0:T(8,128)(2,1)S(1)}, u32[]{:S(2)}, u32[]{:S(2)}) %collective-permute-start.17) | collective-permute-done | bytes 196640 | tf_op jit(solution)/shard_map/ppermute | solution.py:442
  61.8 0.0 collective-permute-done.15
  61.8 0.1 add_convert_fusion
  61.9 0.1 collective-permute-start.20
  62.0 2.2 %collective-permute-start.19 = (bf16[24,1024]{1,0:T(8,128)(2,1)S(1)}, bf16[24,1024]{1,0:T(8,128)(2,1)S(1)}, u32[]{:S(2)}, u32[]{:S(2)}) collective-permute-start(bf16[24,1024]{1,0:T(8,128)(2,1)S(1)} %get-tuple-element.90), channel_id=1, source_target_pairs={{0,8},{1,9},{2,10},{3,11},{4,12},{5,13},{6,14},{7,15},{8,0},{9,1},... | collective-permute-start | bytes 147464 | tf_op jit(solution)/shard_map/ppermute | solution.py:442
  64.2 1.6 %collective-permute-start.18 = (bf16[24,1024]{1,0:T(8,128)(2,1)S(1)}, bf16[24,1024]{1,0:T(8,128)(2,1)S(1)}, u32[]{:S(2)}, u32[]{:S(2)}) collective-permute-start(bf16[24,1024]{1,0:T(8,128)(2,1)S(1)} %get-tuple-element.91), channel_id=1, source_target_pairs={{0,12},{1,13},{2,14},{3,15},{4,0},{5,1},{6,2},{7,3},{8,4},{9,5},{1... | collective-permute-start | bytes 147464 | tf_op jit(solution)/shard_map/ppermute | solution.py:442
  65.8 2.2 %collective-permute-done.20.refs_6_ = bf16[24,1024]{1,0:T(8,128)(2,1)S(1)} collective-permute-done((bf16[24,1024]{1,0:T(8,128)(2,1)S(1)}, bf16[24,1024]{1,0:T(8,128)(2,1)S(1)}, u32[]{:S(2)}, u32[]{:S(2)}) %collective-permute-start.20) | collective-permute-done | bytes 49184 | tf_op jit(solution)/shard_map/ppermute | solution.py:442
  67.9 0.5 collective-permute-done.18.refs_4_
  68.5 1.4 %combine.1 = bf16[128,4096]{1,0:T(8,128)(2,1)} custom-call(bf16[128,64]{1,0:T(8,128)(2,1)S(1)} %get-tuple-element.47.mix_ref, f32[128,1280]{1,0:T(8,128)S(1)} %get-tuple-element.60.refs_0_, f32[128,768]{1,0:T(8,128)S(1)} %get-tuple-element.62.refs_1_, f32[128,2048]{1,0:T(8,128)S(1)} %get-tuple-element.82.refs_2_, ...), custom_call_target="tpu_custom_call" | custom-call | tf_op jit(solution)/shard_map/combine/pallas_call | solution.py:608
  (22 shorter events, 0.2 us)
Async XLA Ops:
  1.0 11.1 %collective-permute-start = (bf16[144,512]{1,0:T(8,128)(2,1)S(1)}, bf16[144,512]{1,0:T(8,128)(2,1)S(1)}, u32[]{:S(2)}, u32[]{:S(2)}) collective-permute-start(bf16[144,512]{1,0:T(8,128)(2,1)S(1)} %pack.1.refs_0_), channel_id=1, source_target_pairs={{0,4},{1,5},{2,6},{3,7},{4,8},{5,9},{6,10},{7,11},{8,12},{9,13},{1... | collective-permute-start | bytes 442376 | tf_op jit(solution)/shard_map/ppermute | solution.py:442
  4.1 16.3 %collective-permute-start.5 = (bf16[144,512]{1,0:T(8,128)(2,1)S(1)}, bf16[144,512]{1,0:T(8,128)(2,1)S(1)}, u32[]{:S(2)}, u32[]{:S(2)}) collective-permute-start(bf16[144,512]{1,0:T(8,128)(2,1)S(1)} %pack.1.refs_0_), channel_id=1, source_target_pairs={{0,0},{1,1},{2,12},{3,13},{4,4},{5,5},{6,6},{7,7},{8,8},{9,9},{10,... | collective-permute-start | bytes 442376 | tf_op jit(solution)/shard_map/ppermute | solution.py:442
  4.7 10.8 %collective-permute-start.2 = (bf16[144,512]{1,0:T(8,128)(2,1)S(1)}, bf16[144,512]{1,0:T(8,128)(2,1)S(1)}, u32[]{:S(2)}, u32[]{:S(2)}) collective-permute-start(bf16[144,512]{1,0:T(8,128)(2,1)S(1)} %pack.1.refs_0_), channel_id=1, source_target_pairs={{0,2},{1,3},{2,0},{3,1},{4,6},{5,7},{6,4},{7,5},{8,10},{9,11},{10,... | collective-permute-start | bytes 442376 | tf_op jit(solution)/shard_map/ppermute | solution.py:442
  9.5 10.8 %collective-permute-start.1 = (bf16[144,512]{1,0:T(8,128)(2,1)S(1)}, bf16[144,512]{1,0:T(8,128)(2,1)S(1)}, u32[]{:S(2)}, u32[]{:S(2)}) collective-permute-start(bf16[144,512]{1,0:T(8,128)(2,1)S(1)} %pack.1.refs_0_), channel_id=1, source_target_pairs={{0,8},{1,9},{2,10},{3,11},{4,12},{5,13},{6,14},{7,15},{8,0},{9,1},... | collective-permute-start | bytes 442376 | tf_op jit(solution)/shard_map/ppermute | solution.py:442
  12.1 8.3 %collective-permute-start.3 = (bf16[144,512]{1,0:T(8,128)(2,1)S(1)}, bf16[144,512]{1,0:T(8,128)(2,1)S(1)}, u32[]{:S(2)}, u32[]{:S(2)}) collective-permute-start(bf16[144,512]{1,0:T(8,128)(2,1)S(1)} %collective-permute-done.refs_1_), channel_id=1, source_target_pairs={{0,0},{1,1},{2,2},{3,3},{4,6},{5,7},{6,4},{7,5},{8,10},{9,11},{10,... | collective-permute-start | bytes 442376 | tf_op jit(solution)/shard_map/ppermute | solution.py:442
  20.4 18.6 %copy-start = (bf16[128,4096]{1,0:T(8,128)(2,1)S(1)}, bf16[128,4096]{1,0:T(8,128)(2,1)}, u32[]{:S(2)}) copy-start(bf16[128,4096]{1,0:T(8,128)(2,1)} %q_ref.5) | copy-start | bytes 3145732
  20.4 18.6 %copy-start.1 = (bf16[128,4096]{1,0:T(8,128)(2,1)S(1)}, bf16[128,4096]{1,0:T(8,128)(2,1)}, u32[]{:S(2)}) copy-start(bf16[128,4096]{1,0:T(8,128)(2,1)} %x_ref.5) | copy-start | bytes 3145732
  20.4 2.5 %collective-permute-start.6 = (bf16[864,512]{1,0:T(8,128)(2,1)S(1)}, bf16[864,512]{1,0:T(8,128)(2,1)S(1)}, u32[]{:S(2)}, u32[]{:S(2)}) collective-permute-start(bf16[864,512]{1,0:T(8,128)(2,1)S(1)} %constant_dynamic-update-slice_fusion), channel_id=1, source_target_pairs={{0,1},{1,0},{2,3},{3,2},{4,5},{5,4},{6,7},{7,6},{8,9},{9,8},{10,11... | collective-permute-start | bytes 2654216 | tf_op jit(solution)/shard_map/ppermute | solution.py:442
  20.5 5.3 %collective-permute-start.4 = (bf16[144,512]{1,0:T(8,128)(2,1)S(1)}, bf16[144,512]{1,0:T(8,128)(2,1)S(1)}, u32[]{:S(2)}, u32[]{:S(2)}) collective-permute-start(bf16[144,512]{1,0:T(8,128)(2,1)S(1)} %collective-permute-done.1.refs_2_), channel_id=1, source_target_pairs={{0,0},{1,1},{2,2},{3,3},{4,4},{5,5},{6,6},{7,7},{8,10},{9,11},{10,... | collective-permute-start | bytes 442376 | tf_op jit(solution)/shard_map/ppermute | solution.py:442
  25.8 1.4 %collective-permute-start.7 = (bf16[144,512]{1,0:T(8,128)(2,1)S(1)}, bf16[144,512]{1,0:T(8,128)(2,1)S(1)}, u32[]{:S(2)}, u32[]{:S(2)}) collective-permute-start(bf16[144,512]{1,0:T(8,128)(2,1)S(1)} %collective-permute-done.4.refs_0_), channel_id=1, source_target_pairs={{0,1},{1,0},{2,3},{3,2},{4,5},{5,4},{6,7},{7,6},{8,9},{9,8},{10,11... | collective-permute-start | bytes 442376 | tf_op jit(solution)/shard_map/ppermute | solution.py:442
  30.0 12.9 %collective-permute-start.8 = (bf16[24,1024]{1,0:T(8,128)(2,1)S(1)}, bf16[24,1024]{1,0:T(8,128)(2,1)S(1)}, u32[]{:S(2)}, u32[]{:S(2)}) collective-permute-start(bf16[24,1024]{1,0:T(8,128)(2,1)S(1)} %get-tuple-element.63), channel_id=1, source_target_pairs={{0,4},{1,5},{2,6},{3,7},{4,8},{5,9},{6,10},{7,11},{8,12},{9,13},{1... | collective-permute-start | bytes 147464 | tf_op jit(solution)/shard_map/ppermute | solution.py:442
  31.5 11.4 %collective-permute-start.9 = (bf16[24,1024]{1,0:T(8,128)(2,1)S(1)}, bf16[24,1024]{1,0:T(8,128)(2,1)S(1)}, u32[]{:S(2)}, u32[]{:S(2)}) collective-permute-start(bf16[24,1024]{1,0:T(8,128)(2,1)S(1)} %get-tuple-element.64), channel_id=1, source_target_pairs={{0,8},{1,9},{2,10},{3,11},{4,12},{5,13},{6,14},{7,15},{8,0},{9,1},... | collective-permute-start | bytes 147464 | tf_op jit(solution)/shard_map/ppermute | solution.py:442
  36.2 6.8 %collective-permute-start.10 = (bf16[24,1024]{1,0:T(8,128)(2,1)S(1)}, bf16[24,1024]{1,0:T(8,128)(2,1)S(1)}, u32[]{:S(2)}, u32[]{:S(2)}) collective-permute-start(bf16[24,1024]{1,0:T(8,128)(2,1)S(1)} %get-tuple-element.65), channel_id=1, source_target_pairs={{0,12},{1,13},{2,14},{3,15},{4,0},{5,1},{6,2},{7,3},{8,4},{9,5},{1... | collective-permute-start | bytes 147464 | tf_op jit(solution)/shard_map/ppermute | solution.py:442
  39.1 4.1 %collective-permute-start.11 = (bf16[24,1024]{1,0:T(8,128)(2,1)S(1)}, bf16[24,1024]{1,0:T(8,128)(2,1)S(1)}, u32[]{:S(2)}, u32[]{:S(2)}) collective-permute-start(bf16[24,1024]{1,0:T(8,128)(2,1)S(1)} %get-tuple-element.59._.refs_0_), channel_id=1, source_target_pairs={{0,2},{1,3},{2,0},{3,1},{4,6},{5,7},{6,4},{7,5},{8,10},{9,11},{10,... | collective-permute-start | bytes 147464 | tf_op jit(solution)/shard_map/ppermute | solution.py:442
  43.2 3.5 %collective-permute-start.13 = (bf16[96,1024]{1,0:T(8,128)(2,1)S(1)}, bf16[96,1024]{1,0:T(8,128)(2,1)S(1)}, u32[]{:S(2)}, u32[]{:S(2)}) collective-permute-start(bf16[96,1024]{1,0:T(8,128)(2,1)S(1)} %pad_maximum_fusion), channel_id=1, source_target_pairs={{0,1},{1,0},{2,3},{3,2},{4,5},{5,4},{6,7},{7,6},{8,9},{9,8},{10,11... | collective-permute-start | bytes 589832 | tf_op jit(solution)/shard_map/ppermute | solution.py:442
  43.3 6.4 %collective-permute-start.12 = (bf16[72,1024]{1,0:T(8,128)(2,1)S(1)}, bf16[72,1024]{1,0:T(8,128)(2,1)S(1)}, u32[]{:S(2)}, u32[]{:S(2)}) collective-permute-start(bf16[72,1024]{1,0:T(8,128)(2,1)S(1)} %constant_dynamic-update-slice_fusion.6.refs_1_), channel_id=1, source_target_pairs={{0,2},{1,3},{2,0},{3,1},{4,6},{5,7},{6,4},{7,5},{8,10},{9,11},{10,... | collective-permute-start | bytes 442376 | tf_op jit(solution)/shard_map/ppermute | solution.py:442
  49.6 1.5 %collective-permute-start.14 = (bf16[96,1024]{1,0:T(8,128)(2,1)S(1)}, bf16[96,1024]{1,0:T(8,128)(2,1)S(1)}, u32[]{:S(2)}, u32[]{:S(2)}) collective-permute-start(bf16[96,1024]{1,0:T(8,128)(2,1)S(1)} %pad_maximum_fusion.1), channel_id=1, source_target_pairs={{0,1},{1,0},{2,3},{3,2},{4,5},{5,4},{6,7},{7,6},{8,9},{9,8},{10,11... | collective-permute-start | bytes 589832 | tf_op jit(solution)/shard_map/ppermute | solution.py:442
  53.2 1.5 %collective-permute-start.16 = (bf16[96,1024]{1,0:T(8,128)(2,1)S(1)}, bf16[96,1024]{1,0:T(8,128)(2,1)S(1)}, u32[]{:S(2)}, u32[]{:S(2)}) collective-permute-start(bf16[96,1024]{1,0:T(8,128)(2,1)S(1)} %get-tuple-element.85), channel_id=1, source_target_pairs={{0,1},{1,0},{2,3},{3,2},{4,5},{5,4},{6,7},{7,6},{8,9},{9,8},{10,11... | collective-permute-start | bytes 589832 | tf_op jit(solution)/shard_map/ppermute | solution.py:442
  54.8 7.0 %collective-permute-start.17 = (bf16[96,1024]{1,0:T(8,128)(2,1)S(1)}, bf16[96,1024]{1,0:T(8,128)(2,1)S(1)}, u32[]{:S(2)}, u32[]{:S(2)}) collective-permute-start(bf16[96,1024]{1,0:T(8,128)(2,1)S(1)} %add_convert_fusion.1), channel_id=1, source_target_pairs={{0,2},{1,3},{2,0},{3,1},{4,6},{5,7},{6,4},{7,5},{8,10},{9,11},{10,... | collective-permute-start | bytes 589832 | tf_op jit(solution)/shard_map/ppermute | solution.py:442
  56.6 5.2 %collective-permute-start.15 = (bf16[96,1024]{1,0:T(8,128)(2,1)S(1)}, bf16[96,1024]{1,0:T(8,128)(2,1)S(1)}, u32[]{:S(2)}, u32[]{:S(2)}) collective-permute-start(bf16[96,1024]{1,0:T(8,128)(2,1)S(1)} %get-tuple-element.84), channel_id=1, source_target_pairs={{0,1},{1,0},{2,3},{3,2},{4,5},{5,4},{6,7},{7,6},{8,9},{9,8},{10,11... | collective-permute-start | bytes 589832 | tf_op jit(solution)/shard_map/ppermute | solution.py:442
  61.9 6.0 %collective-permute-start.20 = (bf16[24,1024]{1,0:T(8,128)(2,1)S(1)}, bf16[24,1024]{1,0:T(8,128)(2,1)S(1)}, u32[]{:S(2)}, u32[]{:S(2)}) collective-permute-start(bf16[24,1024]{1,0:T(8,128)(2,1)S(1)} %get-tuple-element.89), channel_id=1, source_target_pairs={{0,4},{1,5},{2,6},{3,7},{4,8},{5,9},{6,10},{7,11},{8,12},{9,13},{1... | collective-permute-start | bytes 147464 | tf_op jit(solution)/shard_map/ppermute | solution.py:442
  62.0 6.0 %collective-permute-start.19 = (bf16[24,1024]{1,0:T(8,128)(2,1)S(1)}, bf16[24,1024]{1,0:T(8,128)(2,1)S(1)}, u32[]{:S(2)}, u32[]{:S(2)}) collective-permute-start(bf16[24,1024]{1,0:T(8,128)(2,1)S(1)} %get-tuple-element.90), channel_id=1, source_target_pairs={{0,8},{1,9},{2,10},{3,11},{4,12},{5,13},{6,14},{7,15},{8,0},{9,1},... | collective-permute-start | bytes 147464 | tf_op jit(solution)/shard_map/ppermute | solution.py:442
  64.2 4.3 %collective-permute-start.18 = (bf16[24,1024]{1,0:T(8,128)(2,1)S(1)}, bf16[24,1024]{1,0:T(8,128)(2,1)S(1)}, u32[]{:S(2)}, u32[]{:S(2)}) collective-permute-start(bf16[24,1024]{1,0:T(8,128)(2,1)S(1)} %get-tuple-element.91), channel_id=1, source_target_pairs={{0,12},{1,13},{2,14},{3,15},{4,0},{5,1},{6,2},{7,3},{8,4},{9,5},{1... | collective-permute-start | bytes 147464 | tf_op jit(solution)/shard_map/ppermute | solution.py:442

commit v13 on v12

--- a/solution.py
+++ b/solution.py
@@ -557,8 +557,8 @@
             name="own",
         )(pos, held, queries, resid, after, *map(pin, sources))
 
-    half0, done, *weights = own(range(10), sent[0], w_gate, w_up, w_down)
-    half1, late = own(range(10, GROUP), done)
+    half0, done, *weights = own(range(9), sent[0], w_gate, w_up, w_down)
+    half1, late = own(range(9, GROUP), done)
     halves = [half0, half1]
 
     come = [

time: 70.3 us -> 70.3 us (level)
  transfers between devices with their start and end apart: 21 -> 21, of which waited for: 11 -> 10; matrix products, arithmetic and copies ran while one was open for 0% -> 0% of each run, Pallas kernels for 22% -> 22%
where the time goes in v13:
time: 70.3 us; the launch traced here: 70.1 us
  starting transfers between devices  26.8 us (38%)
  Pallas kernels  22.4 us (32%)
  waiting for transfers between devices  20.1 us (29%)
    ppermute x21, starting transfers between devices, move(): return lax.ppermute(value, 'expert', pairs)  26.8 us
    ppermute x21, waiting for transfers between devices, move(): return lax.ppermute(value, 'expert', pairs)  20.1 us
    pallas_call x3, Pallas kernels, own(): pl.pallas_call(functools.partial(own_kernel, n, heads, len(sources)), out...  7.9 us
    pallas_call x2, Pallas kernels, expert(): pl.pallas_call(functools.partial(expert_kernel, n // 2, len(pieces)), out...  4.07 us
    pallas_call x1, Pallas kernels, local(): pl.pallas_call(functools.partial(collect_kernel, n, early_senders), out_s...  2.88 us
    pallas_call x1, Pallas kernels, local(): pl.pallas_call(functools.partial(routed_kernel, n, late_senders), out_sha...  2.76 us
    pallas_call x1, Pallas kernels, local(): pl.pallas_call(functools.partial(select_kernel, planes), out_shape=[jax.S...  2.49 us
  transfers between devices with their start and end apart: 21, of which 10 were waited for; matrix products, arithmetic and copies ran while one was open for 0% of the time, Pallas kernels for 22%

profile of v13, /device:TPU:0, one launch (start us, length us, event | category | flops | bytes accessed | tf_op | source)
XLA Modules:
  0.0 70.1 jit_solution(10988910013508335918)
XLA Ops:
  0.0 1.0 %pack.1.refs_0_ = bf16[144,512]{1,0:T(8,128)(2,1)S(1)} custom-call(s32[1,128]{1,0:T(1,128)} %bitcast.8, bf16[128,256]{1,0:T(8,128)(2,1)} %keys_ref.1, bf16[128,256]{1,0:T(8,128)(2,1)} %values_ref.1), custom_call_target="tpu_custom_call" | custom-call | tf_op jit(solution)/shard_map/pack/pallas_call | solution.py:427
  1.0 3.1 %collective-permute-start = (bf16[144,512]{1,0:T(8,128)(2,1)S(1)}, bf16[144,512]{1,0:T(8,128)(2,1)S(1)}, u32[]{:S(2)}, u32[]{:S(2)}) collective-permute-start(bf16[144,512]{1,0:T(8,128)(2,1)S(1)} %pack.1.refs_0_), channel_id=1, source_target_pairs={{0,4},{1,5},{2,6},{3,7},{4,8},{5,9},{6,10},{7,11},{8,12},{9,13},{1... | collective-permute-start | bytes 442376 | tf_op jit(solution)/shard_map/ppermute | solution.py:442
  4.1 0.7 collective-permute-start.5
  4.7 4.8 %collective-permute-start.2 = (bf16[144,512]{1,0:T(8,128)(2,1)S(1)}, bf16[144,512]{1,0:T(8,128)(2,1)S(1)}, u32[]{:S(2)}, u32[]{:S(2)}) collective-permute-start(bf16[144,512]{1,0:T(8,128)(2,1)S(1)} %pack.1.refs_0_), channel_id=1, source_target_pairs={{0,2},{1,3},{2,0},{3,1},{4,6},{5,7},{6,4},{7,5},{8,10},{9,11},{10,... | collective-permute-start | bytes 442376 | tf_op jit(solution)/shard_map/ppermute | solution.py:442
  9.5 0.0 collective-permute-start.1
  9.5 2.5 %select.1 = (bf16[2,128,384]{2,1,0:T(8,128)(2,1)S(1)}, f32[24,4096]{1,0:T(8,128)S(1)}, f32[8,384]{1,0:T(8,128)S(1)}, bf16[128,64]{1,0:T(8,128)(2,1)S(1)}, bf16[1...) custom-call(s32[1]{0:T(128)} %bitcast.pos_ref, s32[4,128]{1,0:T(4,128)} %bitcast.6, s32[1,128]{1,0:T(1,128)} %bitcast.9, ...), custom_call_target="tpu_custom_call" | custom-call | tf_op jit(solution)/shard_map/select/pallas_call | solution.py:452
  12.0 0.0 collective-permute-done.refs_1_
  12.1 0.7 collective-permute-start.3
  12.8 2.8 %collective-permute-done.2.refs_4_ = bf16[144,512]{1,0:T(8,128)(2,1)S(1)} collective-permute-done((bf16[144,512]{1,0:T(8,128)(2,1)S(1)}, bf16[144,512]{1,0:T(8,128)(2,1)S(1)}, u32[]{:S(2)}, u32[]{:S(2)}) %collective-permute-start.2) | collective-permute-done | bytes 147488 | tf_op jit(solution)/shard_map/ppermute | solution.py:442
  15.5 4.8 %collective-permute-done.1.refs_2_ = bf16[144,512]{1,0:T(8,128)(2,1)S(1)} collective-permute-done((bf16[144,512]{1,0:T(8,128)(2,1)S(1)}, bf16[144,512]{1,0:T(8,128)(2,1)S(1)}, u32[]{:S(2)}, u32[]{:S(2)}) %collective-permute-start.1) | collective-permute-done | bytes 147488 | tf_op jit(solution)/shard_map/ppermute | solution.py:442
  20.3 0.0 collective-permute-done.3.refs_5_
  20.3 0.0 collective-permute-done.5.refs_3_
  20.4 0.0 copy-start
  20.4 0.0 copy-start.1
  20.4 0.1 collective-permute-start.6
  20.5 0.8 %collective-permute-start.4 = (bf16[144,512]{1,0:T(8,128)(2,1)S(1)}, bf16[144,512]{1,0:T(8,128)(2,1)S(1)}, u32[]{:S(2)}, u32[]{:S(2)}) collective-permute-start(bf16[144,512]{1,0:T(8,128)(2,1)S(1)} %collective-permute-done.1.refs_2_), channel_id=1, source_target_pairs={{0,0},{1,1},{2,2},{3,3},{4,4},{5,5},{6,6},{7,7},{8,10},{9,11},{10,... | collective-permute-start | bytes 442376 | tf_op jit(solution)/shard_map/ppermute | solution.py:442
  21.3 1.6 %collective-permute-done.6.refs_6_ = bf16[864,512]{1,0:T(8,128)(2,1)S(1)} collective-permute-done((bf16[864,512]{1,0:T(8,128)(2,1)S(1)}, bf16[864,512]{1,0:T(8,128)(2,1)S(1)}, u32[]{:S(2)}, u32[]{:S(2)}) %collective-permute-start.6) | collective-permute-done | bytes 884768 | tf_op jit(solution)/shard_map/ppermute | solution.py:442
  22.9 2.9 %collect.1._ = bf16[16,144,512]{2,1,0:T(8,128)(2,1)S(1)} custom-call(s32[1]{0:T(128)} %bitcast.pos_ref, bf16[144,512]{1,0:T(8,128)(2,1)S(1)} %pack.1.refs_0_, bf16[144,512]{1,0:T(8,128)(2,1)S(1)} %collective-permute-done.refs_1_, bf16[144,512]{1,0:T(8,128)(2,1)S(1)} %collective-permute-done.1.refs_2_, bf16[144,512]{1,0:T(8,128)(2,1)S(1)} %collective-permute-done.5.refs_3_, ...), custom_call_target="tpu_custom_call" | custom-call | bytes 1000 | tf_op jit(solution)/shard_map/collect/pallas_call | solution.py:499
  25.8 0.0 collective-permute-done.4.refs_0_
  25.8 0.2 collective-permute-start.7
  26.0 1.2 %collective-permute-done.7.refs_1_ = bf16[144,512]{1,0:T(8,128)(2,1)S(1)} collective-permute-done((bf16[144,512]{1,0:T(8,128)(2,1)S(1)}, bf16[144,512]{1,0:T(8,128)(2,1)S(1)}, u32[]{:S(2)}, u32[]{:S(2)}) %collective-permute-start.7) | collective-permute-done | bytes 147488 | tf_op jit(solution)/shard_map/ppermute | solution.py:442
  27.3 2.8 %routed.1 = (bf16[24,1024]{1,0:T(8,128)(2,1)S(1)}, bf16[24,1024]{1,0:T(8,128)(2,1)S(1)}, bf16[24,1024]{1,0:T(8,128)(2,1)S(1)}, bf16[24,1024]{1,0:T(8,128)(2,1)S(1)}, bf16[16,144,512]{2,1,0:T(8,128)(2,1)S(1)}) custom-call(s32[1]{0:T(128)} %bitcast.pos_ref, f32[1,4096]{1,0:T(1,128)} %bitcast.5, ...), custom_call_target="tpu_custom_call", output_to_operand_aliasing={{4}: (5, {})} | custom-call | tf_op jit(solution)/shard_map/routed/pallas_call | solution.py:513
  30.0 1.6 %collective-permute-start.8 = (bf16[24,1024]{1,0:T(8,128)(2,1)S(1)}, bf16[24,1024]{1,0:T(8,128)(2,1)S(1)}, u32[]{:S(2)}, u32[]{:S(2)}) collective-permute-start(bf16[24,1024]{1,0:T(8,128)(2,1)S(1)} %get-tuple-element.63), channel_id=1, source_target_pairs={{0,4},{1,5},{2,6},{3,7},{4,8},{5,9},{6,10},{7,11},{8,12},{9,13},{1... | collective-permute-start | bytes 147464 | tf_op jit(solution)/shard_map/ppermute | solution.py:442
  31.6 5.3 %collective-permute-start.9 = (bf16[24,1024]{1,0:T(8,128)(2,1)S(1)}, bf16[24,1024]{1,0:T(8,128)(2,1)S(1)}, u32[]{:S(2)}, u32[]{:S(2)}) collective-permute-start(bf16[24,1024]{1,0:T(8,128)(2,1)S(1)} %get-tuple-element.64), channel_id=1, source_target_pairs={{0,8},{1,9},{2,10},{3,11},{4,12},{5,13},{6,14},{7,15},{8,0},{9,1},... | collective-permute-start | bytes 147464 | tf_op jit(solution)/shard_map/ppermute | solution.py:442
  36.9 1.4 %collective-permute-start.10 = (bf16[24,1024]{1,0:T(8,128)(2,1)S(1)}, bf16[24,1024]{1,0:T(8,128)(2,1)S(1)}, u32[]{:S(2)}, u32[]{:S(2)}) collective-permute-start(bf16[24,1024]{1,0:T(8,128)(2,1)S(1)} %get-tuple-element.65), channel_id=1, source_target_pairs={{0,12},{1,13},{2,14},{3,15},{4,0},{5,1},{6,2},{7,3},{8,4},{9,5},{1... | collective-permute-start | bytes 147464 | tf_op jit(solution)/shard_map/ppermute | solution.py:442
  38.3 0.3 collective-permute-start.11
  38.6 3.9 %own.3 = (f32[128,1152]{1,0:T(8,128)S(1)}, f32[8,128]{1,0:T(8,128)S(1)}, bf16[4096,384]{1,0:T(8,128)(2,1)S(1)}, bf16[4096,384]{1,0:T(8,128)(2,1)S(1)}, bf16[384,4096]{1,0:T(8,128)(2,1)S(1)}) custom-call(s32[1]{0:T(128)} %bitcast.pos_ref, bf16[16,144,512]{2,1,0:T(8,128)(2,1)S(1)} %get-tuple-element.58.held, bf16[128,4096]{1,0:T(8,128)(2,1)S(1)} %copy-done, ...), custom_call_target="tpu_custom_call" | custom-call | flops 2000000000 | bytes 8000000 | tf_op jit(solution)/shard_map/own/pallas_call | solution.py:535
  42.4 0.0 collective-permute-done.8
  42.5 0.1 collective-permute-start.13
  42.6 1.8 %collective-permute-start.12 = (bf16[72,1024]{1,0:T(8,128)(2,1)S(1)}, bf16[72,1024]{1,0:T(8,128)(2,1)S(1)}, u32[]{:S(2)}, u32[]{:S(2)}) collective-permute-start(bf16[72,1024]{1,0:T(8,128)(2,1)S(1)} %constant_dynamic-update-slice_fusion.6.refs_1_), channel_id=1, source_target_pairs={{0,2},{1,3},{2,0},{3,1},{4,6},{5,7},{6,4},{7,5},{8,10},{9,11},{10,... | collective-permute-start | bytes 442376 | tf_op jit(solution)/shard_map/ppermute | solution.py:442
  44.4 1.6 %own.4 = (f32[128,896]{1,0:T(8,128)S(1)}, f32[8,128]{1,0:T(8,128)S(1)}) custom-call(s32[1]{0:T(128)} %bitcast.pos_ref, bf16[16,144,512]{2,1,0:T(8,128)(2,1)S(1)} %get-tuple-element.58.held, bf16[128,4096]{1,0:T(8,128)(2,1)S(1)} %copy-done, bf16[128,4096]{1,0:T(8,128)(2,1)S(1)} %copy-done.1, f32[8,128]{1,0:T(8,128)S(1)} %get-tuple-element.76._.refs_8_), custom_call_target="tpu_custom_call" | custom-call | flops 2000000000 | bytes 8000000 | tf_op jit(solution)/shard_map/own/pallas_call | solution.py:535
  46.0 2.0 %expert.2 = (bf16[96,1024]{1,0:T(8,128)(2,1)S(1)}, bf16[96,1024]{1,0:T(8,128)(2,1)S(1)}) custom-call(bf16[24,1024]{1,0:T(8,128)(2,1)S(1)} %get-tuple-element.59._.refs_0_, bf16[72,1024]{1,0:T(8,128)(2,1)S(1)} %constant_dynamic-update-slice_fusion.6.refs_1_, bf16[96,1024]{1,0:T(8,128)(2,1)S(1)} %collective-permute-done.13.refs_2_, ...), custom_call_target="tpu_custom_call" | custom-call | flops 600000000 | bytes 2000000 | tf_op jit(solution)/shard_map/expert/pallas_call | solution.py:575
  48.1 0.8 %collective-permute-done.12.refs_1_ = bf16[72,1024]{1,0:T(8,128)(2,1)S(1)} collective-permute-done((bf16[72,1024]{1,0:T(8,128)(2,1)S(1)}, bf16[72,1024]{1,0:T(8,128)(2,1)S(1)}, u32[]{:S(2)}, u32[]{:S(2)}) %collective-permute-start.12) | collective-permute-done | bytes 147488 | tf_op jit(solution)/shard_map/ppermute | solution.py:442
  48.9 0.1 collective-permute-start.14
  49.0 1.4 %collective-permute-done.14.refs_2_ = bf16[96,1024]{1,0:T(8,128)(2,1)S(1)} collective-permute-done((bf16[96,1024]{1,0:T(8,128)(2,1)S(1)}, bf16[96,1024]{1,0:T(8,128)(2,1)S(1)}, u32[]{:S(2)}, u32[]{:S(2)}) %collective-permute-start.14) | collective-permute-done | bytes 196640 | tf_op jit(solution)/shard_map/ppermute | solution.py:442
  50.4 2.0 %expert.3 = (bf16[96,1024]{1,0:T(8,128)(2,1)S(1)}, bf16[96,1024]{1,0:T(8,128)(2,1)S(1)}) custom-call(bf16[24,1024]{1,0:T(8,128)(2,1)S(1)} %collective-permute-done.11.refs_0_, bf16[72,1024]{1,0:T(8,128)(2,1)S(1)} %collective-permute-done.12.refs_1_, bf16[96,1024]{1,0:T(8,128)(2,1)S(1)} %collective-permute-done.14.refs_2_, ...), custom_call_target="tpu_custom_call" | custom-call | flops 600000000 | bytes 2000000 | tf_op jit(solution)/shard_map/expert/pallas_call | solution.py:575
  52.4 0.2 collective-permute-start.16
  52.6 1.3 %collective-permute-done.16 = bf16[96,1024]{1,0:T(8,128)(2,1)S(1)} collective-permute-done((bf16[96,1024]{1,0:T(8,128)(2,1)S(1)}, bf16[96,1024]{1,0:T(8,128)(2,1)S(1)}, u32[]{:S(2)}, u32[]{:S(2)}) %collective-permute-start.16) | collective-permute-done | bytes 196640 | tf_op jit(solution)/shard_map/ppermute | solution.py:442
  54.0 1.8 %collective-permute-start.17 = (bf16[96,1024]{1,0:T(8,128)(2,1)S(1)}, bf16[96,1024]{1,0:T(8,128)(2,1)S(1)}, u32[]{:S(2)}, u32[]{:S(2)}) collective-permute-start(bf16[96,1024]{1,0:T(8,128)(2,1)S(1)} %add_convert_fusion.1), channel_id=1, source_target_pairs={{0,2},{1,3},{2,0},{3,1},{4,6},{5,7},{6,4},{7,5},{8,10},{9,11},{10,... | collective-permute-start | bytes 589832 | tf_op jit(solution)/shard_map/ppermute | solution.py:442
  55.8 2.5 %own.5 = (f32[128,2048]{1,0:T(8,128)S(1)}, f32[8,128]{1,0:T(8,128)S(1)}) custom-call(s32[1]{0:T(128)} %bitcast.pos_ref, bf16[16,144,512]{2,1,0:T(8,128)(2,1)S(1)} %get-tuple-element.58.held, bf16[128,4096]{1,0:T(8,128)(2,1)S(1)} %copy-done, bf16[128,4096]{1,0:T(8,128)(2,1)S(1)} %copy-done.1, bf16[96,1024]{1,0:T(8,128)(2,1)S(1)} %get-tuple-element.81._), custom_call_target="tpu_custom_call" | custom-call | flops 2000000000 | bytes 8000000 | tf_op jit(solution)/shard_map/own/pallas_call | solution.py:535
  58.3 2.7 %collective-permute-done.17 = bf16[96,1024]{1,0:T(8,128)(2,1)S(1)} collective-permute-done((bf16[96,1024]{1,0:T(8,128)(2,1)S(1)}, bf16[96,1024]{1,0:T(8,128)(2,1)S(1)}, u32[]{:S(2)}, u32[]{:S(2)}) %collective-permute-start.17) | collective-permute-done | bytes 196640 | tf_op jit(solution)/shard_map/ppermute | solution.py:442
  61.0 0.1 add_convert_fusion
  61.1 1.5 %collective-permute-start.20 = (bf16[24,1024]{1,0:T(8,128)(2,1)S(1)}, bf16[24,1024]{1,0:T(8,128)(2,1)S(1)}, u32[]{:S(2)}, u32[]{:S(2)}) collective-permute-start(bf16[24,1024]{1,0:T(8,128)(2,1)S(1)} %get-tuple-element.89), channel_id=1, source_target_pairs={{0,4},{1,5},{2,6},{3,7},{4,8},{5,9},{6,10},{7,11},{8,12},{9,13},{1... | collective-permute-start | bytes 147464 | tf_op jit(solution)/shard_map/ppermute | solution.py:442
  62.7 0.8 %collective-permute-start.19 = (bf16[24,1024]{1,0:T(8,128)(2,1)S(1)}, bf16[24,1024]{1,0:T(8,128)(2,1)S(1)}, u32[]{:S(2)}, u32[]{:S(2)}) collective-permute-start(bf16[24,1024]{1,0:T(8,128)(2,1)S(1)} %get-tuple-element.90), channel_id=1, source_target_pairs={{0,8},{1,9},{2,10},{3,11},{4,12},{5,13},{6,14},{7,15},{8,0},{9,1},... | collective-permute-start | bytes 147464 | tf_op jit(solution)/shard_map/ppermute | solution.py:442
  63.4 1.7 %collective-permute-start.18 = (bf16[24,1024]{1,0:T(8,128)(2,1)S(1)}, bf16[24,1024]{1,0:T(8,128)(2,1)S(1)}, u32[]{:S(2)}, u32[]{:S(2)}) collective-permute-start(bf16[24,1024]{1,0:T(8,128)(2,1)S(1)} %get-tuple-element.91), channel_id=1, source_target_pairs={{0,12},{1,13},{2,14},{3,15},{4,0},{5,1},{6,2},{7,3},{8,4},{9,5},{1... | collective-permute-start | bytes 147464 | tf_op jit(solution)/shard_map/ppermute | solution.py:442
  65.1 2.4 %collective-permute-done.20.refs_6_ = bf16[24,1024]{1,0:T(8,128)(2,1)S(1)} collective-permute-done((bf16[24,1024]{1,0:T(8,128)(2,1)S(1)}, bf16[24,1024]{1,0:T(8,128)(2,1)S(1)}, u32[]{:S(2)}, u32[]{:S(2)}) %collective-permute-start.20) | collective-permute-done | bytes 49184 | tf_op jit(solution)/shard_map/ppermute | solution.py:442
  67.6 1.0 %collective-permute-done.19.refs_5_ = bf16[24,1024]{1,0:T(8,128)(2,1)S(1)} collective-permute-done((bf16[24,1024]{1,0:T(8,128)(2,1)S(1)}, bf16[24,1024]{1,0:T(8,128)(2,1)S(1)}, u32[]{:S(2)}, u32[]{:S(2)}) %collective-permute-start.19) | collective-permute-done | bytes 49184 | tf_op jit(solution)/shard_map/ppermute | solution.py:442
  68.6 1.4 %combine.1 = bf16[128,4096]{1,0:T(8,128)(2,1)} custom-call(bf16[128,64]{1,0:T(8,128)(2,1)S(1)} %get-tuple-element.47.mix_ref, f32[128,1152]{1,0:T(8,128)S(1)} %get-tuple-element.60.refs_0_, f32[128,896]{1,0:T(8,128)S(1)} %get-tuple-element.62.refs_1_, f32[128,2048]{1,0:T(8,128)S(1)} %get-tuple-element.82.refs_2_, ...), custom_call_target="tpu_custom_call" | custom-call | tf_op jit(solution)/shard_map/combine/pallas_call | solution.py:608
  (22 shorter events, 0.2 us)
Async XLA Ops:
  1.0 11.1 %collective-permute-start = (bf16[144,512]{1,0:T(8,128)(2,1)S(1)}, bf16[144,512]{1,0:T(8,128)(2,1)S(1)}, u32[]{:S(2)}, u32[]{:S(2)}) collective-permute-start(bf16[144,512]{1,0:T(8,128)(2,1)S(1)} %pack.1.refs_0_), channel_id=1, source_target_pairs={{0,4},{1,5},{2,6},{3,7},{4,8},{5,9},{6,10},{7,11},{8,12},{9,13},{1... | collective-permute-start | bytes 442376 | tf_op jit(solution)/shard_map/ppermute | solution.py:442
  4.1 16.3 %collective-permute-start.5 = (bf16[144,512]{1,0:T(8,128)(2,1)S(1)}, bf16[144,512]{1,0:T(8,128)(2,1)S(1)}, u32[]{:S(2)}, u32[]{:S(2)}) collective-permute-start(bf16[144,512]{1,0:T(8,128)(2,1)S(1)} %pack.1.refs_0_), channel_id=1, source_target_pairs={{0,0},{1,1},{2,12},{3,13},{4,4},{5,5},{6,6},{7,7},{8,8},{9,9},{10,... | collective-permute-start | bytes 442376 | tf_op jit(solution)/shard_map/ppermute | solution.py:442
  4.7 10.8 %collective-permute-start.2 = (bf16[144,512]{1,0:T(8,128)(2,1)S(1)}, bf16[144,512]{1,0:T(8,128)(2,1)S(1)}, u32[]{:S(2)}, u32[]{:S(2)}) collective-permute-start(bf16[144,512]{1,0:T(8,128)(2,1)S(1)} %pack.1.refs_0_), channel_id=1, source_target_pairs={{0,2},{1,3},{2,0},{3,1},{4,6},{5,7},{6,4},{7,5},{8,10},{9,11},{10,... | collective-permute-start | bytes 442376 | tf_op jit(solution)/shard_map/ppermute | solution.py:442
  9.5 10.8 %collective-permute-start.1 = (bf16[144,512]{1,0:T(8,128)(2,1)S(1)}, bf16[144,512]{1,0:T(8,128)(2,1)S(1)}, u32[]{:S(2)}, u32[]{:S(2)}) collective-permute-start(bf16[144,512]{1,0:T(8,128)(2,1)S(1)} %pack.1.refs_0_), channel_id=1, source_target_pairs={{0,8},{1,9},{2,10},{3,11},{4,12},{5,13},{6,14},{7,15},{8,0},{9,1},... | collective-permute-start | bytes 442376 | tf_op jit(solution)/shard_map/ppermute | solution.py:442
  12.1 8.3 %collective-permute-start.3 = (bf16[144,512]{1,0:T(8,128)(2,1)S(1)}, bf16[144,512]{1,0:T(8,128)(2,1)S(1)}, u32[]{:S(2)}, u32[]{:S(2)}) collective-permute-start(bf16[144,512]{1,0:T(8,128)(2,1)S(1)} %collective-permute-done.refs_1_), channel_id=1, source_target_pairs={{0,0},{1,1},{2,2},{3,3},{4,6},{5,7},{6,4},{7,5},{8,10},{9,11},{10,... | collective-permute-start | bytes 442376 | tf_op jit(solution)/shard_map/ppermute | solution.py:442
  20.4 18.2 %copy-start = (bf16[128,4096]{1,0:T(8,128)(2,1)S(1)}, bf16[128,4096]{1,0:T(8,128)(2,1)}, u32[]{:S(2)}) copy-start(bf16[128,4096]{1,0:T(8,128)(2,1)} %q_ref.5) | copy-start | bytes 3145732
  20.4 18.2 %copy-start.1 = (bf16[128,4096]{1,0:T(8,128)(2,1)S(1)}, bf16[128,4096]{1,0:T(8,128)(2,1)}, u32[]{:S(2)}) copy-start(bf16[128,4096]{1,0:T(8,128)(2,1)} %x_ref.5) | copy-start | bytes 3145732
  20.4 2.5 %collective-permute-start.6 = (bf16[864,512]{1,0:T(8,128)(2,1)S(1)}, bf16[864,512]{1,0:T(8,128)(2,1)S(1)}, u32[]{:S(2)}, u32[]{:S(2)}) collective-permute-start(bf16[864,512]{1,0:T(8,128)(2,1)S(1)} %constant_dynamic-update-slice_fusion), channel_id=1, source_target_pairs={{0,1},{1,0},{2,3},{3,2},{4,5},{5,4},{6,7},{7,6},{8,9},{9,8},{10,11... | collective-permute-start | bytes 2654216 | tf_op jit(solution)/shard_map/ppermute | solution.py:442
  20.5 5.3 %collective-permute-start.4 = (bf16[144,512]{1,0:T(8,128)(2,1)S(1)}, bf16[144,512]{1,0:T(8,128)(2,1)S(1)}, u32[]{:S(2)}, u32[]{:S(2)}) collective-permute-start(bf16[144,512]{1,0:T(8,128)(2,1)S(1)} %collective-permute-done.1.refs_2_), channel_id=1, source_target_pairs={{0,0},{1,1},{2,2},{3,3},{4,4},{5,5},{6,6},{7,7},{8,10},{9,11},{10,... | collective-permute-start | bytes 442376 | tf_op jit(solution)/shard_map/ppermute | solution.py:442
  25.8 1.4 %collective-permute-start.7 = (bf16[144,512]{1,0:T(8,128)(2,1)S(1)}, bf16[144,512]{1,0:T(8,128)(2,1)S(1)}, u32[]{:S(2)}, u32[]{:S(2)}) collective-permute-start(bf16[144,512]{1,0:T(8,128)(2,1)S(1)} %collective-permute-done.4.refs_0_), channel_id=1, source_target_pairs={{0,1},{1,0},{2,3},{3,2},{4,5},{5,4},{6,7},{7,6},{8,9},{9,8},{10,11... | collective-permute-start | bytes 442376 | tf_op jit(solution)/shard_map/ppermute | solution.py:442
  30.0 12.4 %collective-permute-start.8 = (bf16[24,1024]{1,0:T(8,128)(2,1)S(1)}, bf16[24,1024]{1,0:T(8,128)(2,1)S(1)}, u32[]{:S(2)}, u32[]{:S(2)}) collective-permute-start(bf16[24,1024]{1,0:T(8,128)(2,1)S(1)} %get-tuple-element.63), channel_id=1, source_target_pairs={{0,4},{1,5},{2,6},{3,7},{4,8},{5,9},{6,10},{7,11},{8,12},{9,13},{1... | collective-permute-start | bytes 147464 | tf_op jit(solution)/shard_map/ppermute | solution.py:442
  31.6 10.9 %collective-permute-start.9 = (bf16[24,1024]{1,0:T(8,128)(2,1)S(1)}, bf16[24,1024]{1,0:T(8,128)(2,1)S(1)}, u32[]{:S(2)}, u32[]{:S(2)}) collective-permute-start(bf16[24,1024]{1,0:T(8,128)(2,1)S(1)} %get-tuple-element.64), channel_id=1, source_target_pairs={{0,8},{1,9},{2,10},{3,11},{4,12},{5,13},{6,14},{7,15},{8,0},{9,1},... | collective-permute-start | bytes 147464 | tf_op jit(solution)/shard_map/ppermute | solution.py:442
  36.9 5.6 %collective-permute-start.10 = (bf16[24,1024]{1,0:T(8,128)(2,1)S(1)}, bf16[24,1024]{1,0:T(8,128)(2,1)S(1)}, u32[]{:S(2)}, u32[]{:S(2)}) collective-permute-start(bf16[24,1024]{1,0:T(8,128)(2,1)S(1)} %get-tuple-element.65), channel_id=1, source_target_pairs={{0,12},{1,13},{2,14},{3,15},{4,0},{5,1},{6,2},{7,3},{8,4},{9,5},{1... | collective-permute-start | bytes 147464 | tf_op jit(solution)/shard_map/ppermute | solution.py:442
  38.3 4.2 %collective-permute-start.11 = (bf16[24,1024]{1,0:T(8,128)(2,1)S(1)}, bf16[24,1024]{1,0:T(8,128)(2,1)S(1)}, u32[]{:S(2)}, u32[]{:S(2)}) collective-permute-start(bf16[24,1024]{1,0:T(8,128)(2,1)S(1)} %get-tuple-element.59._.refs_0_), channel_id=1, source_target_pairs={{0,2},{1,3},{2,0},{3,1},{4,6},{5,7},{6,4},{7,5},{8,10},{9,11},{10,... | collective-permute-start | bytes 147464 | tf_op jit(solution)/shard_map/ppermute | solution.py:442
  42.5 3.5 %collective-permute-start.13 = (bf16[96,1024]{1,0:T(8,128)(2,1)S(1)}, bf16[96,1024]{1,0:T(8,128)(2,1)S(1)}, u32[]{:S(2)}, u32[]{:S(2)}) collective-permute-start(bf16[96,1024]{1,0:T(8,128)(2,1)S(1)} %pad_maximum_fusion), channel_id=1, source_target_pairs={{0,1},{1,0},{2,3},{3,2},{4,5},{5,4},{6,7},{7,6},{8,9},{9,8},{10,11... | collective-permute-start | bytes 589832 | tf_op jit(solution)/shard_map/ppermute | solution.py:442
  42.6 6.3 %collective-permute-start.12 = (bf16[72,1024]{1,0:T(8,128)(2,1)S(1)}, bf16[72,1024]{1,0:T(8,128)(2,1)S(1)}, u32[]{:S(2)}, u32[]{:S(2)}) collective-permute-start(bf16[72,1024]{1,0:T(8,128)(2,1)S(1)} %constant_dynamic-update-slice_fusion.6.refs_1_), channel_id=1, source_target_pairs={{0,2},{1,3},{2,0},{3,1},{4,6},{5,7},{6,4},{7,5},{8,10},{9,11},{10,... | collective-permute-start | bytes 442376 | tf_op jit(solution)/shard_map/ppermute | solution.py:442
  48.9 1.5 %collective-permute-start.14 = (bf16[96,1024]{1,0:T(8,128)(2,1)S(1)}, bf16[96,1024]{1,0:T(8,128)(2,1)S(1)}, u32[]{:S(2)}, u32[]{:S(2)}) collective-permute-start(bf16[96,1024]{1,0:T(8,128)(2,1)S(1)} %pad_maximum_fusion.1), channel_id=1, source_target_pairs={{0,1},{1,0},{2,3},{3,2},{4,5},{5,4},{6,7},{7,6},{8,9},{9,8},{10,11... | collective-permute-start | bytes 589832 | tf_op jit(solution)/shard_map/ppermute | solution.py:442
  52.4 1.5 %collective-permute-start.16 = (bf16[96,1024]{1,0:T(8,128)(2,1)S(1)}, bf16[96,1024]{1,0:T(8,128)(2,1)S(1)}, u32[]{:S(2)}, u32[]{:S(2)}) collective-permute-start(bf16[96,1024]{1,0:T(8,128)(2,1)S(1)} %get-tuple-element.85), channel_id=1, source_target_pairs={{0,1},{1,0},{2,3},{3,2},{4,5},{5,4},{6,7},{7,6},{8,9},{9,8},{10,11... | collective-permute-start | bytes 589832 | tf_op jit(solution)/shard_map/ppermute | solution.py:442
  54.0 7.0 %collective-permute-start.17 = (bf16[96,1024]{1,0:T(8,128)(2,1)S(1)}, bf16[96,1024]{1,0:T(8,128)(2,1)S(1)}, u32[]{:S(2)}, u32[]{:S(2)}) collective-permute-start(bf16[96,1024]{1,0:T(8,128)(2,1)S(1)} %add_convert_fusion.1), channel_id=1, source_target_pairs={{0,2},{1,3},{2,0},{3,1},{4,6},{5,7},{6,4},{7,5},{8,10},{9,11},{10,... | collective-permute-start | bytes 589832 | tf_op jit(solution)/shard_map/ppermute | solution.py:442
  55.8 5.2 %collective-permute-start.15 = (bf16[96,1024]{1,0:T(8,128)(2,1)S(1)}, bf16[96,1024]{1,0:T(8,128)(2,1)S(1)}, u32[]{:S(2)}, u32[]{:S(2)}) collective-permute-start(bf16[96,1024]{1,0:T(8,128)(2,1)S(1)} %get-tuple-element.84), channel_id=1, source_target_pairs={{0,1},{1,0},{2,3},{3,2},{4,5},{5,4},{6,7},{7,6},{8,9},{9,8},{10,11... | collective-permute-start | bytes 589832 | tf_op jit(solution)/shard_map/ppermute | solution.py:442
  61.1 6.4 %collective-permute-start.20 = (bf16[24,1024]{1,0:T(8,128)(2,1)S(1)}, bf16[24,1024]{1,0:T(8,128)(2,1)S(1)}, u32[]{:S(2)}, u32[]{:S(2)}) collective-permute-start(bf16[24,1024]{1,0:T(8,128)(2,1)S(1)} %get-tuple-element.89), channel_id=1, source_target_pairs={{0,4},{1,5},{2,6},{3,7},{4,8},{5,9},{6,10},{7,11},{8,12},{9,13},{1... | collective-permute-start | bytes 147464 | tf_op jit(solution)/shard_map/ppermute | solution.py:442
  62.7 5.9 %collective-permute-start.19 = (bf16[24,1024]{1,0:T(8,128)(2,1)S(1)}, bf16[24,1024]{1,0:T(8,128)(2,1)S(1)}, u32[]{:S(2)}, u32[]{:S(2)}) collective-permute-start(bf16[24,1024]{1,0:T(8,128)(2,1)S(1)} %get-tuple-element.90), channel_id=1, source_target_pairs={{0,8},{1,9},{2,10},{3,11},{4,12},{5,13},{6,14},{7,15},{8,0},{9,1},... | collective-permute-start | bytes 147464 | tf_op jit(solution)/shard_map/ppermute | solution.py:442
  63.4 5.2 %collective-permute-start.18 = (bf16[24,1024]{1,0:T(8,128)(2,1)S(1)}, bf16[24,1024]{1,0:T(8,128)(2,1)S(1)}, u32[]{:S(2)}, u32[]{:S(2)}) collective-permute-start(bf16[24,1024]{1,0:T(8,128)(2,1)S(1)} %get-tuple-element.91), channel_id=1, source_target_pairs={{0,12},{1,13},{2,14},{3,15},{4,0},{5,1},{6,2},{7,3},{8,4},{9,5},{1... | collective-permute-start | bytes 147464 | tf_op jit(solution)/shard_map/ppermute | solution.py:442
